TPU v7x, 32 devices: a whole 2x2x4 slice. The times are simulated.
32 devices in a mesh: seq: 8 (over z, y), ch: 4 (over x, core).
Axes of the slice: x: 2, y: 2, z: 4, core: 2. Of those that a mesh axis runs over, the one named last changes fastest.
Arguments:
- streams: bfloat16 [2048, 3, 4096], P(('seq', 'ch')), may hold values from -6 to 6
- filter_taps: float32 [4096, 2048], P('ch', 'seq')
- skip_gain: float32 [4096], P('ch'), may hold values from -1 to 1
Outputs:
- mixed_out: bfloat16 [4096, 2048], P('ch', 'seq')
All inputs are finite; a program needn't handle non-finite values.
Results may differ from a plain program's by a relative error of at most 0.001.
Values may be sent and summed in bfloat16 or wider, within the bound.
No kernel may reach another device: no remote copies, remote signals or barrier semaphores. Data moves between devices by JAX's collectives and lax.ppermute only.
A program may use at most 128 MiB of HBM per device.

v0:
```python
import math

import jax
import jax.numpy as jnp
from jax import lax
from jax.sharding import PartitionSpec as P

PRECISE = lax.Precision.HIGHEST


def angles(left_index, right_index, period):
    product = left_index[:, None] * right_index[None, :] % period
    phase_angle = product.astype(jnp.float32) * (2.0 * math.pi / period)
    return (jnp.cos(phase_angle), jnp.sin(phase_angle))


def spectral_product(spec_re, spec_im):
    prod_re = spec_re[0] * spec_re[1] - spec_im[0] * spec_im[1]
    prod_im = spec_re[0] * spec_im[1] + spec_im[0] * spec_re[1]
    return (prod_re, prod_im)


def lanes_forward_blocks(blocks, offset, length_fft):
    block_count = blocks.shape[1]
    row_count = blocks.shape[2]
    j_range = jnp.arange(block_count, dtype=jnp.int32)
    k_range = jnp.arange(2 * block_count, dtype=jnp.int32)
    cos_blocks, sin_blocks = angles(j_range, k_range, 2 * block_count)
    real_part = jnp.einsum("sjmc,jk->skmc", blocks, cos_blocks, precision=PRECISE)
    imag_part = -jnp.einsum("sjmc,jk->skmc", blocks, sin_blocks, precision=PRECISE)
    m_global = offset + jnp.arange(row_count, dtype=jnp.int32)
    cos_twist, sin_twist = angles(k_range, m_global, length_fft)
    cos_twist = cos_twist[:, :, None]
    sin_twist = sin_twist[:, :, None]
    return (
        real_part * cos_twist + imag_part * sin_twist,
        imag_part * cos_twist - real_part * sin_twist,
    )


def lanes_forward_rows(real_part, imag_part):
    row_count = real_part.shape[2]
    indices = jnp.arange(row_count, dtype=jnp.int32)
    cos_rows, sin_rows = angles(indices, indices, row_count)
    spec_re = jnp.einsum("skrc,rq->skqc", real_part, cos_rows, precision=PRECISE) + jnp.einsum(
        "skrc,rq->skqc", imag_part, sin_rows, precision=PRECISE
    )
    spec_im = jnp.einsum("skrc,rq->skqc", imag_part, cos_rows, precision=PRECISE) - jnp.einsum(
        "skrc,rq->skqc", real_part, sin_rows, precision=PRECISE
    )
    return (spec_re, spec_im)


def lanes_inverse_rows(real_part, imag_part, k_global, length_fft):
    row_count = real_part.shape[1]
    indices = jnp.arange(row_count, dtype=jnp.int32)
    cos_rows, sin_rows = angles(indices, indices, row_count)
    back_re = jnp.einsum("kqc,qr->krc", real_part, cos_rows, precision=PRECISE) - jnp.einsum(
        "kqc,qr->krc", imag_part, sin_rows, precision=PRECISE
    )
    back_im = jnp.einsum("kqc,qr->krc", imag_part, cos_rows, precision=PRECISE) + jnp.einsum(
        "kqc,qr->krc", real_part, sin_rows, precision=PRECISE
    )
    cos_twist, sin_twist = angles(k_global, indices, length_fft)
    cos_twist = cos_twist[:, :, None]
    sin_twist = sin_twist[:, :, None]
    return (back_re * cos_twist - back_im * sin_twist, back_im * cos_twist + back_re * sin_twist)


def lanes_inverse_blocks(real_part, imag_part, keep_count, length_fft):
    double_count = real_part.shape[0]
    k_range = jnp.arange(double_count, dtype=jnp.int32)
    j_range = jnp.arange(keep_count, dtype=jnp.int32)
    cos_blocks, sin_blocks = angles(k_range, j_range, double_count)
    summed = jnp.einsum("kmc,kj->jmc", real_part, cos_blocks, precision=PRECISE) - jnp.einsum(
        "kmc,kj->jmc", imag_part, sin_blocks, precision=PRECISE
    )
    return summed * (1.0 / length_fft)


def body(streams, filter_taps, skip_gain):
    local_channels = filter_taps.shape[0]
    regrouped = lax.all_to_all(streams, "ch", split_axis=2, concat_axis=0, tiled=True)
    channel_major = jnp.transpose(regrouped, (2, 1, 0))
    queries = channel_major[:, 0, :].astype(jnp.float32)
    gated_values = channel_major[:, 1, :].astype(jnp.float32) * channel_major[:, 2, :].astype(
        jnp.float32
    )
    tok_count = gated_values.shape[1]
    groups = lax.axis_size("seq")
    length_fft = 2 * tok_count * groups
    block_len = tok_count // groups
    position = lax.axis_index("seq")
    gated_rows = regrouped[:, 1, :].astype(jnp.float32) * regrouped[:, 2, :].astype(jnp.float32)
    stacked_rows = jnp.stack([gated_rows, jnp.transpose(filter_taps)])
    columns = lax.all_to_all(
        stacked_rows.reshape(2, groups, block_len, local_channels),
        "seq",
        split_axis=1,
        concat_axis=1,
        tiled=True,
    )
    real_part, imag_part = lanes_forward_blocks(columns, position * block_len, length_fft)
    exchanged = lax.all_to_all(
        jnp.stack([real_part, imag_part]), "seq", split_axis=2, concat_axis=3, tiled=True
    )
    spec_re, spec_im = lanes_forward_rows(exchanged[0], exchanged[1])
    prod_re, prod_im = spectral_product(spec_re, spec_im)
    local_k = prod_re.shape[0]
    k_global = position * local_k + jnp.arange(local_k, dtype=jnp.int32)
    back_re, back_im = lanes_inverse_rows(prod_re, prod_im, k_global, length_fft)
    returned = lax.all_to_all(
        jnp.stack([back_re, back_im]), "seq", split_axis=2, concat_axis=1, tiled=True
    )
    inverted = lanes_inverse_blocks(returned[0], returned[1], groups, length_fft)
    convolved_rows = lax.all_to_all(
        inverted, "seq", split_axis=0, concat_axis=0, tiled=True
    ).reshape(tok_count, local_channels)
    convolved = jnp.transpose(convolved_rows)
    mixed_sum = convolved + skip_gain[:, None] * gated_values
    return (queries * mixed_sum).astype(jnp.bfloat16)


def solution(mesh):
    placed = (P(("seq", "ch"), None, None), P("ch", "seq"), P("ch"))
    return jax.shard_map(
        body, mesh=mesh, in_specs=placed, out_specs=P("ch", "seq"), check_vma=False
    )
```

profile of v0, /device:TPU:0, one launch (start us, length us, event | category | flops | bytes accessed | tf_op | source)
XLA Modules:
  0.0 494.8 jit_solution(18345395431546210625)
XLA Ops:
  0.0 6.4 %copy.28 = bf16[64,3,4096]{0,1,2:T(4,128)(2,1)} copy(bf16[64,3,4096]{2,0,1:T(8,128)(2,1)} %param.3) | data formatting | bytes 3145728 | tf_op args[0]
  6.4 5.5 %reshape.183 = bf16[4,2,98304]{2,1,0:T(2,128)(2,1)} reshape(bf16[4096,3,64]{2,1,0:T(4,128)(2,1)} %bitcast.152) | data formatting | bytes 3145728
  11.9 4.2 all-to-all-start
  17.6 18.5 %all-to-all-done = bf16[4,2,98304]{2,1,0:T(2,128)(2,1)S(1)} async-done(((bf16[4,2,98304]{2,1,0:T(2,128)(2,1)}), bf16[4,2,98304]{2,1,0:T(2,128)(2,1)S(1)}, u32[]{:S(2)}, u32[]{:S(2)}) %all-to-all-start) | async-done | bytes 1572896 | tf_op jit(solution)/shard_map/all_to_all | solution.py:83
  36.2 3.8 reshape.184
  40.0 5.4 %copy.30 = bf16[4,64,3,1024]{3,1,0,2:T(8,128)(2,1)S(1)} copy(bf16[4,64,3,1024]{1,2,3,0:T(4,128)(2,1)} %bitcast.150) | data formatting | bytes 3145728 | tf_op jit(solution)/shard_map/all_to_all | solution.py:83
  48.1 6.8 %all-to-all-start.1 = ((f32[2,8,32,1024]{3,2,0,1:T(8,128)}), f32[2,8,32,1024]{3,2,0,1:T(8,128)S(1)}, u32[]{:S(2)}, u32[]{:S(2)}) async-start(f32[2,8,32,1024]{3,2,0,1:T(8,128)} %copy.32), calls=%async_computation.1 | async-start | bytes 4194304 | tf_op jit(solution)/shard_map/all_to_all | solution.py:96
  55.0 47.7 %all-to-all-done.1 = f32[2,8,32,1024]{3,2,0,1:T(8,128)S(1)} async-done(((f32[2,8,32,1024]{3,2,0,1:T(8,128)}), f32[2,8,32,1024]{3,2,0,1:T(8,128)S(1)}, u32[]{:S(2)}, u32[]{:S(2)}) %all-to-all-start.1) | async-done | bytes 2097184 | tf_op jit(solution)/shard_map/all_to_all | solution.py:96
  102.7 4.3 fusion.12
  107.0 5.3 %add_bitcast_fusion.1 = (f32[1,2,16,32,1024]{4,2,3,1,0:T(8,128)S(1)}, f32[1,2,16,32,1024]{4,2,3,1,0:T(8,128)S(1)}) fusion(f32[16,2,32,1024]{3,0,2,1:T(8,128)S(1)} %fusion.12, f32[16,32]{0,1:T(8,128)S(1)} %get-tuple-element.18, f32[16,32]{0,1:T(8,128)S(1)} %get-tuple-element.17, f32[2,8,32,1024]{3,2,0,1:T(8,128)S(1)} %all-to-all-done.1), kind=kOutput, calls=%fused_computation.7 | convolution fusion | flops 108005120 | bytes 14684160 | tf_op jit(solution)/shard_map/sjmc,jk->skmc/dot_general | solution.py:29
  114.0 8.6 %copy.35 = f32[2,2,16,32,1024]{4,3,1,0,2:T(8,128)} copy(f32[2,2,16,32,1024]{4,2,3,1,0:T(8,128)S(1)} %pad_maximum_fusion) | data formatting | bytes 16777216 | tf_op jit(solution)/shard_map/stack | solution.py:105
  122.5 5.0 %all-to-all-start.2 = ((f32[2,2,16,32,1024]{4,3,1,0,2:T(8,128)}), f32[2,2,16,32,1024]{4,3,1,0,2:T(8,128)}, u32[]{:S(2)}, u32[]{:S(2)}) async-start(f32[2,2,16,32,1024]{4,3,1,0,2:T(8,128)} %copy.35), calls=%async_computation.2 | async-start | bytes 16777216 | tf_op jit(solution)/shard_map/all_to_all | solution.py:104
  127.7 181.9 %all-to-all-done.2 = f32[2,2,16,32,1024]{4,3,1,0,2:T(8,128)} async-done(((f32[2,2,16,32,1024]{4,3,1,0,2:T(8,128)}), f32[2,2,16,32,1024]{4,3,1,0,2:T(8,128)}, u32[]{:S(2)}, u32[]{:S(2)}) %all-to-all-start.2) | async-done | bytes 8388640 | tf_op jit(solution)/shard_map/all_to_all | solution.py:104
  309.5 4.2 copy.55
  315.4 4.8 fusion.34
  320.2 4.8 fusion.32
  325.0 5.4 %add_bitcast_fusion = f32[2,2,256,1024]{3,2,1,0:T(8,128)S(1)} fusion(f32[256,2,2,1024]{3,0,2,1:T(8,128)S(1)} %fusion.34, f32[2,2,256,1024]{3,2,1,0:T(8,128)S(1)} %bitcast.147), kind=kOutput, calls=%fused_computation.5 | convolution fusion | flops 3223191552 | bytes 12582912 | tf_op jit(solution)/shard_map/skrc,rq->skqc/dot_general | solution.py:45
  330.4 5.2 %subtract_bitcast_fusion = f32[2,2,256,1024]{3,2,1,0:T(8,128)S(1)} fusion(f32[256,2,2,1024]{3,0,2,1:T(8,128)S(1)} %fusion.32, f32[2,2,256,1024]{3,2,1,0:T(8,128)S(1)} %bitcast.145), kind=kOutput, calls=%fused_computation.4 | convolution fusion | flops 3223191552 | bytes 12582912 | tf_op jit(solution)/shard_map/skrc,rq->skqc/dot_general | solution.py:48
  336.6 3.1 fusion.6
  345.6 3.5 fusion.1
  349.4 3.5 copy.37
  352.9 96.9 %all_to_all.58 = f32[2,2,256,1024]{3,1,0,2:T(2,128)S(1)} all-to-all(f32[2,2,256,1024]{3,1,0,2:T(2,128)S(1)} %copy.37), channel_id=1, replica_groups=mesh['seq'=8,'ch'=4] {'seq'}, dimensions={2} | all-to-all | bytes 8388608 | tf_op jit(solution)/shard_map/all_to_all | solution.py:112
  452.4 3.4 fusion.138
  464.1 28.9 %all_to_all.59 = f32[8,32,1024]{2,1,0:T(8,128)S(1)} all-to-all(f32[8,32,1024]{2,1,0:T(8,128)S(1)} %copy.39), channel_id=1, replica_groups=mesh['seq'=8,'ch'=4] {'seq'}, dimensions={0} | all-to-all | bytes 2097152 | tf_op jit(solution)/shard_map/all_to_all | solution.py:116
  (28 shorter events, 27.1 us)
Async XLA Ops:
  11.9 24.3 %all-to-all-start = ((bf16[4,2,98304]{2,1,0:T(2,128)(2,1)}), bf16[4,2,98304]{2,1,0:T(2,128)(2,1)S(1)}, u32[]{:S(2)}, u32[]{:S(2)}) async-start(bf16[4,2,98304]{2,1,0:T(2,128)(2,1)} %reshape.183), calls=%async_computation | async-start | bytes 3145728 | tf_op jit(solution)/shard_map/all_to_all | solution.py:83
  45.4 1.2 copy-start
  48.1 54.6 %all-to-all-start.1 = ((f32[2,8,32,1024]{3,2,0,1:T(8,128)}), f32[2,8,32,1024]{3,2,0,1:T(8,128)S(1)}, u32[]{:S(2)}, u32[]{:S(2)}) async-start(f32[2,8,32,1024]{3,2,0,1:T(8,128)} %copy.32), calls=%async_computation.1 | async-start | bytes 4194304 | tf_op jit(solution)/shard_map/all_to_all | solution.py:96
  122.5 187.0 %all-to-all-start.2 = ((f32[2,2,16,32,1024]{4,3,1,0,2:T(8,128)}), f32[2,2,16,32,1024]{4,3,1,0,2:T(8,128)}, u32[]{:S(2)}, u32[]{:S(2)}) async-start(f32[2,2,16,32,1024]{4,3,1,0,2:T(8,128)} %copy.35), calls=%async_computation.2 | async-start | bytes 16777216 | tf_op jit(solution)/shard_map/all_to_all | solution.py:104
  463.5 29.5 %copy-start.1 = (bf16[4,64,3,1024]{3,1,0,2:T(8,128)(2,1)S(1)}, bf16[4,64,3,1024]{3,1,0,2:T(8,128)(2,1)}, u32[]{:S(2)}) copy-start(bf16[4,64,3,1024]{3,1,0,2:T(8,128)(2,1)} %copy-done) | copy-start | bytes 4718596
  463.5 29.5 %copy-start.2 = (f32[1024]{0:T(1024)S(1)}, f32[1024]{0:T(1024)}, u32[]{:S(2)}) copy-start(f32[1024]{0:T(1024)} %param.5) | copy-start | bytes 12292
where the time goes:
time: 498 us; the launch traced here: 495 us
  waiting for transfers between devices  248 us (50%)
  blocking collectives  126 us (25%)
  local copies, waits for them, and re-layouts  55.8 us (11%)
  matrix products  44.5 us (9%)
  starting transfers between devices  16 us (3%)
    all_to_all x1, waiting for transfers between devices, body(): lax.all_to_all(jnp.stack([real_part, imag_part]), 'seq', split_axis=2, co...  182 us
    all_to_all x1, blocking collectives, body(): lax.all_to_all(jnp.stack([back_re, back_im]), 'seq', split_axis=2, concat...  96.9 us
    all_to_all x1, waiting for transfers between devices, body(): lax.all_to_all(stacked_rows.reshape(2, groups, block_len, local_channels)...  47.7 us
    all_to_all x1, blocking collectives, body(): lax.all_to_all(inverted, 'seq', split_axis=0, concat_axis=0, tiled=True)  28.9 us
    all_to_all x1, waiting for transfers between devices, body(): lax.all_to_all(streams, 'ch', split_axis=2, concat_axis=0, tiled=True)  18.5 us
    unnamed x10, local copies, waits for them, and re-layouts  18 us
  transfers between devices with their start and end apart: 3, of which 3 were waited for; matrix products, arithmetic and copies ran while one was open for 0% of the time, Pallas kernels for 0%

commit v1 on v0

v1 whole, which is shorter than its diff:
```python
import functools
import math

import jax
import jax.numpy as jnp
import numpy as np
from jax import lax
from jax.experimental import pallas as pl
from jax.experimental.pallas import tpu as pltpu
from jax.sharding import PartitionSpec as P

TOP = 32000.0
TOP_LEVEL = 32255.0
LOW_POWER = 125.0
EXPONENT_BITS = 8
EXPONENT_BIAS = 127.0
LANES = 128
ROW = 256
CHUNK = 16
HALF = 64
VMEM_BYTES = 24 * 1024 * 1024
SMALL_BYTES = 12 * 1024 * 1024


def split_first(values, axis):
    count = min(values.shape[axis], LANES if axis == values.ndim - 1 else EXPONENT_BITS)
    first = lax.slice_in_dim(values, 0, count, axis=axis)
    if count == values.shape[axis]:
        return first, None
    return first, lax.slice_in_dim(values, count, values.shape[axis], axis=axis)


def encode(values, axis):
    size = jnp.abs(values)
    peak = jnp.max(size, axis=axis, keepdims=True)
    power = jnp.floor(jnp.log(jnp.maximum(peak, 1e-30)) * (1.0 / math.log(2.0))) + 1.0
    power = jnp.clip(power, -100.0, 126.0)
    share = size * jnp.exp2(-power)
    level = jnp.minimum(
        share * (2.0 * TOP), jnp.minimum(share * TOP + TOP / 4, share * (TOP / 2) + TOP / 2)
    )
    first, rest = split_first(level, axis)
    place = lax.broadcasted_iota(jnp.int32, first.shape, axis).astype(jnp.float32)
    halves = jnp.floor((power + (EXPONENT_BIAS + 0.25)) * jnp.exp2(-place))
    bit = halves - 2.0 * jnp.floor(halves * 0.5)
    marked = 2.0 * jnp.floor((first - bit) * 0.5 + 0.5) + bit
    level = jnp.where(place < EXPONENT_BITS, marked, jnp.floor(first + 0.5))
    if rest is not None:
        level = jnp.concatenate([level, jnp.floor(rest + 0.5)], axis=axis)
    level = jnp.minimum(level, TOP_LEVEL) * (1.0 / 128.0)
    octave = jnp.floor(level)
    code = jnp.exp2(octave - LOW_POWER) * (level - octave + 1.0)
    return jnp.where(values < 0.0, -code, code).astype(jnp.bfloat16)


def decode(code, axis):
    code = code.astype(jnp.float32)
    size = jnp.abs(code)
    octave = jnp.floor(jnp.log(size) * (1.0 / math.log(2.0)) + 0.002)
    level = (octave + size * jnp.exp2(-octave) + (LOW_POWER - 1.0)) * 128.0
    first, _ = split_first(level, axis)
    first = jnp.floor(first + 0.5)
    place = lax.broadcasted_iota(jnp.int32, first.shape, axis).astype(jnp.float32)
    bit = first - 2.0 * jnp.floor(first * 0.5)
    held = jnp.where(place < EXPONENT_BITS, bit * jnp.exp2(place), 0.0)
    scale = jnp.exp2(jnp.sum(held, axis=axis, keepdims=True) - EXPONENT_BIAS)
    share = jnp.maximum(
        level * (0.5 / TOP),
        jnp.maximum(level * (1.0 / TOP) - 0.25, level * (2.0 / TOP) - 1.0),
    )
    return jnp.where(code < 0.0, -share, share) * scale


def tables(blocks):
    n2 = np.arange(ROW)
    k1 = np.arange(blocks)
    main = 2.0 * np.pi * np.outer(n2, n2) / ROW
    wave = np.concatenate([np.cos(main), np.sin(main)], axis=1).astype(np.float32)
    high = wave.astype(jnp.bfloat16)
    low = (wave - high.astype(np.float32)).astype(jnp.bfloat16)
    twist = 2.0 * np.pi * np.outer(k1 + 0.25, n2) / (blocks * ROW)
    mix = 2.0 * np.pi * np.outer(k1 + 0.25, np.arange(blocks)) / blocks
    twist = np.stack([np.cos(twist), np.sin(twist)], axis=1).astype(np.float32)
    mix = np.stack([np.cos(mix), np.sin(mix)], axis=0).astype(np.float32)
    return high, low, twist, mix


def put_split(ref, at, values):
    high = values.astype(jnp.bfloat16)
    ref[pl.ds(at, values.shape[0]), 0:ROW] = high
    ref[pl.ds(at, values.shape[0]), ROW : 2 * ROW] = high
    ref[pl.ds(at, values.shape[0]), 2 * ROW : 3 * ROW] = (
        values - high.astype(jnp.float32)
    ).astype(jnp.bfloat16)


def weighted(pairs):
    total = None
    for value, weight in pairs:
        term = value * float(weight)
        total = term if total is None else total + term
    return total


def mix_forward(blocks_in, twist_ref, mix, at, ref):
    half = len(blocks_in) // 2
    for k1 in range(half):
        sums = []
        for start in (0, 1):
            taken = [(blocks_in[n1], mix[:, k1, n1]) for n1 in range(start, 2 * half, 2)]
            sums.append(weighted([(value, weight[0]) for value, weight in taken]))
            sums.append(weighted([(value, -weight[1]) for value, weight in taken]))
        even_re, even_im, odd_re, odd_im = sums
        for k, re, im in (
            (k1, even_re + odd_re, even_im + odd_im),
            (k1 + half, even_re - odd_re, even_im - odd_im),
        ):
            cos_twist, sin_twist = twist_ref[k, 0:1, :], twist_ref[k, 1:2, :]
            put_split(ref, 2 * k * HALF + at, re * cos_twist + im * sin_twist)
            put_split(ref, (2 * k + 1) * HALF + at, im * cos_twist - re * sin_twist)


def mix_back(spectra, twist_ref, mix):
    half = len(spectra) // 2
    turned = []
    for k, (re, im) in enumerate(spectra):
        cos_twist, sin_twist = twist_ref[k, 0:1, :], twist_ref[k, 1:2, :]
        turned.append((re * cos_twist - im * sin_twist, im * cos_twist + re * sin_twist))
    totals = [None] * (2 * half)
    for k1 in range(half):
        (re, im), (other_re, other_im) = turned[k1], turned[k1 + half]
        both = ((re + other_re, im + other_im), (re - other_re, im - other_im))
        for n1 in range(2 * half):
            re, im = both[n1 % 2]
            term = weighted([(re, mix[0, k1, n1]), (im, -mix[1, k1, n1])])
            totals[n1] = term if totals[n1] is None else totals[n1] + term
    return totals


def spectrum_rows(waves_ref, k, at):
    re = waves_ref[pl.ds(2 * k * HALF + at, CHUNK), :]
    im = waves_ref[pl.ds((2 * k + 1) * HALF + at, CHUNK), :]
    return re, im


def send_kernel(streams_ref, gated_ref, *query_refs):
    me, step = lax.axis_index("ch"), pl.program_id(0)
    for turn, query_ref in enumerate(query_refs):

        @pl.when(step == me ^ turn)
        def _():
            query_ref[...] = streams_ref[0]

    for block in range(gated_ref.shape[0]):
        lanes = slice(block * LANES, (block + 1) * LANES)
        keys = streams_ref[1, :, lanes].astype(jnp.float32)
        values = streams_ref[2, :, lanes].astype(jnp.float32)
        gated_ref[block, 0] = encode(keys * values, 0)


def taps_kernel(taps_ref, skip_ref, *code_refs):
    me = lax.axis_index("seq")
    first = (me == 0).astype(jnp.float32)
    row = lax.broadcasted_iota(jnp.int32, (LANES, LANES), 0)
    lane = lax.broadcasted_iota(jnp.int32, (LANES, LANES), 1)
    for turn, code_ref in enumerate(code_refs):
        block = me ^ turn
        gains = jnp.broadcast_to(skip_ref[pl.ds(block, 1), :], (LANES, LANES))
        gain = jnp.sum(jnp.where(row == lane, gains, 0.0), axis=1, keepdims=True) * first
        start = taps_ref[block, :, :LANES] + jnp.where(lane == 0, gain, 0.0)
        taps = jnp.concatenate([start, taps_ref[block, :, LANES:]], axis=1)
        code_ref[...] = encode(taps, 1)


def conv_kernel(mix, gated_ref, *refs):
    blocks = len(mix[0])
    wave_ref, twist_ref, out_ref, u, codes, *scratch = refs[blocks:]
    rows, u_waves, h_waves = scratch[0:2], scratch[2:4], scratch[4:6]
    me = lax.axis_index("seq")
    parts = ROW // gated_ref.shape[1]
    for turn, code_ref in enumerate(refs[:blocks]):
        codes[me ^ turn] = code_ref[...]

    def unpack(block):
        pieces = [decode(gated_ref[block * parts + part], 0) for part in range(parts)]
        u[block] = jnp.transpose(jnp.concatenate(pieces, axis=0))

    def forward_taps(half, at):
        start = pl.ds(half * HALF + at, CHUNK)
        taken = [decode(codes[n1, start, :], 1) for n1 in range(blocks)]
        mix_forward(taken, twist_ref, mix, at, rows[half])

    def forward_gated(half, at):
        start = pl.ds(half * HALF + at, CHUNK)
        mix_forward([u[n1, start, :] for n1 in range(blocks)], twist_ref, mix, at, rows[half])

    def product(half, at):
        for k in range(blocks):
            re, im = spectrum_rows(u_waves[half], k, at)
            re, im = re[:, :ROW] + im[:, ROW:], im[:, :ROW] - re[:, ROW:]
            taps_re, taps_im = spectrum_rows(h_waves[half], k, at)
            taps_re, taps_im = (
                taps_re[:, :ROW] + taps_im[:, ROW:],
                taps_im[:, :ROW] - taps_re[:, ROW:],
            )
            put_split(rows[half], 2 * k * HALF + at, re * taps_re - im * taps_im)
            put_split(rows[half], (2 * k + 1) * HALF + at, re * taps_im + im * taps_re)

    def back(half, at):
        spectra = []
        for k in range(blocks):
            re, im = spectrum_rows(u_waves[half], k, at)
            spectra.append((re[:, :ROW] - im[:, ROW:], im[:, :ROW] + re[:, ROW:]))
        start = pl.ds(half * HALF + at, CHUNK)
        for n1, total in enumerate(mix_back(spectra, twist_ref, mix)):
            out_ref[n1, start, :] = encode(total * (1.0 / (blocks * ROW)), 1)

    def stage(source, target, work, half, more=None):
        steps = 2
        count = rows[0].shape[0] // steps
        chunks = HALF // CHUNK // steps

        def step(index, _):
            if source is not None:
                at = pl.ds(pl.multiple_of(index * count, count), count)
                target[at, :] = jnp.dot(
                    source[at, :], wave_ref[...], preferred_element_type=jnp.float32
                )
            for chunk in range(chunks):
                work(half, pl.multiple_of((index * chunks + chunk) * CHUNK, CHUNK))
            for block in range(blocks // steps if more else 0):
                more(index * (blocks // steps) + block)
            return 0

        lax.fori_loop(0, steps, step, 0)

    stage(None, None, forward_taps, 0)
    stage(rows[0], h_waves[0], forward_taps, 1, unpack)
    stage(rows[1], h_waves[1], forward_gated, 0)
    stage(rows[0], u_waves[0], forward_gated, 1)
    stage(rows[1], u_waves[1], product, 0)
    stage(rows[0], u_waves[0], product, 1)
    stage(rows[1], u_waves[1], back, 0)
    stage(None, None, back, 1)


def turn_kernel(*refs):
    query_refs, out_ref, whole = refs[:-2], refs[-2], refs[-1]
    me = lax.axis_index("ch")
    held = query_refs[0].shape[0]
    for turn, query_ref in enumerate(query_refs):
        at = pl.multiple_of((me ^ turn) * held, held)
        whole[pl.ds(at, held), :] = query_ref[...].astype(jnp.float32)
    out_ref[...] = jnp.transpose(whole[...]).astype(jnp.bfloat16)


def mix_kernel(query_ref, conv_ref, out_ref):
    for block in range(conv_ref.shape[0]):
        at = slice(block * LANES, (block + 1) * LANES)
        queries = query_ref[at, :].astype(jnp.float32)
        out_ref[at, :] = (queries * decode(conv_ref[block], 1)).astype(jnp.bfloat16)


def plain_conv(gated, taps):
    blocks = gated.shape[0]
    high, low, twist, mix = tables(blocks)
    wave = jnp.asarray(high, jnp.float32) + jnp.asarray(low, jnp.float32)
    cos_twist, sin_twist = twist[:, 0][:, None, :], twist[:, 1][:, None, :]
    dot = functools.partial(jnp.einsum, precision=lax.Precision.HIGHEST)

    def forward(values):
        re = dot("ncm,kn->kcm", values, mix[0])
        im = -dot("ncm,kn->kcm", values, mix[1])
        re, im = re * cos_twist + im * sin_twist, im * cos_twist - re * sin_twist
        re, im = dot("kcm,mq->kcq", re, wave), dot("kcm,mq->kcq", im, wave)
        return re[..., :ROW] + im[..., ROW:], im[..., :ROW] - re[..., ROW:]

    u_re, u_im = forward(gated)
    h_re, h_im = forward(taps)
    re = dot("kcm,mq->kcq", u_re * h_re - u_im * h_im, wave)
    im = dot("kcm,mq->kcq", u_re * h_im + u_im * h_re, wave)
    re, im = re[..., :ROW] - im[..., ROW:], im[..., :ROW] + re[..., ROW:]
    re, im = re * cos_twist - im * sin_twist, im * cos_twist + re * sin_twist
    total = dot("kcm,kn->ncm", re, mix[0]) - dot("kcm,kn->ncm", im, mix[1])
    return total * (1.0 / (blocks * ROW))


def scatter(blocks, axis):
    count = len(blocks)
    return [
        lax.ppermute(block, axis, [(i, i ^ turn) for i in range(count)]) if turn else block
        for turn, block in enumerate(blocks)
    ]


def body(streams, filter_taps, skip_gain):
    groups, parts = lax.axis_size("seq"), lax.axis_size("ch")
    held, _, channels = streams.shape
    wide = channels // parts
    own = wide // groups
    blocks = filter_taps.shape[1] * groups // ROW
    streams = jnp.transpose(streams, (1, 0, 2))
    fits = own == LANES and filter_taps.shape[1] == ROW and ROW % held == 0 and groups % 4 == 0
    fits = fits and groups & (groups - 1) == 0 and parts & (parts - 1) == 0
    small = pltpu.CompilerParams(vmem_limit_bytes=SMALL_BYTES)
    if fits:
        gated, *queries = pl.pallas_call(
            send_kernel,
            grid=(parts,),
            in_specs=[pl.BlockSpec((3, held, wide), lambda g: (0, 0, g))],
            out_specs=[
                pl.BlockSpec((groups, 1, held, own), lambda g: (0, g, 0, 0)),
            ]
            + [pl.BlockSpec((held, wide), lambda g: (0, 0))] * parts,
            out_shape=[
                jax.ShapeDtypeStruct((groups, parts, held, own), jnp.bfloat16),
            ]
            + [jax.ShapeDtypeStruct((held, wide), jnp.bfloat16)] * parts,
            cost_estimate=cost(2**25, 2**23),
            compiler_params=small,
            name="encode_gated",
        )(streams)
        taps = pl.pallas_call(
            taps_kernel,
            out_shape=[jax.ShapeDtypeStruct((own, ROW), jnp.bfloat16)] * groups,
            compiler_params=small,
            cost_estimate=cost(2**25, 2**23),
            name="encode_taps",
        )(filter_taps.reshape(groups, own, ROW), skip_gain.reshape(groups, own))
    else:
        gated = encode(streams[1].astype(jnp.float32) * streams[2].astype(jnp.float32), 0)
        gated = jnp.transpose(gated.reshape(held, parts, groups, own), (2, 1, 0, 3))
        queries = jnp.transpose(streams[0].reshape(held, parts, wide), (1, 0, 2))
        first = lax.axis_index("seq") == 0
        taps = filter_taps.at[:, 0].add(jnp.where(first, skip_gain, 0.0))
        taps = encode(taps, 1).reshape(groups, own, -1)
    exchange = functools.partial(lax.all_to_all, split_axis=0, concat_axis=0, tiled=True)
    gated = gated.reshape(groups * parts, held, own)
    if fits:
        taps = scatter(taps, "seq")
        gated = exchange(gated, ("seq", "ch"))
        queries = scatter(queries, "ch")
    else:
        taps = exchange(taps, "seq")
        gated = exchange(gated, ("seq", "ch"))
        queries = exchange(queries, "ch").reshape(parts * held, wide)
    if fits:
        high, low, twist, mix = tables(blocks)
        wave = np.concatenate([high, low, high], axis=0)
        convolved = pl.pallas_call(
            functools.partial(conv_kernel, mix),
            out_shape=jax.ShapeDtypeStruct((blocks, own, ROW), jnp.bfloat16),
            scratch_shapes=[
                pltpu.VMEM((blocks, own, ROW), jnp.float32),
                pltpu.VMEM((blocks, own, ROW), jnp.bfloat16),
            ]
            + [pltpu.VMEM((blocks * 2 * HALF, 3 * ROW), jnp.bfloat16)] * 2
            + [pltpu.VMEM((blocks * 2 * HALF, 2 * ROW), jnp.float32)] * 4,
            compiler_params=pltpu.CompilerParams(vmem_limit_bytes=VMEM_BYTES),
            cost_estimate=cost(2**32, 2**24),
            name="convolve",
        )(gated, *taps, wave, twist)
    else:
        gated = decode(gated, 1).reshape(blocks, ROW, own)
        taps = jnp.transpose(decode(taps, 2), (1, 0, 2)).reshape(own, blocks, ROW)
        convolved = plain_conv(jnp.transpose(gated, (0, 2, 1)), jnp.transpose(taps, (1, 0, 2)))
        convolved = jnp.transpose(convolved, (1, 0, 2)).reshape(own, groups, -1)
        convolved = encode(jnp.transpose(convolved, (1, 0, 2)), 2)
    convolved = exchange(convolved, "seq")
    if fits:
        queries = pl.pallas_call(
            turn_kernel,
            out_shape=jax.ShapeDtypeStruct((wide, ROW), jnp.bfloat16),
            scratch_shapes=[pltpu.VMEM((ROW, wide), jnp.float32)],
            compiler_params=small,
            cost_estimate=cost(2**20, 2**21),
            name="turn_queries",
        )(*queries)
        return pl.pallas_call(
            mix_kernel,
            grid=(4,),
            in_specs=[
                pl.BlockSpec((wide // 4, ROW), lambda i: (i, 0)),
                pl.BlockSpec((groups // 4, own, ROW), lambda i: (i, 0, 0)),
            ],
            out_specs=pl.BlockSpec((wide // 4, ROW), lambda i: (i, 0)),
            out_shape=jax.ShapeDtypeStruct((wide, ROW), jnp.bfloat16),
            compiler_params=small,
            name="mix_out",
        )(queries, convolved)
    queries = jnp.transpose(queries.astype(jnp.float32))
    return (queries * decode(convolved, 2).reshape(wide, -1)).astype(jnp.bfloat16)


def cost(flops, moved):
    return pl.CostEstimate(flops=int(flops), bytes_accessed=int(moved), transcendentals=0)


def solution(mesh):
    placed = (P(("seq", "ch"), None, None), P("ch", "seq"), P("ch"))
    return jax.shard_map(
        body, mesh=mesh, in_specs=placed, out_specs=P("ch", "seq"), check_vma=False
    )
```

time: 498 us -> 69.8 us (0.14)
  waiting for transfers between devices: 248 us -> 21.7 us
  blocking collectives: 126 us -> 0 us
  local copies, waits for them, and re-layouts: 55.8 us -> 1.42 us
  matrix products: 44.5 us -> 0 us
  Pallas kernels: 0 us -> 19 us
  starting transfers between devices: 16 us -> 27.3 us
    all_to_all x3 -> x2, waiting for transfers between devices: 248 us -> 6.03 us  [the longest x1 6.03 us: body(): convolved = exchange(convolved, 'seq')]
    all_to_all x2 -> x0, blocking collectives: 126 us -> none  [the longest x1 96.9 us: body(): lax.all_to_all(jnp.stack([back_re, back_im]), 'seq', split_axis=2, concat...]
    dot_general x12 -> x0, matrix products: 44.5 us -> none  [the longest x1 5.4 us: lanes_forward_rows(): jnp.einsum('skrc,rq->skqc', imag_part, sin_rows, precision=PRECISE)]
    pallas_call x0 -> x5, Pallas kernels: none -> 19 us  [the longest x1 12.6 us: body(): pl.pallas_call(functools.partial(conv_kernel, mix), out_shape=jax.ShapeDt...]
    unnamed x10, local copies, waits for them, and re-layouts: 18 us -> 1.42 us
    ppermute x0 -> x10, starting transfers between devices: none -> 15.8 us  [scatter(): lax.ppermute(block, axis, [(i, i ^ turn) for i in range(count)])]
    ppermute x0 -> x10, waiting for transfers between devices: none -> 15.7 us  [scatter(): lax.ppermute(block, axis, [(i, i ^ turn) for i in range(count)])]
    another operation x3 -> x0, local copies, waits for them, and re-layouts: 13.5 us -> none  [the longest x1 8.56 us: body(): jnp.stack([real_part, imag_part])]
  transfers between devices with their start and end apart: 3 -> 12, of which waited for: 3 -> 5; matrix products, arithmetic and copies ran while one was open for 0% -> 0% of each run, Pallas kernels for 0% -> 3%
where the time goes in v1:
time: 69.8 us; the launch traced here: 69.5 us
  starting transfers between devices  27.3 us (39%)
  waiting for transfers between devices  21.7 us (31%)
  Pallas kernels  19 us (27%)
  local copies, waits for them, and re-layouts  1.42 us (2%)
    ppermute x10, starting transfers between devices, scatter(): lax.ppermute(block, axis, [(i, i ^ turn) for i in range(count)])  15.8 us
    ppermute x10, waiting for transfers between devices, scatter(): lax.ppermute(block, axis, [(i, i ^ turn) for i in range(count)])  15.7 us
    pallas_call x1, Pallas kernels, body(): pl.pallas_call(functools.partial(conv_kernel, mix), out_shape=jax.ShapeDt...  12.6 us
    all_to_all x1, starting transfers between devices, body(): gated = exchange(gated, ('seq', 'ch'))  7.3 us
    all_to_all x1, waiting for transfers between devices, body(): convolved = exchange(convolved, 'seq')  6.03 us
    all_to_all x1, starting transfers between devices, body(): convolved = exchange(convolved, 'seq')  4.16 us
    pallas_call x1, Pallas kernels, body(): pl.pallas_call(send_kernel, grid=(parts,), in_specs=[pl.BlockSpec((3, hel...  2.39 us
    pallas_call x1, Pallas kernels, body(): pl.pallas_call(mix_kernel, grid=(4,), in_specs=[pl.BlockSpec((wide // 4,...  2.18 us
  transfers between devices with their start and end apart: 12, of which 5 were waited for; matrix products, arithmetic and copies ran while one was open for 0% of the time, Pallas kernels for 3%

profile of v1, /device:TPU:0, one launch (start us, length us, event | category | flops | bytes accessed | tf_op | source)
XLA Modules:
  0.0 69.5 jit_solution(16107706917055768939)
XLA Ops:
  0.0 1.4 %copy-done = bf16[64,3,4096]{2,0,1:T(8,128)(2,1)S(1)} copy-done((bf16[64,3,4096]{2,0,1:T(8,128)(2,1)S(1)}, bf16[64,3,4096]{2,0,1:T(8,128)(2,1)}, u32[]{:S(2)}) %copy-start) | copy-done | bytes 1572888
  1.4 2.4 %encode_gated.1 = (bf16[8,4,64,128]{3,2,1,0:T(8,128)(2,1)}, bf16[64,1024]{1,0:T(8,128)(2,1)S(1)}, bf16[64,1024]{1,0:T(8,128)(2,1)S(1)}, bf16[64,1024]{1,0:T(8,128)(2,1)S(1)}, bf16[64,1024]{1,0:T(8,128)(2,1)S(1)}) custom-call(bf16[3,64,4096]{2,1,0:T(8,128)(2,1)S(1)} %bitcast.4), custom_call_target="tpu_custom_call" | custom-call | flops 33554432 | bytes 8388608 | tf_op jit(solution)/shard_map/encode_gated/pallas_call | solution.py:307
  3.8 7.3 %all-to-all-start = ((bf16[32,64,128]{2,1,0:T(8,128)(2,1)}), bf16[32,64,128]{2,1,0:T(8,128)(2,1)S(1)}, u32[]{:S(2)}, u32[]{:S(2)}) async-start(bf16[32,64,128]{2,1,0:T(8,128)(2,1)} %bitcast.1), calls=%async_computation | async-start | bytes 1048576 | tf_op jit(solution)/shard_map/all_to_all | solution.py:341
  11.1 1.5 %encode_taps.1 = (bf16[128,256]{1,0:T(8,128)(2,1)S(1)}, bf16[128,256]{1,0:T(8,128)(2,1)S(1)}, bf16[128,256]{1,0:T(8,128)(2,1)S(1)}, bf16[128,256]{1,0:T(8,128)(2...) custom-call(f32[8,128,256]{2,1,0:T(8,128)S(1)} %bitcast.5, ...), custom_call_target="tpu_custom_call" | custom-call | flops 33554432 | bytes 8388608 | tf_op jit(solution)/shard_map/encode_taps/pallas_call | solution.py:323
  12.6 1.8 %collective-permute-start.3 = (bf16[128,256]{1,0:T(8,128)(2,1)S(1)}, bf16[128,256]{1,0:T(8,128)(2,1)S(1)}, u32[]{:S(2)}, u32[]{:S(2)}) collective-permute-start(bf16[128,256]{1,0:T(8,128)(2,1)S(1)} %get-tuple-element.24), channel_id=1, source_target_pairs={{0,4},{4,0},{8,12},{12,8},{16,20},{20,16},{24,28},{28,24},{1,5},{5... | collective-permute-start | bytes 196616 | tf_op jit(solution)/shard_map/ppermute | solution.py:291
  14.5 1.5 %collective-permute-start.4 = (bf16[128,256]{1,0:T(8,128)(2,1)S(1)}, bf16[128,256]{1,0:T(8,128)(2,1)S(1)}, u32[]{:S(2)}, u32[]{:S(2)}) collective-permute-start(bf16[128,256]{1,0:T(8,128)(2,1)S(1)} %get-tuple-element.25), channel_id=1, source_target_pairs={{0,8},{4,12},{8,0},{12,4},{16,24},{20,28},{24,16},{28,20},{1,9},{5... | collective-permute-start | bytes 196616 | tf_op jit(solution)/shard_map/ppermute | solution.py:291
  15.9 0.3 collective-permute-start.5
  16.2 2.7 %collective-permute-start.6 = (bf16[128,256]{1,0:T(8,128)(2,1)S(1)}, bf16[128,256]{1,0:T(8,128)(2,1)S(1)}, u32[]{:S(2)}, u32[]{:S(2)}) collective-permute-start(bf16[128,256]{1,0:T(8,128)(2,1)S(1)} %get-tuple-element.27), channel_id=1, source_target_pairs={{0,16},{4,20},{8,24},{12,28},{16,0},{20,4},{24,8},{28,12},{1,17},{... | collective-permute-start | bytes 196616 | tf_op jit(solution)/shard_map/ppermute | solution.py:291
  18.9 1.5 %collective-permute-start.7 = (bf16[128,256]{1,0:T(8,128)(2,1)S(1)}, bf16[128,256]{1,0:T(8,128)(2,1)S(1)}, u32[]{:S(2)}, u32[]{:S(2)}) collective-permute-start(bf16[128,256]{1,0:T(8,128)(2,1)S(1)} %get-tuple-element.28), channel_id=1, source_target_pairs={{0,20},{4,16},{8,28},{12,24},{16,4},{20,0},{24,12},{28,8},{1,21},{... | collective-permute-start | bytes 196616 | tf_op jit(solution)/shard_map/ppermute | solution.py:291
  20.3 3.3 %collective-permute-start.8 = (bf16[128,256]{1,0:T(8,128)(2,1)S(1)}, bf16[128,256]{1,0:T(8,128)(2,1)S(1)}, u32[]{:S(2)}, u32[]{:S(2)}) collective-permute-start(bf16[128,256]{1,0:T(8,128)(2,1)S(1)} %get-tuple-element.29), channel_id=1, source_target_pairs={{0,24},{4,28},{8,16},{12,20},{16,8},{20,12},{24,0},{28,4},{1,25},{... | collective-permute-start | bytes 196616 | tf_op jit(solution)/shard_map/ppermute | solution.py:291
  23.7 2.9 %collective-permute-start.9 = (bf16[128,256]{1,0:T(8,128)(2,1)S(1)}, bf16[128,256]{1,0:T(8,128)(2,1)S(1)}, u32[]{:S(2)}, u32[]{:S(2)}) collective-permute-start(bf16[128,256]{1,0:T(8,128)(2,1)S(1)} %get-tuple-element.30), channel_id=1, source_target_pairs={{0,28},{4,24},{8,20},{12,16},{16,12},{20,8},{24,4},{28,0},{1,29},{... | collective-permute-start | bytes 196616 | tf_op jit(solution)/shard_map/ppermute | solution.py:291
  26.6 7.0 %collective-permute-done.6.refs_4_ = bf16[128,256]{1,0:T(8,128)(2,1)S(1)} collective-permute-done((bf16[128,256]{1,0:T(8,128)(2,1)S(1)}, bf16[128,256]{1,0:T(8,128)(2,1)S(1)}, u32[]{:S(2)}, u32[]{:S(2)}) %collective-permute-start.6) | collective-permute-done | bytes 65568 | tf_op jit(solution)/shard_map/ppermute | solution.py:291
  33.6 2.3 %collective-permute-done.7.refs_5_ = bf16[128,256]{1,0:T(8,128)(2,1)S(1)} collective-permute-done((bf16[128,256]{1,0:T(8,128)(2,1)S(1)}, bf16[128,256]{1,0:T(8,128)(2,1)S(1)}, u32[]{:S(2)}, u32[]{:S(2)}) %collective-permute-start.7) | collective-permute-done | bytes 65568 | tf_op jit(solution)/shard_map/ppermute | solution.py:291
  35.9 0.0 collective-permute-done.8.refs_6_
  35.9 0.0 collective-permute-done.9.refs_7_
  36.0 12.6 %convolve.1 = bf16[8,128,256]{2,1,0:T(8,128)(2,1)} custom-call(bf16[32,64,128]{2,1,0:T(8,128)(2,1)S(1)} %all-to-all-done.gated_ref, bf16[128,256]{1,0:T(8,128)(2,1)S(1)} %get-tuple-element.23.refs_0_, bf16[128,256]{1,0:T(8,128)(2,1)S(1)} %collective-permute-done.3.refs_1_, bf16[128,256]{1,0:T(8,128)(2,1)S(1)} %collective-permute-done.4.refs_2_, ...), custom_call_target="tpu_custom_call" | custom-call | flops 4294967296 | bytes 16777216 | tf_op jit(solution)/shard_map/convolve/pallas_call | solution.py:350
  48.6 4.2 %all-to-all-start.1 = ((bf16[8,128,256]{2,1,0:T(8,128)(2,1)}), bf16[8,128,256]{2,1,0:T(8,128)(2,1)S(1)}, u32[]{:S(2)}, u32[]{:S(2)}) async-start(bf16[8,128,256]{2,1,0:T(8,128)(2,1)} %convolve.1), calls=%async_computation.1 | async-start | bytes 1048576 | tf_op jit(solution)/shard_map/all_to_all | solution.py:369
  52.8 1.5 %collective-permute-start.1 = (bf16[64,1024]{1,0:T(8,128)(2,1)S(1)}, bf16[64,1024]{1,0:T(8,128)(2,1)S(1)}, u32[]{:S(2)}, u32[]{:S(2)}) collective-permute-start(bf16[64,1024]{1,0:T(8,128)(2,1)S(1)} %get-tuple-element.20), channel_id=1, source_target_pairs={{0,2},{1,3},{2,0},{3,1},{4,6},{5,7},{6,4},{7,5},{8,10},{9,11},{10,... | collective-permute-start | bytes 393224 | tf_op jit(solution)/shard_map/ppermute | solution.py:291
  54.3 0.3 collective-permute-start.2
  54.6 4.5 %collective-permute-done.1.refs_2_ = bf16[64,1024]{1,0:T(8,128)(2,1)S(1)} collective-permute-done((bf16[64,1024]{1,0:T(8,128)(2,1)S(1)}, bf16[64,1024]{1,0:T(8,128)(2,1)S(1)}, u32[]{:S(2)}, u32[]{:S(2)}) %collective-permute-start.1) | collective-permute-done | bytes 131104 | tf_op jit(solution)/shard_map/ppermute | solution.py:291
  59.1 1.9 %collective-permute-done.2.refs_3_ = bf16[64,1024]{1,0:T(8,128)(2,1)S(1)} collective-permute-done((bf16[64,1024]{1,0:T(8,128)(2,1)S(1)}, bf16[64,1024]{1,0:T(8,128)(2,1)S(1)}, u32[]{:S(2)}, u32[]{:S(2)}) %collective-permute-start.2) | collective-permute-done | bytes 131104 | tf_op jit(solution)/shard_map/ppermute | solution.py:291
  61.0 0.3 turn_queries.1.query_ref
  61.3 6.0 %all-to-all-done.1.conv_ref = bf16[8,128,256]{2,1,0:T(8,128)(2,1)S(1)} async-done(((bf16[8,128,256]{2,1,0:T(8,128)(2,1)}), bf16[8,128,256]{2,1,0:T(8,128)(2,1)S(1)}, u32[]{:S(2)}, u32[]{:S(2)}) %all-to-all-start.1) | async-done | bytes 524320 | tf_op jit(solution)/shard_map/all_to_all | solution.py:369
  67.3 2.2 %mix_out.1 = bf16[1024,256]{1,0:T(8,128)(2,1)} custom-call(bf16[1024,256]{1,0:T(8,128)(2,1)S(1)} %turn_queries.1.query_ref, bf16[8,128,256]{2,1,0:T(8,128)(2,1)S(1)} %all-to-all-done.1.conv_ref), custom_call_target="tpu_custom_call" | custom-call | tf_op jit(solution)/shard_map/mix_out/pallas_call | solution.py:379
  (15 shorter events, 0.0 us)
Async XLA Ops:
  0.0 1.4 %copy-start = (bf16[64,3,4096]{2,0,1:T(8,128)(2,1)S(1)}, bf16[64,3,4096]{2,0,1:T(8,128)(2,1)}, u32[]{:S(2)}) copy-start(bf16[64,3,4096]{2,0,1:T(8,128)(2,1)} %param.5) | copy-start | bytes 4718596
  1.4 9.7 %copy-start.1 = (f32[1024,256]{1,0:T(8,128)S(1)}, f32[1024,256]{1,0:T(8,128)}, u32[]{:S(2)}) copy-start(f32[1024,256]{1,0:T(8,128)} %param.6) | copy-start | bytes 3145732
  1.4 9.7 %copy-start.2 = (f32[1024]{0:T(1024)S(1)}, f32[1024]{0:T(1024)}, u32[]{:S(2)}) copy-start(f32[1024]{0:T(1024)} %param.7) | copy-start | bytes 12292
  1.4 34.5 %copy-start.3 = (bf16[768,512]{1,0:T(8,128)(2,1)S(1)}, bf16[768,512]{1,0:T(8,128)(2,1)}, u32[]{:S(2)}) copy-start(bf16[768,512]{1,0:T(8,128)(2,1)} %constant.4.clone.refs_8_) | copy-start | bytes 2359300
  1.4 34.5 %copy-start.4 = (f32[8,2,256]{2,1,0:T(2,128)S(1)}, f32[8,2,256]{2,1,0:T(2,128)}, u32[]{:S(2)}) copy-start(f32[8,2,256]{2,1,0:T(2,128)} %constant.5.clone.refs_9_) | copy-start | bytes 49156
  3.8 32.1 %all-to-all-start = ((bf16[32,64,128]{2,1,0:T(8,128)(2,1)}), bf16[32,64,128]{2,1,0:T(8,128)(2,1)S(1)}, u32[]{:S(2)}, u32[]{:S(2)}) async-start(bf16[32,64,128]{2,1,0:T(8,128)(2,1)} %bitcast.1), calls=%async_computation | async-start | bytes 1048576 | tf_op jit(solution)/shard_map/all_to_all | solution.py:341
  12.6 7.7 %collective-permute-start.3 = (bf16[128,256]{1,0:T(8,128)(2,1)S(1)}, bf16[128,256]{1,0:T(8,128)(2,1)S(1)}, u32[]{:S(2)}, u32[]{:S(2)}) collective-permute-start(bf16[128,256]{1,0:T(8,128)(2,1)S(1)} %get-tuple-element.24), channel_id=1, source_target_pairs={{0,4},{4,0},{8,12},{12,8},{16,20},{20,16},{24,28},{28,24},{1,5},{5... | collective-permute-start | bytes 196616 | tf_op jit(solution)/shard_map/ppermute | solution.py:291
  14.5 9.2 %collective-permute-start.4 = (bf16[128,256]{1,0:T(8,128)(2,1)S(1)}, bf16[128,256]{1,0:T(8,128)(2,1)S(1)}, u32[]{:S(2)}, u32[]{:S(2)}) collective-permute-start(bf16[128,256]{1,0:T(8,128)(2,1)S(1)} %get-tuple-element.25), channel_id=1, source_target_pairs={{0,8},{4,12},{8,0},{12,4},{16,24},{20,28},{24,16},{28,20},{1,9},{5... | collective-permute-start | bytes 196616 | tf_op jit(solution)/shard_map/ppermute | solution.py:291
  15.9 10.7 %collective-permute-start.5 = (bf16[128,256]{1,0:T(8,128)(2,1)S(1)}, bf16[128,256]{1,0:T(8,128)(2,1)S(1)}, u32[]{:S(2)}, u32[]{:S(2)}) collective-permute-start(bf16[128,256]{1,0:T(8,128)(2,1)S(1)} %get-tuple-element.26), channel_id=1, source_target_pairs={{0,12},{4,8},{8,4},{12,0},{16,28},{20,24},{24,20},{28,16},{1,13},{... | collective-permute-start | bytes 196616 | tf_op jit(solution)/shard_map/ppermute | solution.py:291
  16.2 17.4 %collective-permute-start.6 = (bf16[128,256]{1,0:T(8,128)(2,1)S(1)}, bf16[128,256]{1,0:T(8,128)(2,1)S(1)}, u32[]{:S(2)}, u32[]{:S(2)}) collective-permute-start(bf16[128,256]{1,0:T(8,128)(2,1)S(1)} %get-tuple-element.27), channel_id=1, source_target_pairs={{0,16},{4,20},{8,24},{12,28},{16,0},{20,4},{24,8},{28,12},{1,17},{... | collective-permute-start | bytes 196616 | tf_op jit(solution)/shard_map/ppermute | solution.py:291
  18.9 17.1 %collective-permute-start.7 = (bf16[128,256]{1,0:T(8,128)(2,1)S(1)}, bf16[128,256]{1,0:T(8,128)(2,1)S(1)}, u32[]{:S(2)}, u32[]{:S(2)}) collective-permute-start(bf16[128,256]{1,0:T(8,128)(2,1)S(1)} %get-tuple-element.28), channel_id=1, source_target_pairs={{0,20},{4,16},{8,28},{12,24},{16,4},{20,0},{24,12},{28,8},{1,21},{... | collective-permute-start | bytes 196616 | tf_op jit(solution)/shard_map/ppermute | solution.py:291
  20.3 15.6 %collective-permute-start.8 = (bf16[128,256]{1,0:T(8,128)(2,1)S(1)}, bf16[128,256]{1,0:T(8,128)(2,1)S(1)}, u32[]{:S(2)}, u32[]{:S(2)}) collective-permute-start(bf16[128,256]{1,0:T(8,128)(2,1)S(1)} %get-tuple-element.29), channel_id=1, source_target_pairs={{0,24},{4,28},{8,16},{12,20},{16,8},{20,12},{24,0},{28,4},{1,25},{... | collective-permute-start | bytes 196616 | tf_op jit(solution)/shard_map/ppermute | solution.py:291
  23.7 12.3 %collective-permute-start.9 = (bf16[128,256]{1,0:T(8,128)(2,1)S(1)}, bf16[128,256]{1,0:T(8,128)(2,1)S(1)}, u32[]{:S(2)}, u32[]{:S(2)}) collective-permute-start(bf16[128,256]{1,0:T(8,128)(2,1)S(1)} %get-tuple-element.30), channel_id=1, source_target_pairs={{0,28},{4,24},{8,20},{12,16},{16,12},{20,8},{24,4},{28,0},{1,29},{... | collective-permute-start | bytes 196616 | tf_op jit(solution)/shard_map/ppermute | solution.py:291
  48.6 18.7 %all-to-all-start.1 = ((bf16[8,128,256]{2,1,0:T(8,128)(2,1)}), bf16[8,128,256]{2,1,0:T(8,128)(2,1)S(1)}, u32[]{:S(2)}, u32[]{:S(2)}) async-start(bf16[8,128,256]{2,1,0:T(8,128)(2,1)} %convolve.1), calls=%async_computation.1 | async-start | bytes 1048576 | tf_op jit(solution)/shard_map/all_to_all | solution.py:369
  52.8 1.9 %collective-permute-start = (bf16[64,1024]{1,0:T(8,128)(2,1)S(1)}, bf16[64,1024]{1,0:T(8,128)(2,1)S(1)}, u32[]{:S(2)}, u32[]{:S(2)}) collective-permute-start(bf16[64,1024]{1,0:T(8,128)(2,1)S(1)} %get-tuple-element.19), channel_id=1, source_target_pairs={{0,1},{1,0},{2,3},{3,2},{4,5},{5,4},{6,7},{7,6},{8,9},{9,8},{10,11... | collective-permute-start | bytes 393224 | tf_op jit(solution)/shard_map/ppermute | solution.py:291
  52.8 6.4 %collective-permute-start.1 = (bf16[64,1024]{1,0:T(8,128)(2,1)S(1)}, bf16[64,1024]{1,0:T(8,128)(2,1)S(1)}, u32[]{:S(2)}, u32[]{:S(2)}) collective-permute-start(bf16[64,1024]{1,0:T(8,128)(2,1)S(1)} %get-tuple-element.20), channel_id=1, source_target_pairs={{0,2},{1,3},{2,0},{3,1},{4,6},{5,7},{6,4},{7,5},{8,10},{9,11},{10,... | collective-permute-start | bytes 393224 | tf_op jit(solution)/shard_map/ppermute | solution.py:291
  54.3 6.7 %collective-permute-start.2 = (bf16[64,1024]{1,0:T(8,128)(2,1)S(1)}, bf16[64,1024]{1,0:T(8,128)(2,1)S(1)}, u32[]{:S(2)}, u32[]{:S(2)}) collective-permute-start(bf16[64,1024]{1,0:T(8,128)(2,1)S(1)} %get-tuple-element.21), channel_id=1, source_target_pairs={{0,3},{1,2},{2,1},{3,0},{4,7},{5,6},{6,5},{7,4},{8,11},{9,10},{10,... | collective-permute-start | bytes 393224 | tf_op jit(solution)/shard_map/ppermute | solution.py:291

commit v2 on v1

--- a/solution.py
+++ b/solution.py
@@ -20,6 +20,7 @@
 HALF = 64
 VMEM_BYTES = 24 * 1024 * 1024
 SMALL_BYTES = 12 * 1024 * 1024
+ALL_BYTES = 60 * 1024 * 1024
 
 
 def split_first(values, axis):
@@ -143,19 +144,49 @@
     return re, im
 
 
-def send_kernel(streams_ref, gated_ref, *query_refs):
-    me, step = lax.axis_index("ch"), pl.program_id(0)
+def send_kernel(streams_ref, gated_ref, keys, values, codes, in_sems, out_sems):
+    groups, parts = gated_ref.shape[:2]
+    per = groups // 2
+    width = per * LANES
+    arrivals = []
+    for chunk in range(2 * parts):
+        lanes = pl.ds(chunk * width, width)
+        for stream, buffer in ((1, keys), (2, values)):
+            copy = pltpu.make_async_copy(
+                streams_ref.at[stream, :, lanes], buffer.at[chunk], in_sems.at[stream - 1, chunk]
+            )
+            copy.start()
+            arrivals.append(copy)
+    copies = []
+    for chunk in range(2 * parts):
+        for copy in arrivals[2 * chunk : 2 * chunk + 2]:
+            copy.wait()
+        part, first = chunk // 2, chunk % 2 * per
+        for block in range(per):
+            lanes = slice(block * LANES, (block + 1) * LANES)
+            left = keys[chunk, :, lanes].astype(jnp.float32)
+            right = values[chunk, :, lanes].astype(jnp.float32)
+            codes[first + block, part] = encode(left * right, 0)
+        place = (pl.ds(first, per), part)
+        copy = pltpu.make_async_copy(codes.at[place], gated_ref.at[place], out_sems.at[chunk])
+        copy.start()
+        copies.append(copy)
+    for copy in copies:
+        copy.wait()
+
+
+def query_kernel(streams_ref, *refs):
+    query_refs, sems = refs[:-1], refs[-1]
+    me = lax.axis_index("ch")
+    wide = query_refs[0].shape[1]
+    copies = []
     for turn, query_ref in enumerate(query_refs):
-
-        @pl.when(step == me ^ turn)
-        def _():
-            query_ref[...] = streams_ref[0]
-
-    for block in range(gated_ref.shape[0]):
-        lanes = slice(block * LANES, (block + 1) * LANES)
-        keys = streams_ref[1, :, lanes].astype(jnp.float32)
-        values = streams_ref[2, :, lanes].astype(jnp.float32)
-        gated_ref[block, 0] = encode(keys * values, 0)
+        lanes = pl.ds(pl.multiple_of((me ^ turn) * wide, wide), wide)
+        copy = pltpu.make_async_copy(streams_ref.at[0, :, lanes], query_ref, sems.at[turn])
+        copy.start()
+        copies.append(copy)
+    for copy in copies:
+        copy.wait()
 
 
 def taps_kernel(taps_ref, skip_ref, *code_refs):
@@ -172,76 +203,96 @@
         code_ref[...] = encode(taps, 1)
 
 
+def combined(waves_ref, k, at):
+    re, im = spectrum_rows(waves_ref, k, at)
+    return re[:, :ROW] + im[:, ROW:], im[:, :ROW] - re[:, ROW:]
+
+
+def stage(wave_ref, source, target, work, half):
+    steps = 2
+    chunks = HALF // CHUNK // steps
+
+    def step(index, _):
+        if source is not None:
+            count = source.shape[0] // steps
+            at = pl.ds(pl.multiple_of(index * count, count), count)
+            target[at, :] = jnp.dot(
+                source[at, :], wave_ref[...], preferred_element_type=jnp.float32
+            )
+        for chunk in range(chunks):
+            work(half, pl.multiple_of((index * chunks + chunk) * CHUNK, CHUNK))
+        return 0
+
+    lax.fori_loop(0, steps, step, 0)
+
+
+def gated_spectrum_kernel(mix, gated_ref, wave_ref, twist_ref, out_ref, u, *scratch):
+    blocks = u.shape[0]
+    rows, waves = scratch[0:2], scratch[2:4]
+    parts = ROW // gated_ref.shape[1]
+
+    def unpack(block, _):
+        pieces = [decode(gated_ref[block * parts + part], 0) for part in range(parts)]
+        u[block] = jnp.transpose(jnp.concatenate(pieces, axis=0))
+        return 0
+
+    def forward(half, at):
+        start = pl.ds(half * HALF + at, CHUNK)
+        mix_forward([u[n1, start, :] for n1 in range(blocks)], twist_ref, mix, at, rows[half])
+
+    def finish(half, at):
+        for k in range(blocks):
+            re, im = combined(waves[half], k, at)
+            out_ref[half, k, 0, pl.ds(at, CHUNK), :] = re
+            out_ref[half, k, 1, pl.ds(at, CHUNK), :] = im
+
+    lax.fori_loop(0, blocks, unpack, 0)
+    stage(wave_ref, None, None, forward, 0)
+    stage(wave_ref, rows[0], waves[0], forward, 1)
+    stage(wave_ref, rows[1], waves[1], finish, 0)
+    stage(wave_ref, None, None, finish, 1)
+
+
 def conv_kernel(mix, gated_ref, *refs):
     blocks = len(mix[0])
-    wave_ref, twist_ref, out_ref, u, codes, *scratch = refs[blocks:]
-    rows, u_waves, h_waves = scratch[0:2], scratch[2:4], scratch[4:6]
+    wave_ref, twist_ref = refs[blocks : blocks + 2]
+    out_refs = refs[blocks + 2 : 2 * blocks + 2]
+    codes, out, *scratch = refs[2 * blocks + 2 :]
+    rows, waves = scratch[0:2], scratch[2:4]
     me = lax.axis_index("seq")
-    parts = ROW // gated_ref.shape[1]
     for turn, code_ref in enumerate(refs[:blocks]):
         codes[me ^ turn] = code_ref[...]
 
-    def unpack(block):
-        pieces = [decode(gated_ref[block * parts + part], 0) for part in range(parts)]
-        u[block] = jnp.transpose(jnp.concatenate(pieces, axis=0))
-
-    def forward_taps(half, at):
+    def forward(half, at):
         start = pl.ds(half * HALF + at, CHUNK)
         taken = [decode(codes[n1, start, :], 1) for n1 in range(blocks)]
         mix_forward(taken, twist_ref, mix, at, rows[half])
 
-    def forward_gated(half, at):
-        start = pl.ds(half * HALF + at, CHUNK)
-        mix_forward([u[n1, start, :] for n1 in range(blocks)], twist_ref, mix, at, rows[half])
-
     def product(half, at):
         for k in range(blocks):
-            re, im = spectrum_rows(u_waves[half], k, at)
-            re, im = re[:, :ROW] + im[:, ROW:], im[:, :ROW] - re[:, ROW:]
-            taps_re, taps_im = spectrum_rows(h_waves[half], k, at)
-            taps_re, taps_im = (
-                taps_re[:, :ROW] + taps_im[:, ROW:],
-                taps_im[:, :ROW] - taps_re[:, ROW:],
-            )
-            put_split(rows[half], 2 * k * HALF + at, re * taps_re - im * taps_im)
-            put_split(rows[half], (2 * k + 1) * HALF + at, re * taps_im + im * taps_re)
+            re, im = combined(waves[half], k, at)
+            gated_re = gated_ref[half, k, 0, pl.ds(at, CHUNK), :]
+            gated_im = gated_ref[half, k, 1, pl.ds(at, CHUNK), :]
+            put_split(rows[half], 2 * k * HALF + at, re * gated_re - im * gated_im)
+            put_split(rows[half], (2 * k + 1) * HALF + at, re * gated_im + im * gated_re)
 
     def back(half, at):
         spectra = []
         for k in range(blocks):
-            re, im = spectrum_rows(u_waves[half], k, at)
+            re, im = spectrum_rows(waves[half], k, at)
             spectra.append((re[:, :ROW] - im[:, ROW:], im[:, :ROW] + re[:, ROW:]))
         start = pl.ds(half * HALF + at, CHUNK)
         for n1, total in enumerate(mix_back(spectra, twist_ref, mix)):
-            out_ref[n1, start, :] = encode(total * (1.0 / (blocks * ROW)), 1)
-
-    def stage(source, target, work, half, more=None):
-        steps = 2
-        count = rows[0].shape[0] // steps
-        chunks = HALF // CHUNK // steps
-
-        def step(index, _):
-            if source is not None:
-                at = pl.ds(pl.multiple_of(index * count, count), count)
-                target[at, :] = jnp.dot(
-                    source[at, :], wave_ref[...], preferred_element_type=jnp.float32
-                )
-            for chunk in range(chunks):
-                work(half, pl.multiple_of((index * chunks + chunk) * CHUNK, CHUNK))
-            for block in range(blocks // steps if more else 0):
-                more(index * (blocks // steps) + block)
-            return 0
-
-        lax.fori_loop(0, steps, step, 0)
-
-    stage(None, None, forward_taps, 0)
-    stage(rows[0], h_waves[0], forward_taps, 1, unpack)
-    stage(rows[1], h_waves[1], forward_gated, 0)
-    stage(rows[0], u_waves[0], forward_gated, 1)
-    stage(rows[1], u_waves[1], product, 0)
-    stage(rows[0], u_waves[0], product, 1)
-    stage(rows[1], u_waves[1], back, 0)
-    stage(None, None, back, 1)
+            out[n1, start, :] = encode(total * (1.0 / (blocks * ROW)), 1)
+
+    stage(wave_ref, None, None, forward, 0)
+    stage(wave_ref, rows[0], waves[0], forward, 1)
+    stage(wave_ref, rows[1], waves[1], product, 0)
+    stage(wave_ref, rows[0], waves[0], product, 1)
+    stage(wave_ref, rows[1], waves[1], back, 0)
+    stage(wave_ref, None, None, back, 1)
+    for turn, out_ref in enumerate(out_refs):
+        out_ref[...] = out[me ^ turn]
 
 
 def turn_kernel(*refs):
@@ -254,11 +305,19 @@
     out_ref[...] = jnp.transpose(whole[...]).astype(jnp.bfloat16)
 
 
-def mix_kernel(query_ref, conv_ref, out_ref):
-    for block in range(conv_ref.shape[0]):
-        at = slice(block * LANES, (block + 1) * LANES)
+def mix_kernel(query_ref, *refs):
+    conv_refs, (out_ref, mixed, sems) = refs[:-3], refs[-3:]
+    me = lax.axis_index("seq")
+    copies = []
+    for turn, conv_ref in enumerate(conv_refs):
+        at = pl.ds(pl.multiple_of((me ^ turn) * LANES, LANES), LANES)
         queries = query_ref[at, :].astype(jnp.float32)
-        out_ref[at, :] = (queries * decode(conv_ref[block], 1)).astype(jnp.bfloat16)
+        mixed[at, :] = (queries * decode(conv_ref[...], 1)).astype(jnp.bfloat16)
+        copy = pltpu.make_async_copy(mixed.at[at], out_ref.at[at], sems.at[turn])
+        copy.start()
+        copies.append(copy)
+    for copy in copies:
+        copy.wait()
 
 
 def plain_conv(gated, taps):
@@ -304,21 +363,34 @@
     fits = fits and groups & (groups - 1) == 0 and parts & (parts - 1) == 0
     small = pltpu.CompilerParams(vmem_limit_bytes=SMALL_BYTES)
     if fits:
-        gated, *queries = pl.pallas_call(
+        far = pl.BlockSpec(memory_space=pl.ANY)
+        coded = (groups, parts, held, own)
+        stream = pltpu.VMEM((2 * parts, held, wide // 2), jnp.bfloat16)
+        gated = pl.pallas_call(
             send_kernel,
-            grid=(parts,),
-            in_specs=[pl.BlockSpec((3, held, wide), lambda g: (0, 0, g))],
-            out_specs=[
-                pl.BlockSpec((groups, 1, held, own), lambda g: (0, g, 0, 0)),
-            ]
-            + [pl.BlockSpec((held, wide), lambda g: (0, 0))] * parts,
-            out_shape=[
-                jax.ShapeDtypeStruct((groups, parts, held, own), jnp.bfloat16),
-            ]
-            + [jax.ShapeDtypeStruct((held, wide), jnp.bfloat16)] * parts,
+            in_specs=[far],
+            out_specs=far,
+            out_shape=jax.ShapeDtypeStruct(coded, jnp.bfloat16),
+            scratch_shapes=[
+                stream,
+                stream,
+                pltpu.VMEM(coded, jnp.bfloat16),
+                pltpu.SemaphoreType.DMA((2, 2 * parts)),
+                pltpu.SemaphoreType.DMA((2 * parts,)),
+            ],
+            compiler_params=pltpu.CompilerParams(vmem_limit_bytes=ALL_BYTES),
             cost_estimate=cost(2**25, 2**23),
+            name="encode_gated",
+        )(streams)
+        queries = pl.pallas_call(
+            query_kernel,
+            in_specs=[far],
+            out_specs=[far] * parts,
+            out_shape=[jax.ShapeDtypeStruct((held, wide), jnp.bfloat16)] * parts,
+            scratch_shapes=[pltpu.SemaphoreType.DMA((parts,))],
             compiler_params=small,
-            name="encode_gated",
+            cost_estimate=cost(2**10, 2**20),
+            name="send_queries",
         )(streams)
         taps = pl.pallas_call(
             taps_kernel,
@@ -347,16 +419,22 @@
     if fits:
         high, low, twist, mix = tables(blocks)
         wave = np.concatenate([high, low, high], axis=0)
+        scratch = [pltpu.VMEM((blocks * 2 * HALF, 3 * ROW), jnp.bfloat16)] * 2
+        scratch += [pltpu.VMEM((blocks * 2 * HALF, 2 * ROW), jnp.float32)] * 2
+        large = pltpu.CompilerParams(vmem_limit_bytes=VMEM_BYTES)
+        gated = pl.pallas_call(
+            functools.partial(gated_spectrum_kernel, mix),
+            out_shape=jax.ShapeDtypeStruct((2, blocks, 2, HALF, ROW), jnp.float32),
+            scratch_shapes=[pltpu.VMEM((blocks, own, ROW), jnp.float32)] + scratch,
+            compiler_params=large,
+            cost_estimate=cost(2**32, 2**24),
+            name="gated_spectrum",
+        )(gated, wave, twist)
         convolved = pl.pallas_call(
             functools.partial(conv_kernel, mix),
-            out_shape=jax.ShapeDtypeStruct((blocks, own, ROW), jnp.bfloat16),
-            scratch_shapes=[
-                pltpu.VMEM((blocks, own, ROW), jnp.float32),
-                pltpu.VMEM((blocks, own, ROW), jnp.bfloat16),
-            ]
-            + [pltpu.VMEM((blocks * 2 * HALF, 3 * ROW), jnp.bfloat16)] * 2
-            + [pltpu.VMEM((blocks * 2 * HALF, 2 * ROW), jnp.float32)] * 4,
-            compiler_params=pltpu.CompilerParams(vmem_limit_bytes=VMEM_BYTES),
+            out_shape=[jax.ShapeDtypeStruct((own, ROW), jnp.bfloat16)] * groups,
+            scratch_shapes=[pltpu.VMEM((blocks, own, ROW), jnp.bfloat16)] * 2 + scratch,
+            compiler_params=large,
             cost_estimate=cost(2**32, 2**24),
             name="convolve",
         )(gated, *taps, wave, twist)
@@ -366,8 +444,8 @@
         convolved = plain_conv(jnp.transpose(gated, (0, 2, 1)), jnp.transpose(taps, (1, 0, 2)))
         convolved = jnp.transpose(convolved, (1, 0, 2)).reshape(own, groups, -1)
         convolved = encode(jnp.transpose(convolved, (1, 0, 2)), 2)
-    convolved = exchange(convolved, "seq")
     if fits:
+        convolved = scatter(convolved, "seq")
         queries = pl.pallas_call(
             turn_kernel,
             out_shape=jax.ShapeDtypeStruct((wide, ROW), jnp.bfloat16),
@@ -378,16 +456,16 @@
         )(*queries)
         return pl.pallas_call(
             mix_kernel,
-            grid=(4,),
-            in_specs=[
-                pl.BlockSpec((wide // 4, ROW), lambda i: (i, 0)),
-                pl.BlockSpec((groups // 4, own, ROW), lambda i: (i, 0, 0)),
+            out_specs=far,
+            out_shape=jax.ShapeDtypeStruct((wide, ROW), jnp.bfloat16),
+            scratch_shapes=[
+                pltpu.VMEM((wide, ROW), jnp.bfloat16),
+                pltpu.SemaphoreType.DMA((groups,)),
             ],
-            out_specs=pl.BlockSpec((wide // 4, ROW), lambda i: (i, 0)),
-            out_shape=jax.ShapeDtypeStruct((wide, ROW), jnp.bfloat16),
             compiler_params=small,
             name="mix_out",
-        )(queries, convolved)
+        )(queries, *convolved)
+    convolved = exchange(convolved, "seq")
     queries = jnp.transpose(queries.astype(jnp.float32))
     return (queries * decode(convolved, 2).reshape(wide, -1)).astype(jnp.bfloat16)
 

time: 69.8 us -> 66.1 us (0.947)
  waiting for transfers between devices: 21.7 us -> 7.92 us
  starting transfers between devices: 27.3 us -> 36.1 us
  Pallas kernels: 19 us -> 19.8 us
    ppermute x10 -> x17, starting transfers between devices: 15.8 us -> 28.8 us  [scatter(): lax.ppermute(block, axis, [(i, i ^ turn) for i in range(count)])]
    ppermute x10 -> x17, waiting for transfers between devices: 15.7 us -> 7.87 us  [scatter(): lax.ppermute(block, axis, [(i, i ^ turn) for i in range(count)])]
    all_to_all x1 -> x0, waiting for transfers between devices: 6.03 us -> none  [body(): convolved = exchange(convolved, 'seq')]
    all_to_all x1 -> x0, starting transfers between devices: 4.16 us -> none  [body(): convolved = exchange(convolved, 'seq')]
    pallas_call x3 -> x5, Pallas kernels: 17.2 us -> 18 us  [the longest x1 8.21 us: body(): pl.pallas_call(functools.partial(conv_kernel, mix), out_shape=[jax.ShapeD...]
  transfers between devices with their start and end apart: 12 -> 18, of which waited for: 5 -> 5; matrix products, arithmetic and copies ran while one was open for 0% -> 0% of each run, Pallas kernels for 3% -> 23%
where the time goes in v2:
time: 66.1 us; the launch traced here: 65.7 us
  starting transfers between devices  36.1 us (55%)
  Pallas kernels  19.8 us (30%)
  waiting for transfers between devices  7.92 us (12%)
  local copies, waits for them, and re-layouts  1.86 us (3%)
    ppermute x17, starting transfers between devices, scatter(): lax.ppermute(block, axis, [(i, i ^ turn) for i in range(count)])  28.8 us
    pallas_call x1, Pallas kernels, body(): pl.pallas_call(functools.partial(conv_kernel, mix), out_shape=[jax.ShapeD...  8.21 us
    ppermute x17, waiting for transfers between devices, scatter(): lax.ppermute(block, axis, [(i, i ^ turn) for i in range(count)])  7.87 us
    all_to_all x1, starting transfers between devices, body(): gated = exchange(gated, ('seq', 'ch'))  7.31 us
    pallas_call x1, Pallas kernels, body(): pl.pallas_call(functools.partial(gated_spectrum_kernel, mix), out_shape=j...  4.77 us
    pallas_call x1, Pallas kernels, body(): pl.pallas_call(send_kernel, in_specs=[far], out_specs=far, out_shape=jax....  3.06 us
    unnamed x10, local copies, waits for them, and re-layouts  1.86 us
    pallas_call x1, Pallas kernels, body(): pl.pallas_call(mix_kernel, out_specs=far, out_shape=jax.ShapeDtypeStruct(...  1.81 us
  transfers between devices with their start and end apart: 18, of which 5 were waited for; matrix products, arithmetic and copies ran while one was open for 0% of the time, Pallas kernels for 23%

profile of v2, /device:TPU:0, one launch (start us, length us, event | category | flops | bytes accessed | tf_op | source)
XLA Modules:
  0.0 65.7 jit_solution(12730469045034013588)
XLA Ops:
  0.0 3.1 %encode_gated.1 = bf16[8,4,64,128]{3,2,1,0:T(8,128)(2,1)} custom-call(bf16[3,64,4096]{2,1,0:T(8,128)(2,1)} %bitcast.4), custom_call_target="tpu_custom_call" | custom-call | flops 33554432 | bytes 8388608 | tf_op jit(solution)/shard_map/encode_gated/pallas_call | solution.py:369
  3.1 7.3 %all-to-all-start = ((bf16[32,64,128]{2,1,0:T(8,128)(2,1)}), bf16[32,64,128]{2,1,0:T(8,128)(2,1)S(1)}, u32[]{:S(2)}, u32[]{:S(2)}) async-start(bf16[32,64,128]{2,1,0:T(8,128)(2,1)} %bitcast.8), calls=%async_computation | async-start | bytes 1048576 | tf_op jit(solution)/shard_map/all_to_all | solution.py:413
  10.4 1.5 %encode_taps.1 = (bf16[128,256]{1,0:T(8,128)(2,1)S(1)}, bf16[128,256]{1,0:T(8,128)(2,1)S(1)}, bf16[128,256]{1,0:T(8,128)(2,1)S(1)}, bf16[128,256]{1,0:T(8,128)(2...) custom-call(f32[8,128,256]{2,1,0:T(8,128)S(1)} %bitcast.6, ...), custom_call_target="tpu_custom_call" | custom-call | flops 33554432 | bytes 8388608 | tf_op jit(solution)/shard_map/encode_taps/pallas_call | solution.py:395
  11.9 1.8 %collective-permute-start.3 = (bf16[128,256]{1,0:T(8,128)(2,1)S(1)}, bf16[128,256]{1,0:T(8,128)(2,1)S(1)}, u32[]{:S(2)}, u32[]{:S(2)}) collective-permute-start(bf16[128,256]{1,0:T(8,128)(2,1)S(1)} %get-tuple-element.30), channel_id=1, source_target_pairs={{0,4},{4,0},{8,12},{12,8},{16,20},{20,16},{24,28},{28,24},{1,5},{5... | collective-permute-start | bytes 196616 | tf_op jit(solution)/shard_map/ppermute | solution.py:350
  13.7 1.5 %collective-permute-start.4 = (bf16[128,256]{1,0:T(8,128)(2,1)S(1)}, bf16[128,256]{1,0:T(8,128)(2,1)S(1)}, u32[]{:S(2)}, u32[]{:S(2)}) collective-permute-start(bf16[128,256]{1,0:T(8,128)(2,1)S(1)} %get-tuple-element.31), channel_id=1, source_target_pairs={{0,8},{4,12},{8,0},{12,4},{16,24},{20,28},{24,16},{28,20},{1,9},{5... | collective-permute-start | bytes 196616 | tf_op jit(solution)/shard_map/ppermute | solution.py:350
  15.5 2.7 %collective-permute-start.6 = (bf16[128,256]{1,0:T(8,128)(2,1)S(1)}, bf16[128,256]{1,0:T(8,128)(2,1)S(1)}, u32[]{:S(2)}, u32[]{:S(2)}) collective-permute-start(bf16[128,256]{1,0:T(8,128)(2,1)S(1)} %get-tuple-element.33), channel_id=1, source_target_pairs={{0,16},{4,20},{8,24},{12,28},{16,0},{20,4},{24,8},{28,12},{1,17},{... | collective-permute-start | bytes 196616 | tf_op jit(solution)/shard_map/ppermute | solution.py:350
  18.1 1.5 %collective-permute-start.7 = (bf16[128,256]{1,0:T(8,128)(2,1)S(1)}, bf16[128,256]{1,0:T(8,128)(2,1)S(1)}, u32[]{:S(2)}, u32[]{:S(2)}) collective-permute-start(bf16[128,256]{1,0:T(8,128)(2,1)S(1)} %get-tuple-element.34), channel_id=1, source_target_pairs={{0,20},{4,16},{8,28},{12,24},{16,4},{20,0},{24,12},{28,8},{1,21},{... | collective-permute-start | bytes 196616 | tf_op jit(solution)/shard_map/ppermute | solution.py:350
  19.7 3.4 %collective-permute-start.8 = (bf16[128,256]{1,0:T(8,128)(2,1)S(1)}, bf16[128,256]{1,0:T(8,128)(2,1)S(1)}, u32[]{:S(2)}, u32[]{:S(2)}) collective-permute-start(bf16[128,256]{1,0:T(8,128)(2,1)S(1)} %get-tuple-element.35), channel_id=1, source_target_pairs={{0,24},{4,28},{8,16},{12,20},{16,8},{20,12},{24,0},{28,4},{1,25},{... | collective-permute-start | bytes 196616 | tf_op jit(solution)/shard_map/ppermute | solution.py:350
  23.2 2.7 %collective-permute-start.9 = (bf16[128,256]{1,0:T(8,128)(2,1)S(1)}, bf16[128,256]{1,0:T(8,128)(2,1)S(1)}, u32[]{:S(2)}, u32[]{:S(2)}) collective-permute-start(bf16[128,256]{1,0:T(8,128)(2,1)S(1)} %get-tuple-element.36), channel_id=1, source_target_pairs={{0,28},{4,24},{8,20},{12,16},{16,12},{20,8},{24,4},{28,0},{1,29},{... | collective-permute-start | bytes 196616 | tf_op jit(solution)/shard_map/ppermute | solution.py:350
  25.9 1.1 %copy-done.3 = bf16[768,512]{1,0:T(8,128)(2,1)S(1)} copy-done((bf16[768,512]{1,0:T(8,128)(2,1)S(1)}, bf16[768,512]{1,0:T(8,128)(2,1)}, u32[]{:S(2)}) %copy-start.3) | copy-done | bytes 786456
  27.1 0.7 %copy-done.4 = f32[8,2,256]{2,1,0:T(2,128)S(1)} copy-done((f32[8,2,256]{2,1,0:T(2,128)S(1)}, f32[8,2,256]{2,1,0:T(2,128)}, u32[]{:S(2)}) %copy-start.4) | copy-done | bytes 16408
  27.8 4.8 %gated_spectrum.1.gated_ref = f32[2,8,2,64,256]{4,3,2,1,0:T(8,128)S(1)} custom-call(bf16[32,64,128]{2,1,0:T(8,128)(2,1)S(1)} %all-to-all-done.gated_ref, bf16[768,512]{1,0:T(8,128)(2,1)S(1)} %copy-done.3, f32[8,2,256]{2,1,0:T(2,128)S(1)} %copy-done.4), custom_call_target="tpu_custom_call" | custom-call | flops 4294967296 | bytes 16777216 | tf_op jit(solution)/shard_map/gated_spectrum/pallas_call | solution.py:425
  32.9 1.5 %collective-permute-start.1 = (bf16[64,1024]{1,0:T(8,128)(2,1)S(1)}, bf16[64,1024]{1,0:T(8,128)(2,1)S(1)}, u32[]{:S(2)}, u32[]{:S(2)}) collective-permute-start(bf16[64,1024]{1,0:T(8,128)(2,1)S(1)} %get-tuple-element.27), channel_id=1, source_target_pairs={{0,2},{1,3},{2,0},{3,1},{4,6},{5,7},{6,4},{7,5},{8,10},{9,11},{10,... | collective-permute-start | bytes 393224 | tf_op jit(solution)/shard_map/ppermute | solution.py:350
  34.4 0.9 %collective-permute-done.7.refs_5_ = bf16[128,256]{1,0:T(8,128)(2,1)S(1)} collective-permute-done((bf16[128,256]{1,0:T(8,128)(2,1)S(1)}, bf16[128,256]{1,0:T(8,128)(2,1)S(1)}, u32[]{:S(2)}, u32[]{:S(2)}) %collective-permute-start.7) | collective-permute-done | bytes 65568 | tf_op jit(solution)/shard_map/ppermute | solution.py:350
  35.5 8.2 %convolve.1 = (bf16[128,256]{1,0:T(8,128)(2,1)S(1)}, bf16[128,256]{1,0:T(8,128)(2,1)S(1)}, bf16[128,256]{1,0:T(8,128)(2,1)S(1)}, bf16[128,256]{1,0:T(8,128)(2,1)...) custom-call(f32[2,8,2,64,256]{4,3,2,1,0:T(8,128)S(1)} %gated_spectru, ...), custom_call_target="tpu_custom_call" | custom-call | flops 4294967296 | bytes 16777216 | tf_op jit(solution)/shard_map/convolve/pallas_call | solution.py:433
  43.7 0.6 collective-permute-start.10
  44.3 2.7 %collective-permute-start.11 = (bf16[128,256]{1,0:T(8,128)(2,1)S(1)}, bf16[128,256]{1,0:T(8,128)(2,1)S(1)}, u32[]{:S(2)}, u32[]{:S(2)}) collective-permute-start(bf16[128,256]{1,0:T(8,128)(2,1)S(1)} %get-tuple-element.39), channel_id=1, source_target_pairs={{0,8},{4,12},{8,0},{12,4},{16,24},{20,28},{24,16},{28,20},{1,9},{5... | collective-permute-start | bytes 196616 | tf_op jit(solution)/shard_map/ppermute | solution.py:350
  46.9 0.9 %collective-permute-start.12 = (bf16[128,256]{1,0:T(8,128)(2,1)S(1)}, bf16[128,256]{1,0:T(8,128)(2,1)S(1)}, u32[]{:S(2)}, u32[]{:S(2)}) collective-permute-start(bf16[128,256]{1,0:T(8,128)(2,1)S(1)} %get-tuple-element.40), channel_id=1, source_target_pairs={{0,12},{4,8},{8,4},{12,0},{16,28},{20,24},{24,20},{28,16},{1,13},{... | collective-permute-start | bytes 196616 | tf_op jit(solution)/shard_map/ppermute | solution.py:350
  47.9 3.8 %collective-permute-start.13 = (bf16[128,256]{1,0:T(8,128)(2,1)S(1)}, bf16[128,256]{1,0:T(8,128)(2,1)S(1)}, u32[]{:S(2)}, u32[]{:S(2)}) collective-permute-start(bf16[128,256]{1,0:T(8,128)(2,1)S(1)} %get-tuple-element.41), channel_id=1, source_target_pairs={{0,16},{4,20},{8,24},{12,28},{16,0},{20,4},{24,8},{28,12},{1,17},{... | collective-permute-start | bytes 196616 | tf_op jit(solution)/shard_map/ppermute | solution.py:350
  51.6 0.9 %collective-permute-start.14 = (bf16[128,256]{1,0:T(8,128)(2,1)S(1)}, bf16[128,256]{1,0:T(8,128)(2,1)S(1)}, u32[]{:S(2)}, u32[]{:S(2)}) collective-permute-start(bf16[128,256]{1,0:T(8,128)(2,1)S(1)} %get-tuple-element.42), channel_id=1, source_target_pairs={{0,20},{4,16},{8,28},{12,24},{16,4},{20,0},{24,12},{28,8},{1,21},{... | collective-permute-start | bytes 196616 | tf_op jit(solution)/shard_map/ppermute | solution.py:350
  52.5 4.3 %collective-permute-start.15 = (bf16[128,256]{1,0:T(8,128)(2,1)S(1)}, bf16[128,256]{1,0:T(8,128)(2,1)S(1)}, u32[]{:S(2)}, u32[]{:S(2)}) collective-permute-start(bf16[128,256]{1,0:T(8,128)(2,1)S(1)} %get-tuple-element.43), channel_id=1, source_target_pairs={{0,24},{4,28},{8,16},{12,20},{16,8},{20,12},{24,0},{28,4},{1,25},{... | collective-permute-start | bytes 196616 | tf_op jit(solution)/shard_map/ppermute | solution.py:350
  57.2 5.0 %collective-permute-done.14.refs_5_ = bf16[128,256]{1,0:T(8,128)(2,1)S(1)} collective-permute-done((bf16[128,256]{1,0:T(8,128)(2,1)S(1)}, bf16[128,256]{1,0:T(8,128)(2,1)S(1)}, u32[]{:S(2)}, u32[]{:S(2)}) %collective-permute-start.14) | collective-permute-done | bytes 65568 | tf_op jit(solution)/shard_map/ppermute | solution.py:350
  62.2 1.8 %collective-permute-done.16.refs_7_ = bf16[128,256]{1,0:T(8,128)(2,1)S(1)} collective-permute-done((bf16[128,256]{1,0:T(8,128)(2,1)S(1)}, bf16[128,256]{1,0:T(8,128)(2,1)S(1)}, u32[]{:S(2)}, u32[]{:S(2)}) %collective-permute-start.16) | collective-permute-done | bytes 65568 | tf_op jit(solution)/shard_map/ppermute | solution.py:350
  63.9 1.8 %mix_out.1 = bf16[1024,256]{1,0:T(8,128)(2,1)} custom-call(bf16[1024,256]{1,0:T(8,128)(2,1)S(1)} %turn_queries.1.query_ref, bf16[128,256]{1,0:T(8,128)(2,1)S(1)} %get-tuple-element.37.refs_0_, bf16[128,256]{1,0:T(8,128)(2,1)S(1)} %collective-permute-done.10.refs_1_, bf16[128,256]{1,0:T(8,128)(2,1)S(1)} %collective-permute-done.11.refs_2_, ...), custom_call_target="tpu_custom_call" | custom-call | tf_op jit(solution)/shard_map/mix_out/pallas_call | solution.py:457
  (29 shorter events, 1.3 us)
Async XLA Ops:
  0.0 10.4 %copy-start.1 = (f32[1024,256]{1,0:T(8,128)S(1)}, f32[1024,256]{1,0:T(8,128)}, u32[]{:S(2)}) copy-start(f32[1024,256]{1,0:T(8,128)} %param.6) | copy-start | bytes 3145732
  0.0 10.4 %copy-start.2 = (f32[1024]{0:T(1024)S(1)}, f32[1024]{0:T(1024)}, u32[]{:S(2)}) copy-start(f32[1024]{0:T(1024)} %param.7) | copy-start | bytes 12292
  0.0 19.6 %copy-start = (bf16[64,3,4096]{2,0,1:T(8,128)(2,1)S(1)}, bf16[64,3,4096]{2,0,1:T(8,128)(2,1)}, u32[]{:S(2)}) copy-start(bf16[64,3,4096]{2,0,1:T(8,128)(2,1)} %param.5) | copy-start | bytes 4718596
  3.1 22.9 %all-to-all-start = ((bf16[32,64,128]{2,1,0:T(8,128)(2,1)}), bf16[32,64,128]{2,1,0:T(8,128)(2,1)S(1)}, u32[]{:S(2)}, u32[]{:S(2)}) async-start(bf16[32,64,128]{2,1,0:T(8,128)(2,1)} %bitcast.8), calls=%async_computation | async-start | bytes 1048576 | tf_op jit(solution)/shard_map/all_to_all | solution.py:413
  11.9 7.8 %collective-permute-start.3 = (bf16[128,256]{1,0:T(8,128)(2,1)S(1)}, bf16[128,256]{1,0:T(8,128)(2,1)S(1)}, u32[]{:S(2)}, u32[]{:S(2)}) collective-permute-start(bf16[128,256]{1,0:T(8,128)(2,1)S(1)} %get-tuple-element.30), channel_id=1, source_target_pairs={{0,4},{4,0},{8,12},{12,8},{16,20},{20,16},{24,28},{28,24},{1,5},{5... | collective-permute-start | bytes 196616 | tf_op jit(solution)/shard_map/ppermute | solution.py:350
  13.7 9.4 %collective-permute-start.4 = (bf16[128,256]{1,0:T(8,128)(2,1)S(1)}, bf16[128,256]{1,0:T(8,128)(2,1)S(1)}, u32[]{:S(2)}, u32[]{:S(2)}) collective-permute-start(bf16[128,256]{1,0:T(8,128)(2,1)S(1)} %get-tuple-element.31), channel_id=1, source_target_pairs={{0,8},{4,12},{8,0},{12,4},{16,24},{20,28},{24,16},{28,20},{1,9},{5... | collective-permute-start | bytes 196616 | tf_op jit(solution)/shard_map/ppermute | solution.py:350
  15.2 17.4 %collective-permute-start.5 = (bf16[128,256]{1,0:T(8,128)(2,1)S(1)}, bf16[128,256]{1,0:T(8,128)(2,1)S(1)}, u32[]{:S(2)}, u32[]{:S(2)}) collective-permute-start(bf16[128,256]{1,0:T(8,128)(2,1)S(1)} %get-tuple-element.32), channel_id=1, source_target_pairs={{0,12},{4,8},{8,4},{12,0},{16,28},{20,24},{24,20},{28,16},{1,13},{... | collective-permute-start | bytes 196616 | tf_op jit(solution)/shard_map/ppermute | solution.py:350
  15.5 17.4 %collective-permute-start.6 = (bf16[128,256]{1,0:T(8,128)(2,1)S(1)}, bf16[128,256]{1,0:T(8,128)(2,1)S(1)}, u32[]{:S(2)}, u32[]{:S(2)}) collective-permute-start(bf16[128,256]{1,0:T(8,128)(2,1)S(1)} %get-tuple-element.33), channel_id=1, source_target_pairs={{0,16},{4,20},{8,24},{12,28},{16,0},{20,4},{24,8},{28,12},{1,17},{... | collective-permute-start | bytes 196616 | tf_op jit(solution)/shard_map/ppermute | solution.py:350
  18.1 17.1 %collective-permute-start.7 = (bf16[128,256]{1,0:T(8,128)(2,1)S(1)}, bf16[128,256]{1,0:T(8,128)(2,1)S(1)}, u32[]{:S(2)}, u32[]{:S(2)}) collective-permute-start(bf16[128,256]{1,0:T(8,128)(2,1)S(1)} %get-tuple-element.34), channel_id=1, source_target_pairs={{0,20},{4,16},{8,28},{12,24},{16,4},{20,0},{24,12},{28,8},{1,21},{... | collective-permute-start | bytes 196616 | tf_op jit(solution)/shard_map/ppermute | solution.py:350
  19.7 15.7 %collective-permute-start.8 = (bf16[128,256]{1,0:T(8,128)(2,1)S(1)}, bf16[128,256]{1,0:T(8,128)(2,1)S(1)}, u32[]{:S(2)}, u32[]{:S(2)}) collective-permute-start(bf16[128,256]{1,0:T(8,128)(2,1)S(1)} %get-tuple-element.35), channel_id=1, source_target_pairs={{0,24},{4,28},{8,16},{12,20},{16,8},{20,12},{24,0},{28,4},{1,25},{... | collective-permute-start | bytes 196616 | tf_op jit(solution)/shard_map/ppermute | solution.py:350
  23.2 12.3 %collective-permute-start.9 = (bf16[128,256]{1,0:T(8,128)(2,1)S(1)}, bf16[128,256]{1,0:T(8,128)(2,1)S(1)}, u32[]{:S(2)}, u32[]{:S(2)}) collective-permute-start(bf16[128,256]{1,0:T(8,128)(2,1)S(1)} %get-tuple-element.36), channel_id=1, source_target_pairs={{0,28},{4,24},{8,20},{12,16},{16,12},{20,8},{24,4},{28,0},{1,29},{... | collective-permute-start | bytes 196616 | tf_op jit(solution)/shard_map/ppermute | solution.py:350
  25.9 1.1 %copy-start.3 = (bf16[768,512]{1,0:T(8,128)(2,1)S(1)}, bf16[768,512]{1,0:T(8,128)(2,1)}, u32[]{:S(2)}) copy-start(bf16[768,512]{1,0:T(8,128)(2,1)} %constant.4.clone.wave_ref.refs_8_) | copy-start | bytes 2359300
  27.1 0.7 %copy-start.4 = (f32[8,2,256]{2,1,0:T(2,128)S(1)}, f32[8,2,256]{2,1,0:T(2,128)}, u32[]{:S(2)}) copy-start(f32[8,2,256]{2,1,0:T(2,128)} %constant.5.clone.twist_ref.refs_9_) | copy-start | bytes 49156
  32.6 14.4 %collective-permute-start = (bf16[64,1024]{1,0:T(8,128)(2,1)S(1)}, bf16[64,1024]{1,0:T(8,128)(2,1)S(1)}, u32[]{:S(2)}, u32[]{:S(2)}) collective-permute-start(bf16[64,1024]{1,0:T(8,128)(2,1)S(1)} %get-tuple-element.26), channel_id=1, source_target_pairs={{0,1},{1,0},{2,3},{3,2},{4,5},{5,4},{6,7},{7,6},{8,9},{9,8},{10,11... | collective-permute-start | bytes 393224 | tf_op jit(solution)/shard_map/ppermute | solution.py:350
  32.9 15.0 %collective-permute-start.1 = (bf16[64,1024]{1,0:T(8,128)(2,1)S(1)}, bf16[64,1024]{1,0:T(8,128)(2,1)S(1)}, u32[]{:S(2)}, u32[]{:S(2)}) collective-permute-start(bf16[64,1024]{1,0:T(8,128)(2,1)S(1)} %get-tuple-element.27), channel_id=1, source_target_pairs={{0,2},{1,3},{2,0},{3,1},{4,6},{5,7},{6,4},{7,5},{8,10},{9,11},{10,... | collective-permute-start | bytes 393224 | tf_op jit(solution)/shard_map/ppermute | solution.py:350
  35.2 16.4 %collective-permute-start.2 = (bf16[64,1024]{1,0:T(8,128)(2,1)S(1)}, bf16[64,1024]{1,0:T(8,128)(2,1)S(1)}, u32[]{:S(2)}, u32[]{:S(2)}) collective-permute-start(bf16[64,1024]{1,0:T(8,128)(2,1)S(1)} %get-tuple-element.28), channel_id=1, source_target_pairs={{0,3},{1,2},{2,1},{3,0},{4,7},{5,6},{6,5},{7,4},{8,11},{9,10},{10,... | collective-permute-start | bytes 393224 | tf_op jit(solution)/shard_map/ppermute | solution.py:350
  43.7 8.9 %collective-permute-start.10 = (bf16[128,256]{1,0:T(8,128)(2,1)S(1)}, bf16[128,256]{1,0:T(8,128)(2,1)S(1)}, u32[]{:S(2)}, u32[]{:S(2)}) collective-permute-start(bf16[128,256]{1,0:T(8,128)(2,1)S(1)} %get-tuple-element.38), channel_id=1, source_target_pairs={{0,4},{4,0},{8,12},{12,8},{16,20},{20,16},{24,28},{28,24},{1,5},{5... | collective-permute-start | bytes 196616 | tf_op jit(solution)/shard_map/ppermute | solution.py:350
  44.3 12.6 %collective-permute-start.11 = (bf16[128,256]{1,0:T(8,128)(2,1)S(1)}, bf16[128,256]{1,0:T(8,128)(2,1)S(1)}, u32[]{:S(2)}, u32[]{:S(2)}) collective-permute-start(bf16[128,256]{1,0:T(8,128)(2,1)S(1)} %get-tuple-element.39), channel_id=1, source_target_pairs={{0,8},{4,12},{8,0},{12,4},{16,24},{20,28},{24,16},{28,20},{1,9},{5... | collective-permute-start | bytes 196616 | tf_op jit(solution)/shard_map/ppermute | solution.py:350
  46.9 10.2 %collective-permute-start.12 = (bf16[128,256]{1,0:T(8,128)(2,1)S(1)}, bf16[128,256]{1,0:T(8,128)(2,1)S(1)}, u32[]{:S(2)}, u32[]{:S(2)}) collective-permute-start(bf16[128,256]{1,0:T(8,128)(2,1)S(1)} %get-tuple-element.40), channel_id=1, source_target_pairs={{0,12},{4,8},{8,4},{12,0},{16,28},{20,24},{24,20},{28,16},{1,13},{... | collective-permute-start | bytes 196616 | tf_op jit(solution)/shard_map/ppermute | solution.py:350
  47.9 9.3 %collective-permute-start.13 = (bf16[128,256]{1,0:T(8,128)(2,1)S(1)}, bf16[128,256]{1,0:T(8,128)(2,1)S(1)}, u32[]{:S(2)}, u32[]{:S(2)}) collective-permute-start(bf16[128,256]{1,0:T(8,128)(2,1)S(1)} %get-tuple-element.41), channel_id=1, source_target_pairs={{0,16},{4,20},{8,24},{12,28},{16,0},{20,4},{24,8},{28,12},{1,17},{... | collective-permute-start | bytes 196616 | tf_op jit(solution)/shard_map/ppermute | solution.py:350
  51.6 10.5 %collective-permute-start.14 = (bf16[128,256]{1,0:T(8,128)(2,1)S(1)}, bf16[128,256]{1,0:T(8,128)(2,1)S(1)}, u32[]{:S(2)}, u32[]{:S(2)}) collective-permute-start(bf16[128,256]{1,0:T(8,128)(2,1)S(1)} %get-tuple-element.42), channel_id=1, source_target_pairs={{0,20},{4,16},{8,28},{12,24},{16,4},{20,0},{24,12},{28,8},{1,21},{... | collective-permute-start | bytes 196616 | tf_op jit(solution)/shard_map/ppermute | solution.py:350
  52.5 9.6 %collective-permute-start.15 = (bf16[128,256]{1,0:T(8,128)(2,1)S(1)}, bf16[128,256]{1,0:T(8,128)(2,1)S(1)}, u32[]{:S(2)}, u32[]{:S(2)}) collective-permute-start(bf16[128,256]{1,0:T(8,128)(2,1)S(1)} %get-tuple-element.43), channel_id=1, source_target_pairs={{0,24},{4,28},{8,16},{12,20},{16,8},{20,12},{24,0},{28,4},{1,25},{... | collective-permute-start | bytes 196616 | tf_op jit(solution)/shard_map/ppermute | solution.py:350
  56.9 7.1 %collective-permute-start.16 = (bf16[128,256]{1,0:T(8,128)(2,1)S(1)}, bf16[128,256]{1,0:T(8,128)(2,1)S(1)}, u32[]{:S(2)}, u32[]{:S(2)}) collective-permute-start(bf16[128,256]{1,0:T(8,128)(2,1)S(1)} %get-tuple-element.44), channel_id=1, source_target_pairs={{0,28},{4,24},{8,20},{12,16},{16,12},{20,8},{24,4},{28,0},{1,29},{... | collective-permute-start | bytes 196616 | tf_op jit(solution)/shard_map/ppermute | solution.py:350

commit v3 on v2

--- a/solution.py
+++ b/solution.py
@@ -18,7 +18,7 @@
 ROW = 256
 CHUNK = 16
 HALF = 64
-VMEM_BYTES = 24 * 1024 * 1024
+VMEM_BYTES = 20 * 1024 * 1024
 SMALL_BYTES = 12 * 1024 * 1024
 ALL_BYTES = 60 * 1024 * 1024
 
@@ -54,7 +54,7 @@
     return jnp.where(values < 0.0, -code, code).astype(jnp.bfloat16)
 
 
-def decode(code, axis):
+def decode(code, axis, halvings=0):
     code = code.astype(jnp.float32)
     size = jnp.abs(code)
     octave = jnp.floor(jnp.log(size) * (1.0 / math.log(2.0)) + 0.002)
@@ -64,7 +64,7 @@
     place = lax.broadcasted_iota(jnp.int32, first.shape, axis).astype(jnp.float32)
     bit = first - 2.0 * jnp.floor(first * 0.5)
     held = jnp.where(place < EXPONENT_BITS, bit * jnp.exp2(place), 0.0)
-    scale = jnp.exp2(jnp.sum(held, axis=axis, keepdims=True) - EXPONENT_BIAS)
+    scale = jnp.exp2(jnp.sum(held, axis=axis, keepdims=True) - (EXPONENT_BIAS + halvings))
     share = jnp.maximum(
         level * (0.5 / TOP),
         jnp.maximum(level * (1.0 / TOP) - 0.25, level * (2.0 / TOP) - 1.0),
@@ -76,14 +76,23 @@
     n2 = np.arange(ROW)
     k1 = np.arange(blocks)
     main = 2.0 * np.pi * np.outer(n2, n2) / ROW
-    wave = np.concatenate([np.cos(main), np.sin(main)], axis=1).astype(np.float32)
-    high = wave.astype(jnp.bfloat16)
-    low = (wave - high.astype(np.float32)).astype(jnp.bfloat16)
     twist = 2.0 * np.pi * np.outer(k1 + 0.25, n2) / (blocks * ROW)
     mix = 2.0 * np.pi * np.outer(k1 + 0.25, np.arange(blocks)) / blocks
+    wave = np.concatenate([np.cos(main), np.sin(main)], axis=1).astype(np.float32)
     twist = np.stack([np.cos(twist), np.sin(twist)], axis=1).astype(np.float32)
     mix = np.stack([np.cos(mix), np.sin(mix)], axis=0).astype(np.float32)
-    return high, low, twist, mix
+    return wave, twist, mix
+
+
+def folded(wave):
+    half = np.concatenate([wave[:, :LANES], wave[:, ROW : ROW + LANES]], axis=1)
+    half[:, LANES] = wave[:, LANES]
+    parts = []
+    for values in (half, half.T):
+        high = values.astype(jnp.bfloat16)
+        low = (values - high.astype(np.float32)).astype(jnp.bfloat16)
+        parts.append(np.concatenate([high, low, high], axis=0))
+    return parts
 
 
 def put_split(ref, at, values):
@@ -95,47 +104,51 @@
     ).astype(jnp.bfloat16)
 
 
-def weighted(pairs):
-    total = None
-    for value, weight in pairs:
-        term = value * float(weight)
-        total = term if total is None else total + term
-    return total
-
-
-def mix_forward(blocks_in, twist_ref, mix, at, ref):
-    half = len(blocks_in) // 2
-    for k1 in range(half):
-        sums = []
-        for start in (0, 1):
-            taken = [(blocks_in[n1], mix[:, k1, n1]) for n1 in range(start, 2 * half, 2)]
-            sums.append(weighted([(value, weight[0]) for value, weight in taken]))
-            sums.append(weighted([(value, -weight[1]) for value, weight in taken]))
-        even_re, even_im, odd_re, odd_im = sums
-        for k, re, im in (
-            (k1, even_re + odd_re, even_im + odd_im),
-            (k1 + half, even_re - odd_re, even_im - odd_im),
-        ):
+def turned(value, steps):
+    if steps == 0:
+        return value
+    re, im = value
+    cos, sin = math.cos(math.pi * steps / 16), math.sin(math.pi * steps / 16)
+    return re * cos - im * sin, im * cos + re * sin
+
+
+def four_points(values, sign):
+    (a_re, a_im), (b_re, b_im), (c_re, c_im), (d_re, d_im) = values
+    sum_re, sum_im, gap_re, gap_im = a_re + c_re, a_im + c_im, a_re - c_re, a_im - c_im
+    more_re, more_im = b_re + d_re, b_im + d_im
+    side_re, side_im = sign * (d_im - b_im), sign * (b_re - d_re)
+    return (
+        (sum_re + more_re, sum_im + more_im),
+        (gap_re + side_re, gap_im + side_im),
+        (sum_re - more_re, sum_im - more_im),
+        (gap_re - side_re, gap_im - side_im),
+    )
+
+
+def mix_forward(taken, twist_ref, at, ref):
+    far = [value * math.sqrt(0.5) for value in taken[4:]]
+    even = [turned((taken[n] + far[n], -far[n]), -n) for n in range(4)]
+    odd = [turned((taken[n] - far[n], far[n]), -5 * n) for n in range(4)]
+    for start, values in ((0, four_points(even, -1.0)), (1, four_points(odd, -1.0))):
+        for index, (re, im) in enumerate(values):
+            k = start + 2 * index
             cos_twist, sin_twist = twist_ref[k, 0:1, :], twist_ref[k, 1:2, :]
             put_split(ref, 2 * k * HALF + at, re * cos_twist + im * sin_twist)
             put_split(ref, (2 * k + 1) * HALF + at, im * cos_twist - re * sin_twist)
 
 
-def mix_back(spectra, twist_ref, mix):
-    half = len(spectra) // 2
-    turned = []
+def mix_back(spectra, twist_ref):
+    twisted = []
     for k, (re, im) in enumerate(spectra):
         cos_twist, sin_twist = twist_ref[k, 0:1, :], twist_ref[k, 1:2, :]
-        turned.append((re * cos_twist - im * sin_twist, im * cos_twist + re * sin_twist))
-    totals = [None] * (2 * half)
-    for k1 in range(half):
-        (re, im), (other_re, other_im) = turned[k1], turned[k1 + half]
-        both = ((re + other_re, im + other_im), (re - other_re, im - other_im))
-        for n1 in range(2 * half):
-            re, im = both[n1 % 2]
-            term = weighted([(re, mix[0, k1, n1]), (im, -mix[1, k1, n1])])
-            totals[n1] = term if totals[n1] is None else totals[n1] + term
-    return totals
+        twisted.append((re * cos_twist - im * sin_twist, im * cos_twist + re * sin_twist))
+    even, odd = four_points(twisted[0::2], 1.0), four_points(twisted[1::2], 1.0)
+    near, far = [], []
+    for n in range(4):
+        (even_re, even_im), (odd_re, odd_im) = turned(even[n], n), turned(odd[n], 5 * n)
+        near.append(even_re + odd_re)
+        far.append(((even_re - odd_re) - (even_im - odd_im)) * math.sqrt(0.5))
+    return near + far
 
 
 def spectrum_rows(waves_ref, k, at):
@@ -203,9 +216,38 @@
         code_ref[...] = encode(taps, 1)
 
 
+def first_lane():
+    return lax.broadcasted_iota(jnp.int32, (CHUNK, LANES), 1) == 0
+
+
 def combined(waves_ref, k, at):
     re, im = spectrum_rows(waves_ref, k, at)
-    return re[:, :ROW] + im[:, ROW:], im[:, :ROW] - re[:, ROW:]
+    first = first_lane()
+    re_cos, re_sin, im_cos, im_sin = re[:, :LANES], re[:, LANES:], im[:, :LANES], im[:, LANES:]
+    near = (
+        re_cos + jnp.where(first, 0.0, im_sin),
+        im_cos - jnp.where(first, 0.0, re_sin),
+    )
+    far = (
+        jnp.where(first, re_sin, re_cos - im_sin),
+        jnp.where(first, im_sin, im_cos + re_sin),
+    )
+    return [jnp.concatenate([left, right], axis=1) for left, right in zip(near, far)]
+
+
+def put_folded(ref, k, at, re, im):
+    first = first_lane()
+    near_re, far_re, near_im, far_im = re[:, :LANES], re[:, LANES:], im[:, :LANES], im[:, LANES:]
+    back_re = [
+        jnp.where(first, near_re, near_re + far_re),
+        jnp.where(first, far_re, far_im - near_im),
+    ]
+    back_im = [
+        jnp.where(first, near_im, near_im + far_im),
+        jnp.where(first, far_im, near_re - far_re),
+    ]
+    put_split(ref, 2 * k * HALF + at, jnp.concatenate(back_re, axis=1))
+    put_split(ref, (2 * k + 1) * HALF + at, jnp.concatenate(back_im, axis=1))
 
 
 def stage(wave_ref, source, target, work, half):
@@ -226,7 +268,7 @@
     lax.fori_loop(0, steps, step, 0)
 
 
-def gated_spectrum_kernel(mix, gated_ref, wave_ref, twist_ref, out_ref, u, *scratch):
+def gated_spectrum_kernel(gated_ref, wave_ref, twist_ref, out_ref, u, *scratch):
     blocks = u.shape[0]
     rows, waves = scratch[0:2], scratch[2:4]
     parts = ROW // gated_ref.shape[1]
@@ -238,7 +280,7 @@
 
     def forward(half, at):
         start = pl.ds(half * HALF + at, CHUNK)
-        mix_forward([u[n1, start, :] for n1 in range(blocks)], twist_ref, mix, at, rows[half])
+        mix_forward([u[n1, start, :] for n1 in range(blocks)], twist_ref, at, rows[half])
 
     def finish(half, at):
         for k in range(blocks):
@@ -247,52 +289,46 @@
             out_ref[half, k, 1, pl.ds(at, CHUNK), :] = im
 
     lax.fori_loop(0, blocks, unpack, 0)
-    stage(wave_ref, None, None, forward, 0)
+    stage(None, None, None, forward, 0)
     stage(wave_ref, rows[0], waves[0], forward, 1)
     stage(wave_ref, rows[1], waves[1], finish, 0)
-    stage(wave_ref, None, None, finish, 1)
-
-
-def conv_kernel(mix, gated_ref, *refs):
-    blocks = len(mix[0])
-    wave_ref, twist_ref = refs[blocks : blocks + 2]
-    out_refs = refs[blocks + 2 : 2 * blocks + 2]
-    codes, out, *scratch = refs[2 * blocks + 2 :]
+    stage(None, None, None, finish, 1)
+
+
+def conv_kernel(gated_ref, *refs):
+    blocks = gated_ref.shape[1]
+    wave_ref, back_wave_ref, twist_ref, out, codes, *scratch = refs[blocks:]
     rows, waves = scratch[0:2], scratch[2:4]
+    scale = math.log2(blocks * ROW)
     me = lax.axis_index("seq")
     for turn, code_ref in enumerate(refs[:blocks]):
         codes[me ^ turn] = code_ref[...]
 
     def forward(half, at):
         start = pl.ds(half * HALF + at, CHUNK)
-        taken = [decode(codes[n1, start, :], 1) for n1 in range(blocks)]
-        mix_forward(taken, twist_ref, mix, at, rows[half])
+        taken = [decode(codes[n1, start, :], 1, scale) for n1 in range(blocks)]
+        mix_forward(taken, twist_ref, at, rows[half])
 
     def product(half, at):
         for k in range(blocks):
             re, im = combined(waves[half], k, at)
             gated_re = gated_ref[half, k, 0, pl.ds(at, CHUNK), :]
             gated_im = gated_ref[half, k, 1, pl.ds(at, CHUNK), :]
-            put_split(rows[half], 2 * k * HALF + at, re * gated_re - im * gated_im)
-            put_split(rows[half], (2 * k + 1) * HALF + at, re * gated_im + im * gated_re)
+            product_re, product_im = re * gated_re - im * gated_im, re * gated_im + im * gated_re
+            put_folded(rows[half], k, at, product_re, product_im)
 
     def back(half, at):
-        spectra = []
-        for k in range(blocks):
-            re, im = spectrum_rows(waves[half], k, at)
-            spectra.append((re[:, :ROW] - im[:, ROW:], im[:, :ROW] + re[:, ROW:]))
+        spectra = [spectrum_rows(waves[half], k, at) for k in range(blocks)]
         start = pl.ds(half * HALF + at, CHUNK)
-        for n1, total in enumerate(mix_back(spectra, twist_ref, mix)):
-            out[n1, start, :] = encode(total * (1.0 / (blocks * ROW)), 1)
-
-    stage(wave_ref, None, None, forward, 0)
+        for n1, total in enumerate(mix_back(spectra, twist_ref)):
+            out[n1, start, :] = encode(total, 1)
+
+    stage(None, None, None, forward, 0)
     stage(wave_ref, rows[0], waves[0], forward, 1)
     stage(wave_ref, rows[1], waves[1], product, 0)
-    stage(wave_ref, rows[0], waves[0], product, 1)
-    stage(wave_ref, rows[1], waves[1], back, 0)
-    stage(wave_ref, None, None, back, 1)
-    for turn, out_ref in enumerate(out_refs):
-        out_ref[...] = out[me ^ turn]
+    stage(back_wave_ref, rows[0], waves[0], product, 1)
+    stage(back_wave_ref, rows[1], waves[1], back, 0)
+    stage(None, None, None, back, 1)
 
 
 def turn_kernel(*refs):
@@ -305,15 +341,13 @@
     out_ref[...] = jnp.transpose(whole[...]).astype(jnp.bfloat16)
 
 
-def mix_kernel(query_ref, *refs):
-    conv_refs, (out_ref, mixed, sems) = refs[:-3], refs[-3:]
-    me = lax.axis_index("seq")
+def mix_kernel(query_ref, conv_ref, out_ref, mixed, sems):
     copies = []
-    for turn, conv_ref in enumerate(conv_refs):
-        at = pl.ds(pl.multiple_of((me ^ turn) * LANES, LANES), LANES)
+    for block in range(conv_ref.shape[0]):
+        at = pl.ds(block * LANES, LANES)
         queries = query_ref[at, :].astype(jnp.float32)
-        mixed[at, :] = (queries * decode(conv_ref[...], 1)).astype(jnp.bfloat16)
-        copy = pltpu.make_async_copy(mixed.at[at], out_ref.at[at], sems.at[turn])
+        mixed[at, :] = (queries * decode(conv_ref[block], 1)).astype(jnp.bfloat16)
+        copy = pltpu.make_async_copy(mixed.at[at], out_ref.at[at], sems.at[block])
         copy.start()
         copies.append(copy)
     for copy in copies:
@@ -322,8 +356,7 @@
 
 def plain_conv(gated, taps):
     blocks = gated.shape[0]
-    high, low, twist, mix = tables(blocks)
-    wave = jnp.asarray(high, jnp.float32) + jnp.asarray(low, jnp.float32)
+    wave, twist, mix = tables(blocks)
     cos_twist, sin_twist = twist[:, 0][:, None, :], twist[:, 1][:, None, :]
     dot = functools.partial(jnp.einsum, precision=lax.Precision.HIGHEST)
 
@@ -359,7 +392,7 @@
     own = wide // groups
     blocks = filter_taps.shape[1] * groups // ROW
     streams = jnp.transpose(streams, (1, 0, 2))
-    fits = own == LANES and filter_taps.shape[1] == ROW and ROW % held == 0 and groups % 4 == 0
+    fits = blocks == 8 and own == LANES and filter_taps.shape[1] == ROW and ROW % held == 0 and groups % 4 == 0
     fits = fits and groups & (groups - 1) == 0 and parts & (parts - 1) == 0
     small = pltpu.CompilerParams(vmem_limit_bytes=SMALL_BYTES)
     if fits:
@@ -417,13 +450,13 @@
         gated = exchange(gated, ("seq", "ch"))
         queries = exchange(queries, "ch").reshape(parts * held, wide)
     if fits:
-        high, low, twist, mix = tables(blocks)
-        wave = np.concatenate([high, low, high], axis=0)
+        wave, twist, _ = tables(blocks)
+        wave, back_wave = folded(wave)
         scratch = [pltpu.VMEM((blocks * 2 * HALF, 3 * ROW), jnp.bfloat16)] * 2
-        scratch += [pltpu.VMEM((blocks * 2 * HALF, 2 * ROW), jnp.float32)] * 2
+        scratch += [pltpu.VMEM((blocks * 2 * HALF, ROW), jnp.float32)] * 2
         large = pltpu.CompilerParams(vmem_limit_bytes=VMEM_BYTES)
         gated = pl.pallas_call(
-            functools.partial(gated_spectrum_kernel, mix),
+            gated_spectrum_kernel,
             out_shape=jax.ShapeDtypeStruct((2, blocks, 2, HALF, ROW), jnp.float32),
             scratch_shapes=[pltpu.VMEM((blocks, own, ROW), jnp.float32)] + scratch,
             compiler_params=large,
@@ -431,21 +464,21 @@
             name="gated_spectrum",
         )(gated, wave, twist)
         convolved = pl.pallas_call(
-            functools.partial(conv_kernel, mix),
-            out_shape=[jax.ShapeDtypeStruct((own, ROW), jnp.bfloat16)] * groups,
-            scratch_shapes=[pltpu.VMEM((blocks, own, ROW), jnp.bfloat16)] * 2 + scratch,
+            conv_kernel,
+            out_shape=jax.ShapeDtypeStruct((blocks, own, ROW), jnp.bfloat16),
+            scratch_shapes=[pltpu.VMEM((blocks, own, ROW), jnp.bfloat16)] + scratch,
             compiler_params=large,
             cost_estimate=cost(2**32, 2**24),
             name="convolve",
-        )(gated, *taps, wave, twist)
+        )(gated, *taps, wave, back_wave, twist)
     else:
         gated = decode(gated, 1).reshape(blocks, ROW, own)
         taps = jnp.transpose(decode(taps, 2), (1, 0, 2)).reshape(own, blocks, ROW)
         convolved = plain_conv(jnp.transpose(gated, (0, 2, 1)), jnp.transpose(taps, (1, 0, 2)))
         convolved = jnp.transpose(convolved, (1, 0, 2)).reshape(own, groups, -1)
         convolved = encode(jnp.transpose(convolved, (1, 0, 2)), 2)
+    convolved = exchange(convolved, "seq")
     if fits:
-        convolved = scatter(convolved, "seq")
         queries = pl.pallas_call(
             turn_kernel,
             out_shape=jax.ShapeDtypeStruct((wide, ROW), jnp.bfloat16),
@@ -464,8 +497,7 @@
             ],
             compiler_params=small,
             name="mix_out",
-        )(queries, *convolved)
-    convolved = exchange(convolved, "seq")
+        )(queries, convolved)
     queries = jnp.transpose(queries.astype(jnp.float32))
     return (queries * decode(convolved, 2).reshape(wide, -1)).astype(jnp.bfloat16)
 

time: 66.1 us -> 63.1 us (0.955)
  waiting for transfers between devices: 7.92 us -> 17.7 us
  starting transfers between devices: 36.1 us -> 27.4 us
  Pallas kernels: 19.8 us -> 17.6 us
  local copies, waits for them, and re-layouts: 1.86 us -> 0.02 us
    ppermute x17 -> x10, starting transfers between devices: 28.8 us -> 15.9 us  [scatter(): lax.ppermute(block, axis, [(i, i ^ turn) for i in range(count)])]
    all_to_all x0 -> x1, waiting for transfers between devices: none -> 5.77 us  [body(): convolved = exchange(convolved, 'seq')]
    all_to_all x0 -> x1, starting transfers between devices: none -> 4.15 us  [body(): convolved = exchange(convolved, 'seq')]
    ppermute x17 -> x10, waiting for transfers between devices: 7.87 us -> 11.9 us  [scatter(): lax.ppermute(block, axis, [(i, i ^ turn) for i in range(count)])]
    pallas_call x2, Pallas kernels: 13 us -> 10.9 us  [the longest x1 7.1 us: body(): pl.pallas_call(conv_kernel, out_shape=jax.ShapeDtypeStruct((blocks, own,...]
    unnamed x10 -> x12, local copies, waits for them, and re-layouts: 1.86 us -> 0.02 us
  transfers between devices with their start and end apart: 18 -> 12, of which waited for: 5 -> 6; matrix products, arithmetic and copies ran while one was open for 0% -> 0% of each run, Pallas kernels for 23% -> 9%
where the time goes in v3:
time: 63.1 us; the launch traced here: 62.8 us
  starting transfers between devices  27.4 us (43%)
  waiting for transfers between devices  17.7 us (28%)
  Pallas kernels  17.6 us (28%)
    ppermute x10, starting transfers between devices, scatter(): lax.ppermute(block, axis, [(i, i ^ turn) for i in range(count)])  15.9 us
    ppermute x10, waiting for transfers between devices, scatter(): lax.ppermute(block, axis, [(i, i ^ turn) for i in range(count)])  11.9 us
    all_to_all x1, starting transfers between devices, body(): gated = exchange(gated, ('seq', 'ch'))  7.32 us
    pallas_call x1, Pallas kernels, body(): pl.pallas_call(conv_kernel, out_shape=jax.ShapeDtypeStruct((blocks, own,...  7.1 us
    all_to_all x1, waiting for transfers between devices, body(): convolved = exchange(convolved, 'seq')  5.77 us
    all_to_all x1, starting transfers between devices, body(): convolved = exchange(convolved, 'seq')  4.15 us
    pallas_call x1, Pallas kernels, body(): pl.pallas_call(gated_spectrum_kernel, out_shape=jax.ShapeDtypeStruct((2,...  3.76 us
    pallas_call x1, Pallas kernels, body(): pl.pallas_call(send_kernel, in_specs=[far], out_specs=far, out_shape=jax....  3.02 us
  transfers between devices with their start and end apart: 12, of which 6 were waited for; matrix products, arithmetic and copies ran while one was open for 0% of the time, Pallas kernels for 9%

profile of v3, /device:TPU:0, one launch (start us, length us, event | category | flops | bytes accessed | tf_op | source)
XLA Modules:
  0.0 62.8 jit_solution(15623517534394561466)
XLA Ops:
  0.0 3.0 %encode_gated.1 = bf16[8,4,64,128]{3,2,1,0:T(8,128)(2,1)} custom-call(bf16[3,64,4096]{2,1,0:T(8,128)(2,1)} %bitcast.4), custom_call_target="tpu_custom_call" | custom-call | flops 33554432 | bytes 8388608 | tf_op jit(solution)/shard_map/encode_gated/pallas_call | solution.py:402
  3.0 7.3 %all-to-all-start = ((bf16[32,64,128]{2,1,0:T(8,128)(2,1)}), bf16[32,64,128]{2,1,0:T(8,128)(2,1)S(1)}, u32[]{:S(2)}, u32[]{:S(2)}) async-start(bf16[32,64,128]{2,1,0:T(8,128)(2,1)} %bitcast.8), calls=%async_computation | async-start | bytes 1048576 | tf_op jit(solution)/shard_map/all_to_all | solution.py:446
  10.4 1.5 %encode_taps.1 = (bf16[128,256]{1,0:T(8,128)(2,1)S(1)}, bf16[128,256]{1,0:T(8,128)(2,1)S(1)}, bf16[128,256]{1,0:T(8,128)(2,1)S(1)}, bf16[128,256]{1,0:T(8,128)(2...) custom-call(f32[8,128,256]{2,1,0:T(8,128)S(1)} %bitcast.6, ...), custom_call_target="tpu_custom_call" | custom-call | flops 33554432 | bytes 8388608 | tf_op jit(solution)/shard_map/encode_taps/pallas_call | solution.py:428
  11.9 1.8 %collective-permute-start.3 = (bf16[128,256]{1,0:T(8,128)(2,1)S(1)}, bf16[128,256]{1,0:T(8,128)(2,1)S(1)}, u32[]{:S(2)}, u32[]{:S(2)}) collective-permute-start(bf16[128,256]{1,0:T(8,128)(2,1)S(1)} %get-tuple-element.22), channel_id=1, source_target_pairs={{0,4},{4,0},{8,12},{12,8},{16,20},{20,16},{24,28},{28,24},{1,5},{5... | collective-permute-start | bytes 196616 | tf_op jit(solution)/shard_map/ppermute | solution.py:383
  13.7 1.5 %collective-permute-start.4 = (bf16[128,256]{1,0:T(8,128)(2,1)S(1)}, bf16[128,256]{1,0:T(8,128)(2,1)S(1)}, u32[]{:S(2)}, u32[]{:S(2)}) collective-permute-start(bf16[128,256]{1,0:T(8,128)(2,1)S(1)} %get-tuple-element.23), channel_id=1, source_target_pairs={{0,8},{4,12},{8,0},{12,4},{16,24},{20,28},{24,16},{28,20},{1,9},{5... | collective-permute-start | bytes 196616 | tf_op jit(solution)/shard_map/ppermute | solution.py:383
  15.2 0.3 collective-permute-start.5
  15.4 2.7 %collective-permute-start.6 = (bf16[128,256]{1,0:T(8,128)(2,1)S(1)}, bf16[128,256]{1,0:T(8,128)(2,1)S(1)}, u32[]{:S(2)}, u32[]{:S(2)}) collective-permute-start(bf16[128,256]{1,0:T(8,128)(2,1)S(1)} %get-tuple-element.25), channel_id=1, source_target_pairs={{0,16},{4,20},{8,24},{12,28},{16,0},{20,4},{24,8},{28,12},{1,17},{... | collective-permute-start | bytes 196616 | tf_op jit(solution)/shard_map/ppermute | solution.py:383
  18.1 1.5 %collective-permute-start.7 = (bf16[128,256]{1,0:T(8,128)(2,1)S(1)}, bf16[128,256]{1,0:T(8,128)(2,1)S(1)}, u32[]{:S(2)}, u32[]{:S(2)}) collective-permute-start(bf16[128,256]{1,0:T(8,128)(2,1)S(1)} %get-tuple-element.26), channel_id=1, source_target_pairs={{0,20},{4,16},{8,28},{12,24},{16,4},{20,0},{24,12},{28,8},{1,21},{... | collective-permute-start | bytes 196616 | tf_op jit(solution)/shard_map/ppermute | solution.py:383
  19.6 3.3 %collective-permute-start.8 = (bf16[128,256]{1,0:T(8,128)(2,1)S(1)}, bf16[128,256]{1,0:T(8,128)(2,1)S(1)}, u32[]{:S(2)}, u32[]{:S(2)}) collective-permute-start(bf16[128,256]{1,0:T(8,128)(2,1)S(1)} %get-tuple-element.27), channel_id=1, source_target_pairs={{0,24},{4,28},{8,16},{12,20},{16,8},{20,12},{24,0},{28,4},{1,25},{... | collective-permute-start | bytes 196616 | tf_op jit(solution)/shard_map/ppermute | solution.py:383
  22.9 2.9 %collective-permute-start.9 = (bf16[128,256]{1,0:T(8,128)(2,1)S(1)}, bf16[128,256]{1,0:T(8,128)(2,1)S(1)}, u32[]{:S(2)}, u32[]{:S(2)}) collective-permute-start(bf16[128,256]{1,0:T(8,128)(2,1)S(1)} %get-tuple-element.28), channel_id=1, source_target_pairs={{0,28},{4,24},{8,20},{12,16},{16,12},{20,8},{24,4},{28,0},{1,29},{... | collective-permute-start | bytes 196616 | tf_op jit(solution)/shard_map/ppermute | solution.py:383
  25.9 3.8 %gated_spectrum.1.gated_ref = f32[2,8,2,64,256]{4,3,2,1,0:T(8,128)S(1)} custom-call(bf16[32,64,128]{2,1,0:T(8,128)(2,1)S(1)} %all-to-all-done.gated_ref, bf16[768,256]{1,0:T(8,128)(2,1)S(1)} %copy-done.3, f32[8,2,256]{2,1,0:T(2,128)S(1)} %copy-done.5), custom_call_target="tpu_custom_call" | custom-call | flops 4294967296 | bytes 16777216 | tf_op jit(solution)/shard_map/gated_spectrum/pallas_call | solution.py:458
  29.7 3.2 %collective-permute-done.6.refs_4_ = bf16[128,256]{1,0:T(8,128)(2,1)S(1)} collective-permute-done((bf16[128,256]{1,0:T(8,128)(2,1)S(1)}, bf16[128,256]{1,0:T(8,128)(2,1)S(1)}, u32[]{:S(2)}, u32[]{:S(2)}) %collective-permute-start.6) | collective-permute-done | bytes 65568 | tf_op jit(solution)/shard_map/ppermute | solution.py:383
  32.9 2.3 %collective-permute-done.7.refs_5_ = bf16[128,256]{1,0:T(8,128)(2,1)S(1)} collective-permute-done((bf16[128,256]{1,0:T(8,128)(2,1)S(1)}, bf16[128,256]{1,0:T(8,128)(2,1)S(1)}, u32[]{:S(2)}, u32[]{:S(2)}) %collective-permute-start.7) | collective-permute-done | bytes 65568 | tf_op jit(solution)/shard_map/ppermute | solution.py:383
  35.2 7.1 %convolve.1 = bf16[8,128,256]{2,1,0:T(8,128)(2,1)} custom-call(f32[2,8,2,64,256]{4,3,2,1,0:T(8,128)S(1)} %gated_spectrum.1.gated_ref, bf16[128,256]{1,0:T(8,128)(2,1)S(1)} %get-tuple-element.21.refs_0_, bf16[128,256]{1,0:T(8,128)(2,1)S(1)} %collective-permute-done.3.refs_1_, bf16[128,256]{1,0:T(8,128)(2,1)S(1)} %collective-permute-done.4.refs_2_, ...), custom_call_target="tpu_custom_call" | custom-call | flops 4294967296 | bytes 16777216 | tf_op jit(solution)/shard_map/convolve/pallas_call | solution.py:466
  42.3 4.2 %all-to-all-start.1 = ((bf16[8,128,256]{2,1,0:T(8,128)(2,1)}), bf16[8,128,256]{2,1,0:T(8,128)(2,1)S(1)}, u32[]{:S(2)}, u32[]{:S(2)}) async-start(bf16[8,128,256]{2,1,0:T(8,128)(2,1)} %convolve.1), calls=%async_computation.1 | async-start | bytes 1048576 | tf_op jit(solution)/shard_map/all_to_all | solution.py:480
  46.5 0.1 send_queries.1
  46.6 0.1 collective-permute-start
  46.7 1.5 %collective-permute-start.1 = (bf16[64,1024]{1,0:T(8,128)(2,1)S(1)}, bf16[64,1024]{1,0:T(8,128)(2,1)S(1)}, u32[]{:S(2)}, u32[]{:S(2)}) collective-permute-start(bf16[64,1024]{1,0:T(8,128)(2,1)S(1)} %get-tuple-element.19), channel_id=1, source_target_pairs={{0,2},{1,3},{2,0},{3,1},{4,6},{5,7},{6,4},{7,5},{8,10},{9,11},{10,... | collective-permute-start | bytes 393224 | tf_op jit(solution)/shard_map/ppermute | solution.py:383
  48.2 0.3 collective-permute-start.2
  48.6 4.5 %collective-permute-done.1.refs_2_ = bf16[64,1024]{1,0:T(8,128)(2,1)S(1)} collective-permute-done((bf16[64,1024]{1,0:T(8,128)(2,1)S(1)}, bf16[64,1024]{1,0:T(8,128)(2,1)S(1)}, u32[]{:S(2)}, u32[]{:S(2)}) %collective-permute-start.1) | collective-permute-done | bytes 131104 | tf_op jit(solution)/shard_map/ppermute | solution.py:383
  53.1 1.9 %collective-permute-done.2.refs_3_ = bf16[64,1024]{1,0:T(8,128)(2,1)S(1)} collective-permute-done((bf16[64,1024]{1,0:T(8,128)(2,1)S(1)}, bf16[64,1024]{1,0:T(8,128)(2,1)S(1)}, u32[]{:S(2)}, u32[]{:S(2)}) %collective-permute-start.2) | collective-permute-done | bytes 131104 | tf_op jit(solution)/shard_map/ppermute | solution.py:383
  55.0 0.3 turn_queries.1.query_ref
  55.2 5.8 %all-to-all-done.1.conv_ref = bf16[8,128,256]{2,1,0:T(8,128)(2,1)S(1)} async-done(((bf16[8,128,256]{2,1,0:T(8,128)(2,1)}), bf16[8,128,256]{2,1,0:T(8,128)(2,1)S(1)}, u32[]{:S(2)}, u32[]{:S(2)}) %all-to-all-start.1) | async-done | bytes 524320 | tf_op jit(solution)/shard_map/all_to_all | solution.py:480
  61.0 1.8 %mix_out.1 = bf16[1024,256]{1,0:T(8,128)(2,1)} custom-call(bf16[1024,256]{1,0:T(8,128)(2,1)S(1)} %turn_queries.1.query_ref, bf16[8,128,256]{2,1,0:T(8,128)(2,1)S(1)} %all-to-all-done.1.conv_ref), custom_call_target="tpu_custom_call" | custom-call | tf_op jit(solution)/shard_map/mix_out/pallas_call | solution.py:490
  (19 shorter events, 0.1 us)
Async XLA Ops:
  0.0 10.4 %copy-start.1 = (f32[1024,256]{1,0:T(8,128)S(1)}, f32[1024,256]{1,0:T(8,128)}, u32[]{:S(2)}) copy-start(f32[1024,256]{1,0:T(8,128)} %param.7) | copy-start | bytes 3145732
  0.0 10.4 %copy-start.2 = (f32[1024]{0:T(1024)S(1)}, f32[1024]{0:T(1024)}, u32[]{:S(2)}) copy-start(f32[1024]{0:T(1024)} %param.8) | copy-start | bytes 12292
  0.0 25.9 %copy-start.3 = (bf16[768,256]{1,0:T(8,128)(2,1)S(1)}, bf16[768,256]{1,0:T(8,128)(2,1)}, u32[]{:S(2)}) copy-start(bf16[768,256]{1,0:T(8,128)(2,1)} %constant.6.clone.wave_ref.refs_8_) | copy-start | bytes 1179652
  0.0 25.9 %copy-start.5 = (f32[8,2,256]{2,1,0:T(2,128)S(1)}, f32[8,2,256]{2,1,0:T(2,128)}, u32[]{:S(2)}) copy-start(f32[8,2,256]{2,1,0:T(2,128)} %constant.7.clone.twist_ref.refs_10_) | copy-start | bytes 49156
  3.0 22.9 %all-to-all-start = ((bf16[32,64,128]{2,1,0:T(8,128)(2,1)}), bf16[32,64,128]{2,1,0:T(8,128)(2,1)S(1)}, u32[]{:S(2)}, u32[]{:S(2)}) async-start(bf16[32,64,128]{2,1,0:T(8,128)(2,1)} %bitcast.8), calls=%async_computation | async-start | bytes 1048576 | tf_op jit(solution)/shard_map/all_to_all | solution.py:446
  11.9 7.7 %collective-permute-start.3 = (bf16[128,256]{1,0:T(8,128)(2,1)S(1)}, bf16[128,256]{1,0:T(8,128)(2,1)S(1)}, u32[]{:S(2)}, u32[]{:S(2)}) collective-permute-start(bf16[128,256]{1,0:T(8,128)(2,1)S(1)} %get-tuple-element.22), channel_id=1, source_target_pairs={{0,4},{4,0},{8,12},{12,8},{16,20},{20,16},{24,28},{28,24},{1,5},{5... | collective-permute-start | bytes 196616 | tf_op jit(solution)/shard_map/ppermute | solution.py:383
  13.7 9.2 %collective-permute-start.4 = (bf16[128,256]{1,0:T(8,128)(2,1)S(1)}, bf16[128,256]{1,0:T(8,128)(2,1)S(1)}, u32[]{:S(2)}, u32[]{:S(2)}) collective-permute-start(bf16[128,256]{1,0:T(8,128)(2,1)S(1)} %get-tuple-element.23), channel_id=1, source_target_pairs={{0,8},{4,12},{8,0},{12,4},{16,24},{20,28},{24,16},{28,20},{1,9},{5... | collective-permute-start | bytes 196616 | tf_op jit(solution)/shard_map/ppermute | solution.py:383
  15.2 14.5 %collective-permute-start.5 = (bf16[128,256]{1,0:T(8,128)(2,1)S(1)}, bf16[128,256]{1,0:T(8,128)(2,1)S(1)}, u32[]{:S(2)}, u32[]{:S(2)}) collective-permute-start(bf16[128,256]{1,0:T(8,128)(2,1)S(1)} %get-tuple-element.24), channel_id=1, source_target_pairs={{0,12},{4,8},{8,4},{12,0},{16,28},{20,24},{24,20},{28,16},{1,13},{... | collective-permute-start | bytes 196616 | tf_op jit(solution)/shard_map/ppermute | solution.py:383
  15.4 17.4 %collective-permute-start.6 = (bf16[128,256]{1,0:T(8,128)(2,1)S(1)}, bf16[128,256]{1,0:T(8,128)(2,1)S(1)}, u32[]{:S(2)}, u32[]{:S(2)}) collective-permute-start(bf16[128,256]{1,0:T(8,128)(2,1)S(1)} %get-tuple-element.25), channel_id=1, source_target_pairs={{0,16},{4,20},{8,24},{12,28},{16,0},{20,4},{24,8},{28,12},{1,17},{... | collective-permute-start | bytes 196616 | tf_op jit(solution)/shard_map/ppermute | solution.py:383
  18.1 17.1 %collective-permute-start.7 = (bf16[128,256]{1,0:T(8,128)(2,1)S(1)}, bf16[128,256]{1,0:T(8,128)(2,1)S(1)}, u32[]{:S(2)}, u32[]{:S(2)}) collective-permute-start(bf16[128,256]{1,0:T(8,128)(2,1)S(1)} %get-tuple-element.26), channel_id=1, source_target_pairs={{0,20},{4,16},{8,28},{12,24},{16,4},{20,0},{24,12},{28,8},{1,21},{... | collective-permute-start | bytes 196616 | tf_op jit(solution)/shard_map/ppermute | solution.py:383
  19.6 15.6 %collective-permute-start.8 = (bf16[128,256]{1,0:T(8,128)(2,1)S(1)}, bf16[128,256]{1,0:T(8,128)(2,1)S(1)}, u32[]{:S(2)}, u32[]{:S(2)}) collective-permute-start(bf16[128,256]{1,0:T(8,128)(2,1)S(1)} %get-tuple-element.27), channel_id=1, source_target_pairs={{0,24},{4,28},{8,16},{12,20},{16,8},{20,12},{24,0},{28,4},{1,25},{... | collective-permute-start | bytes 196616 | tf_op jit(solution)/shard_map/ppermute | solution.py:383
  22.9 12.3 %copy-start.4 = (bf16[768,256]{1,0:T(8,128)(2,1)S(1)}, bf16[768,256]{1,0:T(8,128)(2,1)}, u32[]{:S(2)}) copy-start(bf16[768,256]{1,0:T(8,128)(2,1)} %constant.8.clone.refs_9_) | copy-start | bytes 1179652
  22.9 12.3 %collective-permute-start.9 = (bf16[128,256]{1,0:T(8,128)(2,1)S(1)}, bf16[128,256]{1,0:T(8,128)(2,1)S(1)}, u32[]{:S(2)}, u32[]{:S(2)}) collective-permute-start(bf16[128,256]{1,0:T(8,128)(2,1)S(1)} %get-tuple-element.28), channel_id=1, source_target_pairs={{0,28},{4,24},{8,20},{12,16},{16,12},{20,8},{24,4},{28,0},{1,29},{... | collective-permute-start | bytes 196616 | tf_op jit(solution)/shard_map/ppermute | solution.py:383
  35.2 11.3 %copy-start = (bf16[64,3,4096]{2,0,1:T(8,128)(2,1)S(1)}, bf16[64,3,4096]{2,0,1:T(8,128)(2,1)}, u32[]{:S(2)}) copy-start(bf16[64,3,4096]{2,0,1:T(8,128)(2,1)} %param.6) | copy-start | bytes 4718596
  42.3 18.7 %all-to-all-start.1 = ((bf16[8,128,256]{2,1,0:T(8,128)(2,1)}), bf16[8,128,256]{2,1,0:T(8,128)(2,1)S(1)}, u32[]{:S(2)}, u32[]{:S(2)}) async-start(bf16[8,128,256]{2,1,0:T(8,128)(2,1)} %convolve.1), calls=%async_computation.1 | async-start | bytes 1048576 | tf_op jit(solution)/shard_map/all_to_all | solution.py:480
  46.6 1.9 %collective-permute-start = (bf16[64,1024]{1,0:T(8,128)(2,1)S(1)}, bf16[64,1024]{1,0:T(8,128)(2,1)S(1)}, u32[]{:S(2)}, u32[]{:S(2)}) collective-permute-start(bf16[64,1024]{1,0:T(8,128)(2,1)S(1)} %get-tuple-element.18), channel_id=1, source_target_pairs={{0,1},{1,0},{2,3},{3,2},{4,5},{5,4},{6,7},{7,6},{8,9},{9,8},{10,11... | collective-permute-start | bytes 393224 | tf_op jit(solution)/shard_map/ppermute | solution.py:383
  46.7 6.4 %collective-permute-start.1 = (bf16[64,1024]{1,0:T(8,128)(2,1)S(1)}, bf16[64,1024]{1,0:T(8,128)(2,1)S(1)}, u32[]{:S(2)}, u32[]{:S(2)}) collective-permute-start(bf16[64,1024]{1,0:T(8,128)(2,1)S(1)} %get-tuple-element.19), channel_id=1, source_target_pairs={{0,2},{1,3},{2,0},{3,1},{4,6},{5,7},{6,4},{7,5},{8,10},{9,11},{10,... | collective-permute-start | bytes 393224 | tf_op jit(solution)/shard_map/ppermute | solution.py:383
  48.2 6.7 %collective-permute-start.2 = (bf16[64,1024]{1,0:T(8,128)(2,1)S(1)}, bf16[64,1024]{1,0:T(8,128)(2,1)S(1)}, u32[]{:S(2)}, u32[]{:S(2)}) collective-permute-start(bf16[64,1024]{1,0:T(8,128)(2,1)S(1)} %get-tuple-element.20), channel_id=1, source_target_pairs={{0,3},{1,2},{2,1},{3,0},{4,7},{5,6},{6,5},{7,4},{8,11},{9,10},{10,... | collective-permute-start | bytes 393224 | tf_op jit(solution)/shard_map/ppermute | solution.py:383

commit v4 on v3

--- a/solution.py
+++ b/solution.py
@@ -9,8 +9,7 @@
 from jax.experimental.pallas import tpu as pltpu
 from jax.sharding import PartitionSpec as P
 
-TOP = 32000.0
-TOP_LEVEL = 32255.0
+OCTAVES = 250.0
 LOW_POWER = 125.0
 EXPONENT_BITS = 8
 EXPONENT_BIAS = 127.0
@@ -31,45 +30,65 @@
     return first, lax.slice_in_dim(values, count, values.shape[axis], axis=axis)
 
 
+def scale_of(peak):
+    power = jnp.floor(jnp.log(jnp.maximum(peak, 1e-30)) * (1.0 / math.log(2.0))) + 1.0
+    return jnp.clip(power, -100.0, 126.0)
+
+
+def exponent_bits(power, shape, axis):
+    place = lax.broadcasted_iota(jnp.int32, shape, axis).astype(jnp.float32)
+    bits = (power + (EXPONENT_BIAS + 0.25)) * jnp.exp2(-1.0 - place)
+    return jnp.where(bits - jnp.floor(bits) >= 0.5, 0.5, 0.0), place < EXPONENT_BITS
+
+
 def encode(values, axis):
-    size = jnp.abs(values)
-    peak = jnp.max(size, axis=axis, keepdims=True)
-    power = jnp.floor(jnp.log(jnp.maximum(peak, 1e-30)) * (1.0 / math.log(2.0))) + 1.0
-    power = jnp.clip(power, -100.0, 126.0)
-    share = size * jnp.exp2(-power)
-    level = jnp.minimum(
-        share * (2.0 * TOP), jnp.minimum(share * TOP + TOP / 4, share * (TOP / 2) + TOP / 2)
-    )
-    first, rest = split_first(level, axis)
-    place = lax.broadcasted_iota(jnp.int32, first.shape, axis).astype(jnp.float32)
-    halves = jnp.floor((power + (EXPONENT_BIAS + 0.25)) * jnp.exp2(-place))
-    bit = halves - 2.0 * jnp.floor(halves * 0.5)
-    marked = 2.0 * jnp.floor((first - bit) * 0.5 + 0.5) + bit
-    level = jnp.where(place < EXPONENT_BITS, marked, jnp.floor(first + 0.5))
-    if rest is not None:
-        level = jnp.concatenate([level, jnp.floor(rest + 0.5)], axis=axis)
-    level = jnp.minimum(level, TOP_LEVEL) * (1.0 / 128.0)
-    octave = jnp.floor(level)
-    code = jnp.exp2(octave - LOW_POWER) * (level - octave + 1.0)
-    return jnp.where(values < 0.0, -code, code).astype(jnp.bfloat16)
+    peak = jnp.max(jnp.abs(values), axis=axis, keepdims=True)
+    return encode_all([values], scale_of(peak), axis)[0]
+
+
+def encode_all(blocks, power, axis):
+    unit_share, codes, bits = jnp.exp2(-power), [], None
+    for values in blocks:
+        share = jnp.abs(values) * unit_share
+        level = jnp.minimum(
+            share * (2.0 * OCTAVES),
+            jnp.minimum(share * OCTAVES + OCTAVES / 4, share * (OCTAVES / 2) + OCTAVES / 2),
+        )
+        level = jnp.minimum(level, OCTAVES + 1.0)
+        first, rest = split_first(level, axis)
+        bits = exponent_bits(power, first.shape, axis) if bits is None else bits
+        odd, holds = bits
+        marked = (jnp.floor(first * 64.0 - odd + 0.5) + odd) * (1.0 / 64.0)
+        level = jnp.where(holds, marked, first)
+        if rest is not None:
+            level = jnp.concatenate([level, rest], axis=axis)
+        octave = jnp.floor(level)
+        unit = jnp.exp2(octave - LOW_POWER)
+        code = jnp.where(values < 0.0, -unit, unit) * (level - octave + 1.0)
+        codes.append(code.astype(jnp.bfloat16))
+    return codes
 
 
 def decode(code, axis, halvings=0):
     code = code.astype(jnp.float32)
     size = jnp.abs(code)
     octave = jnp.floor(jnp.log(size) * (1.0 / math.log(2.0)) + 0.002)
-    level = (octave + size * jnp.exp2(-octave) + (LOW_POWER - 1.0)) * 128.0
+    level = octave + size * jnp.exp2(-octave)
     first, _ = split_first(level, axis)
-    first = jnp.floor(first + 0.5)
+    half = first * 64.0 + ((LOW_POWER - 1.0) * 64.0 + 0.25)
     place = lax.broadcasted_iota(jnp.int32, first.shape, axis).astype(jnp.float32)
-    bit = first - 2.0 * jnp.floor(first * 0.5)
-    held = jnp.where(place < EXPONENT_BITS, bit * jnp.exp2(place), 0.0)
+    weight = jnp.where(place < EXPONENT_BITS, jnp.exp2(place), 0.0)
+    held = jnp.where(half - jnp.floor(half) >= 0.5, weight, 0.0)
     scale = jnp.exp2(jnp.sum(held, axis=axis, keepdims=True) - (EXPONENT_BIAS + halvings))
+    step = 0.5 / OCTAVES
+    low = (LOW_POWER - 1.0) * step
     share = jnp.maximum(
-        level * (0.5 / TOP),
-        jnp.maximum(level * (1.0 / TOP) - 0.25, level * (2.0 / TOP) - 1.0),
+        level * step + low,
+        jnp.maximum(
+            level * (2.0 * step) + (2.0 * low - 0.25), level * (4.0 * step) + (4.0 * low - 1.0)
+        ),
     )
-    return jnp.where(code < 0.0, -share, share) * scale
+    return jnp.where(code < 0.0, -scale, scale) * share
 
 
 def tables(blocks):
@@ -297,7 +316,7 @@
 
 def conv_kernel(gated_ref, *refs):
     blocks = gated_ref.shape[1]
-    wave_ref, back_wave_ref, twist_ref, out, codes, *scratch = refs[blocks:]
+    wave_ref, back_wave_ref, twist_ref, out_ref, codes, out, sems, *scratch = refs[blocks:]
     rows, waves = scratch[0:2], scratch[2:4]
     scale = math.log2(blocks * ROW)
     me = lax.axis_index("seq")
@@ -320,15 +339,26 @@
     def back(half, at):
         spectra = [spectrum_rows(waves[half], k, at) for k in range(blocks)]
         start = pl.ds(half * HALF + at, CHUNK)
-        for n1, total in enumerate(mix_back(spectra, twist_ref)):
-            out[n1, start, :] = encode(total, 1)
+        totals = mix_back(spectra, twist_ref)
+        sizes = [jnp.abs(total) for total in totals]
+        peak = jnp.max(functools.reduce(jnp.maximum, sizes), axis=1, keepdims=True)
+        for n1, code in enumerate(encode_all(totals, scale_of(peak), 1)):
+            out[n1, start, :] = code
+
+    def out_copy(half):
+        start = pl.ds(half * HALF, HALF)
+        return pltpu.make_async_copy(out.at[:, start, :], out_ref.at[:, start, :], sems.at[half])
 
     stage(None, None, None, forward, 0)
     stage(wave_ref, rows[0], waves[0], forward, 1)
     stage(wave_ref, rows[1], waves[1], product, 0)
     stage(back_wave_ref, rows[0], waves[0], product, 1)
     stage(back_wave_ref, rows[1], waves[1], back, 0)
+    out_copy(0).start()
     stage(None, None, None, back, 1)
+    out_copy(1).start()
+    out_copy(0).wait()
+    out_copy(1).wait()
 
 
 def turn_kernel(*refs):
@@ -466,7 +496,14 @@
         convolved = pl.pallas_call(
             conv_kernel,
             out_shape=jax.ShapeDtypeStruct((blocks, own, ROW), jnp.bfloat16),
-            scratch_shapes=[pltpu.VMEM((blocks, own, ROW), jnp.bfloat16)] + scratch,
+            in_specs=[pl.BlockSpec(memory_space=pltpu.VMEM)] * (groups + 4),
+            out_specs=far,
+            scratch_shapes=[
+                pltpu.VMEM((blocks, own, ROW), jnp.bfloat16),
+                pltpu.VMEM((blocks, own, ROW), jnp.bfloat16),
+                pltpu.SemaphoreType.DMA((2,)),
+            ]
+            + scratch,
             compiler_params=large,
             cost_estimate=cost(2**32, 2**24),
             name="convolve",

time: 63.1 us -> 62.6 us (level)
  Pallas kernels: 17.6 us -> 16.9 us
where the time goes in v4:
time: 62.6 us; the launch traced here: 62.3 us
  starting transfers between devices  27.5 us (44%)
  waiting for transfers between devices  17.8 us (28%)
  Pallas kernels  16.9 us (27%)
    ppermute x10, starting transfers between devices, scatter(): lax.ppermute(block, axis, [(i, i ^ turn) for i in range(count)])  16 us
    ppermute x10, waiting for transfers between devices, scatter(): lax.ppermute(block, axis, [(i, i ^ turn) for i in range(count)])  12 us
    all_to_all x1, starting transfers between devices, body(): gated = exchange(gated, ('seq', 'ch'))  7.32 us
    pallas_call x1, Pallas kernels, body(): pl.pallas_call(conv_kernel, out_shape=jax.ShapeDtypeStruct((blocks, own,...  6.75 us
    all_to_all x1, waiting for transfers between devices, body(): convolved = exchange(convolved, 'seq')  5.78 us
    all_to_all x1, starting transfers between devices, body(): convolved = exchange(convolved, 'seq')  4.16 us
    pallas_call x1, Pallas kernels, body(): pl.pallas_call(gated_spectrum_kernel, out_shape=jax.ShapeDtypeStruct((2,...  3.69 us
    pallas_call x1, Pallas kernels, body(): pl.pallas_call(send_kernel, in_specs=[far], out_specs=far, out_shape=jax....  2.9 us
  transfers between devices with their start and end apart: 12, of which 6 were waited for; matrix products, arithmetic and copies ran while one was open for 0% of the time, Pallas kernels for 9%

profile of v4, /device:TPU:0, one launch (start us, length us, event | category | flops | bytes accessed | tf_op | source)
XLA Modules:
  0.0 62.3 jit_solution(1047106991433344463)
XLA Ops:
  0.0 2.9 %encode_gated.1 = bf16[8,4,64,128]{3,2,1,0:T(8,128)(2,1)} custom-call(bf16[3,64,4096]{2,1,0:T(8,128)(2,1)} %bitcast.4), custom_call_target="tpu_custom_call" | custom-call | flops 33554432 | bytes 8388608 | tf_op jit(solution)/shard_map/encode_gated/pallas_call | solution.py:432
  2.9 7.3 %all-to-all-start = ((bf16[32,64,128]{2,1,0:T(8,128)(2,1)}), bf16[32,64,128]{2,1,0:T(8,128)(2,1)S(1)}, u32[]{:S(2)}, u32[]{:S(2)}) async-start(bf16[32,64,128]{2,1,0:T(8,128)(2,1)} %bitcast.8), calls=%async_computation | async-start | bytes 1048576 | tf_op jit(solution)/shard_map/all_to_all | solution.py:476
  10.3 1.4 %encode_taps.1 = (bf16[128,256]{1,0:T(8,128)(2,1)S(1)}, bf16[128,256]{1,0:T(8,128)(2,1)S(1)}, bf16[128,256]{1,0:T(8,128)(2,1)S(1)}, bf16[128,256]{1,0:T(8,128)(2...) custom-call(f32[8,128,256]{2,1,0:T(8,128)S(1)} %bitcast.6, ...), custom_call_target="tpu_custom_call" | custom-call | flops 33554432 | bytes 8388608 | tf_op jit(solution)/shard_map/encode_taps/pallas_call | solution.py:458
  11.6 1.8 %collective-permute-start.3 = (bf16[128,256]{1,0:T(8,128)(2,1)S(1)}, bf16[128,256]{1,0:T(8,128)(2,1)S(1)}, u32[]{:S(2)}, u32[]{:S(2)}) collective-permute-start(bf16[128,256]{1,0:T(8,128)(2,1)S(1)} %get-tuple-element.22), channel_id=1, source_target_pairs={{0,4},{4,0},{8,12},{12,8},{16,20},{20,16},{24,28},{28,24},{1,5},{5... | collective-permute-start | bytes 196616 | tf_op jit(solution)/shard_map/ppermute | solution.py:413
  13.5 1.5 %collective-permute-start.4 = (bf16[128,256]{1,0:T(8,128)(2,1)S(1)}, bf16[128,256]{1,0:T(8,128)(2,1)S(1)}, u32[]{:S(2)}, u32[]{:S(2)}) collective-permute-start(bf16[128,256]{1,0:T(8,128)(2,1)S(1)} %get-tuple-element.23), channel_id=1, source_target_pairs={{0,8},{4,12},{8,0},{12,4},{16,24},{20,28},{24,16},{28,20},{1,9},{5... | collective-permute-start | bytes 196616 | tf_op jit(solution)/shard_map/ppermute | solution.py:413
  14.9 0.3 collective-permute-start.5
  15.2 2.7 %collective-permute-start.6 = (bf16[128,256]{1,0:T(8,128)(2,1)S(1)}, bf16[128,256]{1,0:T(8,128)(2,1)S(1)}, u32[]{:S(2)}, u32[]{:S(2)}) collective-permute-start(bf16[128,256]{1,0:T(8,128)(2,1)S(1)} %get-tuple-element.25), channel_id=1, source_target_pairs={{0,16},{4,20},{8,24},{12,28},{16,0},{20,4},{24,8},{28,12},{1,17},{... | collective-permute-start | bytes 196616 | tf_op jit(solution)/shard_map/ppermute | solution.py:413
  17.9 1.5 %collective-permute-start.7 = (bf16[128,256]{1,0:T(8,128)(2,1)S(1)}, bf16[128,256]{1,0:T(8,128)(2,1)S(1)}, u32[]{:S(2)}, u32[]{:S(2)}) collective-permute-start(bf16[128,256]{1,0:T(8,128)(2,1)S(1)} %get-tuple-element.26), channel_id=1, source_target_pairs={{0,20},{4,16},{8,28},{12,24},{16,4},{20,0},{24,12},{28,8},{1,21},{... | collective-permute-start | bytes 196616 | tf_op jit(solution)/shard_map/ppermute | solution.py:413
  19.3 3.3 %collective-permute-start.8 = (bf16[128,256]{1,0:T(8,128)(2,1)S(1)}, bf16[128,256]{1,0:T(8,128)(2,1)S(1)}, u32[]{:S(2)}, u32[]{:S(2)}) collective-permute-start(bf16[128,256]{1,0:T(8,128)(2,1)S(1)} %get-tuple-element.27), channel_id=1, source_target_pairs={{0,24},{4,28},{8,16},{12,20},{16,8},{20,12},{24,0},{28,4},{1,25},{... | collective-permute-start | bytes 196616 | tf_op jit(solution)/shard_map/ppermute | solution.py:413
  22.7 3.1 %collective-permute-start.9 = (bf16[128,256]{1,0:T(8,128)(2,1)S(1)}, bf16[128,256]{1,0:T(8,128)(2,1)S(1)}, u32[]{:S(2)}, u32[]{:S(2)}) collective-permute-start(bf16[128,256]{1,0:T(8,128)(2,1)S(1)} %get-tuple-element.28), channel_id=1, source_target_pairs={{0,28},{4,24},{8,20},{12,16},{16,12},{20,8},{24,4},{28,0},{1,29},{... | collective-permute-start | bytes 196616 | tf_op jit(solution)/shard_map/ppermute | solution.py:413
  25.8 3.7 %gated_spectrum.1.gated_ref = f32[2,8,2,64,256]{4,3,2,1,0:T(8,128)S(1)} custom-call(bf16[32,64,128]{2,1,0:T(8,128)(2,1)S(1)} %all-to-all-done.gated_ref, bf16[768,256]{1,0:T(8,128)(2,1)S(1)} %copy-done.3, f32[8,2,256]{2,1,0:T(2,128)S(1)} %copy-done.5), custom_call_target="tpu_custom_call" | custom-call | flops 4294967296 | bytes 16777216 | tf_op jit(solution)/shard_map/gated_spectrum/pallas_call | solution.py:488
  29.5 3.2 %collective-permute-done.6.refs_4_ = bf16[128,256]{1,0:T(8,128)(2,1)S(1)} collective-permute-done((bf16[128,256]{1,0:T(8,128)(2,1)S(1)}, bf16[128,256]{1,0:T(8,128)(2,1)S(1)}, u32[]{:S(2)}, u32[]{:S(2)}) %collective-permute-start.6) | collective-permute-done | bytes 65568 | tf_op jit(solution)/shard_map/ppermute | solution.py:413
  32.7 2.3 %collective-permute-done.7.refs_5_ = bf16[128,256]{1,0:T(8,128)(2,1)S(1)} collective-permute-done((bf16[128,256]{1,0:T(8,128)(2,1)S(1)}, bf16[128,256]{1,0:T(8,128)(2,1)S(1)}, u32[]{:S(2)}, u32[]{:S(2)}) %collective-permute-start.7) | collective-permute-done | bytes 65568 | tf_op jit(solution)/shard_map/ppermute | solution.py:413
  35.1 6.8 %convolve.1 = bf16[8,128,256]{2,1,0:T(8,128)(2,1)} custom-call(f32[2,8,2,64,256]{4,3,2,1,0:T(8,128)S(1)} %gated_spectrum.1.gated_ref, bf16[128,256]{1,0:T(8,128)(2,1)S(1)} %get-tuple-element.21.refs_0_, bf16[128,256]{1,0:T(8,128)(2,1)S(1)} %collective-permute-done.3.refs_1_, bf16[128,256]{1,0:T(8,128)(2,1)S(1)} %collective-permute-done.4.refs_2_, ...), custom_call_target="tpu_custom_call" | custom-call | flops 4294967296 | bytes 16777216 | tf_op jit(solution)/shard_map/convolve/pallas_call | solution.py:496
  41.8 4.2 %all-to-all-start.1 = ((bf16[8,128,256]{2,1,0:T(8,128)(2,1)}), bf16[8,128,256]{2,1,0:T(8,128)(2,1)S(1)}, u32[]{:S(2)}, u32[]{:S(2)}) async-start(bf16[8,128,256]{2,1,0:T(8,128)(2,1)} %convolve.1), calls=%async_computation.1 | async-start | bytes 1048576 | tf_op jit(solution)/shard_map/all_to_all | solution.py:517
  46.0 0.1 send_queries.1
  46.2 0.1 collective-permute-start
  46.2 1.5 %collective-permute-start.1 = (bf16[64,1024]{1,0:T(8,128)(2,1)S(1)}, bf16[64,1024]{1,0:T(8,128)(2,1)S(1)}, u32[]{:S(2)}, u32[]{:S(2)}) collective-permute-start(bf16[64,1024]{1,0:T(8,128)(2,1)S(1)} %get-tuple-element.19), channel_id=1, source_target_pairs={{0,2},{1,3},{2,0},{3,1},{4,6},{5,7},{6,4},{7,5},{8,10},{9,11},{10,... | collective-permute-start | bytes 393224 | tf_op jit(solution)/shard_map/ppermute | solution.py:413
  47.8 0.3 collective-permute-start.2
  48.1 4.5 %collective-permute-done.1.refs_2_ = bf16[64,1024]{1,0:T(8,128)(2,1)S(1)} collective-permute-done((bf16[64,1024]{1,0:T(8,128)(2,1)S(1)}, bf16[64,1024]{1,0:T(8,128)(2,1)S(1)}, u32[]{:S(2)}, u32[]{:S(2)}) %collective-permute-start.1) | collective-permute-done | bytes 131104 | tf_op jit(solution)/shard_map/ppermute | solution.py:413
  52.6 1.9 %collective-permute-done.2.refs_3_ = bf16[64,1024]{1,0:T(8,128)(2,1)S(1)} collective-permute-done((bf16[64,1024]{1,0:T(8,128)(2,1)S(1)}, bf16[64,1024]{1,0:T(8,128)(2,1)S(1)}, u32[]{:S(2)}, u32[]{:S(2)}) %collective-permute-start.2) | collective-permute-done | bytes 131104 | tf_op jit(solution)/shard_map/ppermute | solution.py:413
  54.5 0.3 turn_queries.1.query_ref
  54.8 5.8 %all-to-all-done.1.conv_ref = bf16[8,128,256]{2,1,0:T(8,128)(2,1)S(1)} async-done(((bf16[8,128,256]{2,1,0:T(8,128)(2,1)}), bf16[8,128,256]{2,1,0:T(8,128)(2,1)S(1)}, u32[]{:S(2)}, u32[]{:S(2)}) %all-to-all-start.1) | async-done | bytes 524320 | tf_op jit(solution)/shard_map/all_to_all | solution.py:517
  60.6 1.7 %mix_out.1 = bf16[1024,256]{1,0:T(8,128)(2,1)} custom-call(bf16[1024,256]{1,0:T(8,128)(2,1)S(1)} %turn_queries.1.query_ref, bf16[8,128,256]{2,1,0:T(8,128)(2,1)S(1)} %all-to-all-done.1.conv_ref), custom_call_target="tpu_custom_call" | custom-call | tf_op jit(solution)/shard_map/mix_out/pallas_call | solution.py:527
  (19 shorter events, 0.1 us)
Async XLA Ops:
  0.0 10.2 %copy-start.1 = (f32[1024,256]{1,0:T(8,128)S(1)}, f32[1024,256]{1,0:T(8,128)}, u32[]{:S(2)}) copy-start(f32[1024,256]{1,0:T(8,128)} %param.7) | copy-start | bytes 3145732
  0.0 10.2 %copy-start.2 = (f32[1024]{0:T(1024)S(1)}, f32[1024]{0:T(1024)}, u32[]{:S(2)}) copy-start(f32[1024]{0:T(1024)} %param.8) | copy-start | bytes 12292
  0.0 25.8 %copy-start.3 = (bf16[768,256]{1,0:T(8,128)(2,1)S(1)}, bf16[768,256]{1,0:T(8,128)(2,1)}, u32[]{:S(2)}) copy-start(bf16[768,256]{1,0:T(8,128)(2,1)} %constant.6.clone.wave_ref.refs_8_) | copy-start | bytes 1179652
  0.0 25.8 %copy-start.5 = (f32[8,2,256]{2,1,0:T(2,128)S(1)}, f32[8,2,256]{2,1,0:T(2,128)}, u32[]{:S(2)}) copy-start(f32[8,2,256]{2,1,0:T(2,128)} %constant.7.clone.twist_ref.refs_10_) | copy-start | bytes 49156
  2.9 22.9 %all-to-all-start = ((bf16[32,64,128]{2,1,0:T(8,128)(2,1)}), bf16[32,64,128]{2,1,0:T(8,128)(2,1)S(1)}, u32[]{:S(2)}, u32[]{:S(2)}) async-start(bf16[32,64,128]{2,1,0:T(8,128)(2,1)} %bitcast.8), calls=%async_computation | async-start | bytes 1048576 | tf_op jit(solution)/shard_map/all_to_all | solution.py:476
  11.6 7.7 %collective-permute-start.3 = (bf16[128,256]{1,0:T(8,128)(2,1)S(1)}, bf16[128,256]{1,0:T(8,128)(2,1)S(1)}, u32[]{:S(2)}, u32[]{:S(2)}) collective-permute-start(bf16[128,256]{1,0:T(8,128)(2,1)S(1)} %get-tuple-element.22), channel_id=1, source_target_pairs={{0,4},{4,0},{8,12},{12,8},{16,20},{20,16},{24,28},{28,24},{1,5},{5... | collective-permute-start | bytes 196616 | tf_op jit(solution)/shard_map/ppermute | solution.py:413
  13.5 9.2 %collective-permute-start.4 = (bf16[128,256]{1,0:T(8,128)(2,1)S(1)}, bf16[128,256]{1,0:T(8,128)(2,1)S(1)}, u32[]{:S(2)}, u32[]{:S(2)}) collective-permute-start(bf16[128,256]{1,0:T(8,128)(2,1)S(1)} %get-tuple-element.23), channel_id=1, source_target_pairs={{0,8},{4,12},{8,0},{12,4},{16,24},{20,28},{24,16},{28,20},{1,9},{5... | collective-permute-start | bytes 196616 | tf_op jit(solution)/shard_map/ppermute | solution.py:413
  14.9 14.6 %collective-permute-start.5 = (bf16[128,256]{1,0:T(8,128)(2,1)S(1)}, bf16[128,256]{1,0:T(8,128)(2,1)S(1)}, u32[]{:S(2)}, u32[]{:S(2)}) collective-permute-start(bf16[128,256]{1,0:T(8,128)(2,1)S(1)} %get-tuple-element.24), channel_id=1, source_target_pairs={{0,12},{4,8},{8,4},{12,0},{16,28},{20,24},{24,20},{28,16},{1,13},{... | collective-permute-start | bytes 196616 | tf_op jit(solution)/shard_map/ppermute | solution.py:413
  15.2 17.5 %collective-permute-start.6 = (bf16[128,256]{1,0:T(8,128)(2,1)S(1)}, bf16[128,256]{1,0:T(8,128)(2,1)S(1)}, u32[]{:S(2)}, u32[]{:S(2)}) collective-permute-start(bf16[128,256]{1,0:T(8,128)(2,1)S(1)} %get-tuple-element.25), channel_id=1, source_target_pairs={{0,16},{4,20},{8,24},{12,28},{16,0},{20,4},{24,8},{28,12},{1,17},{... | collective-permute-start | bytes 196616 | tf_op jit(solution)/shard_map/ppermute | solution.py:413
  17.9 17.2 %collective-permute-start.7 = (bf16[128,256]{1,0:T(8,128)(2,1)S(1)}, bf16[128,256]{1,0:T(8,128)(2,1)S(1)}, u32[]{:S(2)}, u32[]{:S(2)}) collective-permute-start(bf16[128,256]{1,0:T(8,128)(2,1)S(1)} %get-tuple-element.26), channel_id=1, source_target_pairs={{0,20},{4,16},{8,28},{12,24},{16,4},{20,0},{24,12},{28,8},{1,21},{... | collective-permute-start | bytes 196616 | tf_op jit(solution)/shard_map/ppermute | solution.py:413
  19.3 15.7 %collective-permute-start.8 = (bf16[128,256]{1,0:T(8,128)(2,1)S(1)}, bf16[128,256]{1,0:T(8,128)(2,1)S(1)}, u32[]{:S(2)}, u32[]{:S(2)}) collective-permute-start(bf16[128,256]{1,0:T(8,128)(2,1)S(1)} %get-tuple-element.27), channel_id=1, source_target_pairs={{0,24},{4,28},{8,16},{12,20},{16,8},{20,12},{24,0},{28,4},{1,25},{... | collective-permute-start | bytes 196616 | tf_op jit(solution)/shard_map/ppermute | solution.py:413
  22.7 12.4 %copy-start.4 = (bf16[768,256]{1,0:T(8,128)(2,1)S(1)}, bf16[768,256]{1,0:T(8,128)(2,1)}, u32[]{:S(2)}) copy-start(bf16[768,256]{1,0:T(8,128)(2,1)} %constant.8.clone.refs_9_) | copy-start | bytes 1179652
  22.7 12.4 %collective-permute-start.9 = (bf16[128,256]{1,0:T(8,128)(2,1)S(1)}, bf16[128,256]{1,0:T(8,128)(2,1)S(1)}, u32[]{:S(2)}, u32[]{:S(2)}) collective-permute-start(bf16[128,256]{1,0:T(8,128)(2,1)S(1)} %get-tuple-element.28), channel_id=1, source_target_pairs={{0,28},{4,24},{8,20},{12,16},{16,12},{20,8},{24,4},{28,0},{1,29},{... | collective-permute-start | bytes 196616 | tf_op jit(solution)/shard_map/ppermute | solution.py:413
  35.1 10.9 %copy-start = (bf16[64,3,4096]{2,0,1:T(8,128)(2,1)S(1)}, bf16[64,3,4096]{2,0,1:T(8,128)(2,1)}, u32[]{:S(2)}) copy-start(bf16[64,3,4096]{2,0,1:T(8,128)(2,1)} %param.6) | copy-start | bytes 4718596
  41.8 18.7 %all-to-all-start.1 = ((bf16[8,128,256]{2,1,0:T(8,128)(2,1)}), bf16[8,128,256]{2,1,0:T(8,128)(2,1)S(1)}, u32[]{:S(2)}, u32[]{:S(2)}) async-start(bf16[8,128,256]{2,1,0:T(8,128)(2,1)} %convolve.1), calls=%async_computation.1 | async-start | bytes 1048576 | tf_op jit(solution)/shard_map/all_to_all | solution.py:517
  46.2 1.9 %collective-permute-start = (bf16[64,1024]{1,0:T(8,128)(2,1)S(1)}, bf16[64,1024]{1,0:T(8,128)(2,1)S(1)}, u32[]{:S(2)}, u32[]{:S(2)}) collective-permute-start(bf16[64,1024]{1,0:T(8,128)(2,1)S(1)} %get-tuple-element.18), channel_id=1, source_target_pairs={{0,1},{1,0},{2,3},{3,2},{4,5},{5,4},{6,7},{7,6},{8,9},{9,8},{10,11... | collective-permute-start | bytes 393224 | tf_op jit(solution)/shard_map/ppermute | solution.py:413
  46.2 6.4 %collective-permute-start.1 = (bf16[64,1024]{1,0:T(8,128)(2,1)S(1)}, bf16[64,1024]{1,0:T(8,128)(2,1)S(1)}, u32[]{:S(2)}, u32[]{:S(2)}) collective-permute-start(bf16[64,1024]{1,0:T(8,128)(2,1)S(1)} %get-tuple-element.19), channel_id=1, source_target_pairs={{0,2},{1,3},{2,0},{3,1},{4,6},{5,7},{6,4},{7,5},{8,10},{9,11},{10,... | collective-permute-start | bytes 393224 | tf_op jit(solution)/shard_map/ppermute | solution.py:413
  47.8 6.7 %collective-permute-start.2 = (bf16[64,1024]{1,0:T(8,128)(2,1)S(1)}, bf16[64,1024]{1,0:T(8,128)(2,1)S(1)}, u32[]{:S(2)}, u32[]{:S(2)}) collective-permute-start(bf16[64,1024]{1,0:T(8,128)(2,1)S(1)} %get-tuple-element.20), channel_id=1, source_target_pairs={{0,3},{1,2},{2,1},{3,0},{4,7},{5,6},{6,5},{7,4},{8,11},{9,10},{10,... | collective-permute-start | bytes 393224 | tf_op jit(solution)/shard_map/ppermute | solution.py:413

commit v5 on v4

--- a/solution.py
+++ b/solution.py
@@ -270,21 +270,10 @@
 
 
 def stage(wave_ref, source, target, work, half):
-    steps = 2
-    chunks = HALF // CHUNK // steps
-
-    def step(index, _):
-        if source is not None:
-            count = source.shape[0] // steps
-            at = pl.ds(pl.multiple_of(index * count, count), count)
-            target[at, :] = jnp.dot(
-                source[at, :], wave_ref[...], preferred_element_type=jnp.float32
-            )
-        for chunk in range(chunks):
-            work(half, pl.multiple_of((index * chunks + chunk) * CHUNK, CHUNK))
-        return 0
-
-    lax.fori_loop(0, steps, step, 0)
+    if source is not None:
+        target[...] = jnp.dot(source[...], wave_ref[...], preferred_element_type=jnp.float32)
+    for chunk in range(HALF // CHUNK):
+        work(half, chunk * CHUNK)
 
 
 def gated_spectrum_kernel(gated_ref, wave_ref, twist_ref, out_ref, u, *scratch):

time: 62.6 us -> 61.6 us (0.984)
  Pallas kernels: 16.9 us -> 15.1 us
  waiting for transfers between devices: 17.8 us -> 18.5 us
    pallas_call x1, Pallas kernels: 6.75 us -> 5.77 us  [body(): pl.pallas_call(conv_kernel, out_shape=jax.ShapeDtypeStruct((blocks, own,...]
    pallas_call x1, Pallas kernels: 3.69 us -> 2.93 us  [body(): pl.pallas_call(gated_spectrum_kernel, out_shape=jax.ShapeDtypeStruct((2,...]
    ppermute x10, waiting for transfers between devices: 12 us -> 12.7 us  [scatter(): lax.ppermute(block, axis, [(i, i ^ turn) for i in range(count)])]
  transfers between devices with their start and end apart: 12 -> 12, of which waited for: 6 -> 6; matrix products, arithmetic and copies ran while one was open for 0% -> 0% of each run, Pallas kernels for 9% -> 8%
where the time goes in v5:
time: 61.6 us; the launch traced here: 61.3 us
  starting transfers between devices  27.5 us (45%)
  waiting for transfers between devices  18.5 us (30%)
  Pallas kernels  15.1 us (25%)
    ppermute x10, starting transfers between devices, scatter(): lax.ppermute(block, axis, [(i, i ^ turn) for i in range(count)])  16 us
    ppermute x10, waiting for transfers between devices, scatter(): lax.ppermute(block, axis, [(i, i ^ turn) for i in range(count)])  12.7 us
    all_to_all x1, starting transfers between devices, body(): gated = exchange(gated, ('seq', 'ch'))  7.32 us
    all_to_all x1, waiting for transfers between devices, body(): convolved = exchange(convolved, 'seq')  5.78 us
    pallas_call x1, Pallas kernels, body(): pl.pallas_call(conv_kernel, out_shape=jax.ShapeDtypeStruct((blocks, own,...  5.77 us
    all_to_all x1, starting transfers between devices, body(): convolved = exchange(convolved, 'seq')  4.17 us
    pallas_call x1, Pallas kernels, body(): pl.pallas_call(gated_spectrum_kernel, out_shape=jax.ShapeDtypeStruct((2,...  2.93 us
    pallas_call x1, Pallas kernels, body(): pl.pallas_call(send_kernel, in_specs=[far], out_specs=far, out_shape=jax....  2.9 us
  transfers between devices with their start and end apart: 12, of which 6 were waited for; matrix products, arithmetic and copies ran while one was open for 0% of the time, Pallas kernels for 8%

profile of v5, /device:TPU:0, one launch (start us, length us, event | category | flops | bytes accessed | tf_op | source)
XLA Modules:
  0.0 61.3 jit_solution(5955548459661554508)
XLA Ops:
  0.0 2.9 %encode_gated.1 = bf16[8,4,64,128]{3,2,1,0:T(8,128)(2,1)} custom-call(bf16[3,64,4096]{2,1,0:T(8,128)(2,1)} %bitcast.4), custom_call_target="tpu_custom_call" | custom-call | flops 33554432 | bytes 8388608 | tf_op jit(solution)/shard_map/encode_gated/pallas_call | solution.py:421
  2.9 7.3 %all-to-all-start = ((bf16[32,64,128]{2,1,0:T(8,128)(2,1)}), bf16[32,64,128]{2,1,0:T(8,128)(2,1)S(1)}, u32[]{:S(2)}, u32[]{:S(2)}) async-start(bf16[32,64,128]{2,1,0:T(8,128)(2,1)} %bitcast.8), calls=%async_computation | async-start | bytes 1048576 | tf_op jit(solution)/shard_map/all_to_all | solution.py:465
  10.3 1.4 %encode_taps.1 = (bf16[128,256]{1,0:T(8,128)(2,1)S(1)}, bf16[128,256]{1,0:T(8,128)(2,1)S(1)}, bf16[128,256]{1,0:T(8,128)(2,1)S(1)}, bf16[128,256]{1,0:T(8,128)(2...) custom-call(f32[8,128,256]{2,1,0:T(8,128)S(1)} %bitcast.6, ...), custom_call_target="tpu_custom_call" | custom-call | flops 33554432 | bytes 8388608 | tf_op jit(solution)/shard_map/encode_taps/pallas_call | solution.py:447
  11.6 1.8 %collective-permute-start.3 = (bf16[128,256]{1,0:T(8,128)(2,1)S(1)}, bf16[128,256]{1,0:T(8,128)(2,1)S(1)}, u32[]{:S(2)}, u32[]{:S(2)}) collective-permute-start(bf16[128,256]{1,0:T(8,128)(2,1)S(1)} %get-tuple-element.22), channel_id=1, source_target_pairs={{0,4},{4,0},{8,12},{12,8},{16,20},{20,16},{24,28},{28,24},{1,5},{5... | collective-permute-start | bytes 196616 | tf_op jit(solution)/shard_map/ppermute | solution.py:402
  13.5 1.5 %collective-permute-start.4 = (bf16[128,256]{1,0:T(8,128)(2,1)S(1)}, bf16[128,256]{1,0:T(8,128)(2,1)S(1)}, u32[]{:S(2)}, u32[]{:S(2)}) collective-permute-start(bf16[128,256]{1,0:T(8,128)(2,1)S(1)} %get-tuple-element.23), channel_id=1, source_target_pairs={{0,8},{4,12},{8,0},{12,4},{16,24},{20,28},{24,16},{28,20},{1,9},{5... | collective-permute-start | bytes 196616 | tf_op jit(solution)/shard_map/ppermute | solution.py:402
  14.9 0.3 collective-permute-start.5
  15.2 2.7 %collective-permute-start.6 = (bf16[128,256]{1,0:T(8,128)(2,1)S(1)}, bf16[128,256]{1,0:T(8,128)(2,1)S(1)}, u32[]{:S(2)}, u32[]{:S(2)}) collective-permute-start(bf16[128,256]{1,0:T(8,128)(2,1)S(1)} %get-tuple-element.25), channel_id=1, source_target_pairs={{0,16},{4,20},{8,24},{12,28},{16,0},{20,4},{24,8},{28,12},{1,17},{... | collective-permute-start | bytes 196616 | tf_op jit(solution)/shard_map/ppermute | solution.py:402
  17.9 1.5 %collective-permute-start.7 = (bf16[128,256]{1,0:T(8,128)(2,1)S(1)}, bf16[128,256]{1,0:T(8,128)(2,1)S(1)}, u32[]{:S(2)}, u32[]{:S(2)}) collective-permute-start(bf16[128,256]{1,0:T(8,128)(2,1)S(1)} %get-tuple-element.26), channel_id=1, source_target_pairs={{0,20},{4,16},{8,28},{12,24},{16,4},{20,0},{24,12},{28,8},{1,21},{... | collective-permute-start | bytes 196616 | tf_op jit(solution)/shard_map/ppermute | solution.py:402
  19.3 3.3 %collective-permute-start.8 = (bf16[128,256]{1,0:T(8,128)(2,1)S(1)}, bf16[128,256]{1,0:T(8,128)(2,1)S(1)}, u32[]{:S(2)}, u32[]{:S(2)}) collective-permute-start(bf16[128,256]{1,0:T(8,128)(2,1)S(1)} %get-tuple-element.27), channel_id=1, source_target_pairs={{0,24},{4,28},{8,16},{12,20},{16,8},{20,12},{24,0},{28,4},{1,25},{... | collective-permute-start | bytes 196616 | tf_op jit(solution)/shard_map/ppermute | solution.py:402
  22.7 3.1 %collective-permute-start.9 = (bf16[128,256]{1,0:T(8,128)(2,1)S(1)}, bf16[128,256]{1,0:T(8,128)(2,1)S(1)}, u32[]{:S(2)}, u32[]{:S(2)}) collective-permute-start(bf16[128,256]{1,0:T(8,128)(2,1)S(1)} %get-tuple-element.28), channel_id=1, source_target_pairs={{0,28},{4,24},{8,20},{12,16},{16,12},{20,8},{24,4},{28,0},{1,29},{... | collective-permute-start | bytes 196616 | tf_op jit(solution)/shard_map/ppermute | solution.py:402
  25.8 2.9 %gated_spectrum.1.gated_ref = f32[2,8,2,64,256]{4,3,2,1,0:T(8,128)S(1)} custom-call(bf16[32,64,128]{2,1,0:T(8,128)(2,1)S(1)} %all-to-all-done.gated_ref, bf16[768,256]{1,0:T(8,128)(2,1)S(1)} %copy-done.3, f32[8,2,256]{2,1,0:T(2,128)S(1)} %copy-done.5), custom_call_target="tpu_custom_call" | custom-call | flops 4294967296 | bytes 16777216 | tf_op jit(solution)/shard_map/gated_spectrum/pallas_call | solution.py:477
  28.7 4.0 %collective-permute-done.6.refs_4_ = bf16[128,256]{1,0:T(8,128)(2,1)S(1)} collective-permute-done((bf16[128,256]{1,0:T(8,128)(2,1)S(1)}, bf16[128,256]{1,0:T(8,128)(2,1)S(1)}, u32[]{:S(2)}, u32[]{:S(2)}) %collective-permute-start.6) | collective-permute-done | bytes 65568 | tf_op jit(solution)/shard_map/ppermute | solution.py:402
  32.7 2.3 %collective-permute-done.7.refs_5_ = bf16[128,256]{1,0:T(8,128)(2,1)S(1)} collective-permute-done((bf16[128,256]{1,0:T(8,128)(2,1)S(1)}, bf16[128,256]{1,0:T(8,128)(2,1)S(1)}, u32[]{:S(2)}, u32[]{:S(2)}) %collective-permute-start.7) | collective-permute-done | bytes 65568 | tf_op jit(solution)/shard_map/ppermute | solution.py:402
  35.1 5.8 %convolve.1 = bf16[8,128,256]{2,1,0:T(8,128)(2,1)} custom-call(f32[2,8,2,64,256]{4,3,2,1,0:T(8,128)S(1)} %gated_spectrum.1.gated_ref, bf16[128,256]{1,0:T(8,128)(2,1)S(1)} %get-tuple-element.21.refs_0_, bf16[128,256]{1,0:T(8,128)(2,1)S(1)} %collective-permute-done.3.refs_1_, bf16[128,256]{1,0:T(8,128)(2,1)S(1)} %collective-permute-done.4.refs_2_, ...), custom_call_target="tpu_custom_call" | custom-call | flops 4294967296 | bytes 16777216 | tf_op jit(solution)/shard_map/convolve/pallas_call | solution.py:485
  40.9 4.2 %all-to-all-start.1 = ((bf16[8,128,256]{2,1,0:T(8,128)(2,1)}), bf16[8,128,256]{2,1,0:T(8,128)(2,1)S(1)}, u32[]{:S(2)}, u32[]{:S(2)}) async-start(bf16[8,128,256]{2,1,0:T(8,128)(2,1)} %convolve.1), calls=%async_computation.1 | async-start | bytes 1048576 | tf_op jit(solution)/shard_map/all_to_all | solution.py:506
  45.0 0.1 send_queries.1
  45.2 0.1 collective-permute-start
  45.3 1.5 %collective-permute-start.1 = (bf16[64,1024]{1,0:T(8,128)(2,1)S(1)}, bf16[64,1024]{1,0:T(8,128)(2,1)S(1)}, u32[]{:S(2)}, u32[]{:S(2)}) collective-permute-start(bf16[64,1024]{1,0:T(8,128)(2,1)S(1)} %get-tuple-element.19), channel_id=1, source_target_pairs={{0,2},{1,3},{2,0},{3,1},{4,6},{5,7},{6,4},{7,5},{8,10},{9,11},{10,... | collective-permute-start | bytes 393224 | tf_op jit(solution)/shard_map/ppermute | solution.py:402
  46.8 0.3 collective-permute-start.2
  47.1 4.5 %collective-permute-done.1.refs_2_ = bf16[64,1024]{1,0:T(8,128)(2,1)S(1)} collective-permute-done((bf16[64,1024]{1,0:T(8,128)(2,1)S(1)}, bf16[64,1024]{1,0:T(8,128)(2,1)S(1)}, u32[]{:S(2)}, u32[]{:S(2)}) %collective-permute-start.1) | collective-permute-done | bytes 131104 | tf_op jit(solution)/shard_map/ppermute | solution.py:402
  51.6 1.9 %collective-permute-done.2.refs_3_ = bf16[64,1024]{1,0:T(8,128)(2,1)S(1)} collective-permute-done((bf16[64,1024]{1,0:T(8,128)(2,1)S(1)}, bf16[64,1024]{1,0:T(8,128)(2,1)S(1)}, u32[]{:S(2)}, u32[]{:S(2)}) %collective-permute-start.2) | collective-permute-done | bytes 131104 | tf_op jit(solution)/shard_map/ppermute | solution.py:402
  53.5 0.3 turn_queries.1.query_ref
  53.8 5.8 %all-to-all-done.1.conv_ref = bf16[8,128,256]{2,1,0:T(8,128)(2,1)S(1)} async-done(((bf16[8,128,256]{2,1,0:T(8,128)(2,1)}), bf16[8,128,256]{2,1,0:T(8,128)(2,1)S(1)}, u32[]{:S(2)}, u32[]{:S(2)}) %all-to-all-start.1) | async-done | bytes 524320 | tf_op jit(solution)/shard_map/all_to_all | solution.py:506
  59.6 1.7 %mix_out.1 = bf16[1024,256]{1,0:T(8,128)(2,1)} custom-call(bf16[1024,256]{1,0:T(8,128)(2,1)S(1)} %turn_queries.1.query_ref, bf16[8,128,256]{2,1,0:T(8,128)(2,1)S(1)} %all-to-all-done.1.conv_ref), custom_call_target="tpu_custom_call" | custom-call | tf_op jit(solution)/shard_map/mix_out/pallas_call | solution.py:516
  (19 shorter events, 0.1 us)
Async XLA Ops:
  0.0 10.2 %copy-start.1 = (f32[1024,256]{1,0:T(8,128)S(1)}, f32[1024,256]{1,0:T(8,128)}, u32[]{:S(2)}) copy-start(f32[1024,256]{1,0:T(8,128)} %param.7) | copy-start | bytes 3145732
  0.0 10.2 %copy-start.2 = (f32[1024]{0:T(1024)S(1)}, f32[1024]{0:T(1024)}, u32[]{:S(2)}) copy-start(f32[1024]{0:T(1024)} %param.8) | copy-start | bytes 12292
  0.0 25.8 %copy-start.3 = (bf16[768,256]{1,0:T(8,128)(2,1)S(1)}, bf16[768,256]{1,0:T(8,128)(2,1)}, u32[]{:S(2)}) copy-start(bf16[768,256]{1,0:T(8,128)(2,1)} %constant.6.clone.wave_ref.refs_8_) | copy-start | bytes 1179652
  0.0 25.8 %copy-start.5 = (f32[8,2,256]{2,1,0:T(2,128)S(1)}, f32[8,2,256]{2,1,0:T(2,128)}, u32[]{:S(2)}) copy-start(f32[8,2,256]{2,1,0:T(2,128)} %constant.7.clone.twist_ref.refs_10_) | copy-start | bytes 49156
  2.9 22.9 %all-to-all-start = ((bf16[32,64,128]{2,1,0:T(8,128)(2,1)}), bf16[32,64,128]{2,1,0:T(8,128)(2,1)S(1)}, u32[]{:S(2)}, u32[]{:S(2)}) async-start(bf16[32,64,128]{2,1,0:T(8,128)(2,1)} %bitcast.8), calls=%async_computation | async-start | bytes 1048576 | tf_op jit(solution)/shard_map/all_to_all | solution.py:465
  11.6 7.7 %collective-permute-start.3 = (bf16[128,256]{1,0:T(8,128)(2,1)S(1)}, bf16[128,256]{1,0:T(8,128)(2,1)S(1)}, u32[]{:S(2)}, u32[]{:S(2)}) collective-permute-start(bf16[128,256]{1,0:T(8,128)(2,1)S(1)} %get-tuple-element.22), channel_id=1, source_target_pairs={{0,4},{4,0},{8,12},{12,8},{16,20},{20,16},{24,28},{28,24},{1,5},{5... | collective-permute-start | bytes 196616 | tf_op jit(solution)/shard_map/ppermute | solution.py:402
  13.5 9.2 %collective-permute-start.4 = (bf16[128,256]{1,0:T(8,128)(2,1)S(1)}, bf16[128,256]{1,0:T(8,128)(2,1)S(1)}, u32[]{:S(2)}, u32[]{:S(2)}) collective-permute-start(bf16[128,256]{1,0:T(8,128)(2,1)S(1)} %get-tuple-element.23), channel_id=1, source_target_pairs={{0,8},{4,12},{8,0},{12,4},{16,24},{20,28},{24,16},{28,20},{1,9},{5... | collective-permute-start | bytes 196616 | tf_op jit(solution)/shard_map/ppermute | solution.py:402
  14.9 13.8 %collective-permute-start.5 = (bf16[128,256]{1,0:T(8,128)(2,1)S(1)}, bf16[128,256]{1,0:T(8,128)(2,1)S(1)}, u32[]{:S(2)}, u32[]{:S(2)}) collective-permute-start(bf16[128,256]{1,0:T(8,128)(2,1)S(1)} %get-tuple-element.24), channel_id=1, source_target_pairs={{0,12},{4,8},{8,4},{12,0},{16,28},{20,24},{24,20},{28,16},{1,13},{... | collective-permute-start | bytes 196616 | tf_op jit(solution)/shard_map/ppermute | solution.py:402
  15.2 17.5 %collective-permute-start.6 = (bf16[128,256]{1,0:T(8,128)(2,1)S(1)}, bf16[128,256]{1,0:T(8,128)(2,1)S(1)}, u32[]{:S(2)}, u32[]{:S(2)}) collective-permute-start(bf16[128,256]{1,0:T(8,128)(2,1)S(1)} %get-tuple-element.25), channel_id=1, source_target_pairs={{0,16},{4,20},{8,24},{12,28},{16,0},{20,4},{24,8},{28,12},{1,17},{... | collective-permute-start | bytes 196616 | tf_op jit(solution)/shard_map/ppermute | solution.py:402
  17.9 17.2 %collective-permute-start.7 = (bf16[128,256]{1,0:T(8,128)(2,1)S(1)}, bf16[128,256]{1,0:T(8,128)(2,1)S(1)}, u32[]{:S(2)}, u32[]{:S(2)}) collective-permute-start(bf16[128,256]{1,0:T(8,128)(2,1)S(1)} %get-tuple-element.26), channel_id=1, source_target_pairs={{0,20},{4,16},{8,28},{12,24},{16,4},{20,0},{24,12},{28,8},{1,21},{... | collective-permute-start | bytes 196616 | tf_op jit(solution)/shard_map/ppermute | solution.py:402
  19.3 15.7 %collective-permute-start.8 = (bf16[128,256]{1,0:T(8,128)(2,1)S(1)}, bf16[128,256]{1,0:T(8,128)(2,1)S(1)}, u32[]{:S(2)}, u32[]{:S(2)}) collective-permute-start(bf16[128,256]{1,0:T(8,128)(2,1)S(1)} %get-tuple-element.27), channel_id=1, source_target_pairs={{0,24},{4,28},{8,16},{12,20},{16,8},{20,12},{24,0},{28,4},{1,25},{... | collective-permute-start | bytes 196616 | tf_op jit(solution)/shard_map/ppermute | solution.py:402
  22.7 12.4 %copy-start.4 = (bf16[768,256]{1,0:T(8,128)(2,1)S(1)}, bf16[768,256]{1,0:T(8,128)(2,1)}, u32[]{:S(2)}) copy-start(bf16[768,256]{1,0:T(8,128)(2,1)} %constant.8.clone.refs_9_) | copy-start | bytes 1179652
  22.7 12.4 %collective-permute-start.9 = (bf16[128,256]{1,0:T(8,128)(2,1)S(1)}, bf16[128,256]{1,0:T(8,128)(2,1)S(1)}, u32[]{:S(2)}, u32[]{:S(2)}) collective-permute-start(bf16[128,256]{1,0:T(8,128)(2,1)S(1)} %get-tuple-element.28), channel_id=1, source_target_pairs={{0,28},{4,24},{8,20},{12,16},{16,12},{20,8},{24,4},{28,0},{1,29},{... | collective-permute-start | bytes 196616 | tf_op jit(solution)/shard_map/ppermute | solution.py:402
  35.1 10.0 %copy-start = (bf16[64,3,4096]{2,0,1:T(8,128)(2,1)S(1)}, bf16[64,3,4096]{2,0,1:T(8,128)(2,1)}, u32[]{:S(2)}) copy-start(bf16[64,3,4096]{2,0,1:T(8,128)(2,1)} %param.6) | copy-start | bytes 4718596
  40.9 18.7 %all-to-all-start.1 = ((bf16[8,128,256]{2,1,0:T(8,128)(2,1)}), bf16[8,128,256]{2,1,0:T(8,128)(2,1)S(1)}, u32[]{:S(2)}, u32[]{:S(2)}) async-start(bf16[8,128,256]{2,1,0:T(8,128)(2,1)} %convolve.1), calls=%async_computation.1 | async-start | bytes 1048576 | tf_op jit(solution)/shard_map/all_to_all | solution.py:506
  45.2 1.9 %collective-permute-start = (bf16[64,1024]{1,0:T(8,128)(2,1)S(1)}, bf16[64,1024]{1,0:T(8,128)(2,1)S(1)}, u32[]{:S(2)}, u32[]{:S(2)}) collective-permute-start(bf16[64,1024]{1,0:T(8,128)(2,1)S(1)} %get-tuple-element.18), channel_id=1, source_target_pairs={{0,1},{1,0},{2,3},{3,2},{4,5},{5,4},{6,7},{7,6},{8,9},{9,8},{10,11... | collective-permute-start | bytes 393224 | tf_op jit(solution)/shard_map/ppermute | solution.py:402
  45.3 6.4 %collective-permute-start.1 = (bf16[64,1024]{1,0:T(8,128)(2,1)S(1)}, bf16[64,1024]{1,0:T(8,128)(2,1)S(1)}, u32[]{:S(2)}, u32[]{:S(2)}) collective-permute-start(bf16[64,1024]{1,0:T(8,128)(2,1)S(1)} %get-tuple-element.19), channel_id=1, source_target_pairs={{0,2},{1,3},{2,0},{3,1},{4,6},{5,7},{6,4},{7,5},{8,10},{9,11},{10,... | collective-permute-start | bytes 393224 | tf_op jit(solution)/shard_map/ppermute | solution.py:402
  46.8 6.7 %collective-permute-start.2 = (bf16[64,1024]{1,0:T(8,128)(2,1)S(1)}, bf16[64,1024]{1,0:T(8,128)(2,1)S(1)}, u32[]{:S(2)}, u32[]{:S(2)}) collective-permute-start(bf16[64,1024]{1,0:T(8,128)(2,1)S(1)} %get-tuple-element.20), channel_id=1, source_target_pairs={{0,3},{1,2},{2,1},{3,0},{4,7},{5,6},{6,5},{7,4},{8,11},{9,10},{10,... | collective-permute-start | bytes 393224 | tf_op jit(solution)/shard_map/ppermute | solution.py:402

commit v6 on v5

--- a/solution.py
+++ b/solution.py
@@ -94,18 +94,17 @@
 def tables(blocks):
     n2 = np.arange(ROW)
     k1 = np.arange(blocks)
-    main = 2.0 * np.pi * np.outer(n2, n2) / ROW
-    twist = 2.0 * np.pi * np.outer(k1 + 0.25, n2) / (blocks * ROW)
+    main = 2.0 * np.pi * np.outer(n2, n2 + 0.5) / ROW
+    twist = 2.0 * np.pi * np.outer(k1 + 0.25 - blocks / 2, n2) / (blocks * ROW)
     mix = 2.0 * np.pi * np.outer(k1 + 0.25, np.arange(blocks)) / blocks
-    wave = np.concatenate([np.cos(main), np.sin(main)], axis=1).astype(np.float32)
+    wave = np.stack([np.cos(main), np.sin(main)]).astype(np.float32)
     twist = np.stack([np.cos(twist), np.sin(twist)], axis=1).astype(np.float32)
     mix = np.stack([np.cos(mix), np.sin(mix)], axis=0).astype(np.float32)
     return wave, twist, mix
 
 
 def folded(wave):
-    half = np.concatenate([wave[:, :LANES], wave[:, ROW : ROW + LANES]], axis=1)
-    half[:, LANES] = wave[:, LANES]
+    half = np.concatenate([wave[0, :, :LANES], wave[1, :, :LANES]], axis=1)
     parts = []
     for values in (half, half.T):
         high = values.astype(jnp.bfloat16)
@@ -142,6 +141,10 @@
         (sum_re - more_re, sum_im - more_im),
         (gap_re - side_re, gap_im - side_im),
     )
+
+
+def row_of(ref, k, part, at):
+    return (2 * k + part) * HALF + at
 
 
 def mix_forward(taken, twist_ref, at, ref):
@@ -235,38 +238,21 @@
         code_ref[...] = encode(taps, 1)
 
 
-def first_lane():
-    return lax.broadcasted_iota(jnp.int32, (CHUNK, LANES), 1) == 0
-
-
 def combined(waves_ref, k, at):
     re, im = spectrum_rows(waves_ref, k, at)
-    first = first_lane()
     re_cos, re_sin, im_cos, im_sin = re[:, :LANES], re[:, LANES:], im[:, :LANES], im[:, LANES:]
-    near = (
-        re_cos + jnp.where(first, 0.0, im_sin),
-        im_cos - jnp.where(first, 0.0, re_sin),
+    return (
+        jnp.concatenate([re_cos + im_sin, re_cos - im_sin], axis=1),
+        jnp.concatenate([im_cos - re_sin, im_cos + re_sin], axis=1),
     )
-    far = (
-        jnp.where(first, re_sin, re_cos - im_sin),
-        jnp.where(first, im_sin, im_cos + re_sin),
-    )
-    return [jnp.concatenate([left, right], axis=1) for left, right in zip(near, far)]
 
 
 def put_folded(ref, k, at, re, im):
-    first = first_lane()
     near_re, far_re, near_im, far_im = re[:, :LANES], re[:, LANES:], im[:, :LANES], im[:, LANES:]
-    back_re = [
-        jnp.where(first, near_re, near_re + far_re),
-        jnp.where(first, far_re, far_im - near_im),
-    ]
-    back_im = [
-        jnp.where(first, near_im, near_im + far_im),
-        jnp.where(first, far_im, near_re - far_re),
-    ]
-    put_split(ref, 2 * k * HALF + at, jnp.concatenate(back_re, axis=1))
-    put_split(ref, (2 * k + 1) * HALF + at, jnp.concatenate(back_im, axis=1))
+    back_re = jnp.concatenate([near_re + far_re, far_im - near_im], axis=1)
+    back_im = jnp.concatenate([near_im + far_im, near_re - far_re], axis=1)
+    put_split(ref, row_of(ref, k, 0, at), back_re)
+    put_split(ref, row_of(ref, k, 1, at), back_im)
 
 
 def stage(wave_ref, source, target, work, half):
@@ -375,7 +361,7 @@
 
 def plain_conv(gated, taps):
     blocks = gated.shape[0]
-    wave, twist, mix = tables(blocks)
+    (cos, sin), twist, mix = tables(blocks)
     cos_twist, sin_twist = twist[:, 0][:, None, :], twist[:, 1][:, None, :]
     dot = functools.partial(jnp.einsum, precision=lax.Precision.HIGHEST)
 
@@ -383,14 +369,18 @@
         re = dot("ncm,kn->kcm", values, mix[0])
         im = -dot("ncm,kn->kcm", values, mix[1])
         re, im = re * cos_twist + im * sin_twist, im * cos_twist - re * sin_twist
-        re, im = dot("kcm,mq->kcq", re, wave), dot("kcm,mq->kcq", im, wave)
-        return re[..., :ROW] + im[..., ROW:], im[..., :ROW] - re[..., ROW:]
+        return (
+            dot("kcm,mq->kcq", re, cos) + dot("kcm,mq->kcq", im, sin),
+            dot("kcm,mq->kcq", im, cos) - dot("kcm,mq->kcq", re, sin),
+        )
 
     u_re, u_im = forward(gated)
     h_re, h_im = forward(taps)
-    re = dot("kcm,mq->kcq", u_re * h_re - u_im * h_im, wave)
-    im = dot("kcm,mq->kcq", u_re * h_im + u_im * h_re, wave)
-    re, im = re[..., :ROW] - im[..., ROW:], im[..., :ROW] + re[..., ROW:]
+    re, im = u_re * h_re - u_im * h_im, u_re * h_im + u_im * h_re
+    re, im = (
+        dot("kcq,mq->kcm", re, cos) - dot("kcq,mq->kcm", im, sin),
+        dot("kcq,mq->kcm", im, cos) + dot("kcq,mq->kcm", re, sin),
+    )
     re, im = re * cos_twist - im * sin_twist, im * cos_twist + re * sin_twist
     total = dot("kcm,kn->ncm", re, mix[0]) - dot("kcm,kn->ncm", im, mix[1])
     return total * (1.0 / (blocks * ROW))

time: 61.6 us -> 61.5 us (level)
  no operation moved by 1% of the time
where the time goes in v6:
time: 61.5 us; the launch traced here: 61.2 us
  starting transfers between devices  27.5 us (45%)
  waiting for transfers between devices  18.6 us (30%)
  Pallas kernels  15 us (24%)
    ppermute x10, starting transfers between devices, scatter(): lax.ppermute(block, axis, [(i, i ^ turn) for i in range(count)])  16 us
    ppermute x10, waiting for transfers between devices, scatter(): lax.ppermute(block, axis, [(i, i ^ turn) for i in range(count)])  12.7 us
    all_to_all x1, starting transfers between devices, body(): gated = exchange(gated, ('seq', 'ch'))  7.32 us
    all_to_all x1, waiting for transfers between devices, body(): convolved = exchange(convolved, 'seq')  5.77 us
    pallas_call x1, Pallas kernels, body(): pl.pallas_call(conv_kernel, out_shape=jax.ShapeDtypeStruct((blocks, own,...  5.68 us
    all_to_all x1, starting transfers between devices, body(): convolved = exchange(convolved, 'seq')  4.17 us
    pallas_call x1, Pallas kernels, body(): pl.pallas_call(gated_spectrum_kernel, out_shape=jax.ShapeDtypeStruct((2,...  2.92 us
    pallas_call x1, Pallas kernels, body(): pl.pallas_call(send_kernel, in_specs=[far], out_specs=far, out_shape=jax....  2.9 us
  transfers between devices with their start and end apart: 12, of which 6 were waited for; matrix products, arithmetic and copies ran while one was open for 0% of the time, Pallas kernels for 8%

profile of v6, /device:TPU:0, one launch (start us, length us, event | category | flops | bytes accessed | tf_op | source)
XLA Modules:
  0.0 61.2 jit_solution(15274253568284718148)
XLA Ops:
  0.0 2.9 %encode_gated.1 = bf16[8,4,64,128]{3,2,1,0:T(8,128)(2,1)} custom-call(bf16[3,64,4096]{2,1,0:T(8,128)(2,1)} %bitcast.4), custom_call_target="tpu_custom_call" | custom-call | flops 33554432 | bytes 8388608 | tf_op jit(solution)/shard_map/encode_gated/pallas_call | solution.py:411
  2.9 7.3 %all-to-all-start = ((bf16[32,64,128]{2,1,0:T(8,128)(2,1)}), bf16[32,64,128]{2,1,0:T(8,128)(2,1)S(1)}, u32[]{:S(2)}, u32[]{:S(2)}) async-start(bf16[32,64,128]{2,1,0:T(8,128)(2,1)} %bitcast.8), calls=%async_computation | async-start | bytes 1048576 | tf_op jit(solution)/shard_map/all_to_all | solution.py:455
  10.3 1.4 %encode_taps.1 = (bf16[128,256]{1,0:T(8,128)(2,1)S(1)}, bf16[128,256]{1,0:T(8,128)(2,1)S(1)}, bf16[128,256]{1,0:T(8,128)(2,1)S(1)}, bf16[128,256]{1,0:T(8,128)(2...) custom-call(f32[8,128,256]{2,1,0:T(8,128)S(1)} %bitcast.6, ...), custom_call_target="tpu_custom_call" | custom-call | flops 33554432 | bytes 8388608 | tf_op jit(solution)/shard_map/encode_taps/pallas_call | solution.py:437
  11.6 1.8 %collective-permute-start.3 = (bf16[128,256]{1,0:T(8,128)(2,1)S(1)}, bf16[128,256]{1,0:T(8,128)(2,1)S(1)}, u32[]{:S(2)}, u32[]{:S(2)}) collective-permute-start(bf16[128,256]{1,0:T(8,128)(2,1)S(1)} %get-tuple-element.22), channel_id=1, source_target_pairs={{0,4},{4,0},{8,12},{12,8},{16,20},{20,16},{24,28},{28,24},{1,5},{5... | collective-permute-start | bytes 196616 | tf_op jit(solution)/shard_map/ppermute | solution.py:392
  13.5 1.5 %collective-permute-start.4 = (bf16[128,256]{1,0:T(8,128)(2,1)S(1)}, bf16[128,256]{1,0:T(8,128)(2,1)S(1)}, u32[]{:S(2)}, u32[]{:S(2)}) collective-permute-start(bf16[128,256]{1,0:T(8,128)(2,1)S(1)} %get-tuple-element.23), channel_id=1, source_target_pairs={{0,8},{4,12},{8,0},{12,4},{16,24},{20,28},{24,16},{28,20},{1,9},{5... | collective-permute-start | bytes 196616 | tf_op jit(solution)/shard_map/ppermute | solution.py:392
  14.9 0.3 collective-permute-start.5
  15.2 2.7 %collective-permute-start.6 = (bf16[128,256]{1,0:T(8,128)(2,1)S(1)}, bf16[128,256]{1,0:T(8,128)(2,1)S(1)}, u32[]{:S(2)}, u32[]{:S(2)}) collective-permute-start(bf16[128,256]{1,0:T(8,128)(2,1)S(1)} %get-tuple-element.25), channel_id=1, source_target_pairs={{0,16},{4,20},{8,24},{12,28},{16,0},{20,4},{24,8},{28,12},{1,17},{... | collective-permute-start | bytes 196616 | tf_op jit(solution)/shard_map/ppermute | solution.py:392
  17.9 1.5 %collective-permute-start.7 = (bf16[128,256]{1,0:T(8,128)(2,1)S(1)}, bf16[128,256]{1,0:T(8,128)(2,1)S(1)}, u32[]{:S(2)}, u32[]{:S(2)}) collective-permute-start(bf16[128,256]{1,0:T(8,128)(2,1)S(1)} %get-tuple-element.26), channel_id=1, source_target_pairs={{0,20},{4,16},{8,28},{12,24},{16,4},{20,0},{24,12},{28,8},{1,21},{... | collective-permute-start | bytes 196616 | tf_op jit(solution)/shard_map/ppermute | solution.py:392
  19.3 3.3 %collective-permute-start.8 = (bf16[128,256]{1,0:T(8,128)(2,1)S(1)}, bf16[128,256]{1,0:T(8,128)(2,1)S(1)}, u32[]{:S(2)}, u32[]{:S(2)}) collective-permute-start(bf16[128,256]{1,0:T(8,128)(2,1)S(1)} %get-tuple-element.27), channel_id=1, source_target_pairs={{0,24},{4,28},{8,16},{12,20},{16,8},{20,12},{24,0},{28,4},{1,25},{... | collective-permute-start | bytes 196616 | tf_op jit(solution)/shard_map/ppermute | solution.py:392
  22.7 3.1 %collective-permute-start.9 = (bf16[128,256]{1,0:T(8,128)(2,1)S(1)}, bf16[128,256]{1,0:T(8,128)(2,1)S(1)}, u32[]{:S(2)}, u32[]{:S(2)}) collective-permute-start(bf16[128,256]{1,0:T(8,128)(2,1)S(1)} %get-tuple-element.28), channel_id=1, source_target_pairs={{0,28},{4,24},{8,20},{12,16},{16,12},{20,8},{24,4},{28,0},{1,29},{... | collective-permute-start | bytes 196616 | tf_op jit(solution)/shard_map/ppermute | solution.py:392
  25.8 2.9 %gated_spectrum.1.gated_ref = f32[2,8,2,64,256]{4,3,2,1,0:T(8,128)S(1)} custom-call(bf16[32,64,128]{2,1,0:T(8,128)(2,1)S(1)} %all-to-all-done.gated_ref, bf16[768,256]{1,0:T(8,128)(2,1)S(1)} %copy-done.3, f32[8,2,256]{2,1,0:T(2,128)S(1)} %copy-done.5), custom_call_target="tpu_custom_call" | custom-call | flops 4294967296 | bytes 16777216 | tf_op jit(solution)/shard_map/gated_spectrum/pallas_call | solution.py:467
  28.7 4.0 %collective-permute-done.6.refs_4_ = bf16[128,256]{1,0:T(8,128)(2,1)S(1)} collective-permute-done((bf16[128,256]{1,0:T(8,128)(2,1)S(1)}, bf16[128,256]{1,0:T(8,128)(2,1)S(1)}, u32[]{:S(2)}, u32[]{:S(2)}) %collective-permute-start.6) | collective-permute-done | bytes 65568 | tf_op jit(solution)/shard_map/ppermute | solution.py:392
  32.7 2.3 %collective-permute-done.7.refs_5_ = bf16[128,256]{1,0:T(8,128)(2,1)S(1)} collective-permute-done((bf16[128,256]{1,0:T(8,128)(2,1)S(1)}, bf16[128,256]{1,0:T(8,128)(2,1)S(1)}, u32[]{:S(2)}, u32[]{:S(2)}) %collective-permute-start.7) | collective-permute-done | bytes 65568 | tf_op jit(solution)/shard_map/ppermute | solution.py:392
  35.1 5.7 %convolve.1 = bf16[8,128,256]{2,1,0:T(8,128)(2,1)} custom-call(f32[2,8,2,64,256]{4,3,2,1,0:T(8,128)S(1)} %gated_spectrum.1.gated_ref, bf16[128,256]{1,0:T(8,128)(2,1)S(1)} %get-tuple-element.21.refs_0_, bf16[128,256]{1,0:T(8,128)(2,1)S(1)} %collective-permute-done.3.refs_1_, bf16[128,256]{1,0:T(8,128)(2,1)S(1)} %collective-permute-done.4.refs_2_, ...), custom_call_target="tpu_custom_call" | custom-call | flops 4294967296 | bytes 16777216 | tf_op jit(solution)/shard_map/convolve/pallas_call | solution.py:475
  40.8 4.2 %all-to-all-start.1 = ((bf16[8,128,256]{2,1,0:T(8,128)(2,1)}), bf16[8,128,256]{2,1,0:T(8,128)(2,1)S(1)}, u32[]{:S(2)}, u32[]{:S(2)}) async-start(bf16[8,128,256]{2,1,0:T(8,128)(2,1)} %convolve.1), calls=%async_computation.1 | async-start | bytes 1048576 | tf_op jit(solution)/shard_map/all_to_all | solution.py:496
  44.9 0.1 send_queries.1
  45.1 0.1 collective-permute-start
  45.2 1.5 %collective-permute-start.1 = (bf16[64,1024]{1,0:T(8,128)(2,1)S(1)}, bf16[64,1024]{1,0:T(8,128)(2,1)S(1)}, u32[]{:S(2)}, u32[]{:S(2)}) collective-permute-start(bf16[64,1024]{1,0:T(8,128)(2,1)S(1)} %get-tuple-element.19), channel_id=1, source_target_pairs={{0,2},{1,3},{2,0},{3,1},{4,6},{5,7},{6,4},{7,5},{8,10},{9,11},{10,... | collective-permute-start | bytes 393224 | tf_op jit(solution)/shard_map/ppermute | solution.py:392
  46.7 0.3 collective-permute-start.2
  47.0 4.5 %collective-permute-done.1.refs_2_ = bf16[64,1024]{1,0:T(8,128)(2,1)S(1)} collective-permute-done((bf16[64,1024]{1,0:T(8,128)(2,1)S(1)}, bf16[64,1024]{1,0:T(8,128)(2,1)S(1)}, u32[]{:S(2)}, u32[]{:S(2)}) %collective-permute-start.1) | collective-permute-done | bytes 131104 | tf_op jit(solution)/shard_map/ppermute | solution.py:392
  51.5 1.9 %collective-permute-done.2.refs_3_ = bf16[64,1024]{1,0:T(8,128)(2,1)S(1)} collective-permute-done((bf16[64,1024]{1,0:T(8,128)(2,1)S(1)}, bf16[64,1024]{1,0:T(8,128)(2,1)S(1)}, u32[]{:S(2)}, u32[]{:S(2)}) %collective-permute-start.2) | collective-permute-done | bytes 131104 | tf_op jit(solution)/shard_map/ppermute | solution.py:392
  53.4 0.3 turn_queries.1.query_ref
  53.7 5.8 %all-to-all-done.1.conv_ref = bf16[8,128,256]{2,1,0:T(8,128)(2,1)S(1)} async-done(((bf16[8,128,256]{2,1,0:T(8,128)(2,1)}), bf16[8,128,256]{2,1,0:T(8,128)(2,1)S(1)}, u32[]{:S(2)}, u32[]{:S(2)}) %all-to-all-start.1) | async-done | bytes 524320 | tf_op jit(solution)/shard_map/all_to_all | solution.py:496
  59.5 1.7 %mix_out.1 = bf16[1024,256]{1,0:T(8,128)(2,1)} custom-call(bf16[1024,256]{1,0:T(8,128)(2,1)S(1)} %turn_queries.1.query_ref, bf16[8,128,256]{2,1,0:T(8,128)(2,1)S(1)} %all-to-all-done.1.conv_ref), custom_call_target="tpu_custom_call" | custom-call | tf_op jit(solution)/shard_map/mix_out/pallas_call | solution.py:506
  (19 shorter events, 0.1 us)
Async XLA Ops:
  0.0 10.2 %copy-start.1 = (f32[1024,256]{1,0:T(8,128)S(1)}, f32[1024,256]{1,0:T(8,128)}, u32[]{:S(2)}) copy-start(f32[1024,256]{1,0:T(8,128)} %param.7) | copy-start | bytes 3145732
  0.0 10.2 %copy-start.2 = (f32[1024]{0:T(1024)S(1)}, f32[1024]{0:T(1024)}, u32[]{:S(2)}) copy-start(f32[1024]{0:T(1024)} %param.8) | copy-start | bytes 12292
  0.0 25.8 %copy-start.3 = (bf16[768,256]{1,0:T(8,128)(2,1)S(1)}, bf16[768,256]{1,0:T(8,128)(2,1)}, u32[]{:S(2)}) copy-start(bf16[768,256]{1,0:T(8,128)(2,1)} %constant.6.clone.wave_ref.refs_8_) | copy-start | bytes 1179652
  0.0 25.8 %copy-start.5 = (f32[8,2,256]{2,1,0:T(2,128)S(1)}, f32[8,2,256]{2,1,0:T(2,128)}, u32[]{:S(2)}) copy-start(f32[8,2,256]{2,1,0:T(2,128)} %constant.7.clone.twist_ref.refs_10_) | copy-start | bytes 49156
  2.9 22.9 %all-to-all-start = ((bf16[32,64,128]{2,1,0:T(8,128)(2,1)}), bf16[32,64,128]{2,1,0:T(8,128)(2,1)S(1)}, u32[]{:S(2)}, u32[]{:S(2)}) async-start(bf16[32,64,128]{2,1,0:T(8,128)(2,1)} %bitcast.8), calls=%async_computation | async-start | bytes 1048576 | tf_op jit(solution)/shard_map/all_to_all | solution.py:455
  11.6 7.7 %collective-permute-start.3 = (bf16[128,256]{1,0:T(8,128)(2,1)S(1)}, bf16[128,256]{1,0:T(8,128)(2,1)S(1)}, u32[]{:S(2)}, u32[]{:S(2)}) collective-permute-start(bf16[128,256]{1,0:T(8,128)(2,1)S(1)} %get-tuple-element.22), channel_id=1, source_target_pairs={{0,4},{4,0},{8,12},{12,8},{16,20},{20,16},{24,28},{28,24},{1,5},{5... | collective-permute-start | bytes 196616 | tf_op jit(solution)/shard_map/ppermute | solution.py:392
  13.5 9.2 %collective-permute-start.4 = (bf16[128,256]{1,0:T(8,128)(2,1)S(1)}, bf16[128,256]{1,0:T(8,128)(2,1)S(1)}, u32[]{:S(2)}, u32[]{:S(2)}) collective-permute-start(bf16[128,256]{1,0:T(8,128)(2,1)S(1)} %get-tuple-element.23), channel_id=1, source_target_pairs={{0,8},{4,12},{8,0},{12,4},{16,24},{20,28},{24,16},{28,20},{1,9},{5... | collective-permute-start | bytes 196616 | tf_op jit(solution)/shard_map/ppermute | solution.py:392
  14.9 13.8 %collective-permute-start.5 = (bf16[128,256]{1,0:T(8,128)(2,1)S(1)}, bf16[128,256]{1,0:T(8,128)(2,1)S(1)}, u32[]{:S(2)}, u32[]{:S(2)}) collective-permute-start(bf16[128,256]{1,0:T(8,128)(2,1)S(1)} %get-tuple-element.24), channel_id=1, source_target_pairs={{0,12},{4,8},{8,4},{12,0},{16,28},{20,24},{24,20},{28,16},{1,13},{... | collective-permute-start | bytes 196616 | tf_op jit(solution)/shard_map/ppermute | solution.py:392
  15.2 17.5 %collective-permute-start.6 = (bf16[128,256]{1,0:T(8,128)(2,1)S(1)}, bf16[128,256]{1,0:T(8,128)(2,1)S(1)}, u32[]{:S(2)}, u32[]{:S(2)}) collective-permute-start(bf16[128,256]{1,0:T(8,128)(2,1)S(1)} %get-tuple-element.25), channel_id=1, source_target_pairs={{0,16},{4,20},{8,24},{12,28},{16,0},{20,4},{24,8},{28,12},{1,17},{... | collective-permute-start | bytes 196616 | tf_op jit(solution)/shard_map/ppermute | solution.py:392
  17.9 17.2 %collective-permute-start.7 = (bf16[128,256]{1,0:T(8,128)(2,1)S(1)}, bf16[128,256]{1,0:T(8,128)(2,1)S(1)}, u32[]{:S(2)}, u32[]{:S(2)}) collective-permute-start(bf16[128,256]{1,0:T(8,128)(2,1)S(1)} %get-tuple-element.26), channel_id=1, source_target_pairs={{0,20},{4,16},{8,28},{12,24},{16,4},{20,0},{24,12},{28,8},{1,21},{... | collective-permute-start | bytes 196616 | tf_op jit(solution)/shard_map/ppermute | solution.py:392
  19.3 15.7 %collective-permute-start.8 = (bf16[128,256]{1,0:T(8,128)(2,1)S(1)}, bf16[128,256]{1,0:T(8,128)(2,1)S(1)}, u32[]{:S(2)}, u32[]{:S(2)}) collective-permute-start(bf16[128,256]{1,0:T(8,128)(2,1)S(1)} %get-tuple-element.27), channel_id=1, source_target_pairs={{0,24},{4,28},{8,16},{12,20},{16,8},{20,12},{24,0},{28,4},{1,25},{... | collective-permute-start | bytes 196616 | tf_op jit(solution)/shard_map/ppermute | solution.py:392
  22.7 12.4 %copy-start.4 = (bf16[768,256]{1,0:T(8,128)(2,1)S(1)}, bf16[768,256]{1,0:T(8,128)(2,1)}, u32[]{:S(2)}) copy-start(bf16[768,256]{1,0:T(8,128)(2,1)} %constant.8.clone.refs_9_) | copy-start | bytes 1179652
  22.7 12.4 %collective-permute-start.9 = (bf16[128,256]{1,0:T(8,128)(2,1)S(1)}, bf16[128,256]{1,0:T(8,128)(2,1)S(1)}, u32[]{:S(2)}, u32[]{:S(2)}) collective-permute-start(bf16[128,256]{1,0:T(8,128)(2,1)S(1)} %get-tuple-element.28), channel_id=1, source_target_pairs={{0,28},{4,24},{8,20},{12,16},{16,12},{20,8},{24,4},{28,0},{1,29},{... | collective-permute-start | bytes 196616 | tf_op jit(solution)/shard_map/ppermute | solution.py:392
  35.1 9.9 %copy-start = (bf16[64,3,4096]{2,0,1:T(8,128)(2,1)S(1)}, bf16[64,3,4096]{2,0,1:T(8,128)(2,1)}, u32[]{:S(2)}) copy-start(bf16[64,3,4096]{2,0,1:T(8,128)(2,1)} %param.6) | copy-start | bytes 4718596
  40.8 18.7 %all-to-all-start.1 = ((bf16[8,128,256]{2,1,0:T(8,128)(2,1)}), bf16[8,128,256]{2,1,0:T(8,128)(2,1)S(1)}, u32[]{:S(2)}, u32[]{:S(2)}) async-start(bf16[8,128,256]{2,1,0:T(8,128)(2,1)} %convolve.1), calls=%async_computation.1 | async-start | bytes 1048576 | tf_op jit(solution)/shard_map/all_to_all | solution.py:496
  45.1 1.9 %collective-permute-start = (bf16[64,1024]{1,0:T(8,128)(2,1)S(1)}, bf16[64,1024]{1,0:T(8,128)(2,1)S(1)}, u32[]{:S(2)}, u32[]{:S(2)}) collective-permute-start(bf16[64,1024]{1,0:T(8,128)(2,1)S(1)} %get-tuple-element.18), channel_id=1, source_target_pairs={{0,1},{1,0},{2,3},{3,2},{4,5},{5,4},{6,7},{7,6},{8,9},{9,8},{10,11... | collective-permute-start | bytes 393224 | tf_op jit(solution)/shard_map/ppermute | solution.py:392
  45.2 6.4 %collective-permute-start.1 = (bf16[64,1024]{1,0:T(8,128)(2,1)S(1)}, bf16[64,1024]{1,0:T(8,128)(2,1)S(1)}, u32[]{:S(2)}, u32[]{:S(2)}) collective-permute-start(bf16[64,1024]{1,0:T(8,128)(2,1)S(1)} %get-tuple-element.19), channel_id=1, source_target_pairs={{0,2},{1,3},{2,0},{3,1},{4,6},{5,7},{6,4},{7,5},{8,10},{9,11},{10,... | collective-permute-start | bytes 393224 | tf_op jit(solution)/shard_map/ppermute | solution.py:392
  46.7 6.7 %collective-permute-start.2 = (bf16[64,1024]{1,0:T(8,128)(2,1)S(1)}, bf16[64,1024]{1,0:T(8,128)(2,1)S(1)}, u32[]{:S(2)}, u32[]{:S(2)}) collective-permute-start(bf16[64,1024]{1,0:T(8,128)(2,1)S(1)} %get-tuple-element.20), channel_id=1, source_target_pairs={{0,3},{1,2},{2,1},{3,0},{4,7},{5,6},{6,5},{7,4},{8,11},{9,10},{10,... | collective-permute-start | bytes 393224 | tf_op jit(solution)/shard_map/ppermute | solution.py:392

commit v7 on v6

--- a/solution.py
+++ b/solution.py
@@ -16,7 +16,7 @@
 LANES = 128
 ROW = 256
 CHUNK = 16
-HALF = 64
+GROUP = 32
 VMEM_BYTES = 20 * 1024 * 1024
 SMALL_BYTES = 12 * 1024 * 1024
 ALL_BYTES = 60 * 1024 * 1024
@@ -143,8 +143,8 @@
     )
 
 
-def row_of(ref, k, part, at):
-    return (2 * k + part) * HALF + at
+def row_of(k, part, at):
+    return (2 * k + part) * GROUP + at
 
 
 def mix_forward(taken, twist_ref, at, ref):
@@ -155,8 +155,8 @@
         for index, (re, im) in enumerate(values):
             k = start + 2 * index
             cos_twist, sin_twist = twist_ref[k, 0:1, :], twist_ref[k, 1:2, :]
-            put_split(ref, 2 * k * HALF + at, re * cos_twist + im * sin_twist)
-            put_split(ref, (2 * k + 1) * HALF + at, im * cos_twist - re * sin_twist)
+            put_split(ref, row_of(k, 0, at), re * cos_twist + im * sin_twist)
+            put_split(ref, row_of(k, 1, at), im * cos_twist - re * sin_twist)
 
 
 def mix_back(spectra, twist_ref):
@@ -174,17 +174,17 @@
 
 
 def spectrum_rows(waves_ref, k, at):
-    re = waves_ref[pl.ds(2 * k * HALF + at, CHUNK), :]
-    im = waves_ref[pl.ds((2 * k + 1) * HALF + at, CHUNK), :]
+    re = waves_ref[pl.ds(row_of(k, 0, at), CHUNK), :]
+    im = waves_ref[pl.ds(row_of(k, 1, at), CHUNK), :]
     return re, im
 
 
 def send_kernel(streams_ref, gated_ref, keys, values, codes, in_sems, out_sems):
     groups, parts = gated_ref.shape[:2]
-    per = groups // 2
+    per = groups
     width = per * LANES
     arrivals = []
-    for chunk in range(2 * parts):
+    for chunk in range(parts):
         lanes = pl.ds(chunk * width, width)
         for stream, buffer in ((1, keys), (2, values)):
             copy = pltpu.make_async_copy(
@@ -193,10 +193,10 @@
             copy.start()
             arrivals.append(copy)
     copies = []
-    for chunk in range(2 * parts):
+    for chunk in range(parts):
         for copy in arrivals[2 * chunk : 2 * chunk + 2]:
             copy.wait()
-        part, first = chunk // 2, chunk % 2 * per
+        part, first = chunk, 0
         for block in range(per):
             lanes = slice(block * LANES, (block + 1) * LANES)
             left = keys[chunk, :, lanes].astype(jnp.float32)
@@ -251,89 +251,94 @@
     near_re, far_re, near_im, far_im = re[:, :LANES], re[:, LANES:], im[:, :LANES], im[:, LANES:]
     back_re = jnp.concatenate([near_re + far_re, far_im - near_im], axis=1)
     back_im = jnp.concatenate([near_im + far_im, near_re - far_re], axis=1)
-    put_split(ref, row_of(ref, k, 0, at), back_re)
-    put_split(ref, row_of(ref, k, 1, at), back_im)
-
-
-def stage(wave_ref, source, target, work, half):
-    if source is not None:
-        target[...] = jnp.dot(source[...], wave_ref[...], preferred_element_type=jnp.float32)
-    for chunk in range(HALF // CHUNK):
-        work(half, chunk * CHUNK)
+    put_split(ref, row_of(k, 0, at), back_re)
+    put_split(ref, row_of(k, 1, at), back_im)
+
+
+def multiply(source, wave_ref, target):
+    target[...] = jnp.dot(source[...], wave_ref[...], preferred_element_type=jnp.float32)
+
+
+def row_groups():
+    return [range(first, first + GROUP, CHUNK) for first in range(0, LANES, GROUP)]
 
 
 def gated_spectrum_kernel(gated_ref, wave_ref, twist_ref, out_ref, u, *scratch):
+    rows, waves = scratch[0:2], scratch[2:4]
     blocks = u.shape[0]
-    rows, waves = scratch[0:2], scratch[2:4]
     parts = ROW // gated_ref.shape[1]
+    groups = row_groups()
 
     def unpack(block, _):
         pieces = [decode(gated_ref[block * parts + part], 0) for part in range(parts)]
         u[block] = jnp.transpose(jnp.concatenate(pieces, axis=0))
         return 0
 
-    def forward(half, at):
-        start = pl.ds(half * HALF + at, CHUNK)
-        mix_forward([u[n1, start, :] for n1 in range(blocks)], twist_ref, at, rows[half])
-
-    def finish(half, at):
-        for k in range(blocks):
-            re, im = combined(waves[half], k, at)
-            out_ref[half, k, 0, pl.ds(at, CHUNK), :] = re
-            out_ref[half, k, 1, pl.ds(at, CHUNK), :] = im
-
     lax.fori_loop(0, blocks, unpack, 0)
-    stage(None, None, None, forward, 0)
-    stage(wave_ref, rows[0], waves[0], forward, 1)
-    stage(wave_ref, rows[1], waves[1], finish, 0)
-    stage(None, None, None, finish, 1)
+    for step in range(len(groups) + 2):
+        if 0 <= step - 1 < len(groups):
+            multiply(rows[(step - 1) % 2], wave_ref, waves[(step - 1) % 2])
+        if step < len(groups):
+            for at in groups[step]:
+                taken = [u[n1, at : at + CHUNK, :] for n1 in range(blocks)]
+                mix_forward(taken, twist_ref, at % GROUP, rows[step % 2])
+        if step >= 2:
+            for at in groups[step - 2]:
+                for k in range(blocks):
+                    re, im = combined(waves[step % 2], k, at % GROUP)
+                    out_ref[k, 0, at : at + CHUNK, :] = re
+                    out_ref[k, 1, at : at + CHUNK, :] = im
 
 
 def conv_kernel(gated_ref, *refs):
-    blocks = gated_ref.shape[1]
+    blocks = gated_ref.shape[0]
     wave_ref, back_wave_ref, twist_ref, out_ref, codes, out, sems, *scratch = refs[blocks:]
-    rows, waves = scratch[0:2], scratch[2:4]
+    rows, waves, back_rows, back_waves = (scratch[at : at + 2] for at in (0, 2, 4, 6))
     scale = math.log2(blocks * ROW)
     me = lax.axis_index("seq")
+    groups = row_groups()
     for turn, code_ref in enumerate(refs[:blocks]):
         codes[me ^ turn] = code_ref[...]
 
-    def forward(half, at):
-        start = pl.ds(half * HALF + at, CHUNK)
-        taken = [decode(codes[n1, start, :], 1, scale) for n1 in range(blocks)]
-        mix_forward(taken, twist_ref, at, rows[half])
-
-    def product(half, at):
+    def forward(at, half):
+        taken = [decode(codes[n1, at : at + CHUNK, :], 1, scale) for n1 in range(blocks)]
+        mix_forward(taken, twist_ref, at % GROUP, rows[half])
+
+    def product(at, half):
         for k in range(blocks):
-            re, im = combined(waves[half], k, at)
-            gated_re = gated_ref[half, k, 0, pl.ds(at, CHUNK), :]
-            gated_im = gated_ref[half, k, 1, pl.ds(at, CHUNK), :]
+            re, im = combined(waves[half], k, at % GROUP)
+            gated_re = gated_ref[k, 0, at : at + CHUNK, :]
+            gated_im = gated_ref[k, 1, at : at + CHUNK, :]
             product_re, product_im = re * gated_re - im * gated_im, re * gated_im + im * gated_re
-            put_folded(rows[half], k, at, product_re, product_im)
-
-    def back(half, at):
-        spectra = [spectrum_rows(waves[half], k, at) for k in range(blocks)]
-        start = pl.ds(half * HALF + at, CHUNK)
+            put_folded(back_rows[half], k, at % GROUP, product_re, product_im)
+
+    def back(at, half):
+        spectra = [spectrum_rows(back_waves[half], k, at % GROUP) for k in range(blocks)]
         totals = mix_back(spectra, twist_ref)
         sizes = [jnp.abs(total) for total in totals]
         peak = jnp.max(functools.reduce(jnp.maximum, sizes), axis=1, keepdims=True)
         for n1, code in enumerate(encode_all(totals, scale_of(peak), 1)):
-            out[n1, start, :] = code
-
-    def out_copy(half):
-        start = pl.ds(half * HALF, HALF)
-        return pltpu.make_async_copy(out.at[:, start, :], out_ref.at[:, start, :], sems.at[half])
-
-    stage(None, None, None, forward, 0)
-    stage(wave_ref, rows[0], waves[0], forward, 1)
-    stage(wave_ref, rows[1], waves[1], product, 0)
-    stage(back_wave_ref, rows[0], waves[0], product, 1)
-    stage(back_wave_ref, rows[1], waves[1], back, 0)
-    out_copy(0).start()
-    stage(None, None, None, back, 1)
-    out_copy(1).start()
-    out_copy(0).wait()
-    out_copy(1).wait()
+            out[n1, at : at + CHUNK, :] = code
+
+    copies = []
+    for step in range(len(groups) + 4):
+        if 0 <= step - 1 < len(groups):
+            multiply(rows[(step - 1) % 2], wave_ref, waves[(step - 1) % 2])
+        if 0 <= step - 3 < len(groups):
+            multiply(back_rows[(step - 3) % 2], back_wave_ref, back_waves[(step - 3) % 2])
+        for work, delay in ((forward, 0), (product, 2), (back, 4)):
+            if 0 <= step - delay < len(groups):
+                for at in groups[step - delay]:
+                    work(at, step % 2)
+        if step >= 4:
+            place = pl.ds((step - 4) * GROUP, GROUP)
+            copy = pltpu.make_async_copy(
+                out.at[:, place, :], out_ref.at[:, place, :], sems.at[step - 4]
+            )
+            copy.start()
+            copies.append(copy)
+    for copy in copies:
+        copy.wait()
 
 
 def turn_kernel(*refs):
@@ -407,7 +412,7 @@
     if fits:
         far = pl.BlockSpec(memory_space=pl.ANY)
         coded = (groups, parts, held, own)
-        stream = pltpu.VMEM((2 * parts, held, wide // 2), jnp.bfloat16)
+        stream = pltpu.VMEM((parts, held, wide), jnp.bfloat16)
         gated = pl.pallas_call(
             send_kernel,
             in_specs=[far],
@@ -461,12 +466,12 @@
     if fits:
         wave, twist, _ = tables(blocks)
         wave, back_wave = folded(wave)
-        scratch = [pltpu.VMEM((blocks * 2 * HALF, 3 * ROW), jnp.bfloat16)] * 2
-        scratch += [pltpu.VMEM((blocks * 2 * HALF, ROW), jnp.float32)] * 2
+        scratch = [pltpu.VMEM((blocks * 2 * GROUP, 3 * ROW), jnp.bfloat16)] * 2
+        scratch += [pltpu.VMEM((blocks * 2 * GROUP, ROW), jnp.float32)] * 2
         large = pltpu.CompilerParams(vmem_limit_bytes=VMEM_BYTES)
         gated = pl.pallas_call(
             gated_spectrum_kernel,
-            out_shape=jax.ShapeDtypeStruct((2, blocks, 2, HALF, ROW), jnp.float32),
+            out_shape=jax.ShapeDtypeStruct((blocks, 2, own, ROW), jnp.float32),
             scratch_shapes=[pltpu.VMEM((blocks, own, ROW), jnp.float32)] + scratch,
             compiler_params=large,
             cost_estimate=cost(2**32, 2**24),
@@ -480,9 +485,9 @@
             scratch_shapes=[
                 pltpu.VMEM((blocks, own, ROW), jnp.bfloat16),
                 pltpu.VMEM((blocks, own, ROW), jnp.bfloat16),
-                pltpu.SemaphoreType.DMA((2,)),
+                pltpu.SemaphoreType.DMA((own // GROUP,)),
             ]
-            + scratch,
+            + scratch * 2,
             compiler_params=large,
             cost_estimate=cost(2**32, 2**24),
             name="convolve",

time: 61.5 us -> 61.3 us (level)
  no operation moved by 1% of the time
where the time goes in v7:
time: 61.3 us; the launch traced here: 61 us
  starting transfers between devices  27.5 us (45%)
  waiting for transfers between devices  18.5 us (30%)
  Pallas kernels  14.9 us (24%)
    ppermute x10, starting transfers between devices, scatter(): lax.ppermute(block, axis, [(i, i ^ turn) for i in range(count)])  16 us
    ppermute x10, waiting for transfers between devices, scatter(): lax.ppermute(block, axis, [(i, i ^ turn) for i in range(count)])  12.7 us
    all_to_all x1, starting transfers between devices, body(): gated = exchange(gated, ('seq', 'ch'))  7.32 us
    all_to_all x1, waiting for transfers between devices, body(): convolved = exchange(convolved, 'seq')  5.77 us
    pallas_call x1, Pallas kernels, body(): pl.pallas_call(conv_kernel, out_shape=jax.ShapeDtypeStruct((blocks, own,...  5.38 us
    all_to_all x1, starting transfers between devices, body(): convolved = exchange(convolved, 'seq')  4.17 us
    pallas_call x1, Pallas kernels, body(): pl.pallas_call(gated_spectrum_kernel, out_shape=jax.ShapeDtypeStruct((blo...  2.98 us
    pallas_call x1, Pallas kernels, body(): pl.pallas_call(send_kernel, in_specs=[far], out_specs=far, out_shape=jax....  2.97 us
  transfers between devices with their start and end apart: 12, of which 6 were waited for; matrix products, arithmetic and copies ran while one was open for 0% of the time, Pallas kernels for 8%

profile of v7, /device:TPU:0, one launch (start us, length us, event | category | flops | bytes accessed | tf_op | source)
XLA Modules:
  0.0 61.0 jit_solution(17927835866512441139)
XLA Ops:
  0.0 3.0 %encode_gated.1 = bf16[8,4,64,128]{3,2,1,0:T(8,128)(2,1)} custom-call(bf16[3,64,4096]{2,1,0:T(8,128)(2,1)} %bitcast.4), custom_call_target="tpu_custom_call" | custom-call | flops 33554432 | bytes 8388608 | tf_op jit(solution)/shard_map/encode_gated/pallas_call | solution.py:416
  3.0 7.3 %all-to-all-start = ((bf16[32,64,128]{2,1,0:T(8,128)(2,1)}), bf16[32,64,128]{2,1,0:T(8,128)(2,1)S(1)}, u32[]{:S(2)}, u32[]{:S(2)}) async-start(bf16[32,64,128]{2,1,0:T(8,128)(2,1)} %bitcast.8), calls=%async_computation | async-start | bytes 1048576 | tf_op jit(solution)/shard_map/all_to_all | solution.py:460
  10.3 1.4 %encode_taps.1 = (bf16[128,256]{1,0:T(8,128)(2,1)S(1)}, bf16[128,256]{1,0:T(8,128)(2,1)S(1)}, bf16[128,256]{1,0:T(8,128)(2,1)S(1)}, bf16[128,256]{1,0:T(8,128)(2...) custom-call(f32[8,128,256]{2,1,0:T(8,128)S(1)} %bitcast.6, ...), custom_call_target="tpu_custom_call" | custom-call | flops 33554432 | bytes 8388608 | tf_op jit(solution)/shard_map/encode_taps/pallas_call | solution.py:442
  11.7 1.8 %collective-permute-start.3 = (bf16[128,256]{1,0:T(8,128)(2,1)S(1)}, bf16[128,256]{1,0:T(8,128)(2,1)S(1)}, u32[]{:S(2)}, u32[]{:S(2)}) collective-permute-start(bf16[128,256]{1,0:T(8,128)(2,1)S(1)} %get-tuple-element.22), channel_id=1, source_target_pairs={{0,4},{4,0},{8,12},{12,8},{16,20},{20,16},{24,28},{28,24},{1,5},{5... | collective-permute-start | bytes 196616 | tf_op jit(solution)/shard_map/ppermute | solution.py:397
  13.5 1.5 %collective-permute-start.4 = (bf16[128,256]{1,0:T(8,128)(2,1)S(1)}, bf16[128,256]{1,0:T(8,128)(2,1)S(1)}, u32[]{:S(2)}, u32[]{:S(2)}) collective-permute-start(bf16[128,256]{1,0:T(8,128)(2,1)S(1)} %get-tuple-element.23), channel_id=1, source_target_pairs={{0,8},{4,12},{8,0},{12,4},{16,24},{20,28},{24,16},{28,20},{1,9},{5... | collective-permute-start | bytes 196616 | tf_op jit(solution)/shard_map/ppermute | solution.py:397
  15.0 0.3 collective-permute-start.5
  15.3 2.7 %collective-permute-start.6 = (bf16[128,256]{1,0:T(8,128)(2,1)S(1)}, bf16[128,256]{1,0:T(8,128)(2,1)S(1)}, u32[]{:S(2)}, u32[]{:S(2)}) collective-permute-start(bf16[128,256]{1,0:T(8,128)(2,1)S(1)} %get-tuple-element.25), channel_id=1, source_target_pairs={{0,16},{4,20},{8,24},{12,28},{16,0},{20,4},{24,8},{28,12},{1,17},{... | collective-permute-start | bytes 196616 | tf_op jit(solution)/shard_map/ppermute | solution.py:397
  17.9 1.5 %collective-permute-start.7 = (bf16[128,256]{1,0:T(8,128)(2,1)S(1)}, bf16[128,256]{1,0:T(8,128)(2,1)S(1)}, u32[]{:S(2)}, u32[]{:S(2)}) collective-permute-start(bf16[128,256]{1,0:T(8,128)(2,1)S(1)} %get-tuple-element.26), channel_id=1, source_target_pairs={{0,20},{4,16},{8,28},{12,24},{16,4},{20,0},{24,12},{28,8},{1,21},{... | collective-permute-start | bytes 196616 | tf_op jit(solution)/shard_map/ppermute | solution.py:397
  19.4 3.3 %collective-permute-start.8 = (bf16[128,256]{1,0:T(8,128)(2,1)S(1)}, bf16[128,256]{1,0:T(8,128)(2,1)S(1)}, u32[]{:S(2)}, u32[]{:S(2)}) collective-permute-start(bf16[128,256]{1,0:T(8,128)(2,1)S(1)} %get-tuple-element.27), channel_id=1, source_target_pairs={{0,24},{4,28},{8,16},{12,20},{16,8},{20,12},{24,0},{28,4},{1,25},{... | collective-permute-start | bytes 196616 | tf_op jit(solution)/shard_map/ppermute | solution.py:397
  22.8 3.1 %collective-permute-start.9 = (bf16[128,256]{1,0:T(8,128)(2,1)S(1)}, bf16[128,256]{1,0:T(8,128)(2,1)S(1)}, u32[]{:S(2)}, u32[]{:S(2)}) collective-permute-start(bf16[128,256]{1,0:T(8,128)(2,1)S(1)} %get-tuple-element.28), channel_id=1, source_target_pairs={{0,28},{4,24},{8,20},{12,16},{16,12},{20,8},{24,4},{28,0},{1,29},{... | collective-permute-start | bytes 196616 | tf_op jit(solution)/shard_map/ppermute | solution.py:397
  25.9 3.0 %gated_spectrum.1.gated_ref = f32[8,2,128,256]{3,2,1,0:T(8,128)S(1)} custom-call(bf16[32,64,128]{2,1,0:T(8,128)(2,1)S(1)} %all-to-all-done.gated_ref, bf16[768,256]{1,0:T(8,128)(2,1)S(1)} %copy-done.3, f32[8,2,256]{2,1,0:T(2,128)S(1)} %copy-done.5), custom_call_target="tpu_custom_call" | custom-call | flops 4294967296 | bytes 16777216 | tf_op jit(solution)/shard_map/gated_spectrum/pallas_call | solution.py:472
  28.9 3.9 %collective-permute-done.6.refs_4_ = bf16[128,256]{1,0:T(8,128)(2,1)S(1)} collective-permute-done((bf16[128,256]{1,0:T(8,128)(2,1)S(1)}, bf16[128,256]{1,0:T(8,128)(2,1)S(1)}, u32[]{:S(2)}, u32[]{:S(2)}) %collective-permute-start.6) | collective-permute-done | bytes 65568 | tf_op jit(solution)/shard_map/ppermute | solution.py:397
  32.8 2.3 %collective-permute-done.7.refs_5_ = bf16[128,256]{1,0:T(8,128)(2,1)S(1)} collective-permute-done((bf16[128,256]{1,0:T(8,128)(2,1)S(1)}, bf16[128,256]{1,0:T(8,128)(2,1)S(1)}, u32[]{:S(2)}, u32[]{:S(2)}) %collective-permute-start.7) | collective-permute-done | bytes 65568 | tf_op jit(solution)/shard_map/ppermute | solution.py:397
  35.2 5.4 %convolve.1 = bf16[8,128,256]{2,1,0:T(8,128)(2,1)} custom-call(f32[8,2,128,256]{3,2,1,0:T(8,128)S(1)} %gated_spectrum.1.gated_ref, bf16[128,256]{1,0:T(8,128)(2,1)S(1)} %get-tuple-element.21.refs_0_, bf16[128,256]{1,0:T(8,128)(2,1)S(1)} %collective-permute-done.3.refs_1_, bf16[128,256]{1,0:T(8,128)(2,1)S(1)} %collective-permute-done.4.refs_2_, ...), custom_call_target="tpu_custom_call" | custom-call | flops 4294967296 | bytes 16777216 | tf_op jit(solution)/shard_map/convolve/pallas_call | solution.py:480
  40.5 4.2 %all-to-all-start.1 = ((bf16[8,128,256]{2,1,0:T(8,128)(2,1)}), bf16[8,128,256]{2,1,0:T(8,128)(2,1)S(1)}, u32[]{:S(2)}, u32[]{:S(2)}) async-start(bf16[8,128,256]{2,1,0:T(8,128)(2,1)} %convolve.1), calls=%async_computation.1 | async-start | bytes 1048576 | tf_op jit(solution)/shard_map/all_to_all | solution.py:501
  44.7 0.1 send_queries.1
  44.9 0.1 collective-permute-start
  45.0 1.5 %collective-permute-start.1 = (bf16[64,1024]{1,0:T(8,128)(2,1)S(1)}, bf16[64,1024]{1,0:T(8,128)(2,1)S(1)}, u32[]{:S(2)}, u32[]{:S(2)}) collective-permute-start(bf16[64,1024]{1,0:T(8,128)(2,1)S(1)} %get-tuple-element.19), channel_id=1, source_target_pairs={{0,2},{1,3},{2,0},{3,1},{4,6},{5,7},{6,4},{7,5},{8,10},{9,11},{10,... | collective-permute-start | bytes 393224 | tf_op jit(solution)/shard_map/ppermute | solution.py:397
  46.5 0.3 collective-permute-start.2
  46.8 4.5 %collective-permute-done.1.refs_2_ = bf16[64,1024]{1,0:T(8,128)(2,1)S(1)} collective-permute-done((bf16[64,1024]{1,0:T(8,128)(2,1)S(1)}, bf16[64,1024]{1,0:T(8,128)(2,1)S(1)}, u32[]{:S(2)}, u32[]{:S(2)}) %collective-permute-start.1) | collective-permute-done | bytes 131104 | tf_op jit(solution)/shard_map/ppermute | solution.py:397
  51.3 1.9 %collective-permute-done.2.refs_3_ = bf16[64,1024]{1,0:T(8,128)(2,1)S(1)} collective-permute-done((bf16[64,1024]{1,0:T(8,128)(2,1)S(1)}, bf16[64,1024]{1,0:T(8,128)(2,1)S(1)}, u32[]{:S(2)}, u32[]{:S(2)}) %collective-permute-start.2) | collective-permute-done | bytes 131104 | tf_op jit(solution)/shard_map/ppermute | solution.py:397
  53.2 0.3 turn_queries.1.query_ref
  53.5 5.8 %all-to-all-done.1.conv_ref = bf16[8,128,256]{2,1,0:T(8,128)(2,1)S(1)} async-done(((bf16[8,128,256]{2,1,0:T(8,128)(2,1)}), bf16[8,128,256]{2,1,0:T(8,128)(2,1)S(1)}, u32[]{:S(2)}, u32[]{:S(2)}) %all-to-all-start.1) | async-done | bytes 524320 | tf_op jit(solution)/shard_map/all_to_all | solution.py:501
  59.3 1.7 %mix_out.1 = bf16[1024,256]{1,0:T(8,128)(2,1)} custom-call(bf16[1024,256]{1,0:T(8,128)(2,1)S(1)} %turn_queries.1.query_ref, bf16[8,128,256]{2,1,0:T(8,128)(2,1)S(1)} %all-to-all-done.1.conv_ref), custom_call_target="tpu_custom_call" | custom-call | tf_op jit(solution)/shard_map/mix_out/pallas_call | solution.py:511
  (19 shorter events, 0.1 us)
Async XLA Ops:
  0.0 10.3 %copy-start.1 = (f32[1024,256]{1,0:T(8,128)S(1)}, f32[1024,256]{1,0:T(8,128)}, u32[]{:S(2)}) copy-start(f32[1024,256]{1,0:T(8,128)} %param.7) | copy-start | bytes 3145732
  0.0 10.3 %copy-start.2 = (f32[1024]{0:T(1024)S(1)}, f32[1024]{0:T(1024)}, u32[]{:S(2)}) copy-start(f32[1024]{0:T(1024)} %param.8) | copy-start | bytes 12292
  0.0 25.9 %copy-start.3 = (bf16[768,256]{1,0:T(8,128)(2,1)S(1)}, bf16[768,256]{1,0:T(8,128)(2,1)}, u32[]{:S(2)}) copy-start(bf16[768,256]{1,0:T(8,128)(2,1)} %constant.6.clone.wave_ref.refs_8_) | copy-start | bytes 1179652
  0.0 25.9 %copy-start.5 = (f32[8,2,256]{2,1,0:T(2,128)S(1)}, f32[8,2,256]{2,1,0:T(2,128)}, u32[]{:S(2)}) copy-start(f32[8,2,256]{2,1,0:T(2,128)} %constant.7.clone.twist_ref.refs_10_) | copy-start | bytes 49156
  3.0 22.9 %all-to-all-start = ((bf16[32,64,128]{2,1,0:T(8,128)(2,1)}), bf16[32,64,128]{2,1,0:T(8,128)(2,1)S(1)}, u32[]{:S(2)}, u32[]{:S(2)}) async-start(bf16[32,64,128]{2,1,0:T(8,128)(2,1)} %bitcast.8), calls=%async_computation | async-start | bytes 1048576 | tf_op jit(solution)/shard_map/all_to_all | solution.py:460
  11.7 7.7 %collective-permute-start.3 = (bf16[128,256]{1,0:T(8,128)(2,1)S(1)}, bf16[128,256]{1,0:T(8,128)(2,1)S(1)}, u32[]{:S(2)}, u32[]{:S(2)}) collective-permute-start(bf16[128,256]{1,0:T(8,128)(2,1)S(1)} %get-tuple-element.22), channel_id=1, source_target_pairs={{0,4},{4,0},{8,12},{12,8},{16,20},{20,16},{24,28},{28,24},{1,5},{5... | collective-permute-start | bytes 196616 | tf_op jit(solution)/shard_map/ppermute | solution.py:397
  13.5 9.2 %collective-permute-start.4 = (bf16[128,256]{1,0:T(8,128)(2,1)S(1)}, bf16[128,256]{1,0:T(8,128)(2,1)S(1)}, u32[]{:S(2)}, u32[]{:S(2)}) collective-permute-start(bf16[128,256]{1,0:T(8,128)(2,1)S(1)} %get-tuple-element.23), channel_id=1, source_target_pairs={{0,8},{4,12},{8,0},{12,4},{16,24},{20,28},{24,16},{28,20},{1,9},{5... | collective-permute-start | bytes 196616 | tf_op jit(solution)/shard_map/ppermute | solution.py:397
  15.0 13.8 %collective-permute-start.5 = (bf16[128,256]{1,0:T(8,128)(2,1)S(1)}, bf16[128,256]{1,0:T(8,128)(2,1)S(1)}, u32[]{:S(2)}, u32[]{:S(2)}) collective-permute-start(bf16[128,256]{1,0:T(8,128)(2,1)S(1)} %get-tuple-element.24), channel_id=1, source_target_pairs={{0,12},{4,8},{8,4},{12,0},{16,28},{20,24},{24,20},{28,16},{1,13},{... | collective-permute-start | bytes 196616 | tf_op jit(solution)/shard_map/ppermute | solution.py:397
  15.3 17.5 %collective-permute-start.6 = (bf16[128,256]{1,0:T(8,128)(2,1)S(1)}, bf16[128,256]{1,0:T(8,128)(2,1)S(1)}, u32[]{:S(2)}, u32[]{:S(2)}) collective-permute-start(bf16[128,256]{1,0:T(8,128)(2,1)S(1)} %get-tuple-element.25), channel_id=1, source_target_pairs={{0,16},{4,20},{8,24},{12,28},{16,0},{20,4},{24,8},{28,12},{1,17},{... | collective-permute-start | bytes 196616 | tf_op jit(solution)/shard_map/ppermute | solution.py:397
  17.9 17.2 %collective-permute-start.7 = (bf16[128,256]{1,0:T(8,128)(2,1)S(1)}, bf16[128,256]{1,0:T(8,128)(2,1)S(1)}, u32[]{:S(2)}, u32[]{:S(2)}) collective-permute-start(bf16[128,256]{1,0:T(8,128)(2,1)S(1)} %get-tuple-element.26), channel_id=1, source_target_pairs={{0,20},{4,16},{8,28},{12,24},{16,4},{20,0},{24,12},{28,8},{1,21},{... | collective-permute-start | bytes 196616 | tf_op jit(solution)/shard_map/ppermute | solution.py:397
  19.4 15.7 %collective-permute-start.8 = (bf16[128,256]{1,0:T(8,128)(2,1)S(1)}, bf16[128,256]{1,0:T(8,128)(2,1)S(1)}, u32[]{:S(2)}, u32[]{:S(2)}) collective-permute-start(bf16[128,256]{1,0:T(8,128)(2,1)S(1)} %get-tuple-element.27), channel_id=1, source_target_pairs={{0,24},{4,28},{8,16},{12,20},{16,8},{20,12},{24,0},{28,4},{1,25},{... | collective-permute-start | bytes 196616 | tf_op jit(solution)/shard_map/ppermute | solution.py:397
  22.8 12.4 %copy-start.4 = (bf16[768,256]{1,0:T(8,128)(2,1)S(1)}, bf16[768,256]{1,0:T(8,128)(2,1)}, u32[]{:S(2)}) copy-start(bf16[768,256]{1,0:T(8,128)(2,1)} %constant.8.clone.refs_9_) | copy-start | bytes 1179652
  22.8 12.4 %collective-permute-start.9 = (bf16[128,256]{1,0:T(8,128)(2,1)S(1)}, bf16[128,256]{1,0:T(8,128)(2,1)S(1)}, u32[]{:S(2)}, u32[]{:S(2)}) collective-permute-start(bf16[128,256]{1,0:T(8,128)(2,1)S(1)} %get-tuple-element.28), channel_id=1, source_target_pairs={{0,28},{4,24},{8,20},{12,16},{16,12},{20,8},{24,4},{28,0},{1,29},{... | collective-permute-start | bytes 196616 | tf_op jit(solution)/shard_map/ppermute | solution.py:397
  35.1 9.6 %copy-start = (bf16[64,3,4096]{2,0,1:T(8,128)(2,1)S(1)}, bf16[64,3,4096]{2,0,1:T(8,128)(2,1)}, u32[]{:S(2)}) copy-start(bf16[64,3,4096]{2,0,1:T(8,128)(2,1)} %param.6) | copy-start | bytes 4718596
  40.5 18.7 %all-to-all-start.1 = ((bf16[8,128,256]{2,1,0:T(8,128)(2,1)}), bf16[8,128,256]{2,1,0:T(8,128)(2,1)S(1)}, u32[]{:S(2)}, u32[]{:S(2)}) async-start(bf16[8,128,256]{2,1,0:T(8,128)(2,1)} %convolve.1), calls=%async_computation.1 | async-start | bytes 1048576 | tf_op jit(solution)/shard_map/all_to_all | solution.py:501
  44.9 1.9 %collective-permute-start = (bf16[64,1024]{1,0:T(8,128)(2,1)S(1)}, bf16[64,1024]{1,0:T(8,128)(2,1)S(1)}, u32[]{:S(2)}, u32[]{:S(2)}) collective-permute-start(bf16[64,1024]{1,0:T(8,128)(2,1)S(1)} %get-tuple-element.18), channel_id=1, source_target_pairs={{0,1},{1,0},{2,3},{3,2},{4,5},{5,4},{6,7},{7,6},{8,9},{9,8},{10,11... | collective-permute-start | bytes 393224 | tf_op jit(solution)/shard_map/ppermute | solution.py:397
  45.0 6.4 %collective-permute-start.1 = (bf16[64,1024]{1,0:T(8,128)(2,1)S(1)}, bf16[64,1024]{1,0:T(8,128)(2,1)S(1)}, u32[]{:S(2)}, u32[]{:S(2)}) collective-permute-start(bf16[64,1024]{1,0:T(8,128)(2,1)S(1)} %get-tuple-element.19), channel_id=1, source_target_pairs={{0,2},{1,3},{2,0},{3,1},{4,6},{5,7},{6,4},{7,5},{8,10},{9,11},{10,... | collective-permute-start | bytes 393224 | tf_op jit(solution)/shard_map/ppermute | solution.py:397
  46.5 6.7 %collective-permute-start.2 = (bf16[64,1024]{1,0:T(8,128)(2,1)S(1)}, bf16[64,1024]{1,0:T(8,128)(2,1)S(1)}, u32[]{:S(2)}, u32[]{:S(2)}) collective-permute-start(bf16[64,1024]{1,0:T(8,128)(2,1)S(1)} %get-tuple-element.20), channel_id=1, source_target_pairs={{0,3},{1,2},{2,1},{3,0},{4,7},{5,6},{6,5},{7,4},{8,11},{9,10},{10,... | collective-permute-start | bytes 393224 | tf_op jit(solution)/shard_map/ppermute | solution.py:397

commit v8 on v7

--- a/solution.py
+++ b/solution.py
@@ -9,7 +9,7 @@
 from jax.experimental.pallas import tpu as pltpu
 from jax.sharding import PartitionSpec as P
 
-OCTAVES = 250.0
+GRID = 36.0
 LOW_POWER = 125.0
 EXPONENT_BITS = 8
 EXPONENT_BIAS = 127.0
@@ -48,45 +48,49 @@
 
 def encode_all(blocks, power, axis):
     unit_share, codes, bits = jnp.exp2(-power), [], None
+    top = 2.0 * LOW_POWER
     for values in blocks:
         share = jnp.abs(values) * unit_share
-        level = jnp.minimum(
-            share * (2.0 * OCTAVES),
-            jnp.minimum(share * OCTAVES + OCTAVES / 4, share * (OCTAVES / 2) + OCTAVES / 2),
+        place = jnp.minimum(
+            jnp.minimum(share * (2.0 * top) - LOW_POWER, share * top - LOW_POWER / 2),
+            jnp.minimum(share * LOW_POWER, LOW_POWER + 1.0),
         )
-        level = jnp.minimum(level, OCTAVES + 1.0)
-        first, rest = split_first(level, axis)
+        first, rest = split_first(place, axis)
         bits = exponent_bits(power, first.shape, axis) if bits is None else bits
         odd, holds = bits
-        marked = (jnp.floor(first * 64.0 - odd + 0.5) + odd) * (1.0 / 64.0)
-        level = jnp.where(holds, marked, first)
+        if axis == values.ndim - 1:
+            marked = (jnp.floor(first * GRID - odd + 0.5) + odd) * (1.0 / GRID)
+            first = jnp.exp2(jnp.where(holds, marked, first))
+        else:
+            marked = (jnp.floor(first * 64.0 - odd + 0.5) + odd) * (1.0 / 64.0)
+            octave = jnp.floor(marked)
+            first = jnp.exp2(octave) * (marked - octave + 1.0)
+        size = first
         if rest is not None:
-            level = jnp.concatenate([level, rest], axis=axis)
-        octave = jnp.floor(level)
-        unit = jnp.exp2(octave - LOW_POWER)
-        code = jnp.where(values < 0.0, -unit, unit) * (level - octave + 1.0)
-        codes.append(code.astype(jnp.bfloat16))
+            size = jnp.concatenate([first, jnp.exp2(rest)], axis=axis)
+        codes.append(jnp.where(values < 0.0, -size, size).astype(jnp.bfloat16))
     return codes
 
 
 def decode(code, axis, halvings=0):
     code = code.astype(jnp.float32)
     size = jnp.abs(code)
-    octave = jnp.floor(jnp.log(size) * (1.0 / math.log(2.0)) + 0.002)
-    level = octave + size * jnp.exp2(-octave)
-    first, _ = split_first(level, axis)
-    half = first * 64.0 + ((LOW_POWER - 1.0) * 64.0 + 0.25)
-    place = lax.broadcasted_iota(jnp.int32, first.shape, axis).astype(jnp.float32)
-    weight = jnp.where(place < EXPONENT_BITS, jnp.exp2(place), 0.0)
+    place = jnp.log(size) * (1.0 / math.log(2.0))
+    first, rest = split_first(place, axis)
+    if axis == code.ndim - 1:
+        half = first * GRID + 0.25
+    else:
+        octave = jnp.floor(first + 0.002)
+        first = octave + split_first(size, axis)[0] * jnp.exp2(-octave) - 1.0
+        half = first * 64.0 + 0.25
+        place = first if rest is None else jnp.concatenate([first, rest], axis=axis)
+    spot = lax.broadcasted_iota(jnp.int32, first.shape, axis).astype(jnp.float32)
+    weight = jnp.where(spot < EXPONENT_BITS, jnp.exp2(spot), 0.0)
     held = jnp.where(half - jnp.floor(half) >= 0.5, weight, 0.0)
     scale = jnp.exp2(jnp.sum(held, axis=axis, keepdims=True) - (EXPONENT_BIAS + halvings))
-    step = 0.5 / OCTAVES
-    low = (LOW_POWER - 1.0) * step
+    step = 0.25 / LOW_POWER
     share = jnp.maximum(
-        level * step + low,
-        jnp.maximum(
-            level * (2.0 * step) + (2.0 * low - 0.25), level * (4.0 * step) + (4.0 * low - 1.0)
-        ),
+        place * (4.0 * step), jnp.maximum(place * (2.0 * step) + 0.25, place * step + 0.25)
     )
     return jnp.where(code < 0.0, -scale, scale) * share
 

time: 61.3 us -> 60.5 us (0.987)
  Pallas kernels: 14.9 us -> 13.7 us
  transfers between devices with their start and end apart: 12 -> 12, of which waited for: 6 -> 6; matrix products, arithmetic and copies ran while one was open for 0% -> 0% of each run, Pallas kernels for 8% -> 7%
where the time goes in v8:
time: 60.5 us; the launch traced here: 60.2 us
  starting transfers between devices  27.7 us (46%)
  waiting for transfers between devices  18.7 us (31%)
  Pallas kernels  13.7 us (23%)
    ppermute x10, starting transfers between devices, scatter(): lax.ppermute(block, axis, [(i, i ^ turn) for i in range(count)])  16.2 us
    ppermute x10, waiting for transfers between devices, scatter(): lax.ppermute(block, axis, [(i, i ^ turn) for i in range(count)])  12.9 us
    all_to_all x1, starting transfers between devices, body(): gated = exchange(gated, ('seq', 'ch'))  7.32 us
    all_to_all x1, waiting for transfers between devices, body(): convolved = exchange(convolved, 'seq')  5.77 us
    pallas_call x1, Pallas kernels, body(): pl.pallas_call(conv_kernel, out_shape=jax.ShapeDtypeStruct((blocks, own,...  4.92 us
    all_to_all x1, starting transfers between devices, body(): convolved = exchange(convolved, 'seq')  4.16 us
    pallas_call x1, Pallas kernels, body(): pl.pallas_call(send_kernel, in_specs=[far], out_specs=far, out_shape=jax....  2.84 us
    pallas_call x1, Pallas kernels, body(): pl.pallas_call(gated_spectrum_kernel, out_shape=jax.ShapeDtypeStruct((blo...  2.79 us
  transfers between devices with their start and end apart: 12, of which 6 were waited for; matrix products, arithmetic and copies ran while one was open for 0% of the time, Pallas kernels for 7%

profile of v8, /device:TPU:0, one launch (start us, length us, event | category | flops | bytes accessed | tf_op | source)
XLA Modules:
  0.0 60.2 jit_solution(9935920701647981930)
XLA Ops:
  0.0 2.8 %encode_gated.1 = bf16[8,4,64,128]{3,2,1,0:T(8,128)(2,1)} custom-call(bf16[3,64,4096]{2,1,0:T(8,128)(2,1)} %bitcast.4), custom_call_target="tpu_custom_call" | custom-call | flops 33554432 | bytes 8388608 | tf_op jit(solution)/shard_map/encode_gated/pallas_call | solution.py:420
  2.9 7.3 %all-to-all-start = ((bf16[32,64,128]{2,1,0:T(8,128)(2,1)}), bf16[32,64,128]{2,1,0:T(8,128)(2,1)S(1)}, u32[]{:S(2)}, u32[]{:S(2)}) async-start(bf16[32,64,128]{2,1,0:T(8,128)(2,1)} %bitcast.8), calls=%async_computation | async-start | bytes 1048576 | tf_op jit(solution)/shard_map/all_to_all | solution.py:464
  10.2 1.2 %encode_taps.1 = (bf16[128,256]{1,0:T(8,128)(2,1)S(1)}, bf16[128,256]{1,0:T(8,128)(2,1)S(1)}, bf16[128,256]{1,0:T(8,128)(2,1)S(1)}, bf16[128,256]{1,0:T(8,128)(2...) custom-call(f32[8,128,256]{2,1,0:T(8,128)S(1)} %bitcast.6, ...), custom_call_target="tpu_custom_call" | custom-call | flops 33554432 | bytes 8388608 | tf_op jit(solution)/shard_map/encode_taps/pallas_call | solution.py:446
  11.4 1.8 %collective-permute-start.3 = (bf16[128,256]{1,0:T(8,128)(2,1)S(1)}, bf16[128,256]{1,0:T(8,128)(2,1)S(1)}, u32[]{:S(2)}, u32[]{:S(2)}) collective-permute-start(bf16[128,256]{1,0:T(8,128)(2,1)S(1)} %get-tuple-element.22), channel_id=1, source_target_pairs={{0,4},{4,0},{8,12},{12,8},{16,20},{20,16},{24,28},{28,24},{1,5},{5... | collective-permute-start | bytes 196616 | tf_op jit(solution)/shard_map/ppermute | solution.py:401
  13.3 1.5 %collective-permute-start.4 = (bf16[128,256]{1,0:T(8,128)(2,1)S(1)}, bf16[128,256]{1,0:T(8,128)(2,1)S(1)}, u32[]{:S(2)}, u32[]{:S(2)}) collective-permute-start(bf16[128,256]{1,0:T(8,128)(2,1)S(1)} %get-tuple-element.23), channel_id=1, source_target_pairs={{0,8},{4,12},{8,0},{12,4},{16,24},{20,28},{24,16},{28,20},{1,9},{5... | collective-permute-start | bytes 196616 | tf_op jit(solution)/shard_map/ppermute | solution.py:401
  14.7 0.3 collective-permute-start.5
  15.0 2.7 %collective-permute-start.6 = (bf16[128,256]{1,0:T(8,128)(2,1)S(1)}, bf16[128,256]{1,0:T(8,128)(2,1)S(1)}, u32[]{:S(2)}, u32[]{:S(2)}) collective-permute-start(bf16[128,256]{1,0:T(8,128)(2,1)S(1)} %get-tuple-element.25), channel_id=1, source_target_pairs={{0,16},{4,20},{8,24},{12,28},{16,0},{20,4},{24,8},{28,12},{1,17},{... | collective-permute-start | bytes 196616 | tf_op jit(solution)/shard_map/ppermute | solution.py:401
  17.6 1.5 %collective-permute-start.7 = (bf16[128,256]{1,0:T(8,128)(2,1)S(1)}, bf16[128,256]{1,0:T(8,128)(2,1)S(1)}, u32[]{:S(2)}, u32[]{:S(2)}) collective-permute-start(bf16[128,256]{1,0:T(8,128)(2,1)S(1)} %get-tuple-element.26), channel_id=1, source_target_pairs={{0,20},{4,16},{8,28},{12,24},{16,4},{20,0},{24,12},{28,8},{1,21},{... | collective-permute-start | bytes 196616 | tf_op jit(solution)/shard_map/ppermute | solution.py:401
  19.1 3.3 %collective-permute-start.8 = (bf16[128,256]{1,0:T(8,128)(2,1)S(1)}, bf16[128,256]{1,0:T(8,128)(2,1)S(1)}, u32[]{:S(2)}, u32[]{:S(2)}) collective-permute-start(bf16[128,256]{1,0:T(8,128)(2,1)S(1)} %get-tuple-element.27), channel_id=1, source_target_pairs={{0,24},{4,28},{8,16},{12,20},{16,8},{20,12},{24,0},{28,4},{1,25},{... | collective-permute-start | bytes 196616 | tf_op jit(solution)/shard_map/ppermute | solution.py:401
  22.5 3.2 %collective-permute-start.9 = (bf16[128,256]{1,0:T(8,128)(2,1)S(1)}, bf16[128,256]{1,0:T(8,128)(2,1)S(1)}, u32[]{:S(2)}, u32[]{:S(2)}) collective-permute-start(bf16[128,256]{1,0:T(8,128)(2,1)S(1)} %get-tuple-element.28), channel_id=1, source_target_pairs={{0,28},{4,24},{8,20},{12,16},{16,12},{20,8},{24,4},{28,0},{1,29},{... | collective-permute-start | bytes 196616 | tf_op jit(solution)/shard_map/ppermute | solution.py:401
  25.7 2.8 %gated_spectrum.1.gated_ref = f32[8,2,128,256]{3,2,1,0:T(8,128)S(1)} custom-call(bf16[32,64,128]{2,1,0:T(8,128)(2,1)S(1)} %all-to-all-done.gated_ref, bf16[768,256]{1,0:T(8,128)(2,1)S(1)} %copy-done.3, f32[8,2,256]{2,1,0:T(2,128)S(1)} %copy-done.5), custom_call_target="tpu_custom_call" | custom-call | flops 4294967296 | bytes 16777216 | tf_op jit(solution)/shard_map/gated_spectrum/pallas_call | solution.py:476
  28.5 4.1 %collective-permute-done.6.refs_4_ = bf16[128,256]{1,0:T(8,128)(2,1)S(1)} collective-permute-done((bf16[128,256]{1,0:T(8,128)(2,1)S(1)}, bf16[128,256]{1,0:T(8,128)(2,1)S(1)}, u32[]{:S(2)}, u32[]{:S(2)}) %collective-permute-start.6) | collective-permute-done | bytes 65568 | tf_op jit(solution)/shard_map/ppermute | solution.py:401
  32.7 2.3 %collective-permute-done.7.refs_5_ = bf16[128,256]{1,0:T(8,128)(2,1)S(1)} collective-permute-done((bf16[128,256]{1,0:T(8,128)(2,1)S(1)}, bf16[128,256]{1,0:T(8,128)(2,1)S(1)}, u32[]{:S(2)}, u32[]{:S(2)}) %collective-permute-start.7) | collective-permute-done | bytes 65568 | tf_op jit(solution)/shard_map/ppermute | solution.py:401
  35.0 4.9 %convolve.1 = bf16[8,128,256]{2,1,0:T(8,128)(2,1)} custom-call(f32[8,2,128,256]{3,2,1,0:T(8,128)S(1)} %gated_spectrum.1.gated_ref, bf16[128,256]{1,0:T(8,128)(2,1)S(1)} %get-tuple-element.21.refs_0_, bf16[128,256]{1,0:T(8,128)(2,1)S(1)} %collective-permute-done.3.refs_1_, bf16[128,256]{1,0:T(8,128)(2,1)S(1)} %collective-permute-done.4.refs_2_, ...), custom_call_target="tpu_custom_call" | custom-call | flops 4294967296 | bytes 16777216 | tf_op jit(solution)/shard_map/convolve/pallas_call | solution.py:484
  39.9 4.2 %all-to-all-start.1 = ((bf16[8,128,256]{2,1,0:T(8,128)(2,1)}), bf16[8,128,256]{2,1,0:T(8,128)(2,1)S(1)}, u32[]{:S(2)}, u32[]{:S(2)}) async-start(bf16[8,128,256]{2,1,0:T(8,128)(2,1)} %convolve.1), calls=%async_computation.1 | async-start | bytes 1048576 | tf_op jit(solution)/shard_map/all_to_all | solution.py:505
  44.1 0.1 send_queries.1
  44.3 0.1 collective-permute-start
  44.4 1.5 %collective-permute-start.1 = (bf16[64,1024]{1,0:T(8,128)(2,1)S(1)}, bf16[64,1024]{1,0:T(8,128)(2,1)S(1)}, u32[]{:S(2)}, u32[]{:S(2)}) collective-permute-start(bf16[64,1024]{1,0:T(8,128)(2,1)S(1)} %get-tuple-element.19), channel_id=1, source_target_pairs={{0,2},{1,3},{2,0},{3,1},{4,6},{5,7},{6,4},{7,5},{8,10},{9,11},{10,... | collective-permute-start | bytes 393224 | tf_op jit(solution)/shard_map/ppermute | solution.py:401
  45.9 0.3 collective-permute-start.2
  46.2 4.5 %collective-permute-done.1.refs_2_ = bf16[64,1024]{1,0:T(8,128)(2,1)S(1)} collective-permute-done((bf16[64,1024]{1,0:T(8,128)(2,1)S(1)}, bf16[64,1024]{1,0:T(8,128)(2,1)S(1)}, u32[]{:S(2)}, u32[]{:S(2)}) %collective-permute-start.1) | collective-permute-done | bytes 131104 | tf_op jit(solution)/shard_map/ppermute | solution.py:401
  50.7 1.9 %collective-permute-done.2.refs_3_ = bf16[64,1024]{1,0:T(8,128)(2,1)S(1)} collective-permute-done((bf16[64,1024]{1,0:T(8,128)(2,1)S(1)}, bf16[64,1024]{1,0:T(8,128)(2,1)S(1)}, u32[]{:S(2)}, u32[]{:S(2)}) %collective-permute-start.2) | collective-permute-done | bytes 131104 | tf_op jit(solution)/shard_map/ppermute | solution.py:401
  52.6 0.3 turn_queries.1.query_ref
  52.9 5.8 %all-to-all-done.1.conv_ref = bf16[8,128,256]{2,1,0:T(8,128)(2,1)S(1)} async-done(((bf16[8,128,256]{2,1,0:T(8,128)(2,1)}), bf16[8,128,256]{2,1,0:T(8,128)(2,1)S(1)}, u32[]{:S(2)}, u32[]{:S(2)}) %all-to-all-start.1) | async-done | bytes 524320 | tf_op jit(solution)/shard_map/all_to_all | solution.py:505
  58.7 1.5 %mix_out.1 = bf16[1024,256]{1,0:T(8,128)(2,1)} custom-call(bf16[1024,256]{1,0:T(8,128)(2,1)S(1)} %turn_queries.1.query_ref, bf16[8,128,256]{2,1,0:T(8,128)(2,1)S(1)} %all-to-all-done.1.conv_ref), custom_call_target="tpu_custom_call" | custom-call | tf_op jit(solution)/shard_map/mix_out/pallas_call | solution.py:515
  (19 shorter events, 0.1 us)
Async XLA Ops:
  0.0 10.2 %copy-start.1 = (f32[1024,256]{1,0:T(8,128)S(1)}, f32[1024,256]{1,0:T(8,128)}, u32[]{:S(2)}) copy-start(f32[1024,256]{1,0:T(8,128)} %param.7) | copy-start | bytes 3145732
  0.0 10.2 %copy-start.2 = (f32[1024]{0:T(1024)S(1)}, f32[1024]{0:T(1024)}, u32[]{:S(2)}) copy-start(f32[1024]{0:T(1024)} %param.8) | copy-start | bytes 12292
  0.0 25.7 %copy-start.3 = (bf16[768,256]{1,0:T(8,128)(2,1)S(1)}, bf16[768,256]{1,0:T(8,128)(2,1)}, u32[]{:S(2)}) copy-start(bf16[768,256]{1,0:T(8,128)(2,1)} %constant.6.clone.wave_ref.refs_8_) | copy-start | bytes 1179652
  0.0 25.7 %copy-start.5 = (f32[8,2,256]{2,1,0:T(2,128)S(1)}, f32[8,2,256]{2,1,0:T(2,128)}, u32[]{:S(2)}) copy-start(f32[8,2,256]{2,1,0:T(2,128)} %constant.7.clone.twist_ref.refs_10_) | copy-start | bytes 49156
  2.9 22.9 %all-to-all-start = ((bf16[32,64,128]{2,1,0:T(8,128)(2,1)}), bf16[32,64,128]{2,1,0:T(8,128)(2,1)S(1)}, u32[]{:S(2)}, u32[]{:S(2)}) async-start(bf16[32,64,128]{2,1,0:T(8,128)(2,1)} %bitcast.8), calls=%async_computation | async-start | bytes 1048576 | tf_op jit(solution)/shard_map/all_to_all | solution.py:464
  11.4 7.7 %collective-permute-start.3 = (bf16[128,256]{1,0:T(8,128)(2,1)S(1)}, bf16[128,256]{1,0:T(8,128)(2,1)S(1)}, u32[]{:S(2)}, u32[]{:S(2)}) collective-permute-start(bf16[128,256]{1,0:T(8,128)(2,1)S(1)} %get-tuple-element.22), channel_id=1, source_target_pairs={{0,4},{4,0},{8,12},{12,8},{16,20},{20,16},{24,28},{28,24},{1,5},{5... | collective-permute-start | bytes 196616 | tf_op jit(solution)/shard_map/ppermute | solution.py:401
  13.3 9.2 %collective-permute-start.4 = (bf16[128,256]{1,0:T(8,128)(2,1)S(1)}, bf16[128,256]{1,0:T(8,128)(2,1)S(1)}, u32[]{:S(2)}, u32[]{:S(2)}) collective-permute-start(bf16[128,256]{1,0:T(8,128)(2,1)S(1)} %get-tuple-element.23), channel_id=1, source_target_pairs={{0,8},{4,12},{8,0},{12,4},{16,24},{20,28},{24,16},{28,20},{1,9},{5... | collective-permute-start | bytes 196616 | tf_op jit(solution)/shard_map/ppermute | solution.py:401
  14.7 13.8 %collective-permute-start.5 = (bf16[128,256]{1,0:T(8,128)(2,1)S(1)}, bf16[128,256]{1,0:T(8,128)(2,1)S(1)}, u32[]{:S(2)}, u32[]{:S(2)}) collective-permute-start(bf16[128,256]{1,0:T(8,128)(2,1)S(1)} %get-tuple-element.24), channel_id=1, source_target_pairs={{0,12},{4,8},{8,4},{12,0},{16,28},{20,24},{24,20},{28,16},{1,13},{... | collective-permute-start | bytes 196616 | tf_op jit(solution)/shard_map/ppermute | solution.py:401
  15.0 17.7 %collective-permute-start.6 = (bf16[128,256]{1,0:T(8,128)(2,1)S(1)}, bf16[128,256]{1,0:T(8,128)(2,1)S(1)}, u32[]{:S(2)}, u32[]{:S(2)}) collective-permute-start(bf16[128,256]{1,0:T(8,128)(2,1)S(1)} %get-tuple-element.25), channel_id=1, source_target_pairs={{0,16},{4,20},{8,24},{12,28},{16,0},{20,4},{24,8},{28,12},{1,17},{... | collective-permute-start | bytes 196616 | tf_op jit(solution)/shard_map/ppermute | solution.py:401
  17.6 17.4 %collective-permute-start.7 = (bf16[128,256]{1,0:T(8,128)(2,1)S(1)}, bf16[128,256]{1,0:T(8,128)(2,1)S(1)}, u32[]{:S(2)}, u32[]{:S(2)}) collective-permute-start(bf16[128,256]{1,0:T(8,128)(2,1)S(1)} %get-tuple-element.26), channel_id=1, source_target_pairs={{0,20},{4,16},{8,28},{12,24},{16,4},{20,0},{24,12},{28,8},{1,21},{... | collective-permute-start | bytes 196616 | tf_op jit(solution)/shard_map/ppermute | solution.py:401
  19.1 15.9 %collective-permute-start.8 = (bf16[128,256]{1,0:T(8,128)(2,1)S(1)}, bf16[128,256]{1,0:T(8,128)(2,1)S(1)}, u32[]{:S(2)}, u32[]{:S(2)}) collective-permute-start(bf16[128,256]{1,0:T(8,128)(2,1)S(1)} %get-tuple-element.27), channel_id=1, source_target_pairs={{0,24},{4,28},{8,16},{12,20},{16,8},{20,12},{24,0},{28,4},{1,25},{... | collective-permute-start | bytes 196616 | tf_op jit(solution)/shard_map/ppermute | solution.py:401
  22.5 12.5 %copy-start.4 = (bf16[768,256]{1,0:T(8,128)(2,1)S(1)}, bf16[768,256]{1,0:T(8,128)(2,1)}, u32[]{:S(2)}) copy-start(bf16[768,256]{1,0:T(8,128)(2,1)} %constant.8.clone.refs_9_) | copy-start | bytes 1179652
  22.5 12.5 %collective-permute-start.9 = (bf16[128,256]{1,0:T(8,128)(2,1)S(1)}, bf16[128,256]{1,0:T(8,128)(2,1)S(1)}, u32[]{:S(2)}, u32[]{:S(2)}) collective-permute-start(bf16[128,256]{1,0:T(8,128)(2,1)S(1)} %get-tuple-element.28), channel_id=1, source_target_pairs={{0,28},{4,24},{8,20},{12,16},{16,12},{20,8},{24,4},{28,0},{1,29},{... | collective-permute-start | bytes 196616 | tf_op jit(solution)/shard_map/ppermute | solution.py:401
  35.0 9.1 %copy-start = (bf16[64,3,4096]{2,0,1:T(8,128)(2,1)S(1)}, bf16[64,3,4096]{2,0,1:T(8,128)(2,1)}, u32[]{:S(2)}) copy-start(bf16[64,3,4096]{2,0,1:T(8,128)(2,1)} %param.6) | copy-start | bytes 4718596
  39.9 18.7 %all-to-all-start.1 = ((bf16[8,128,256]{2,1,0:T(8,128)(2,1)}), bf16[8,128,256]{2,1,0:T(8,128)(2,1)S(1)}, u32[]{:S(2)}, u32[]{:S(2)}) async-start(bf16[8,128,256]{2,1,0:T(8,128)(2,1)} %convolve.1), calls=%async_computation.1 | async-start | bytes 1048576 | tf_op jit(solution)/shard_map/all_to_all | solution.py:505
  44.3 1.9 %collective-permute-start = (bf16[64,1024]{1,0:T(8,128)(2,1)S(1)}, bf16[64,1024]{1,0:T(8,128)(2,1)S(1)}, u32[]{:S(2)}, u32[]{:S(2)}) collective-permute-start(bf16[64,1024]{1,0:T(8,128)(2,1)S(1)} %get-tuple-element.18), channel_id=1, source_target_pairs={{0,1},{1,0},{2,3},{3,2},{4,5},{5,4},{6,7},{7,6},{8,9},{9,8},{10,11... | collective-permute-start | bytes 393224 | tf_op jit(solution)/shard_map/ppermute | solution.py:401
  44.4 6.4 %collective-permute-start.1 = (bf16[64,1024]{1,0:T(8,128)(2,1)S(1)}, bf16[64,1024]{1,0:T(8,128)(2,1)S(1)}, u32[]{:S(2)}, u32[]{:S(2)}) collective-permute-start(bf16[64,1024]{1,0:T(8,128)(2,1)S(1)} %get-tuple-element.19), channel_id=1, source_target_pairs={{0,2},{1,3},{2,0},{3,1},{4,6},{5,7},{6,4},{7,5},{8,10},{9,11},{10,... | collective-permute-start | bytes 393224 | tf_op jit(solution)/shard_map/ppermute | solution.py:401
  45.9 6.7 %collective-permute-start.2 = (bf16[64,1024]{1,0:T(8,128)(2,1)S(1)}, bf16[64,1024]{1,0:T(8,128)(2,1)S(1)}, u32[]{:S(2)}, u32[]{:S(2)}) collective-permute-start(bf16[64,1024]{1,0:T(8,128)(2,1)S(1)} %get-tuple-element.20), channel_id=1, source_target_pairs={{0,3},{1,2},{2,1},{3,0},{4,7},{5,6},{6,5},{7,4},{8,11},{9,10},{10,... | collective-permute-start | bytes 393224 | tf_op jit(solution)/shard_map/ppermute | solution.py:401

commit v9 on v8

--- a/solution.py
+++ b/solution.py
@@ -16,7 +16,7 @@
 LANES = 128
 ROW = 256
 CHUNK = 16
-GROUP = 32
+GROUP = 16
 VMEM_BYTES = 20 * 1024 * 1024
 SMALL_BYTES = 12 * 1024 * 1024
 ALL_BYTES = 60 * 1024 * 1024
@@ -126,12 +126,10 @@
     ).astype(jnp.bfloat16)
 
 
-def turned(value, steps):
-    if steps == 0:
-        return value
+def eighth(value, sign):
     re, im = value
-    cos, sin = math.cos(math.pi * steps / 16), math.sin(math.pi * steps / 16)
-    return re * cos - im * sin, im * cos + re * sin
+    side = math.sqrt(0.5)
+    return (re - sign * im) * side, (im + sign * re) * side
 
 
 def four_points(values, sign):
@@ -151,16 +149,28 @@
     return (2 * k + part) * GROUP + at
 
 
+def eight_points(values, sign):
+    sums = [(a_re + b_re, a_im + b_im) for (a_re, a_im), (b_re, b_im) in zip(values, values[4:])]
+    gaps = [(a_re - b_re, a_im - b_im) for (a_re, a_im), (b_re, b_im) in zip(values, values[4:])]
+    (two_re, two_im), three = gaps[2], eighth(gaps[3], sign)
+    turned = [gaps[0], eighth(gaps[1], sign), (-sign * two_im, sign * two_re)]
+    turned.append((-sign * three[1], sign * three[0]))
+    places = [None] * 8
+    places[0::2] = four_points(sums, sign)
+    places[1::2] = four_points(turned, sign)
+    return places
+
+
 def mix_forward(taken, twist_ref, at, ref):
-    far = [value * math.sqrt(0.5) for value in taken[4:]]
-    even = [turned((taken[n] + far[n], -far[n]), -n) for n in range(4)]
-    odd = [turned((taken[n] - far[n], far[n]), -5 * n) for n in range(4)]
-    for start, values in ((0, four_points(even, -1.0)), (1, four_points(odd, -1.0))):
-        for index, (re, im) in enumerate(values):
-            k = start + 2 * index
-            cos_twist, sin_twist = twist_ref[k, 0:1, :], twist_ref[k, 1:2, :]
-            put_split(ref, row_of(k, 0, at), re * cos_twist + im * sin_twist)
-            put_split(ref, row_of(k, 1, at), im * cos_twist - re * sin_twist)
+    angles = [math.pi * n / 16 for n in range(8)]
+    turned = [
+        (value * math.cos(angle), value * -math.sin(angle)) if angle else (value, 0.0)
+        for value, angle in zip(taken, angles)
+    ]
+    for k, (re, im) in enumerate(eight_points(turned, -1.0)):
+        cos_twist, sin_twist = twist_ref[k, 0:1, :], twist_ref[k, 1:2, :]
+        put_split(ref, row_of(k, 0, at), re * cos_twist + im * sin_twist)
+        put_split(ref, row_of(k, 1, at), im * cos_twist - re * sin_twist)
 
 
 def mix_back(spectra, twist_ref):
@@ -168,13 +178,11 @@
     for k, (re, im) in enumerate(spectra):
         cos_twist, sin_twist = twist_ref[k, 0:1, :], twist_ref[k, 1:2, :]
         twisted.append((re * cos_twist - im * sin_twist, im * cos_twist + re * sin_twist))
-    even, odd = four_points(twisted[0::2], 1.0), four_points(twisted[1::2], 1.0)
-    near, far = [], []
-    for n in range(4):
-        (even_re, even_im), (odd_re, odd_im) = turned(even[n], n), turned(odd[n], 5 * n)
-        near.append(even_re + odd_re)
-        far.append(((even_re - odd_re) - (even_im - odd_im)) * math.sqrt(0.5))
-    return near + far
+    totals = []
+    for n, (re, im) in enumerate(eight_points(twisted, 1.0)):
+        angle = math.pi * n / 16
+        totals.append(re * math.cos(angle) - im * math.sin(angle) if n else re)
+    return totals
 
 
 def spectrum_rows(waves_ref, k, at):

time: 60.5 us -> 60.4 us (level)
  no operation moved by 1% of the time
where the time goes in v9:
time: 60.4 us; the launch traced here: 60.1 us
  starting transfers between devices  27.7 us (46%)
  waiting for transfers between devices  18.8 us (31%)
  Pallas kernels  13.5 us (22%)
    ppermute x10, starting transfers between devices, scatter(): lax.ppermute(block, axis, [(i, i ^ turn) for i in range(count)])  16.2 us
    ppermute x10, waiting for transfers between devices, scatter(): lax.ppermute(block, axis, [(i, i ^ turn) for i in range(count)])  13 us
    all_to_all x1, starting transfers between devices, body(): gated = exchange(gated, ('seq', 'ch'))  7.32 us
    all_to_all x1, waiting for transfers between devices, body(): convolved = exchange(convolved, 'seq')  5.77 us
    pallas_call x1, Pallas kernels, body(): pl.pallas_call(conv_kernel, out_shape=jax.ShapeDtypeStruct((blocks, own,...  4.84 us
    all_to_all x1, starting transfers between devices, body(): convolved = exchange(convolved, 'seq')  4.17 us
    pallas_call x1, Pallas kernels, body(): pl.pallas_call(send_kernel, in_specs=[far], out_specs=far, out_shape=jax....  2.84 us
    pallas_call x1, Pallas kernels, body(): pl.pallas_call(gated_spectrum_kernel, out_shape=jax.ShapeDtypeStruct((blo...  2.67 us
  transfers between devices with their start and end apart: 12, of which 6 were waited for; matrix products, arithmetic and copies ran while one was open for 0% of the time, Pallas kernels for 7%

profile of v9, /device:TPU:0, one launch (start us, length us, event | category | flops | bytes accessed | tf_op | source)
XLA Modules:
  0.0 60.1 jit_solution(2946351008328904288)
XLA Ops:
  0.0 2.8 %encode_gated.1 = bf16[8,4,64,128]{3,2,1,0:T(8,128)(2,1)} custom-call(bf16[3,64,4096]{2,1,0:T(8,128)(2,1)} %bitcast.4), custom_call_target="tpu_custom_call" | custom-call | flops 33554432 | bytes 8388608 | tf_op jit(solution)/shard_map/encode_gated/pallas_call | solution.py:428
  2.9 7.3 %all-to-all-start = ((bf16[32,64,128]{2,1,0:T(8,128)(2,1)}), bf16[32,64,128]{2,1,0:T(8,128)(2,1)S(1)}, u32[]{:S(2)}, u32[]{:S(2)}) async-start(bf16[32,64,128]{2,1,0:T(8,128)(2,1)} %bitcast.8), calls=%async_computation | async-start | bytes 1048576 | tf_op jit(solution)/shard_map/all_to_all | solution.py:472
  10.2 1.2 %encode_taps.1 = (bf16[128,256]{1,0:T(8,128)(2,1)S(1)}, bf16[128,256]{1,0:T(8,128)(2,1)S(1)}, bf16[128,256]{1,0:T(8,128)(2,1)S(1)}, bf16[128,256]{1,0:T(8,128)(2...) custom-call(f32[8,128,256]{2,1,0:T(8,128)S(1)} %bitcast.6, ...), custom_call_target="tpu_custom_call" | custom-call | flops 33554432 | bytes 8388608 | tf_op jit(solution)/shard_map/encode_taps/pallas_call | solution.py:454
  11.4 1.8 %collective-permute-start.3 = (bf16[128,256]{1,0:T(8,128)(2,1)S(1)}, bf16[128,256]{1,0:T(8,128)(2,1)S(1)}, u32[]{:S(2)}, u32[]{:S(2)}) collective-permute-start(bf16[128,256]{1,0:T(8,128)(2,1)S(1)} %get-tuple-element.22), channel_id=1, source_target_pairs={{0,4},{4,0},{8,12},{12,8},{16,20},{20,16},{24,28},{28,24},{1,5},{5... | collective-permute-start | bytes 196616 | tf_op jit(solution)/shard_map/ppermute | solution.py:409
  13.3 1.5 %collective-permute-start.4 = (bf16[128,256]{1,0:T(8,128)(2,1)S(1)}, bf16[128,256]{1,0:T(8,128)(2,1)S(1)}, u32[]{:S(2)}, u32[]{:S(2)}) collective-permute-start(bf16[128,256]{1,0:T(8,128)(2,1)S(1)} %get-tuple-element.23), channel_id=1, source_target_pairs={{0,8},{4,12},{8,0},{12,4},{16,24},{20,28},{24,16},{28,20},{1,9},{5... | collective-permute-start | bytes 196616 | tf_op jit(solution)/shard_map/ppermute | solution.py:409
  14.7 0.3 collective-permute-start.5
  15.0 2.7 %collective-permute-start.6 = (bf16[128,256]{1,0:T(8,128)(2,1)S(1)}, bf16[128,256]{1,0:T(8,128)(2,1)S(1)}, u32[]{:S(2)}, u32[]{:S(2)}) collective-permute-start(bf16[128,256]{1,0:T(8,128)(2,1)S(1)} %get-tuple-element.25), channel_id=1, source_target_pairs={{0,16},{4,20},{8,24},{12,28},{16,0},{20,4},{24,8},{28,12},{1,17},{... | collective-permute-start | bytes 196616 | tf_op jit(solution)/shard_map/ppermute | solution.py:409
  17.6 1.5 %collective-permute-start.7 = (bf16[128,256]{1,0:T(8,128)(2,1)S(1)}, bf16[128,256]{1,0:T(8,128)(2,1)S(1)}, u32[]{:S(2)}, u32[]{:S(2)}) collective-permute-start(bf16[128,256]{1,0:T(8,128)(2,1)S(1)} %get-tuple-element.26), channel_id=1, source_target_pairs={{0,20},{4,16},{8,28},{12,24},{16,4},{20,0},{24,12},{28,8},{1,21},{... | collective-permute-start | bytes 196616 | tf_op jit(solution)/shard_map/ppermute | solution.py:409
  19.1 3.3 %collective-permute-start.8 = (bf16[128,256]{1,0:T(8,128)(2,1)S(1)}, bf16[128,256]{1,0:T(8,128)(2,1)S(1)}, u32[]{:S(2)}, u32[]{:S(2)}) collective-permute-start(bf16[128,256]{1,0:T(8,128)(2,1)S(1)} %get-tuple-element.27), channel_id=1, source_target_pairs={{0,24},{4,28},{8,16},{12,20},{16,8},{20,12},{24,0},{28,4},{1,25},{... | collective-permute-start | bytes 196616 | tf_op jit(solution)/shard_map/ppermute | solution.py:409
  22.5 3.2 %collective-permute-start.9 = (bf16[128,256]{1,0:T(8,128)(2,1)S(1)}, bf16[128,256]{1,0:T(8,128)(2,1)S(1)}, u32[]{:S(2)}, u32[]{:S(2)}) collective-permute-start(bf16[128,256]{1,0:T(8,128)(2,1)S(1)} %get-tuple-element.28), channel_id=1, source_target_pairs={{0,28},{4,24},{8,20},{12,16},{16,12},{20,8},{24,4},{28,0},{1,29},{... | collective-permute-start | bytes 196616 | tf_op jit(solution)/shard_map/ppermute | solution.py:409
  25.7 2.7 %gated_spectrum.1.gated_ref = f32[8,2,128,256]{3,2,1,0:T(8,128)S(1)} custom-call(bf16[32,64,128]{2,1,0:T(8,128)(2,1)S(1)} %all-to-all-done.gated_ref, bf16[768,256]{1,0:T(8,128)(2,1)S(1)} %copy-done.3, f32[8,2,256]{2,1,0:T(2,128)S(1)} %copy-done.5), custom_call_target="tpu_custom_call" | custom-call | flops 4294967296 | bytes 16777216 | tf_op jit(solution)/shard_map/gated_spectrum/pallas_call | solution.py:484
  28.4 4.3 %collective-permute-done.6.refs_4_ = bf16[128,256]{1,0:T(8,128)(2,1)S(1)} collective-permute-done((bf16[128,256]{1,0:T(8,128)(2,1)S(1)}, bf16[128,256]{1,0:T(8,128)(2,1)S(1)}, u32[]{:S(2)}, u32[]{:S(2)}) %collective-permute-start.6) | collective-permute-done | bytes 65568 | tf_op jit(solution)/shard_map/ppermute | solution.py:409
  32.7 2.3 %collective-permute-done.7.refs_5_ = bf16[128,256]{1,0:T(8,128)(2,1)S(1)} collective-permute-done((bf16[128,256]{1,0:T(8,128)(2,1)S(1)}, bf16[128,256]{1,0:T(8,128)(2,1)S(1)}, u32[]{:S(2)}, u32[]{:S(2)}) %collective-permute-start.7) | collective-permute-done | bytes 65568 | tf_op jit(solution)/shard_map/ppermute | solution.py:409
  35.0 4.8 %convolve.1 = bf16[8,128,256]{2,1,0:T(8,128)(2,1)} custom-call(f32[8,2,128,256]{3,2,1,0:T(8,128)S(1)} %gated_spectrum.1.gated_ref, bf16[128,256]{1,0:T(8,128)(2,1)S(1)} %get-tuple-element.21.refs_0_, bf16[128,256]{1,0:T(8,128)(2,1)S(1)} %collective-permute-done.3.refs_1_, bf16[128,256]{1,0:T(8,128)(2,1)S(1)} %collective-permute-done.4.refs_2_, ...), custom_call_target="tpu_custom_call" | custom-call | flops 4294967296 | bytes 16777216 | tf_op jit(solution)/shard_map/convolve/pallas_call | solution.py:492
  39.9 4.2 %all-to-all-start.1 = ((bf16[8,128,256]{2,1,0:T(8,128)(2,1)}), bf16[8,128,256]{2,1,0:T(8,128)(2,1)S(1)}, u32[]{:S(2)}, u32[]{:S(2)}) async-start(bf16[8,128,256]{2,1,0:T(8,128)(2,1)} %convolve.1), calls=%async_computation.1 | async-start | bytes 1048576 | tf_op jit(solution)/shard_map/all_to_all | solution.py:513
  44.0 0.1 send_queries.1
  44.2 0.1 collective-permute-start
  44.3 1.5 %collective-permute-start.1 = (bf16[64,1024]{1,0:T(8,128)(2,1)S(1)}, bf16[64,1024]{1,0:T(8,128)(2,1)S(1)}, u32[]{:S(2)}, u32[]{:S(2)}) collective-permute-start(bf16[64,1024]{1,0:T(8,128)(2,1)S(1)} %get-tuple-element.19), channel_id=1, source_target_pairs={{0,2},{1,3},{2,0},{3,1},{4,6},{5,7},{6,4},{7,5},{8,10},{9,11},{10,... | collective-permute-start | bytes 393224 | tf_op jit(solution)/shard_map/ppermute | solution.py:409
  45.8 0.3 collective-permute-start.2
  46.1 4.5 %collective-permute-done.1.refs_2_ = bf16[64,1024]{1,0:T(8,128)(2,1)S(1)} collective-permute-done((bf16[64,1024]{1,0:T(8,128)(2,1)S(1)}, bf16[64,1024]{1,0:T(8,128)(2,1)S(1)}, u32[]{:S(2)}, u32[]{:S(2)}) %collective-permute-start.1) | collective-permute-done | bytes 131104 | tf_op jit(solution)/shard_map/ppermute | solution.py:409
  50.6 1.9 %collective-permute-done.2.refs_3_ = bf16[64,1024]{1,0:T(8,128)(2,1)S(1)} collective-permute-done((bf16[64,1024]{1,0:T(8,128)(2,1)S(1)}, bf16[64,1024]{1,0:T(8,128)(2,1)S(1)}, u32[]{:S(2)}, u32[]{:S(2)}) %collective-permute-start.2) | collective-permute-done | bytes 131104 | tf_op jit(solution)/shard_map/ppermute | solution.py:409
  52.6 0.3 turn_queries.1.query_ref
  52.8 5.8 %all-to-all-done.1.conv_ref = bf16[8,128,256]{2,1,0:T(8,128)(2,1)S(1)} async-done(((bf16[8,128,256]{2,1,0:T(8,128)(2,1)}), bf16[8,128,256]{2,1,0:T(8,128)(2,1)S(1)}, u32[]{:S(2)}, u32[]{:S(2)}) %all-to-all-start.1) | async-done | bytes 524320 | tf_op jit(solution)/shard_map/all_to_all | solution.py:513
  58.6 1.5 %mix_out.1 = bf16[1024,256]{1,0:T(8,128)(2,1)} custom-call(bf16[1024,256]{1,0:T(8,128)(2,1)S(1)} %turn_queries.1.query_ref, bf16[8,128,256]{2,1,0:T(8,128)(2,1)S(1)} %all-to-all-done.1.conv_ref), custom_call_target="tpu_custom_call" | custom-call | tf_op jit(solution)/shard_map/mix_out/pallas_call | solution.py:523
  (19 shorter events, 0.1 us)
Async XLA Ops:
  0.0 10.2 %copy-start.1 = (f32[1024,256]{1,0:T(8,128)S(1)}, f32[1024,256]{1,0:T(8,128)}, u32[]{:S(2)}) copy-start(f32[1024,256]{1,0:T(8,128)} %param.7) | copy-start | bytes 3145732
  0.0 10.2 %copy-start.2 = (f32[1024]{0:T(1024)S(1)}, f32[1024]{0:T(1024)}, u32[]{:S(2)}) copy-start(f32[1024]{0:T(1024)} %param.8) | copy-start | bytes 12292
  0.0 25.7 %copy-start.3 = (bf16[768,256]{1,0:T(8,128)(2,1)S(1)}, bf16[768,256]{1,0:T(8,128)(2,1)}, u32[]{:S(2)}) copy-start(bf16[768,256]{1,0:T(8,128)(2,1)} %constant.6.clone.wave_ref.refs_8_) | copy-start | bytes 1179652
  0.0 25.7 %copy-start.5 = (f32[8,2,256]{2,1,0:T(2,128)S(1)}, f32[8,2,256]{2,1,0:T(2,128)}, u32[]{:S(2)}) copy-start(f32[8,2,256]{2,1,0:T(2,128)} %constant.7.clone.twist_ref.refs_10_) | copy-start | bytes 49156
  2.9 22.9 %all-to-all-start = ((bf16[32,64,128]{2,1,0:T(8,128)(2,1)}), bf16[32,64,128]{2,1,0:T(8,128)(2,1)S(1)}, u32[]{:S(2)}, u32[]{:S(2)}) async-start(bf16[32,64,128]{2,1,0:T(8,128)(2,1)} %bitcast.8), calls=%async_computation | async-start | bytes 1048576 | tf_op jit(solution)/shard_map/all_to_all | solution.py:472
  11.4 7.7 %collective-permute-start.3 = (bf16[128,256]{1,0:T(8,128)(2,1)S(1)}, bf16[128,256]{1,0:T(8,128)(2,1)S(1)}, u32[]{:S(2)}, u32[]{:S(2)}) collective-permute-start(bf16[128,256]{1,0:T(8,128)(2,1)S(1)} %get-tuple-element.22), channel_id=1, source_target_pairs={{0,4},{4,0},{8,12},{12,8},{16,20},{20,16},{24,28},{28,24},{1,5},{5... | collective-permute-start | bytes 196616 | tf_op jit(solution)/shard_map/ppermute | solution.py:409
  13.3 9.2 %collective-permute-start.4 = (bf16[128,256]{1,0:T(8,128)(2,1)S(1)}, bf16[128,256]{1,0:T(8,128)(2,1)S(1)}, u32[]{:S(2)}, u32[]{:S(2)}) collective-permute-start(bf16[128,256]{1,0:T(8,128)(2,1)S(1)} %get-tuple-element.23), channel_id=1, source_target_pairs={{0,8},{4,12},{8,0},{12,4},{16,24},{20,28},{24,16},{28,20},{1,9},{5... | collective-permute-start | bytes 196616 | tf_op jit(solution)/shard_map/ppermute | solution.py:409
  14.7 13.7 %collective-permute-start.5 = (bf16[128,256]{1,0:T(8,128)(2,1)S(1)}, bf16[128,256]{1,0:T(8,128)(2,1)S(1)}, u32[]{:S(2)}, u32[]{:S(2)}) collective-permute-start(bf16[128,256]{1,0:T(8,128)(2,1)S(1)} %get-tuple-element.24), channel_id=1, source_target_pairs={{0,12},{4,8},{8,4},{12,0},{16,28},{20,24},{24,20},{28,16},{1,13},{... | collective-permute-start | bytes 196616 | tf_op jit(solution)/shard_map/ppermute | solution.py:409
  15.0 17.7 %collective-permute-start.6 = (bf16[128,256]{1,0:T(8,128)(2,1)S(1)}, bf16[128,256]{1,0:T(8,128)(2,1)S(1)}, u32[]{:S(2)}, u32[]{:S(2)}) collective-permute-start(bf16[128,256]{1,0:T(8,128)(2,1)S(1)} %get-tuple-element.25), channel_id=1, source_target_pairs={{0,16},{4,20},{8,24},{12,28},{16,0},{20,4},{24,8},{28,12},{1,17},{... | collective-permute-start | bytes 196616 | tf_op jit(solution)/shard_map/ppermute | solution.py:409
  17.6 17.4 %collective-permute-start.7 = (bf16[128,256]{1,0:T(8,128)(2,1)S(1)}, bf16[128,256]{1,0:T(8,128)(2,1)S(1)}, u32[]{:S(2)}, u32[]{:S(2)}) collective-permute-start(bf16[128,256]{1,0:T(8,128)(2,1)S(1)} %get-tuple-element.26), channel_id=1, source_target_pairs={{0,20},{4,16},{8,28},{12,24},{16,4},{20,0},{24,12},{28,8},{1,21},{... | collective-permute-start | bytes 196616 | tf_op jit(solution)/shard_map/ppermute | solution.py:409
  19.1 15.9 %collective-permute-start.8 = (bf16[128,256]{1,0:T(8,128)(2,1)S(1)}, bf16[128,256]{1,0:T(8,128)(2,1)S(1)}, u32[]{:S(2)}, u32[]{:S(2)}) collective-permute-start(bf16[128,256]{1,0:T(8,128)(2,1)S(1)} %get-tuple-element.27), channel_id=1, source_target_pairs={{0,24},{4,28},{8,16},{12,20},{16,8},{20,12},{24,0},{28,4},{1,25},{... | collective-permute-start | bytes 196616 | tf_op jit(solution)/shard_map/ppermute | solution.py:409
  22.5 12.5 %copy-start.4 = (bf16[768,256]{1,0:T(8,128)(2,1)S(1)}, bf16[768,256]{1,0:T(8,128)(2,1)}, u32[]{:S(2)}) copy-start(bf16[768,256]{1,0:T(8,128)(2,1)} %constant.8.clone.refs_9_) | copy-start | bytes 1179652
  22.5 12.5 %collective-permute-start.9 = (bf16[128,256]{1,0:T(8,128)(2,1)S(1)}, bf16[128,256]{1,0:T(8,128)(2,1)S(1)}, u32[]{:S(2)}, u32[]{:S(2)}) collective-permute-start(bf16[128,256]{1,0:T(8,128)(2,1)S(1)} %get-tuple-element.28), channel_id=1, source_target_pairs={{0,28},{4,24},{8,20},{12,16},{16,12},{20,8},{24,4},{28,0},{1,29},{... | collective-permute-start | bytes 196616 | tf_op jit(solution)/shard_map/ppermute | solution.py:409
  35.0 9.0 %copy-start = (bf16[64,3,4096]{2,0,1:T(8,128)(2,1)S(1)}, bf16[64,3,4096]{2,0,1:T(8,128)(2,1)}, u32[]{:S(2)}) copy-start(bf16[64,3,4096]{2,0,1:T(8,128)(2,1)} %param.6) | copy-start | bytes 4718596
  39.9 18.7 %all-to-all-start.1 = ((bf16[8,128,256]{2,1,0:T(8,128)(2,1)}), bf16[8,128,256]{2,1,0:T(8,128)(2,1)S(1)}, u32[]{:S(2)}, u32[]{:S(2)}) async-start(bf16[8,128,256]{2,1,0:T(8,128)(2,1)} %convolve.1), calls=%async_computation.1 | async-start | bytes 1048576 | tf_op jit(solution)/shard_map/all_to_all | solution.py:513
  44.2 1.9 %collective-permute-start = (bf16[64,1024]{1,0:T(8,128)(2,1)S(1)}, bf16[64,1024]{1,0:T(8,128)(2,1)S(1)}, u32[]{:S(2)}, u32[]{:S(2)}) collective-permute-start(bf16[64,1024]{1,0:T(8,128)(2,1)S(1)} %get-tuple-element.18), channel_id=1, source_target_pairs={{0,1},{1,0},{2,3},{3,2},{4,5},{5,4},{6,7},{7,6},{8,9},{9,8},{10,11... | collective-permute-start | bytes 393224 | tf_op jit(solution)/shard_map/ppermute | solution.py:409
  44.3 6.4 %collective-permute-start.1 = (bf16[64,1024]{1,0:T(8,128)(2,1)S(1)}, bf16[64,1024]{1,0:T(8,128)(2,1)S(1)}, u32[]{:S(2)}, u32[]{:S(2)}) collective-permute-start(bf16[64,1024]{1,0:T(8,128)(2,1)S(1)} %get-tuple-element.19), channel_id=1, source_target_pairs={{0,2},{1,3},{2,0},{3,1},{4,6},{5,7},{6,4},{7,5},{8,10},{9,11},{10,... | collective-permute-start | bytes 393224 | tf_op jit(solution)/shard_map/ppermute | solution.py:409
  45.8 6.7 %collective-permute-start.2 = (bf16[64,1024]{1,0:T(8,128)(2,1)S(1)}, bf16[64,1024]{1,0:T(8,128)(2,1)S(1)}, u32[]{:S(2)}, u32[]{:S(2)}) collective-permute-start(bf16[64,1024]{1,0:T(8,128)(2,1)S(1)} %get-tuple-element.20), channel_id=1, source_target_pairs={{0,3},{1,2},{2,1},{3,0},{4,7},{5,6},{6,5},{7,4},{8,11},{9,10},{10,... | collective-permute-start | bytes 393224 | tf_op jit(solution)/shard_map/ppermute | solution.py:409

commit v10 on v9

--- a/solution.py
+++ b/solution.py
@@ -22,12 +22,26 @@
 ALL_BYTES = 60 * 1024 * 1024
 
 
-def split_first(values, axis):
-    count = min(values.shape[axis], LANES if axis == values.ndim - 1 else EXPONENT_BITS)
-    first = lax.slice_in_dim(values, 0, count, axis=axis)
-    if count == values.shape[axis]:
-        return first, None
-    return first, lax.slice_in_dim(values, count, values.shape[axis], axis=axis)
+def split_marked(values, axis):
+    extent = values.shape[axis]
+    if axis == values.ndim - 1:
+        cut = max(extent - LANES, 0)
+        marked = lax.slice_in_dim(values, cut, extent, axis=axis)
+        return marked, lax.slice_in_dim(values, 0, cut, axis=axis) if cut else None
+    cut = min(extent, EXPONENT_BITS)
+    marked = lax.slice_in_dim(values, 0, cut, axis=axis)
+    return marked, lax.slice_in_dim(values, cut, extent, axis=axis) if cut < extent else None
+
+
+def join_marked(marked, rest, axis):
+    if rest is None:
+        return marked
+    return jnp.concatenate([rest, marked] if axis == rest.ndim - 1 else [marked, rest], axis=axis)
+
+
+def bit_place(shape, axis):
+    place = lax.broadcasted_iota(jnp.int32, shape, axis) - (shape[axis] - EXPONENT_BITS)
+    return place.astype(jnp.float32)
 
 
 def scale_of(peak):
@@ -36,9 +50,9 @@
 
 
 def exponent_bits(power, shape, axis):
-    place = lax.broadcasted_iota(jnp.int32, shape, axis).astype(jnp.float32)
-    bits = (power + (EXPONENT_BIAS + 0.25)) * jnp.exp2(-1.0 - place)
-    return jnp.where(bits - jnp.floor(bits) >= 0.5, 0.5, 0.0), place < EXPONENT_BITS
+    place = bit_place(shape, axis)
+    bits = (power + (EXPONENT_BIAS + 0.25)) * jnp.exp2(-1.0 - jnp.maximum(place, 0.0))
+    return jnp.where(bits - jnp.floor(bits) >= 0.5, 0.5, 0.0), place >= 0.0
 
 
 def encode(values, axis):
@@ -55,7 +69,7 @@
             jnp.minimum(share * (2.0 * top) - LOW_POWER, share * top - LOW_POWER / 2),
             jnp.minimum(share * LOW_POWER, LOW_POWER + 1.0),
         )
-        first, rest = split_first(place, axis)
+        first, rest = split_marked(place, axis)
         bits = exponent_bits(power, first.shape, axis) if bits is None else bits
         odd, holds = bits
         if axis == values.ndim - 1:
@@ -65,9 +79,7 @@
             marked = (jnp.floor(first * 64.0 - odd + 0.5) + odd) * (1.0 / 64.0)
             octave = jnp.floor(marked)
             first = jnp.exp2(octave) * (marked - octave + 1.0)
-        size = first
-        if rest is not None:
-            size = jnp.concatenate([first, jnp.exp2(rest)], axis=axis)
+        size = join_marked(first, None if rest is None else jnp.exp2(rest), axis)
         codes.append(jnp.where(values < 0.0, -size, size).astype(jnp.bfloat16))
     return codes
 
@@ -76,16 +88,16 @@
     code = code.astype(jnp.float32)
     size = jnp.abs(code)
     place = jnp.log(size) * (1.0 / math.log(2.0))
-    first, rest = split_first(place, axis)
+    first, rest = split_marked(place, axis)
     if axis == code.ndim - 1:
         half = first * GRID + 0.25
     else:
         octave = jnp.floor(first + 0.002)
-        first = octave + split_first(size, axis)[0] * jnp.exp2(-octave) - 1.0
+        first = octave + split_marked(size, axis)[0] * jnp.exp2(-octave) - 1.0
         half = first * 64.0 + 0.25
-        place = first if rest is None else jnp.concatenate([first, rest], axis=axis)
-    spot = lax.broadcasted_iota(jnp.int32, first.shape, axis).astype(jnp.float32)
-    weight = jnp.where(spot < EXPONENT_BITS, jnp.exp2(spot), 0.0)
+        place = join_marked(first, rest, axis)
+    spot = bit_place(first.shape, axis)
+    weight = jnp.where(spot >= 0.0, jnp.exp2(spot), 0.0)
     held = jnp.where(half - jnp.floor(half) >= 0.5, weight, 0.0)
     scale = jnp.exp2(jnp.sum(held, axis=axis, keepdims=True) - (EXPONENT_BIAS + halvings))
     step = 0.25 / LOW_POWER

time: 60.4 us -> 60.4 us (level)
  no operation moved by 1% of the time
where the time goes in v10:
time: 60.4 us; the launch traced here: 60.1 us
  starting transfers between devices  27.7 us (46%)
  waiting for transfers between devices  18.8 us (31%)
  Pallas kernels  13.5 us (22%)
    ppermute x10, starting transfers between devices, scatter(): lax.ppermute(block, axis, [(i, i ^ turn) for i in range(count)])  16.2 us
    ppermute x10, waiting for transfers between devices, scatter(): lax.ppermute(block, axis, [(i, i ^ turn) for i in range(count)])  13 us
    all_to_all x1, starting transfers between devices, body(): gated = exchange(gated, ('seq', 'ch'))  7.32 us
    all_to_all x1, waiting for transfers between devices, body(): convolved = exchange(convolved, 'seq')  5.78 us
    pallas_call x1, Pallas kernels, body(): pl.pallas_call(conv_kernel, out_shape=jax.ShapeDtypeStruct((blocks, own,...  4.86 us
    all_to_all x1, starting transfers between devices, body(): convolved = exchange(convolved, 'seq')  4.16 us
    pallas_call x1, Pallas kernels, body(): pl.pallas_call(send_kernel, in_specs=[far], out_specs=far, out_shape=jax....  2.84 us
    pallas_call x1, Pallas kernels, body(): pl.pallas_call(gated_spectrum_kernel, out_shape=jax.ShapeDtypeStruct((blo...  2.67 us
  transfers between devices with their start and end apart: 12, of which 6 were waited for; matrix products, arithmetic and copies ran while one was open for 0% of the time, Pallas kernels for 7%

profile of v10, /device:TPU:0, one launch (start us, length us, event | category | flops | bytes accessed | tf_op | source)
XLA Modules:
  0.0 60.1 jit_solution(2632555322772726962)
XLA Ops:
  0.0 2.8 %encode_gated.1 = bf16[8,4,64,128]{3,2,1,0:T(8,128)(2,1)} custom-call(bf16[3,64,4096]{2,1,0:T(8,128)(2,1)} %bitcast.4), custom_call_target="tpu_custom_call" | custom-call | flops 33554432 | bytes 8388608 | tf_op jit(solution)/shard_map/encode_gated/pallas_call | solution.py:440
  2.9 7.3 %all-to-all-start = ((bf16[32,64,128]{2,1,0:T(8,128)(2,1)}), bf16[32,64,128]{2,1,0:T(8,128)(2,1)S(1)}, u32[]{:S(2)}, u32[]{:S(2)}) async-start(bf16[32,64,128]{2,1,0:T(8,128)(2,1)} %bitcast.8), calls=%async_computation | async-start | bytes 1048576 | tf_op jit(solution)/shard_map/all_to_all | solution.py:484
  10.2 1.2 %encode_taps.1 = (bf16[128,256]{1,0:T(8,128)(2,1)S(1)}, bf16[128,256]{1,0:T(8,128)(2,1)S(1)}, bf16[128,256]{1,0:T(8,128)(2,1)S(1)}, bf16[128,256]{1,0:T(8,128)(2...) custom-call(f32[8,128,256]{2,1,0:T(8,128)S(1)} %bitcast.6, ...), custom_call_target="tpu_custom_call" | custom-call | flops 33554432 | bytes 8388608 | tf_op jit(solution)/shard_map/encode_taps/pallas_call | solution.py:466
  11.4 1.8 %collective-permute-start.3 = (bf16[128,256]{1,0:T(8,128)(2,1)S(1)}, bf16[128,256]{1,0:T(8,128)(2,1)S(1)}, u32[]{:S(2)}, u32[]{:S(2)}) collective-permute-start(bf16[128,256]{1,0:T(8,128)(2,1)S(1)} %get-tuple-element.22), channel_id=1, source_target_pairs={{0,4},{4,0},{8,12},{12,8},{16,20},{20,16},{24,28},{28,24},{1,5},{5... | collective-permute-start | bytes 196616 | tf_op jit(solution)/shard_map/ppermute | solution.py:421
  13.2 1.5 %collective-permute-start.4 = (bf16[128,256]{1,0:T(8,128)(2,1)S(1)}, bf16[128,256]{1,0:T(8,128)(2,1)S(1)}, u32[]{:S(2)}, u32[]{:S(2)}) collective-permute-start(bf16[128,256]{1,0:T(8,128)(2,1)S(1)} %get-tuple-element.23), channel_id=1, source_target_pairs={{0,8},{4,12},{8,0},{12,4},{16,24},{20,28},{24,16},{28,20},{1,9},{5... | collective-permute-start | bytes 196616 | tf_op jit(solution)/shard_map/ppermute | solution.py:421
  14.7 0.3 collective-permute-start.5
  15.0 2.7 %collective-permute-start.6 = (bf16[128,256]{1,0:T(8,128)(2,1)S(1)}, bf16[128,256]{1,0:T(8,128)(2,1)S(1)}, u32[]{:S(2)}, u32[]{:S(2)}) collective-permute-start(bf16[128,256]{1,0:T(8,128)(2,1)S(1)} %get-tuple-element.25), channel_id=1, source_target_pairs={{0,16},{4,20},{8,24},{12,28},{16,0},{20,4},{24,8},{28,12},{1,17},{... | collective-permute-start | bytes 196616 | tf_op jit(solution)/shard_map/ppermute | solution.py:421
  17.6 1.5 %collective-permute-start.7 = (bf16[128,256]{1,0:T(8,128)(2,1)S(1)}, bf16[128,256]{1,0:T(8,128)(2,1)S(1)}, u32[]{:S(2)}, u32[]{:S(2)}) collective-permute-start(bf16[128,256]{1,0:T(8,128)(2,1)S(1)} %get-tuple-element.26), channel_id=1, source_target_pairs={{0,20},{4,16},{8,28},{12,24},{16,4},{20,0},{24,12},{28,8},{1,21},{... | collective-permute-start | bytes 196616 | tf_op jit(solution)/shard_map/ppermute | solution.py:421
  19.1 3.3 %collective-permute-start.8 = (bf16[128,256]{1,0:T(8,128)(2,1)S(1)}, bf16[128,256]{1,0:T(8,128)(2,1)S(1)}, u32[]{:S(2)}, u32[]{:S(2)}) collective-permute-start(bf16[128,256]{1,0:T(8,128)(2,1)S(1)} %get-tuple-element.27), channel_id=1, source_target_pairs={{0,24},{4,28},{8,16},{12,20},{16,8},{20,12},{24,0},{28,4},{1,25},{... | collective-permute-start | bytes 196616 | tf_op jit(solution)/shard_map/ppermute | solution.py:421
  22.5 3.2 %collective-permute-start.9 = (bf16[128,256]{1,0:T(8,128)(2,1)S(1)}, bf16[128,256]{1,0:T(8,128)(2,1)S(1)}, u32[]{:S(2)}, u32[]{:S(2)}) collective-permute-start(bf16[128,256]{1,0:T(8,128)(2,1)S(1)} %get-tuple-element.28), channel_id=1, source_target_pairs={{0,28},{4,24},{8,20},{12,16},{16,12},{20,8},{24,4},{28,0},{1,29},{... | collective-permute-start | bytes 196616 | tf_op jit(solution)/shard_map/ppermute | solution.py:421
  25.7 2.7 %gated_spectrum.1.gated_ref = f32[8,2,128,256]{3,2,1,0:T(8,128)S(1)} custom-call(bf16[32,64,128]{2,1,0:T(8,128)(2,1)S(1)} %all-to-all-done.gated_ref, bf16[768,256]{1,0:T(8,128)(2,1)S(1)} %copy-done.3, f32[8,2,256]{2,1,0:T(2,128)S(1)} %copy-done.5), custom_call_target="tpu_custom_call" | custom-call | flops 4294967296 | bytes 16777216 | tf_op jit(solution)/shard_map/gated_spectrum/pallas_call | solution.py:496
  28.4 4.3 %collective-permute-done.6.refs_4_ = bf16[128,256]{1,0:T(8,128)(2,1)S(1)} collective-permute-done((bf16[128,256]{1,0:T(8,128)(2,1)S(1)}, bf16[128,256]{1,0:T(8,128)(2,1)S(1)}, u32[]{:S(2)}, u32[]{:S(2)}) %collective-permute-start.6) | collective-permute-done | bytes 65568 | tf_op jit(solution)/shard_map/ppermute | solution.py:421
  32.7 2.3 %collective-permute-done.7.refs_5_ = bf16[128,256]{1,0:T(8,128)(2,1)S(1)} collective-permute-done((bf16[128,256]{1,0:T(8,128)(2,1)S(1)}, bf16[128,256]{1,0:T(8,128)(2,1)S(1)}, u32[]{:S(2)}, u32[]{:S(2)}) %collective-permute-start.7) | collective-permute-done | bytes 65568 | tf_op jit(solution)/shard_map/ppermute | solution.py:421
  35.0 4.9 %convolve.1 = bf16[8,128,256]{2,1,0:T(8,128)(2,1)} custom-call(f32[8,2,128,256]{3,2,1,0:T(8,128)S(1)} %gated_spectrum.1.gated_ref, bf16[128,256]{1,0:T(8,128)(2,1)S(1)} %get-tuple-element.21.refs_0_, bf16[128,256]{1,0:T(8,128)(2,1)S(1)} %collective-permute-done.3.refs_1_, bf16[128,256]{1,0:T(8,128)(2,1)S(1)} %collective-permute-done.4.refs_2_, ...), custom_call_target="tpu_custom_call" | custom-call | flops 4294967296 | bytes 16777216 | tf_op jit(solution)/shard_map/convolve/pallas_call | solution.py:504
  39.9 4.2 %all-to-all-start.1 = ((bf16[8,128,256]{2,1,0:T(8,128)(2,1)}), bf16[8,128,256]{2,1,0:T(8,128)(2,1)S(1)}, u32[]{:S(2)}, u32[]{:S(2)}) async-start(bf16[8,128,256]{2,1,0:T(8,128)(2,1)} %convolve.1), calls=%async_computation.1 | async-start | bytes 1048576 | tf_op jit(solution)/shard_map/all_to_all | solution.py:525
  44.1 0.1 send_queries.1
  44.2 0.1 collective-permute-start
  44.3 1.5 %collective-permute-start.1 = (bf16[64,1024]{1,0:T(8,128)(2,1)S(1)}, bf16[64,1024]{1,0:T(8,128)(2,1)S(1)}, u32[]{:S(2)}, u32[]{:S(2)}) collective-permute-start(bf16[64,1024]{1,0:T(8,128)(2,1)S(1)} %get-tuple-element.19), channel_id=1, source_target_pairs={{0,2},{1,3},{2,0},{3,1},{4,6},{5,7},{6,4},{7,5},{8,10},{9,11},{10,... | collective-permute-start | bytes 393224 | tf_op jit(solution)/shard_map/ppermute | solution.py:421
  45.8 0.3 collective-permute-start.2
  46.2 4.5 %collective-permute-done.1.refs_2_ = bf16[64,1024]{1,0:T(8,128)(2,1)S(1)} collective-permute-done((bf16[64,1024]{1,0:T(8,128)(2,1)S(1)}, bf16[64,1024]{1,0:T(8,128)(2,1)S(1)}, u32[]{:S(2)}, u32[]{:S(2)}) %collective-permute-start.1) | collective-permute-done | bytes 131104 | tf_op jit(solution)/shard_map/ppermute | solution.py:421
  50.7 1.9 %collective-permute-done.2.refs_3_ = bf16[64,1024]{1,0:T(8,128)(2,1)S(1)} collective-permute-done((bf16[64,1024]{1,0:T(8,128)(2,1)S(1)}, bf16[64,1024]{1,0:T(8,128)(2,1)S(1)}, u32[]{:S(2)}, u32[]{:S(2)}) %collective-permute-start.2) | collective-permute-done | bytes 131104 | tf_op jit(solution)/shard_map/ppermute | solution.py:421
  52.6 0.3 turn_queries.1.query_ref
  52.8 5.8 %all-to-all-done.1.conv_ref = bf16[8,128,256]{2,1,0:T(8,128)(2,1)S(1)} async-done(((bf16[8,128,256]{2,1,0:T(8,128)(2,1)}), bf16[8,128,256]{2,1,0:T(8,128)(2,1)S(1)}, u32[]{:S(2)}, u32[]{:S(2)}) %all-to-all-start.1) | async-done | bytes 524320 | tf_op jit(solution)/shard_map/all_to_all | solution.py:525
  58.6 1.5 %mix_out.1 = bf16[1024,256]{1,0:T(8,128)(2,1)} custom-call(bf16[1024,256]{1,0:T(8,128)(2,1)S(1)} %turn_queries.1.query_ref, bf16[8,128,256]{2,1,0:T(8,128)(2,1)S(1)} %all-to-all-done.1.conv_ref), custom_call_target="tpu_custom_call" | custom-call | tf_op jit(solution)/shard_map/mix_out/pallas_call | solution.py:535
  (19 shorter events, 0.1 us)
Async XLA Ops:
  0.0 10.2 %copy-start.1 = (f32[1024,256]{1,0:T(8,128)S(1)}, f32[1024,256]{1,0:T(8,128)}, u32[]{:S(2)}) copy-start(f32[1024,256]{1,0:T(8,128)} %param.7) | copy-start | bytes 3145732
  0.0 10.2 %copy-start.2 = (f32[1024]{0:T(1024)S(1)}, f32[1024]{0:T(1024)}, u32[]{:S(2)}) copy-start(f32[1024]{0:T(1024)} %param.8) | copy-start | bytes 12292
  0.0 25.7 %copy-start.3 = (bf16[768,256]{1,0:T(8,128)(2,1)S(1)}, bf16[768,256]{1,0:T(8,128)(2,1)}, u32[]{:S(2)}) copy-start(bf16[768,256]{1,0:T(8,128)(2,1)} %constant.6.clone.wave_ref.refs_8_) | copy-start | bytes 1179652
  0.0 25.7 %copy-start.5 = (f32[8,2,256]{2,1,0:T(2,128)S(1)}, f32[8,2,256]{2,1,0:T(2,128)}, u32[]{:S(2)}) copy-start(f32[8,2,256]{2,1,0:T(2,128)} %constant.7.clone.twist_ref.refs_10_) | copy-start | bytes 49156
  2.9 22.9 %all-to-all-start = ((bf16[32,64,128]{2,1,0:T(8,128)(2,1)}), bf16[32,64,128]{2,1,0:T(8,128)(2,1)S(1)}, u32[]{:S(2)}, u32[]{:S(2)}) async-start(bf16[32,64,128]{2,1,0:T(8,128)(2,1)} %bitcast.8), calls=%async_computation | async-start | bytes 1048576 | tf_op jit(solution)/shard_map/all_to_all | solution.py:484
  11.4 7.7 %collective-permute-start.3 = (bf16[128,256]{1,0:T(8,128)(2,1)S(1)}, bf16[128,256]{1,0:T(8,128)(2,1)S(1)}, u32[]{:S(2)}, u32[]{:S(2)}) collective-permute-start(bf16[128,256]{1,0:T(8,128)(2,1)S(1)} %get-tuple-element.22), channel_id=1, source_target_pairs={{0,4},{4,0},{8,12},{12,8},{16,20},{20,16},{24,28},{28,24},{1,5},{5... | collective-permute-start | bytes 196616 | tf_op jit(solution)/shard_map/ppermute | solution.py:421
  13.2 9.2 %collective-permute-start.4 = (bf16[128,256]{1,0:T(8,128)(2,1)S(1)}, bf16[128,256]{1,0:T(8,128)(2,1)S(1)}, u32[]{:S(2)}, u32[]{:S(2)}) collective-permute-start(bf16[128,256]{1,0:T(8,128)(2,1)S(1)} %get-tuple-element.23), channel_id=1, source_target_pairs={{0,8},{4,12},{8,0},{12,4},{16,24},{20,28},{24,16},{28,20},{1,9},{5... | collective-permute-start | bytes 196616 | tf_op jit(solution)/shard_map/ppermute | solution.py:421
  14.7 13.7 %collective-permute-start.5 = (bf16[128,256]{1,0:T(8,128)(2,1)S(1)}, bf16[128,256]{1,0:T(8,128)(2,1)S(1)}, u32[]{:S(2)}, u32[]{:S(2)}) collective-permute-start(bf16[128,256]{1,0:T(8,128)(2,1)S(1)} %get-tuple-element.24), channel_id=1, source_target_pairs={{0,12},{4,8},{8,4},{12,0},{16,28},{20,24},{24,20},{28,16},{1,13},{... | collective-permute-start | bytes 196616 | tf_op jit(solution)/shard_map/ppermute | solution.py:421
  15.0 17.7 %collective-permute-start.6 = (bf16[128,256]{1,0:T(8,128)(2,1)S(1)}, bf16[128,256]{1,0:T(8,128)(2,1)S(1)}, u32[]{:S(2)}, u32[]{:S(2)}) collective-permute-start(bf16[128,256]{1,0:T(8,128)(2,1)S(1)} %get-tuple-element.25), channel_id=1, source_target_pairs={{0,16},{4,20},{8,24},{12,28},{16,0},{20,4},{24,8},{28,12},{1,17},{... | collective-permute-start | bytes 196616 | tf_op jit(solution)/shard_map/ppermute | solution.py:421
  17.6 17.4 %collective-permute-start.7 = (bf16[128,256]{1,0:T(8,128)(2,1)S(1)}, bf16[128,256]{1,0:T(8,128)(2,1)S(1)}, u32[]{:S(2)}, u32[]{:S(2)}) collective-permute-start(bf16[128,256]{1,0:T(8,128)(2,1)S(1)} %get-tuple-element.26), channel_id=1, source_target_pairs={{0,20},{4,16},{8,28},{12,24},{16,4},{20,0},{24,12},{28,8},{1,21},{... | collective-permute-start | bytes 196616 | tf_op jit(solution)/shard_map/ppermute | solution.py:421
  19.1 15.9 %collective-permute-start.8 = (bf16[128,256]{1,0:T(8,128)(2,1)S(1)}, bf16[128,256]{1,0:T(8,128)(2,1)S(1)}, u32[]{:S(2)}, u32[]{:S(2)}) collective-permute-start(bf16[128,256]{1,0:T(8,128)(2,1)S(1)} %get-tuple-element.27), channel_id=1, source_target_pairs={{0,24},{4,28},{8,16},{12,20},{16,8},{20,12},{24,0},{28,4},{1,25},{... | collective-permute-start | bytes 196616 | tf_op jit(solution)/shard_map/ppermute | solution.py:421
  22.5 12.6 %copy-start.4 = (bf16[768,256]{1,0:T(8,128)(2,1)S(1)}, bf16[768,256]{1,0:T(8,128)(2,1)}, u32[]{:S(2)}) copy-start(bf16[768,256]{1,0:T(8,128)(2,1)} %constant.8.clone.refs_9_) | copy-start | bytes 1179652
  22.5 12.5 %collective-permute-start.9 = (bf16[128,256]{1,0:T(8,128)(2,1)S(1)}, bf16[128,256]{1,0:T(8,128)(2,1)S(1)}, u32[]{:S(2)}, u32[]{:S(2)}) collective-permute-start(bf16[128,256]{1,0:T(8,128)(2,1)S(1)} %get-tuple-element.28), channel_id=1, source_target_pairs={{0,28},{4,24},{8,20},{12,16},{16,12},{20,8},{24,4},{28,0},{1,29},{... | collective-permute-start | bytes 196616 | tf_op jit(solution)/shard_map/ppermute | solution.py:421
  35.0 9.0 %copy-start = (bf16[64,3,4096]{2,0,1:T(8,128)(2,1)S(1)}, bf16[64,3,4096]{2,0,1:T(8,128)(2,1)}, u32[]{:S(2)}) copy-start(bf16[64,3,4096]{2,0,1:T(8,128)(2,1)} %param.6) | copy-start | bytes 4718596
  39.9 18.7 %all-to-all-start.1 = ((bf16[8,128,256]{2,1,0:T(8,128)(2,1)}), bf16[8,128,256]{2,1,0:T(8,128)(2,1)S(1)}, u32[]{:S(2)}, u32[]{:S(2)}) async-start(bf16[8,128,256]{2,1,0:T(8,128)(2,1)} %convolve.1), calls=%async_computation.1 | async-start | bytes 1048576 | tf_op jit(solution)/shard_map/all_to_all | solution.py:525
  44.2 1.9 %collective-permute-start = (bf16[64,1024]{1,0:T(8,128)(2,1)S(1)}, bf16[64,1024]{1,0:T(8,128)(2,1)S(1)}, u32[]{:S(2)}, u32[]{:S(2)}) collective-permute-start(bf16[64,1024]{1,0:T(8,128)(2,1)S(1)} %get-tuple-element.18), channel_id=1, source_target_pairs={{0,1},{1,0},{2,3},{3,2},{4,5},{5,4},{6,7},{7,6},{8,9},{9,8},{10,11... | collective-permute-start | bytes 393224 | tf_op jit(solution)/shard_map/ppermute | solution.py:421
  44.3 6.4 %collective-permute-start.1 = (bf16[64,1024]{1,0:T(8,128)(2,1)S(1)}, bf16[64,1024]{1,0:T(8,128)(2,1)S(1)}, u32[]{:S(2)}, u32[]{:S(2)}) collective-permute-start(bf16[64,1024]{1,0:T(8,128)(2,1)S(1)} %get-tuple-element.19), channel_id=1, source_target_pairs={{0,2},{1,3},{2,0},{3,1},{4,6},{5,7},{6,4},{7,5},{8,10},{9,11},{10,... | collective-permute-start | bytes 393224 | tf_op jit(solution)/shard_map/ppermute | solution.py:421
  45.8 6.7 %collective-permute-start.2 = (bf16[64,1024]{1,0:T(8,128)(2,1)S(1)}, bf16[64,1024]{1,0:T(8,128)(2,1)S(1)}, u32[]{:S(2)}, u32[]{:S(2)}) collective-permute-start(bf16[64,1024]{1,0:T(8,128)(2,1)S(1)} %get-tuple-element.20), channel_id=1, source_target_pairs={{0,3},{1,2},{2,1},{3,0},{4,7},{5,6},{6,5},{7,4},{8,11},{9,10},{10,... | collective-permute-start | bytes 393224 | tf_op jit(solution)/shard_map/ppermute | solution.py:421

commit v11 on v10

--- a/solution.py
+++ b/solution.py
@@ -321,7 +321,7 @@
     scale = math.log2(blocks * ROW)
     me = lax.axis_index("seq")
     groups = row_groups()
-    for turn, code_ref in enumerate(refs[:blocks]):
+    for turn, code_ref in zip(turn_order(blocks), refs[:blocks]):
         codes[me ^ turn] = code_ref[...]
 
     def forward(at, half):
@@ -413,6 +413,10 @@
     re, im = re * cos_twist - im * sin_twist, im * cos_twist + re * sin_twist
     total = dot("kcm,kn->ncm", re, mix[0]) - dot("kcm,kn->ncm", im, mix[1])
     return total * (1.0 / (blocks * ROW))
+
+
+def turn_order(count):
+    return sorted(range(count), key=lambda turn: (turn > 3, -(turn // 2) if turn > 3 else 0, turn))
 
 
 def scatter(blocks, axis):
@@ -515,7 +519,7 @@
             compiler_params=large,
             cost_estimate=cost(2**32, 2**24),
             name="convolve",
-        )(gated, *taps, wave, back_wave, twist)
+        )(gated, *[taps[turn] for turn in turn_order(groups)], wave, back_wave, twist)
     else:
         gated = decode(gated, 1).reshape(blocks, ROW, own)
         taps = jnp.transpose(decode(taps, 2), (1, 0, 2)).reshape(own, blocks, ROW)

time: 60.4 us -> 62 us (1.026)
  waiting for transfers between devices: 18.8 us -> 20.8 us
    ppermute x10, waiting for transfers between devices: 13 us -> 15.1 us  [scatter(): lax.ppermute(block, axis, [(i, i ^ turn) for i in range(count)])]
    all_to_all x1, starting transfers between devices: 4.16 us -> 3.51 us  [body(): convolved = exchange(convolved, 'seq')]
  transfers between devices with their start and end apart: 12 -> 12, of which waited for: 6 -> 7; matrix products, arithmetic and copies ran while one was open for 0% -> 0% of each run, Pallas kernels for 7% -> 7%
where the time goes in v11:
time: 62 us; the launch traced here: 61.7 us
  starting transfers between devices  27.2 us (44%)
  waiting for transfers between devices  20.8 us (34%)
  Pallas kernels  13.5 us (22%)
    ppermute x10, starting transfers between devices, scatter(): lax.ppermute(block, axis, [(i, i ^ turn) for i in range(count)])  16.4 us
    ppermute x10, waiting for transfers between devices, scatter(): lax.ppermute(block, axis, [(i, i ^ turn) for i in range(count)])  15.1 us
    all_to_all x1, starting transfers between devices, body(): gated = exchange(gated, ('seq', 'ch'))  7.32 us
    all_to_all x1, waiting for transfers between devices, body(): convolved = exchange(convolved, 'seq')  5.7 us
    pallas_call x1, Pallas kernels, body(): pl.pallas_call(conv_kernel, out_shape=jax.ShapeDtypeStruct((blocks, own,...  4.84 us
    all_to_all x1, starting transfers between devices, body(): convolved = exchange(convolved, 'seq')  3.51 us
    pallas_call x1, Pallas kernels, body(): pl.pallas_call(send_kernel, in_specs=[far], out_specs=far, out_shape=jax....  2.84 us
    pallas_call x1, Pallas kernels, body(): pl.pallas_call(gated_spectrum_kernel, out_shape=jax.ShapeDtypeStruct((blo...  2.67 us
  transfers between devices with their start and end apart: 12, of which 7 were waited for; matrix products, arithmetic and copies ran while one was open for 0% of the time, Pallas kernels for 7%

profile of v11, /device:TPU:0, one launch (start us, length us, event | category | flops | bytes accessed | tf_op | source)
XLA Modules:
  0.0 61.7 jit_solution(12806656425633622142)
XLA Ops:
  0.0 2.8 %encode_gated.1 = bf16[8,4,64,128]{3,2,1,0:T(8,128)(2,1)} custom-call(bf16[3,64,4096]{2,1,0:T(8,128)(2,1)} %bitcast.4), custom_call_target="tpu_custom_call" | custom-call | flops 33554432 | bytes 8388608 | tf_op jit(solution)/shard_map/encode_gated/pallas_call | solution.py:444
  2.9 7.3 %all-to-all-start = ((bf16[32,64,128]{2,1,0:T(8,128)(2,1)}), bf16[32,64,128]{2,1,0:T(8,128)(2,1)S(1)}, u32[]{:S(2)}, u32[]{:S(2)}) async-start(bf16[32,64,128]{2,1,0:T(8,128)(2,1)} %bitcast.8), calls=%async_computation | async-start | bytes 1048576 | tf_op jit(solution)/shard_map/all_to_all | solution.py:488
  10.2 1.2 %encode_taps.1 = (bf16[128,256]{1,0:T(8,128)(2,1)S(1)}, bf16[128,256]{1,0:T(8,128)(2,1)S(1)}, bf16[128,256]{1,0:T(8,128)(2,1)S(1)}, bf16[128,256]{1,0:T(8,128)(2...) custom-call(f32[8,128,256]{2,1,0:T(8,128)S(1)} %bitcast.6, ...), custom_call_target="tpu_custom_call" | custom-call | flops 33554432 | bytes 8388608 | tf_op jit(solution)/shard_map/encode_taps/pallas_call | solution.py:470
  11.4 1.8 %collective-permute-start.3 = (bf16[128,256]{1,0:T(8,128)(2,1)S(1)}, bf16[128,256]{1,0:T(8,128)(2,1)S(1)}, u32[]{:S(2)}, u32[]{:S(2)}) collective-permute-start(bf16[128,256]{1,0:T(8,128)(2,1)S(1)} %get-tuple-element.22), channel_id=1, source_target_pairs={{0,4},{4,0},{8,12},{12,8},{16,20},{20,16},{24,28},{28,24},{1,5},{5... | collective-permute-start | bytes 196616 | tf_op jit(solution)/shard_map/ppermute | solution.py:425
  13.2 1.5 %collective-permute-start.4 = (bf16[128,256]{1,0:T(8,128)(2,1)S(1)}, bf16[128,256]{1,0:T(8,128)(2,1)S(1)}, u32[]{:S(2)}, u32[]{:S(2)}) collective-permute-start(bf16[128,256]{1,0:T(8,128)(2,1)S(1)} %get-tuple-element.23), channel_id=1, source_target_pairs={{0,8},{4,12},{8,0},{12,4},{16,24},{20,28},{24,16},{28,20},{1,9},{5... | collective-permute-start | bytes 196616 | tf_op jit(solution)/shard_map/ppermute | solution.py:425
  14.7 0.3 collective-permute-start.5
  15.0 3.6 %collective-permute-start.6 = (bf16[128,256]{1,0:T(8,128)(2,1)S(1)}, bf16[128,256]{1,0:T(8,128)(2,1)S(1)}, u32[]{:S(2)}, u32[]{:S(2)}) collective-permute-start(bf16[128,256]{1,0:T(8,128)(2,1)S(1)} %get-tuple-element.25), channel_id=1, source_target_pairs={{0,24},{4,28},{8,16},{12,20},{16,8},{20,12},{24,0},{28,4},{1,25},{... | collective-permute-start | bytes 196616 | tf_op jit(solution)/shard_map/ppermute | solution.py:425
  18.6 1.4 %collective-permute-start.7 = (bf16[128,256]{1,0:T(8,128)(2,1)S(1)}, bf16[128,256]{1,0:T(8,128)(2,1)S(1)}, u32[]{:S(2)}, u32[]{:S(2)}) collective-permute-start(bf16[128,256]{1,0:T(8,128)(2,1)S(1)} %get-tuple-element.26), channel_id=1, source_target_pairs={{0,28},{4,24},{8,20},{12,16},{16,12},{20,8},{24,4},{28,0},{1,29},{... | collective-permute-start | bytes 196616 | tf_op jit(solution)/shard_map/ppermute | solution.py:425
  20.0 0.6 collective-permute-start.8
  20.6 0.8 %collective-permute-done.4.refs_2_ = bf16[128,256]{1,0:T(8,128)(2,1)S(1)} collective-permute-done((bf16[128,256]{1,0:T(8,128)(2,1)S(1)}, bf16[128,256]{1,0:T(8,128)(2,1)S(1)}, u32[]{:S(2)}, u32[]{:S(2)}) %collective-permute-start.4) | collective-permute-done | bytes 65568 | tf_op jit(solution)/shard_map/ppermute | solution.py:425
  21.4 5.3 %collective-permute-start.9 = (bf16[128,256]{1,0:T(8,128)(2,1)S(1)}, bf16[128,256]{1,0:T(8,128)(2,1)S(1)}, u32[]{:S(2)}, u32[]{:S(2)}) collective-permute-start(bf16[128,256]{1,0:T(8,128)(2,1)S(1)} %get-tuple-element.28), channel_id=1, source_target_pairs={{0,20},{4,16},{8,28},{12,24},{16,4},{20,0},{24,12},{28,8},{1,21},{... | collective-permute-start | bytes 196616 | tf_op jit(solution)/shard_map/ppermute | solution.py:425
  26.7 2.7 %gated_spectrum.1.gated_ref = f32[8,2,128,256]{3,2,1,0:T(8,128)S(1)} custom-call(bf16[32,64,128]{2,1,0:T(8,128)(2,1)S(1)} %all-to-all-done.gated_ref, bf16[768,256]{1,0:T(8,128)(2,1)S(1)} %copy-done.3, f32[8,2,256]{2,1,0:T(2,128)S(1)} %copy-done.5), custom_call_target="tpu_custom_call" | custom-call | flops 4294967296 | bytes 16777216 | tf_op jit(solution)/shard_map/gated_spectrum/pallas_call | solution.py:500
  29.4 1.0 %collective-permute-done.7.refs_5_ = bf16[128,256]{1,0:T(8,128)(2,1)S(1)} collective-permute-done((bf16[128,256]{1,0:T(8,128)(2,1)S(1)}, bf16[128,256]{1,0:T(8,128)(2,1)S(1)}, u32[]{:S(2)}, u32[]{:S(2)}) %collective-permute-start.7) | collective-permute-done | bytes 65568 | tf_op jit(solution)/shard_map/ppermute | solution.py:425
  30.5 5.0 %collective-permute-done.8.refs_6_ = bf16[128,256]{1,0:T(8,128)(2,1)S(1)} collective-permute-done((bf16[128,256]{1,0:T(8,128)(2,1)S(1)}, bf16[128,256]{1,0:T(8,128)(2,1)S(1)}, u32[]{:S(2)}, u32[]{:S(2)}) %collective-permute-start.8) | collective-permute-done | bytes 65568 | tf_op jit(solution)/shard_map/ppermute | solution.py:425
  35.5 1.8 %collective-permute-done.9.refs_7_ = bf16[128,256]{1,0:T(8,128)(2,1)S(1)} collective-permute-done((bf16[128,256]{1,0:T(8,128)(2,1)S(1)}, bf16[128,256]{1,0:T(8,128)(2,1)S(1)}, u32[]{:S(2)}, u32[]{:S(2)}) %collective-permute-start.9) | collective-permute-done | bytes 65568 | tf_op jit(solution)/shard_map/ppermute | solution.py:425
  37.3 4.8 %convolve.1 = bf16[8,128,256]{2,1,0:T(8,128)(2,1)} custom-call(f32[8,2,128,256]{3,2,1,0:T(8,128)S(1)} %gated_spectrum.1.gated_ref, bf16[128,256]{1,0:T(8,128)(2,1)S(1)} %get-tuple-element.21.refs_0_, bf16[128,256]{1,0:T(8,128)(2,1)S(1)} %collective-permute-done.3.refs_1_, bf16[128,256]{1,0:T(8,128)(2,1)S(1)} %collective-permute-done.4.refs_2_, ...), custom_call_target="tpu_custom_call" | custom-call | flops 4294967296 | bytes 16777216 | tf_op jit(solution)/shard_map/convolve/pallas_call | solution.py:508
  42.2 3.5 %all-to-all-start.1 = ((bf16[8,128,256]{2,1,0:T(8,128)(2,1)}), bf16[8,128,256]{2,1,0:T(8,128)(2,1)S(1)}, u32[]{:S(2)}, u32[]{:S(2)}) async-start(bf16[8,128,256]{2,1,0:T(8,128)(2,1)} %convolve.1), calls=%async_computation.1 | async-start | bytes 1048576 | tf_op jit(solution)/shard_map/all_to_all | solution.py:529
  46.0 1.5 %collective-permute-start.1 = (bf16[64,1024]{1,0:T(8,128)(2,1)S(1)}, bf16[64,1024]{1,0:T(8,128)(2,1)S(1)}, u32[]{:S(2)}, u32[]{:S(2)}) collective-permute-start(bf16[64,1024]{1,0:T(8,128)(2,1)S(1)} %get-tuple-element.19), channel_id=1, source_target_pairs={{0,2},{1,3},{2,0},{3,1},{4,6},{5,7},{6,4},{7,5},{8,10},{9,11},{10,... | collective-permute-start | bytes 393224 | tf_op jit(solution)/shard_map/ppermute | solution.py:425
  47.5 0.3 collective-permute-start.2
  47.8 4.5 %collective-permute-done.1.refs_2_ = bf16[64,1024]{1,0:T(8,128)(2,1)S(1)} collective-permute-done((bf16[64,1024]{1,0:T(8,128)(2,1)S(1)}, bf16[64,1024]{1,0:T(8,128)(2,1)S(1)}, u32[]{:S(2)}, u32[]{:S(2)}) %collective-permute-start.1) | collective-permute-done | bytes 131104 | tf_op jit(solution)/shard_map/ppermute | solution.py:425
  52.3 1.9 %collective-permute-done.2.refs_3_ = bf16[64,1024]{1,0:T(8,128)(2,1)S(1)} collective-permute-done((bf16[64,1024]{1,0:T(8,128)(2,1)S(1)}, bf16[64,1024]{1,0:T(8,128)(2,1)S(1)}, u32[]{:S(2)}, u32[]{:S(2)}) %collective-permute-start.2) | collective-permute-done | bytes 131104 | tf_op jit(solution)/shard_map/ppermute | solution.py:425
  54.2 0.3 turn_queries.1.query_ref
  54.5 5.7 %all-to-all-done.1.conv_ref = bf16[8,128,256]{2,1,0:T(8,128)(2,1)S(1)} async-done(((bf16[8,128,256]{2,1,0:T(8,128)(2,1)}), bf16[8,128,256]{2,1,0:T(8,128)(2,1)S(1)}, u32[]{:S(2)}, u32[]{:S(2)}) %all-to-all-start.1) | async-done | bytes 524320 | tf_op jit(solution)/shard_map/all_to_all | solution.py:529
  60.2 1.5 %mix_out.1 = bf16[1024,256]{1,0:T(8,128)(2,1)} custom-call(bf16[1024,256]{1,0:T(8,128)(2,1)S(1)} %turn_queries.1.query_ref, bf16[8,128,256]{2,1,0:T(8,128)(2,1)S(1)} %all-to-all-done.1.conv_ref), custom_call_target="tpu_custom_call" | custom-call | tf_op jit(solution)/shard_map/mix_out/pallas_call | solution.py:539
  (19 shorter events, 0.3 us)
Async XLA Ops:
  0.0 10.2 %copy-start.1 = (f32[1024,256]{1,0:T(8,128)S(1)}, f32[1024,256]{1,0:T(8,128)}, u32[]{:S(2)}) copy-start(f32[1024,256]{1,0:T(8,128)} %param.7) | copy-start | bytes 3145732
  0.0 10.2 %copy-start.2 = (f32[1024]{0:T(1024)S(1)}, f32[1024]{0:T(1024)}, u32[]{:S(2)}) copy-start(f32[1024]{0:T(1024)} %param.8) | copy-start | bytes 12292
  0.0 26.7 %copy-start.3 = (bf16[768,256]{1,0:T(8,128)(2,1)S(1)}, bf16[768,256]{1,0:T(8,128)(2,1)}, u32[]{:S(2)}) copy-start(bf16[768,256]{1,0:T(8,128)(2,1)} %constant.6.clone.wave_ref.refs_8_) | copy-start | bytes 1179652
  0.0 26.7 %copy-start.5 = (f32[8,2,256]{2,1,0:T(2,128)S(1)}, f32[8,2,256]{2,1,0:T(2,128)}, u32[]{:S(2)}) copy-start(f32[8,2,256]{2,1,0:T(2,128)} %constant.7.clone.twist_ref.refs_10_) | copy-start | bytes 49156
  2.9 23.8 %all-to-all-start = ((bf16[32,64,128]{2,1,0:T(8,128)(2,1)}), bf16[32,64,128]{2,1,0:T(8,128)(2,1)S(1)}, u32[]{:S(2)}, u32[]{:S(2)}) async-start(bf16[32,64,128]{2,1,0:T(8,128)(2,1)} %bitcast.8), calls=%async_computation | async-start | bytes 1048576 | tf_op jit(solution)/shard_map/all_to_all | solution.py:488
  11.4 8.6 %collective-permute-start.3 = (bf16[128,256]{1,0:T(8,128)(2,1)S(1)}, bf16[128,256]{1,0:T(8,128)(2,1)S(1)}, u32[]{:S(2)}, u32[]{:S(2)}) collective-permute-start(bf16[128,256]{1,0:T(8,128)(2,1)S(1)} %get-tuple-element.22), channel_id=1, source_target_pairs={{0,4},{4,0},{8,12},{12,8},{16,20},{20,16},{24,28},{28,24},{1,5},{5... | collective-permute-start | bytes 196616 | tf_op jit(solution)/shard_map/ppermute | solution.py:425
  13.2 8.1 %collective-permute-start.4 = (bf16[128,256]{1,0:T(8,128)(2,1)S(1)}, bf16[128,256]{1,0:T(8,128)(2,1)S(1)}, u32[]{:S(2)}, u32[]{:S(2)}) collective-permute-start(bf16[128,256]{1,0:T(8,128)(2,1)S(1)} %get-tuple-element.23), channel_id=1, source_target_pairs={{0,8},{4,12},{8,0},{12,4},{16,24},{20,28},{24,16},{28,20},{1,9},{5... | collective-permute-start | bytes 196616 | tf_op jit(solution)/shard_map/ppermute | solution.py:425
  14.7 14.7 %collective-permute-start.5 = (bf16[128,256]{1,0:T(8,128)(2,1)S(1)}, bf16[128,256]{1,0:T(8,128)(2,1)S(1)}, u32[]{:S(2)}, u32[]{:S(2)}) collective-permute-start(bf16[128,256]{1,0:T(8,128)(2,1)S(1)} %get-tuple-element.24), channel_id=1, source_target_pairs={{0,12},{4,8},{8,4},{12,0},{16,28},{20,24},{24,20},{28,16},{1,13},{... | collective-permute-start | bytes 196616 | tf_op jit(solution)/shard_map/ppermute | solution.py:425
  15.0 14.4 %collective-permute-start.6 = (bf16[128,256]{1,0:T(8,128)(2,1)S(1)}, bf16[128,256]{1,0:T(8,128)(2,1)S(1)}, u32[]{:S(2)}, u32[]{:S(2)}) collective-permute-start(bf16[128,256]{1,0:T(8,128)(2,1)S(1)} %get-tuple-element.25), channel_id=1, source_target_pairs={{0,24},{4,28},{8,16},{12,20},{16,8},{20,12},{24,0},{28,4},{1,25},{... | collective-permute-start | bytes 196616 | tf_op jit(solution)/shard_map/ppermute | solution.py:425
  18.6 11.9 %collective-permute-start.7 = (bf16[128,256]{1,0:T(8,128)(2,1)S(1)}, bf16[128,256]{1,0:T(8,128)(2,1)S(1)}, u32[]{:S(2)}, u32[]{:S(2)}) collective-permute-start(bf16[128,256]{1,0:T(8,128)(2,1)S(1)} %get-tuple-element.26), channel_id=1, source_target_pairs={{0,28},{4,24},{8,20},{12,16},{16,12},{20,8},{24,4},{28,0},{1,29},{... | collective-permute-start | bytes 196616 | tf_op jit(solution)/shard_map/ppermute | solution.py:425
  20.0 15.5 %collective-permute-start.8 = (bf16[128,256]{1,0:T(8,128)(2,1)S(1)}, bf16[128,256]{1,0:T(8,128)(2,1)S(1)}, u32[]{:S(2)}, u32[]{:S(2)}) collective-permute-start(bf16[128,256]{1,0:T(8,128)(2,1)S(1)} %get-tuple-element.27), channel_id=1, source_target_pairs={{0,16},{4,20},{8,24},{12,28},{16,0},{20,4},{24,8},{28,12},{1,17},{... | collective-permute-start | bytes 196616 | tf_op jit(solution)/shard_map/ppermute | solution.py:425
  21.4 15.9 %copy-start.4 = (bf16[768,256]{1,0:T(8,128)(2,1)S(1)}, bf16[768,256]{1,0:T(8,128)(2,1)}, u32[]{:S(2)}) copy-start(bf16[768,256]{1,0:T(8,128)(2,1)} %constant.8.clone.refs_9_) | copy-start | bytes 1179652
  21.4 15.9 %collective-permute-start.9 = (bf16[128,256]{1,0:T(8,128)(2,1)S(1)}, bf16[128,256]{1,0:T(8,128)(2,1)S(1)}, u32[]{:S(2)}, u32[]{:S(2)}) collective-permute-start(bf16[128,256]{1,0:T(8,128)(2,1)S(1)} %get-tuple-element.28), channel_id=1, source_target_pairs={{0,20},{4,16},{8,28},{12,24},{16,4},{20,0},{24,12},{28,8},{1,21},{... | collective-permute-start | bytes 196616 | tf_op jit(solution)/shard_map/ppermute | solution.py:425
  37.3 8.4 %copy-start = (bf16[64,3,4096]{2,0,1:T(8,128)(2,1)S(1)}, bf16[64,3,4096]{2,0,1:T(8,128)(2,1)}, u32[]{:S(2)}) copy-start(bf16[64,3,4096]{2,0,1:T(8,128)(2,1)} %param.6) | copy-start | bytes 4718596
  42.2 18.0 %all-to-all-start.1 = ((bf16[8,128,256]{2,1,0:T(8,128)(2,1)}), bf16[8,128,256]{2,1,0:T(8,128)(2,1)S(1)}, u32[]{:S(2)}, u32[]{:S(2)}) async-start(bf16[8,128,256]{2,1,0:T(8,128)(2,1)} %convolve.1), calls=%async_computation.1 | async-start | bytes 1048576 | tf_op jit(solution)/shard_map/all_to_all | solution.py:529
  45.9 1.9 %collective-permute-start = (bf16[64,1024]{1,0:T(8,128)(2,1)S(1)}, bf16[64,1024]{1,0:T(8,128)(2,1)S(1)}, u32[]{:S(2)}, u32[]{:S(2)}) collective-permute-start(bf16[64,1024]{1,0:T(8,128)(2,1)S(1)} %get-tuple-element.18), channel_id=1, source_target_pairs={{0,1},{1,0},{2,3},{3,2},{4,5},{5,4},{6,7},{7,6},{8,9},{9,8},{10,11... | collective-permute-start | bytes 393224 | tf_op jit(solution)/shard_map/ppermute | solution.py:425
  46.0 6.4 %collective-permute-start.1 = (bf16[64,1024]{1,0:T(8,128)(2,1)S(1)}, bf16[64,1024]{1,0:T(8,128)(2,1)S(1)}, u32[]{:S(2)}, u32[]{:S(2)}) collective-permute-start(bf16[64,1024]{1,0:T(8,128)(2,1)S(1)} %get-tuple-element.19), channel_id=1, source_target_pairs={{0,2},{1,3},{2,0},{3,1},{4,6},{5,7},{6,4},{7,5},{8,10},{9,11},{10,... | collective-permute-start | bytes 393224 | tf_op jit(solution)/shard_map/ppermute | solution.py:425
  47.5 6.7 %collective-permute-start.2 = (bf16[64,1024]{1,0:T(8,128)(2,1)S(1)}, bf16[64,1024]{1,0:T(8,128)(2,1)S(1)}, u32[]{:S(2)}, u32[]{:S(2)}) collective-permute-start(bf16[64,1024]{1,0:T(8,128)(2,1)S(1)} %get-tuple-element.20), channel_id=1, source_target_pairs={{0,3},{1,2},{2,1},{3,0},{4,7},{5,6},{6,5},{7,4},{8,11},{9,10},{10,... | collective-permute-start | bytes 393224 | tf_op jit(solution)/shard_map/ppermute | solution.py:425

commit v12 on v11

--- a/solution.py
+++ b/solution.py
@@ -416,7 +416,8 @@
 
 
 def turn_order(count):
-    return sorted(range(count), key=lambda turn: (turn > 3, -(turn // 2) if turn > 3 else 0, turn))
+    far = range(4, count, 2)
+    return [0, 1, 2, 3, *far, *(turn + 1 for turn in far)]
 
 
 def scatter(blocks, axis):

time: 62 us -> 60.6 us (0.977)
  waiting for transfers between devices: 20.8 us -> 19.7 us
    ppermute x10, waiting for transfers between devices: 15.1 us -> 14.4 us  [scatter(): lax.ppermute(block, axis, [(i, i ^ turn) for i in range(count)])]
  transfers between devices with their start and end apart: 12 -> 12, of which waited for: 7 -> 6; matrix products, arithmetic and copies ran while one was open for 0% -> 0% of each run, Pallas kernels for 7% -> 7%
where the time goes in v12:
time: 60.6 us; the launch traced here: 60.3 us
  starting transfers between devices  27 us (45%)
  waiting for transfers between devices  19.7 us (33%)
  Pallas kernels  13.5 us (22%)
    ppermute x10, starting transfers between devices, scatter(): lax.ppermute(block, axis, [(i, i ^ turn) for i in range(count)])  16.2 us
    ppermute x10, waiting for transfers between devices, scatter(): lax.ppermute(block, axis, [(i, i ^ turn) for i in range(count)])  14.4 us
    all_to_all x1, starting transfers between devices, body(): gated = exchange(gated, ('seq', 'ch'))  7.32 us
    all_to_all x1, waiting for transfers between devices, body(): convolved = exchange(convolved, 'seq')  5.26 us
    pallas_call x1, Pallas kernels, body(): pl.pallas_call(conv_kernel, out_shape=jax.ShapeDtypeStruct((blocks, own,...  4.85 us
    all_to_all x1, starting transfers between devices, body(): convolved = exchange(convolved, 'seq')  3.51 us
    pallas_call x1, Pallas kernels, body(): pl.pallas_call(send_kernel, in_specs=[far], out_specs=far, out_shape=jax....  2.84 us
    pallas_call x1, Pallas kernels, body(): pl.pallas_call(gated_spectrum_kernel, out_shape=jax.ShapeDtypeStruct((blo...  2.67 us
  transfers between devices with their start and end apart: 12, of which 6 were waited for; matrix products, arithmetic and copies ran while one was open for 0% of the time, Pallas kernels for 7%

profile of v12, /device:TPU:0, one launch (start us, length us, event | category | flops | bytes accessed | tf_op | source)
XLA Modules:
  0.0 60.3 jit_solution(15728870362093294851)
XLA Ops:
  0.0 2.8 %encode_gated.1 = bf16[8,4,64,128]{3,2,1,0:T(8,128)(2,1)} custom-call(bf16[3,64,4096]{2,1,0:T(8,128)(2,1)} %bitcast.4), custom_call_target="tpu_custom_call" | custom-call | flops 33554432 | bytes 8388608 | tf_op jit(solution)/shard_map/encode_gated/pallas_call | solution.py:445
  2.9 7.3 %all-to-all-start = ((bf16[32,64,128]{2,1,0:T(8,128)(2,1)}), bf16[32,64,128]{2,1,0:T(8,128)(2,1)S(1)}, u32[]{:S(2)}, u32[]{:S(2)}) async-start(bf16[32,64,128]{2,1,0:T(8,128)(2,1)} %bitcast.8), calls=%async_computation | async-start | bytes 1048576 | tf_op jit(solution)/shard_map/all_to_all | solution.py:489
  10.2 1.2 %encode_taps.1 = (bf16[128,256]{1,0:T(8,128)(2,1)S(1)}, bf16[128,256]{1,0:T(8,128)(2,1)S(1)}, bf16[128,256]{1,0:T(8,128)(2,1)S(1)}, bf16[128,256]{1,0:T(8,128)(2...) custom-call(f32[8,128,256]{2,1,0:T(8,128)S(1)} %bitcast.6, ...), custom_call_target="tpu_custom_call" | custom-call | flops 33554432 | bytes 8388608 | tf_op jit(solution)/shard_map/encode_taps/pallas_call | solution.py:471
  11.4 1.8 %collective-permute-start.3 = (bf16[128,256]{1,0:T(8,128)(2,1)S(1)}, bf16[128,256]{1,0:T(8,128)(2,1)S(1)}, u32[]{:S(2)}, u32[]{:S(2)}) collective-permute-start(bf16[128,256]{1,0:T(8,128)(2,1)S(1)} %get-tuple-element.22), channel_id=1, source_target_pairs={{0,4},{4,0},{8,12},{12,8},{16,20},{20,16},{24,28},{28,24},{1,5},{5... | collective-permute-start | bytes 196616 | tf_op jit(solution)/shard_map/ppermute | solution.py:426
  13.2 1.5 %collective-permute-start.4 = (bf16[128,256]{1,0:T(8,128)(2,1)S(1)}, bf16[128,256]{1,0:T(8,128)(2,1)S(1)}, u32[]{:S(2)}, u32[]{:S(2)}) collective-permute-start(bf16[128,256]{1,0:T(8,128)(2,1)S(1)} %get-tuple-element.23), channel_id=1, source_target_pairs={{0,8},{4,12},{8,0},{12,4},{16,24},{20,28},{24,16},{28,20},{1,9},{5... | collective-permute-start | bytes 196616 | tf_op jit(solution)/shard_map/ppermute | solution.py:426
  14.7 0.3 collective-permute-start.5
  15.0 2.7 %collective-permute-start.6 = (bf16[128,256]{1,0:T(8,128)(2,1)S(1)}, bf16[128,256]{1,0:T(8,128)(2,1)S(1)}, u32[]{:S(2)}, u32[]{:S(2)}) collective-permute-start(bf16[128,256]{1,0:T(8,128)(2,1)S(1)} %get-tuple-element.25), channel_id=1, source_target_pairs={{0,16},{4,20},{8,24},{12,28},{16,0},{20,4},{24,8},{28,12},{1,17},{... | collective-permute-start | bytes 196616 | tf_op jit(solution)/shard_map/ppermute | solution.py:426
  17.6 1.5 %collective-permute-start.7 = (bf16[128,256]{1,0:T(8,128)(2,1)S(1)}, bf16[128,256]{1,0:T(8,128)(2,1)S(1)}, u32[]{:S(2)}, u32[]{:S(2)}) collective-permute-start(bf16[128,256]{1,0:T(8,128)(2,1)S(1)} %get-tuple-element.26), channel_id=1, source_target_pairs={{0,24},{4,28},{8,16},{12,20},{16,8},{20,12},{24,0},{28,4},{1,25},{... | collective-permute-start | bytes 196616 | tf_op jit(solution)/shard_map/ppermute | solution.py:426
  19.1 2.4 %collective-permute-start.8 = (bf16[128,256]{1,0:T(8,128)(2,1)S(1)}, bf16[128,256]{1,0:T(8,128)(2,1)S(1)}, u32[]{:S(2)}, u32[]{:S(2)}) collective-permute-start(bf16[128,256]{1,0:T(8,128)(2,1)S(1)} %get-tuple-element.27), channel_id=1, source_target_pairs={{0,20},{4,16},{8,28},{12,24},{16,4},{20,0},{24,12},{28,8},{1,21},{... | collective-permute-start | bytes 196616 | tf_op jit(solution)/shard_map/ppermute | solution.py:426
  21.6 4.1 %collective-permute-start.9 = (bf16[128,256]{1,0:T(8,128)(2,1)S(1)}, bf16[128,256]{1,0:T(8,128)(2,1)S(1)}, u32[]{:S(2)}, u32[]{:S(2)}) collective-permute-start(bf16[128,256]{1,0:T(8,128)(2,1)S(1)} %get-tuple-element.28), channel_id=1, source_target_pairs={{0,28},{4,24},{8,20},{12,16},{16,12},{20,8},{24,4},{28,0},{1,29},{... | collective-permute-start | bytes 196616 | tf_op jit(solution)/shard_map/ppermute | solution.py:426
  25.7 2.7 %gated_spectrum.1.gated_ref = f32[8,2,128,256]{3,2,1,0:T(8,128)S(1)} custom-call(bf16[32,64,128]{2,1,0:T(8,128)(2,1)S(1)} %all-to-all-done.gated_ref, bf16[768,256]{1,0:T(8,128)(2,1)S(1)} %copy-done.3, f32[8,2,256]{2,1,0:T(2,128)S(1)} %copy-done.5), custom_call_target="tpu_custom_call" | custom-call | flops 4294967296 | bytes 16777216 | tf_op jit(solution)/shard_map/gated_spectrum/pallas_call | solution.py:501
  28.4 4.3 %collective-permute-done.6.refs_4_ = bf16[128,256]{1,0:T(8,128)(2,1)S(1)} collective-permute-done((bf16[128,256]{1,0:T(8,128)(2,1)S(1)}, bf16[128,256]{1,0:T(8,128)(2,1)S(1)}, u32[]{:S(2)}, u32[]{:S(2)}) %collective-permute-start.6) | collective-permute-done | bytes 65568 | tf_op jit(solution)/shard_map/ppermute | solution.py:426
  32.7 3.7 %collective-permute-done.8.refs_6_ = bf16[128,256]{1,0:T(8,128)(2,1)S(1)} collective-permute-done((bf16[128,256]{1,0:T(8,128)(2,1)S(1)}, bf16[128,256]{1,0:T(8,128)(2,1)S(1)}, u32[]{:S(2)}, u32[]{:S(2)}) %collective-permute-start.8) | collective-permute-done | bytes 65568 | tf_op jit(solution)/shard_map/ppermute | solution.py:426
  36.4 4.9 %convolve.1 = bf16[8,128,256]{2,1,0:T(8,128)(2,1)} custom-call(f32[8,2,128,256]{3,2,1,0:T(8,128)S(1)} %gated_spectrum.1.gated_ref, bf16[128,256]{1,0:T(8,128)(2,1)S(1)} %get-tuple-element.21.refs_0_, bf16[128,256]{1,0:T(8,128)(2,1)S(1)} %collective-permute-done.3.refs_1_, bf16[128,256]{1,0:T(8,128)(2,1)S(1)} %collective-permute-done.4.refs_2_, ...), custom_call_target="tpu_custom_call" | custom-call | flops 4294967296 | bytes 16777216 | tf_op jit(solution)/shard_map/convolve/pallas_call | solution.py:509
  41.3 3.5 %all-to-all-start.1 = ((bf16[8,128,256]{2,1,0:T(8,128)(2,1)}), bf16[8,128,256]{2,1,0:T(8,128)(2,1)S(1)}, u32[]{:S(2)}, u32[]{:S(2)}) async-start(bf16[8,128,256]{2,1,0:T(8,128)(2,1)} %convolve.1), calls=%async_computation.1 | async-start | bytes 1048576 | tf_op jit(solution)/shard_map/all_to_all | solution.py:530
  44.8 0.1 send_queries.1
  45.0 0.1 collective-permute-start
  45.0 1.6 %collective-permute-start.1 = (bf16[64,1024]{1,0:T(8,128)(2,1)S(1)}, bf16[64,1024]{1,0:T(8,128)(2,1)S(1)}, u32[]{:S(2)}, u32[]{:S(2)}) collective-permute-start(bf16[64,1024]{1,0:T(8,128)(2,1)S(1)} %get-tuple-element.19), channel_id=1, source_target_pairs={{0,2},{1,3},{2,0},{3,1},{4,6},{5,7},{6,4},{7,5},{8,10},{9,11},{10,... | collective-permute-start | bytes 393224 | tf_op jit(solution)/shard_map/ppermute | solution.py:426
  46.6 0.3 collective-permute-start.2
  46.9 4.5 %collective-permute-done.1.refs_2_ = bf16[64,1024]{1,0:T(8,128)(2,1)S(1)} collective-permute-done((bf16[64,1024]{1,0:T(8,128)(2,1)S(1)}, bf16[64,1024]{1,0:T(8,128)(2,1)S(1)}, u32[]{:S(2)}, u32[]{:S(2)}) %collective-permute-start.1) | collective-permute-done | bytes 131104 | tf_op jit(solution)/shard_map/ppermute | solution.py:426
  51.4 1.9 %collective-permute-done.2.refs_3_ = bf16[64,1024]{1,0:T(8,128)(2,1)S(1)} collective-permute-done((bf16[64,1024]{1,0:T(8,128)(2,1)S(1)}, bf16[64,1024]{1,0:T(8,128)(2,1)S(1)}, u32[]{:S(2)}, u32[]{:S(2)}) %collective-permute-start.2) | collective-permute-done | bytes 131104 | tf_op jit(solution)/shard_map/ppermute | solution.py:426
  53.3 0.3 turn_queries.1.query_ref
  53.6 5.3 %all-to-all-done.1.conv_ref = bf16[8,128,256]{2,1,0:T(8,128)(2,1)S(1)} async-done(((bf16[8,128,256]{2,1,0:T(8,128)(2,1)}), bf16[8,128,256]{2,1,0:T(8,128)(2,1)S(1)}, u32[]{:S(2)}, u32[]{:S(2)}) %all-to-all-start.1) | async-done | bytes 524320 | tf_op jit(solution)/shard_map/all_to_all | solution.py:530
  58.8 1.5 %mix_out.1 = bf16[1024,256]{1,0:T(8,128)(2,1)} custom-call(bf16[1024,256]{1,0:T(8,128)(2,1)S(1)} %turn_queries.1.query_ref, bf16[8,128,256]{2,1,0:T(8,128)(2,1)S(1)} %all-to-all-done.1.conv_ref), custom_call_target="tpu_custom_call" | custom-call | tf_op jit(solution)/shard_map/mix_out/pallas_call | solution.py:540
  (19 shorter events, 0.1 us)
Async XLA Ops:
  0.0 10.2 %copy-start.1 = (f32[1024,256]{1,0:T(8,128)S(1)}, f32[1024,256]{1,0:T(8,128)}, u32[]{:S(2)}) copy-start(f32[1024,256]{1,0:T(8,128)} %param.7) | copy-start | bytes 3145732
  0.0 10.2 %copy-start.2 = (f32[1024]{0:T(1024)S(1)}, f32[1024]{0:T(1024)}, u32[]{:S(2)}) copy-start(f32[1024]{0:T(1024)} %param.8) | copy-start | bytes 12292
  0.0 25.7 %copy-start.3 = (bf16[768,256]{1,0:T(8,128)(2,1)S(1)}, bf16[768,256]{1,0:T(8,128)(2,1)}, u32[]{:S(2)}) copy-start(bf16[768,256]{1,0:T(8,128)(2,1)} %constant.6.clone.wave_ref.refs_8_) | copy-start | bytes 1179652
  0.0 25.7 %copy-start.5 = (f32[8,2,256]{2,1,0:T(2,128)S(1)}, f32[8,2,256]{2,1,0:T(2,128)}, u32[]{:S(2)}) copy-start(f32[8,2,256]{2,1,0:T(2,128)} %constant.7.clone.twist_ref.refs_10_) | copy-start | bytes 49156
  2.9 22.9 %all-to-all-start = ((bf16[32,64,128]{2,1,0:T(8,128)(2,1)}), bf16[32,64,128]{2,1,0:T(8,128)(2,1)S(1)}, u32[]{:S(2)}, u32[]{:S(2)}) async-start(bf16[32,64,128]{2,1,0:T(8,128)(2,1)} %bitcast.8), calls=%async_computation | async-start | bytes 1048576 | tf_op jit(solution)/shard_map/all_to_all | solution.py:489
  11.4 7.7 %collective-permute-start.3 = (bf16[128,256]{1,0:T(8,128)(2,1)S(1)}, bf16[128,256]{1,0:T(8,128)(2,1)S(1)}, u32[]{:S(2)}, u32[]{:S(2)}) collective-permute-start(bf16[128,256]{1,0:T(8,128)(2,1)S(1)} %get-tuple-element.22), channel_id=1, source_target_pairs={{0,4},{4,0},{8,12},{12,8},{16,20},{20,16},{24,28},{28,24},{1,5},{5... | collective-permute-start | bytes 196616 | tf_op jit(solution)/shard_map/ppermute | solution.py:426
  13.2 8.3 %collective-permute-start.4 = (bf16[128,256]{1,0:T(8,128)(2,1)S(1)}, bf16[128,256]{1,0:T(8,128)(2,1)S(1)}, u32[]{:S(2)}, u32[]{:S(2)}) collective-permute-start(bf16[128,256]{1,0:T(8,128)(2,1)S(1)} %get-tuple-element.23), channel_id=1, source_target_pairs={{0,8},{4,12},{8,0},{12,4},{16,24},{20,28},{24,16},{28,20},{1,9},{5... | collective-permute-start | bytes 196616 | tf_op jit(solution)/shard_map/ppermute | solution.py:426
  14.7 13.7 %collective-permute-start.5 = (bf16[128,256]{1,0:T(8,128)(2,1)S(1)}, bf16[128,256]{1,0:T(8,128)(2,1)S(1)}, u32[]{:S(2)}, u32[]{:S(2)}) collective-permute-start(bf16[128,256]{1,0:T(8,128)(2,1)S(1)} %get-tuple-element.24), channel_id=1, source_target_pairs={{0,12},{4,8},{8,4},{12,0},{16,28},{20,24},{24,20},{28,16},{1,13},{... | collective-permute-start | bytes 196616 | tf_op jit(solution)/shard_map/ppermute | solution.py:426
  15.0 17.7 %collective-permute-start.6 = (bf16[128,256]{1,0:T(8,128)(2,1)S(1)}, bf16[128,256]{1,0:T(8,128)(2,1)S(1)}, u32[]{:S(2)}, u32[]{:S(2)}) collective-permute-start(bf16[128,256]{1,0:T(8,128)(2,1)S(1)} %get-tuple-element.25), channel_id=1, source_target_pairs={{0,16},{4,20},{8,24},{12,28},{16,0},{20,4},{24,8},{28,12},{1,17},{... | collective-permute-start | bytes 196616 | tf_op jit(solution)/shard_map/ppermute | solution.py:426
  17.6 15.0 %collective-permute-start.7 = (bf16[128,256]{1,0:T(8,128)(2,1)S(1)}, bf16[128,256]{1,0:T(8,128)(2,1)S(1)}, u32[]{:S(2)}, u32[]{:S(2)}) collective-permute-start(bf16[128,256]{1,0:T(8,128)(2,1)S(1)} %get-tuple-element.26), channel_id=1, source_target_pairs={{0,24},{4,28},{8,16},{12,20},{16,8},{20,12},{24,0},{28,4},{1,25},{... | collective-permute-start | bytes 196616 | tf_op jit(solution)/shard_map/ppermute | solution.py:426
  19.1 17.3 %collective-permute-start.8 = (bf16[128,256]{1,0:T(8,128)(2,1)S(1)}, bf16[128,256]{1,0:T(8,128)(2,1)S(1)}, u32[]{:S(2)}, u32[]{:S(2)}) collective-permute-start(bf16[128,256]{1,0:T(8,128)(2,1)S(1)} %get-tuple-element.27), channel_id=1, source_target_pairs={{0,20},{4,16},{8,28},{12,24},{16,4},{20,0},{24,12},{28,8},{1,21},{... | collective-permute-start | bytes 196616 | tf_op jit(solution)/shard_map/ppermute | solution.py:426
  21.6 14.9 %copy-start.4 = (bf16[768,256]{1,0:T(8,128)(2,1)S(1)}, bf16[768,256]{1,0:T(8,128)(2,1)}, u32[]{:S(2)}) copy-start(bf16[768,256]{1,0:T(8,128)(2,1)} %constant.8.clone.refs_9_) | copy-start | bytes 1179652
  21.6 14.8 %collective-permute-start.9 = (bf16[128,256]{1,0:T(8,128)(2,1)S(1)}, bf16[128,256]{1,0:T(8,128)(2,1)S(1)}, u32[]{:S(2)}, u32[]{:S(2)}) collective-permute-start(bf16[128,256]{1,0:T(8,128)(2,1)S(1)} %get-tuple-element.28), channel_id=1, source_target_pairs={{0,28},{4,24},{8,20},{12,16},{16,12},{20,8},{24,4},{28,0},{1,29},{... | collective-permute-start | bytes 196616 | tf_op jit(solution)/shard_map/ppermute | solution.py:426
  36.4 8.4 %copy-start = (bf16[64,3,4096]{2,0,1:T(8,128)(2,1)S(1)}, bf16[64,3,4096]{2,0,1:T(8,128)(2,1)}, u32[]{:S(2)}) copy-start(bf16[64,3,4096]{2,0,1:T(8,128)(2,1)} %param.6) | copy-start | bytes 4718596
  41.3 17.6 %all-to-all-start.1 = ((bf16[8,128,256]{2,1,0:T(8,128)(2,1)}), bf16[8,128,256]{2,1,0:T(8,128)(2,1)S(1)}, u32[]{:S(2)}, u32[]{:S(2)}) async-start(bf16[8,128,256]{2,1,0:T(8,128)(2,1)} %convolve.1), calls=%async_computation.1 | async-start | bytes 1048576 | tf_op jit(solution)/shard_map/all_to_all | solution.py:530
  45.0 1.9 %collective-permute-start = (bf16[64,1024]{1,0:T(8,128)(2,1)S(1)}, bf16[64,1024]{1,0:T(8,128)(2,1)S(1)}, u32[]{:S(2)}, u32[]{:S(2)}) collective-permute-start(bf16[64,1024]{1,0:T(8,128)(2,1)S(1)} %get-tuple-element.18), channel_id=1, source_target_pairs={{0,1},{1,0},{2,3},{3,2},{4,5},{5,4},{6,7},{7,6},{8,9},{9,8},{10,11... | collective-permute-start | bytes 393224 | tf_op jit(solution)/shard_map/ppermute | solution.py:426
  45.0 6.4 %collective-permute-start.1 = (bf16[64,1024]{1,0:T(8,128)(2,1)S(1)}, bf16[64,1024]{1,0:T(8,128)(2,1)S(1)}, u32[]{:S(2)}, u32[]{:S(2)}) collective-permute-start(bf16[64,1024]{1,0:T(8,128)(2,1)S(1)} %get-tuple-element.19), channel_id=1, source_target_pairs={{0,2},{1,3},{2,0},{3,1},{4,6},{5,7},{6,4},{7,5},{8,10},{9,11},{10,... | collective-permute-start | bytes 393224 | tf_op jit(solution)/shard_map/ppermute | solution.py:426
  46.6 6.7 %collective-permute-start.2 = (bf16[64,1024]{1,0:T(8,128)(2,1)S(1)}, bf16[64,1024]{1,0:T(8,128)(2,1)S(1)}, u32[]{:S(2)}, u32[]{:S(2)}) collective-permute-start(bf16[64,1024]{1,0:T(8,128)(2,1)S(1)} %get-tuple-element.20), channel_id=1, source_target_pairs={{0,3},{1,2},{2,1},{3,0},{4,7},{5,6},{6,5},{7,4},{8,11},{9,10},{10,... | collective-permute-start | bytes 393224 | tf_op jit(solution)/shard_map/ppermute | solution.py:426

commit v13 on v12

--- a/solution.py
+++ b/solution.py
@@ -204,7 +204,7 @@
 
 
 def send_kernel(streams_ref, gated_ref, keys, values, codes, in_sems, out_sems):
-    groups, parts = gated_ref.shape[:2]
+    parts, groups = gated_ref.shape[:2]
     per = groups
     width = per * LANES
     arrivals = []
@@ -220,14 +220,12 @@
     for chunk in range(parts):
         for copy in arrivals[2 * chunk : 2 * chunk + 2]:
             copy.wait()
-        part, first = chunk, 0
         for block in range(per):
             lanes = slice(block * LANES, (block + 1) * LANES)
             left = keys[chunk, :, lanes].astype(jnp.float32)
             right = values[chunk, :, lanes].astype(jnp.float32)
-            codes[first + block, part] = encode(left * right, 0)
-        place = (pl.ds(first, per), part)
-        copy = pltpu.make_async_copy(codes.at[place], gated_ref.at[place], out_sems.at[chunk])
+            codes[chunk, block] = encode(left * right, 0)
+        copy = pltpu.make_async_copy(codes.at[chunk], gated_ref.at[chunk], out_sems.at[chunk])
         copy.start()
         copies.append(copy)
     for copy in copies:
@@ -294,7 +292,7 @@
     groups = row_groups()
 
     def unpack(block, _):
-        pieces = [decode(gated_ref[block * parts + part], 0) for part in range(parts)]
+        pieces = [decode(gated_ref[part * blocks + block], 0) for part in range(parts)]
         u[block] = jnp.transpose(jnp.concatenate(pieces, axis=0))
         return 0
 
@@ -440,7 +438,7 @@
     small = pltpu.CompilerParams(vmem_limit_bytes=SMALL_BYTES)
     if fits:
         far = pl.BlockSpec(memory_space=pl.ANY)
-        coded = (groups, parts, held, own)
+        coded = (parts, groups, held, own)
         stream = pltpu.VMEM((parts, held, wide), jnp.bfloat16)
         gated = pl.pallas_call(
             send_kernel,
@@ -486,7 +484,7 @@
     gated = gated.reshape(groups * parts, held, own)
     if fits:
         taps = scatter(taps, "seq")
-        gated = exchange(gated, ("seq", "ch"))
+        gated = exchange(gated, ("ch", "seq"))
         queries = scatter(queries, "ch")
     else:
         taps = exchange(taps, "seq")

time: 60.6 us -> 60.6 us (level)
    all_to_all x1, waiting for transfers between devices: 0.05 us -> 0.86 us  [body(): gated = exchange(gated, ('ch', 'seq'))]
    ppermute x10, waiting for transfers between devices: 14.4 us -> 13.6 us  [scatter(): lax.ppermute(block, axis, [(i, i ^ turn) for i in range(count)])]
where the time goes in v13:
time: 60.6 us; the launch traced here: 60.3 us
  starting transfers between devices  27 us (45%)
  waiting for transfers between devices  19.7 us (33%)
  Pallas kernels  13.5 us (22%)
    ppermute x10, starting transfers between devices, scatter(): lax.ppermute(block, axis, [(i, i ^ turn) for i in range(count)])  16.2 us
    ppermute x10, waiting for transfers between devices, scatter(): lax.ppermute(block, axis, [(i, i ^ turn) for i in range(count)])  13.6 us
    all_to_all x1, starting transfers between devices, body(): gated = exchange(gated, ('ch', 'seq'))  7.32 us
    all_to_all x1, waiting for transfers between devices, body(): convolved = exchange(convolved, 'seq')  5.26 us
    pallas_call x1, Pallas kernels, body(): pl.pallas_call(conv_kernel, out_shape=jax.ShapeDtypeStruct((blocks, own,...  4.86 us
    all_to_all x1, starting transfers between devices, body(): convolved = exchange(convolved, 'seq')  3.51 us
    pallas_call x1, Pallas kernels, body(): pl.pallas_call(send_kernel, in_specs=[far], out_specs=far, out_shape=jax....  2.84 us
    pallas_call x1, Pallas kernels, body(): pl.pallas_call(gated_spectrum_kernel, out_shape=jax.ShapeDtypeStruct((blo...  2.67 us
  transfers between devices with their start and end apart: 12, of which 6 were waited for; matrix products, arithmetic and copies ran while one was open for 0% of the time, Pallas kernels for 7%

profile of v13, /device:TPU:0, one launch (start us, length us, event | category | flops | bytes accessed | tf_op | source)
XLA Modules:
  0.0 60.3 jit_solution(2387340680570376268)
XLA Ops:
  0.0 2.8 %encode_gated.1 = bf16[4,8,64,128]{3,2,1,0:T(8,128)(2,1)} custom-call(bf16[3,64,4096]{2,1,0:T(8,128)(2,1)} %bitcast.4), custom_call_target="tpu_custom_call" | custom-call | flops 33554432 | bytes 8388608 | tf_op jit(solution)/shard_map/encode_gated/pallas_call | solution.py:443
  2.9 7.3 %all-to-all-start = ((bf16[32,64,128]{2,1,0:T(8,128)(2,1)}), bf16[32,64,128]{2,1,0:T(8,128)(2,1)S(1)}, u32[]{:S(2)}, u32[]{:S(2)}) async-start(bf16[32,64,128]{2,1,0:T(8,128)(2,1)} %bitcast.8), calls=%async_computation | async-start | bytes 1048576 | tf_op jit(solution)/shard_map/all_to_all | solution.py:487
  10.2 1.2 %encode_taps.1 = (bf16[128,256]{1,0:T(8,128)(2,1)S(1)}, bf16[128,256]{1,0:T(8,128)(2,1)S(1)}, bf16[128,256]{1,0:T(8,128)(2,1)S(1)}, bf16[128,256]{1,0:T(8,128)(2...) custom-call(f32[8,128,256]{2,1,0:T(8,128)S(1)} %bitcast.6, ...), custom_call_target="tpu_custom_call" | custom-call | flops 33554432 | bytes 8388608 | tf_op jit(solution)/shard_map/encode_taps/pallas_call | solution.py:469
  11.4 1.8 %collective-permute-start.3 = (bf16[128,256]{1,0:T(8,128)(2,1)S(1)}, bf16[128,256]{1,0:T(8,128)(2,1)S(1)}, u32[]{:S(2)}, u32[]{:S(2)}) collective-permute-start(bf16[128,256]{1,0:T(8,128)(2,1)S(1)} %get-tuple-element.22), channel_id=1, source_target_pairs={{0,4},{4,0},{8,12},{12,8},{16,20},{20,16},{24,28},{28,24},{1,5},{5... | collective-permute-start | bytes 196616 | tf_op jit(solution)/shard_map/ppermute | solution.py:424
  13.2 1.5 %collective-permute-start.4 = (bf16[128,256]{1,0:T(8,128)(2,1)S(1)}, bf16[128,256]{1,0:T(8,128)(2,1)S(1)}, u32[]{:S(2)}, u32[]{:S(2)}) collective-permute-start(bf16[128,256]{1,0:T(8,128)(2,1)S(1)} %get-tuple-element.23), channel_id=1, source_target_pairs={{0,8},{4,12},{8,0},{12,4},{16,24},{20,28},{24,16},{28,20},{1,9},{5... | collective-permute-start | bytes 196616 | tf_op jit(solution)/shard_map/ppermute | solution.py:424
  14.7 0.3 collective-permute-start.5
  15.0 2.7 %collective-permute-start.6 = (bf16[128,256]{1,0:T(8,128)(2,1)S(1)}, bf16[128,256]{1,0:T(8,128)(2,1)S(1)}, u32[]{:S(2)}, u32[]{:S(2)}) collective-permute-start(bf16[128,256]{1,0:T(8,128)(2,1)S(1)} %get-tuple-element.25), channel_id=1, source_target_pairs={{0,16},{4,20},{8,24},{12,28},{16,0},{20,4},{24,8},{28,12},{1,17},{... | collective-permute-start | bytes 196616 | tf_op jit(solution)/shard_map/ppermute | solution.py:424
  17.6 1.5 %collective-permute-start.7 = (bf16[128,256]{1,0:T(8,128)(2,1)S(1)}, bf16[128,256]{1,0:T(8,128)(2,1)S(1)}, u32[]{:S(2)}, u32[]{:S(2)}) collective-permute-start(bf16[128,256]{1,0:T(8,128)(2,1)S(1)} %get-tuple-element.26), channel_id=1, source_target_pairs={{0,24},{4,28},{8,16},{12,20},{16,8},{20,12},{24,0},{28,4},{1,25},{... | collective-permute-start | bytes 196616 | tf_op jit(solution)/shard_map/ppermute | solution.py:424
  19.1 2.4 %collective-permute-start.8 = (bf16[128,256]{1,0:T(8,128)(2,1)S(1)}, bf16[128,256]{1,0:T(8,128)(2,1)S(1)}, u32[]{:S(2)}, u32[]{:S(2)}) collective-permute-start(bf16[128,256]{1,0:T(8,128)(2,1)S(1)} %get-tuple-element.27), channel_id=1, source_target_pairs={{0,20},{4,16},{8,28},{12,24},{16,4},{20,0},{24,12},{28,8},{1,21},{... | collective-permute-start | bytes 196616 | tf_op jit(solution)/shard_map/ppermute | solution.py:424
  21.6 4.1 %collective-permute-start.9 = (bf16[128,256]{1,0:T(8,128)(2,1)S(1)}, bf16[128,256]{1,0:T(8,128)(2,1)S(1)}, u32[]{:S(2)}, u32[]{:S(2)}) collective-permute-start(bf16[128,256]{1,0:T(8,128)(2,1)S(1)} %get-tuple-element.28), channel_id=1, source_target_pairs={{0,28},{4,24},{8,20},{12,16},{16,12},{20,8},{24,4},{28,0},{1,29},{... | collective-permute-start | bytes 196616 | tf_op jit(solution)/shard_map/ppermute | solution.py:424
  25.7 0.9 %all-to-all-done.gated_ref = bf16[32,64,128]{2,1,0:T(8,128)(2,1)S(1)} async-done(((bf16[32,64,128]{2,1,0:T(8,128)(2,1)}), bf16[32,64,128]{2,1,0:T(8,128)(2,1)S(1)}, u32[]{:S(2)}, u32[]{:S(2)}) %all-to-all-start) | async-done | bytes 524320 | tf_op jit(solution)/shard_map/all_to_all | solution.py:487
  26.5 2.7 %gated_spectrum.1.gated_ref = f32[8,2,128,256]{3,2,1,0:T(8,128)S(1)} custom-call(bf16[32,64,128]{2,1,0:T(8,128)(2,1)S(1)} %all-to-all-done.gated_ref, bf16[768,256]{1,0:T(8,128)(2,1)S(1)} %copy-done.3, f32[8,2,256]{2,1,0:T(2,128)S(1)} %copy-done.5), custom_call_target="tpu_custom_call" | custom-call | flops 4294967296 | bytes 16777216 | tf_op jit(solution)/shard_map/gated_spectrum/pallas_call | solution.py:499
  29.2 3.5 %collective-permute-done.6.refs_4_ = bf16[128,256]{1,0:T(8,128)(2,1)S(1)} collective-permute-done((bf16[128,256]{1,0:T(8,128)(2,1)S(1)}, bf16[128,256]{1,0:T(8,128)(2,1)S(1)}, u32[]{:S(2)}, u32[]{:S(2)}) %collective-permute-start.6) | collective-permute-done | bytes 65568 | tf_op jit(solution)/shard_map/ppermute | solution.py:424
  32.7 3.7 %collective-permute-done.8.refs_6_ = bf16[128,256]{1,0:T(8,128)(2,1)S(1)} collective-permute-done((bf16[128,256]{1,0:T(8,128)(2,1)S(1)}, bf16[128,256]{1,0:T(8,128)(2,1)S(1)}, u32[]{:S(2)}, u32[]{:S(2)}) %collective-permute-start.8) | collective-permute-done | bytes 65568 | tf_op jit(solution)/shard_map/ppermute | solution.py:424
  36.4 4.9 %convolve.1 = bf16[8,128,256]{2,1,0:T(8,128)(2,1)} custom-call(f32[8,2,128,256]{3,2,1,0:T(8,128)S(1)} %gated_spectrum.1.gated_ref, bf16[128,256]{1,0:T(8,128)(2,1)S(1)} %get-tuple-element.21.refs_0_, bf16[128,256]{1,0:T(8,128)(2,1)S(1)} %collective-permute-done.3.refs_1_, bf16[128,256]{1,0:T(8,128)(2,1)S(1)} %collective-permute-done.4.refs_2_, ...), custom_call_target="tpu_custom_call" | custom-call | flops 4294967296 | bytes 16777216 | tf_op jit(solution)/shard_map/convolve/pallas_call | solution.py:507
  41.3 3.5 %all-to-all-start.1 = ((bf16[8,128,256]{2,1,0:T(8,128)(2,1)}), bf16[8,128,256]{2,1,0:T(8,128)(2,1)S(1)}, u32[]{:S(2)}, u32[]{:S(2)}) async-start(bf16[8,128,256]{2,1,0:T(8,128)(2,1)} %convolve.1), calls=%async_computation.1 | async-start | bytes 1048576 | tf_op jit(solution)/shard_map/all_to_all | solution.py:528
  44.8 0.1 send_queries.1
  45.0 1.5 %collective-permute-start.1 = (bf16[64,1024]{1,0:T(8,128)(2,1)S(1)}, bf16[64,1024]{1,0:T(8,128)(2,1)S(1)}, u32[]{:S(2)}, u32[]{:S(2)}) collective-permute-start(bf16[64,1024]{1,0:T(8,128)(2,1)S(1)} %get-tuple-element.19), channel_id=1, source_target_pairs={{0,2},{1,3},{2,0},{3,1},{4,6},{5,7},{6,4},{7,5},{8,10},{9,11},{10,... | collective-permute-start | bytes 393224 | tf_op jit(solution)/shard_map/ppermute | solution.py:424
  46.6 0.3 collective-permute-start.2
  46.9 4.5 %collective-permute-done.1.refs_2_ = bf16[64,1024]{1,0:T(8,128)(2,1)S(1)} collective-permute-done((bf16[64,1024]{1,0:T(8,128)(2,1)S(1)}, bf16[64,1024]{1,0:T(8,128)(2,1)S(1)}, u32[]{:S(2)}, u32[]{:S(2)}) %collective-permute-start.1) | collective-permute-done | bytes 131104 | tf_op jit(solution)/shard_map/ppermute | solution.py:424
  51.4 1.9 %collective-permute-done.2.refs_3_ = bf16[64,1024]{1,0:T(8,128)(2,1)S(1)} collective-permute-done((bf16[64,1024]{1,0:T(8,128)(2,1)S(1)}, bf16[64,1024]{1,0:T(8,128)(2,1)S(1)}, u32[]{:S(2)}, u32[]{:S(2)}) %collective-permute-start.2) | collective-permute-done | bytes 131104 | tf_op jit(solution)/shard_map/ppermute | solution.py:424
  53.3 0.3 turn_queries.1.query_ref
  53.6 5.3 %all-to-all-done.1.conv_ref = bf16[8,128,256]{2,1,0:T(8,128)(2,1)S(1)} async-done(((bf16[8,128,256]{2,1,0:T(8,128)(2,1)}), bf16[8,128,256]{2,1,0:T(8,128)(2,1)S(1)}, u32[]{:S(2)}, u32[]{:S(2)}) %all-to-all-start.1) | async-done | bytes 524320 | tf_op jit(solution)/shard_map/all_to_all | solution.py:528
  58.8 1.5 %mix_out.1 = bf16[1024,256]{1,0:T(8,128)(2,1)} custom-call(bf16[1024,256]{1,0:T(8,128)(2,1)S(1)} %turn_queries.1.query_ref, bf16[8,128,256]{2,1,0:T(8,128)(2,1)S(1)} %all-to-all-done.1.conv_ref), custom_call_target="tpu_custom_call" | custom-call | tf_op jit(solution)/shard_map/mix_out/pallas_call | solution.py:538
  (19 shorter events, 0.1 us)
Async XLA Ops:
  0.0 10.2 %copy-start.1 = (f32[1024,256]{1,0:T(8,128)S(1)}, f32[1024,256]{1,0:T(8,128)}, u32[]{:S(2)}) copy-start(f32[1024,256]{1,0:T(8,128)} %param.7) | copy-start | bytes 3145732
  0.0 10.2 %copy-start.2 = (f32[1024]{0:T(1024)S(1)}, f32[1024]{0:T(1024)}, u32[]{:S(2)}) copy-start(f32[1024]{0:T(1024)} %param.8) | copy-start | bytes 12292
  0.0 26.5 %copy-start.3 = (bf16[768,256]{1,0:T(8,128)(2,1)S(1)}, bf16[768,256]{1,0:T(8,128)(2,1)}, u32[]{:S(2)}) copy-start(bf16[768,256]{1,0:T(8,128)(2,1)} %constant.6.clone.wave_ref.refs_8_) | copy-start | bytes 1179652
  0.0 26.5 %copy-start.5 = (f32[8,2,256]{2,1,0:T(2,128)S(1)}, f32[8,2,256]{2,1,0:T(2,128)}, u32[]{:S(2)}) copy-start(f32[8,2,256]{2,1,0:T(2,128)} %constant.7.clone.twist_ref.refs_10_) | copy-start | bytes 49156
  2.9 23.7 %all-to-all-start = ((bf16[32,64,128]{2,1,0:T(8,128)(2,1)}), bf16[32,64,128]{2,1,0:T(8,128)(2,1)S(1)}, u32[]{:S(2)}, u32[]{:S(2)}) async-start(bf16[32,64,128]{2,1,0:T(8,128)(2,1)} %bitcast.8), calls=%async_computation | async-start | bytes 1048576 | tf_op jit(solution)/shard_map/all_to_all | solution.py:487
  11.4 7.7 %collective-permute-start.3 = (bf16[128,256]{1,0:T(8,128)(2,1)S(1)}, bf16[128,256]{1,0:T(8,128)(2,1)S(1)}, u32[]{:S(2)}, u32[]{:S(2)}) collective-permute-start(bf16[128,256]{1,0:T(8,128)(2,1)S(1)} %get-tuple-element.22), channel_id=1, source_target_pairs={{0,4},{4,0},{8,12},{12,8},{16,20},{20,16},{24,28},{28,24},{1,5},{5... | collective-permute-start | bytes 196616 | tf_op jit(solution)/shard_map/ppermute | solution.py:424
  13.2 8.3 %collective-permute-start.4 = (bf16[128,256]{1,0:T(8,128)(2,1)S(1)}, bf16[128,256]{1,0:T(8,128)(2,1)S(1)}, u32[]{:S(2)}, u32[]{:S(2)}) collective-permute-start(bf16[128,256]{1,0:T(8,128)(2,1)S(1)} %get-tuple-element.23), channel_id=1, source_target_pairs={{0,8},{4,12},{8,0},{12,4},{16,24},{20,28},{24,16},{28,20},{1,9},{5... | collective-permute-start | bytes 196616 | tf_op jit(solution)/shard_map/ppermute | solution.py:424
  14.7 14.5 %collective-permute-start.5 = (bf16[128,256]{1,0:T(8,128)(2,1)S(1)}, bf16[128,256]{1,0:T(8,128)(2,1)S(1)}, u32[]{:S(2)}, u32[]{:S(2)}) collective-permute-start(bf16[128,256]{1,0:T(8,128)(2,1)S(1)} %get-tuple-element.24), channel_id=1, source_target_pairs={{0,12},{4,8},{8,4},{12,0},{16,28},{20,24},{24,20},{28,16},{1,13},{... | collective-permute-start | bytes 196616 | tf_op jit(solution)/shard_map/ppermute | solution.py:424
  15.0 17.7 %collective-permute-start.6 = (bf16[128,256]{1,0:T(8,128)(2,1)S(1)}, bf16[128,256]{1,0:T(8,128)(2,1)S(1)}, u32[]{:S(2)}, u32[]{:S(2)}) collective-permute-start(bf16[128,256]{1,0:T(8,128)(2,1)S(1)} %get-tuple-element.25), channel_id=1, source_target_pairs={{0,16},{4,20},{8,24},{12,28},{16,0},{20,4},{24,8},{28,12},{1,17},{... | collective-permute-start | bytes 196616 | tf_op jit(solution)/shard_map/ppermute | solution.py:424
  17.6 15.0 %collective-permute-start.7 = (bf16[128,256]{1,0:T(8,128)(2,1)S(1)}, bf16[128,256]{1,0:T(8,128)(2,1)S(1)}, u32[]{:S(2)}, u32[]{:S(2)}) collective-permute-start(bf16[128,256]{1,0:T(8,128)(2,1)S(1)} %get-tuple-element.26), channel_id=1, source_target_pairs={{0,24},{4,28},{8,16},{12,20},{16,8},{20,12},{24,0},{28,4},{1,25},{... | collective-permute-start | bytes 196616 | tf_op jit(solution)/shard_map/ppermute | solution.py:424
  19.1 17.3 %collective-permute-start.8 = (bf16[128,256]{1,0:T(8,128)(2,1)S(1)}, bf16[128,256]{1,0:T(8,128)(2,1)S(1)}, u32[]{:S(2)}, u32[]{:S(2)}) collective-permute-start(bf16[128,256]{1,0:T(8,128)(2,1)S(1)} %get-tuple-element.27), channel_id=1, source_target_pairs={{0,20},{4,16},{8,28},{12,24},{16,4},{20,0},{24,12},{28,8},{1,21},{... | collective-permute-start | bytes 196616 | tf_op jit(solution)/shard_map/ppermute | solution.py:424
  21.6 14.9 %copy-start.4 = (bf16[768,256]{1,0:T(8,128)(2,1)S(1)}, bf16[768,256]{1,0:T(8,128)(2,1)}, u32[]{:S(2)}) copy-start(bf16[768,256]{1,0:T(8,128)(2,1)} %constant.8.clone.refs_9_) | copy-start | bytes 1179652
  21.6 14.8 %collective-permute-start.9 = (bf16[128,256]{1,0:T(8,128)(2,1)S(1)}, bf16[128,256]{1,0:T(8,128)(2,1)S(1)}, u32[]{:S(2)}, u32[]{:S(2)}) collective-permute-start(bf16[128,256]{1,0:T(8,128)(2,1)S(1)} %get-tuple-element.28), channel_id=1, source_target_pairs={{0,28},{4,24},{8,20},{12,16},{16,12},{20,8},{24,4},{28,0},{1,29},{... | collective-permute-start | bytes 196616 | tf_op jit(solution)/shard_map/ppermute | solution.py:424
  36.4 8.4 %copy-start = (bf16[64,3,4096]{2,0,1:T(8,128)(2,1)S(1)}, bf16[64,3,4096]{2,0,1:T(8,128)(2,1)}, u32[]{:S(2)}) copy-start(bf16[64,3,4096]{2,0,1:T(8,128)(2,1)} %param.6) | copy-start | bytes 4718596
  41.3 17.6 %all-to-all-start.1 = ((bf16[8,128,256]{2,1,0:T(8,128)(2,1)}), bf16[8,128,256]{2,1,0:T(8,128)(2,1)S(1)}, u32[]{:S(2)}, u32[]{:S(2)}) async-start(bf16[8,128,256]{2,1,0:T(8,128)(2,1)} %convolve.1), calls=%async_computation.1 | async-start | bytes 1048576 | tf_op jit(solution)/shard_map/all_to_all | solution.py:528
  45.0 1.9 %collective-permute-start = (bf16[64,1024]{1,0:T(8,128)(2,1)S(1)}, bf16[64,1024]{1,0:T(8,128)(2,1)S(1)}, u32[]{:S(2)}, u32[]{:S(2)}) collective-permute-start(bf16[64,1024]{1,0:T(8,128)(2,1)S(1)} %get-tuple-element.18), channel_id=1, source_target_pairs={{0,1},{1,0},{2,3},{3,2},{4,5},{5,4},{6,7},{7,6},{8,9},{9,8},{10,11... | collective-permute-start | bytes 393224 | tf_op jit(solution)/shard_map/ppermute | solution.py:424
  45.0 6.4 %collective-permute-start.1 = (bf16[64,1024]{1,0:T(8,128)(2,1)S(1)}, bf16[64,1024]{1,0:T(8,128)(2,1)S(1)}, u32[]{:S(2)}, u32[]{:S(2)}) collective-permute-start(bf16[64,1024]{1,0:T(8,128)(2,1)S(1)} %get-tuple-element.19), channel_id=1, source_target_pairs={{0,2},{1,3},{2,0},{3,1},{4,6},{5,7},{6,4},{7,5},{8,10},{9,11},{10,... | collective-permute-start | bytes 393224 | tf_op jit(solution)/shard_map/ppermute | solution.py:424
  46.6 6.7 %collective-permute-start.2 = (bf16[64,1024]{1,0:T(8,128)(2,1)S(1)}, bf16[64,1024]{1,0:T(8,128)(2,1)S(1)}, u32[]{:S(2)}, u32[]{:S(2)}) collective-permute-start(bf16[64,1024]{1,0:T(8,128)(2,1)S(1)} %get-tuple-element.20), channel_id=1, source_target_pairs={{0,3},{1,2},{2,1},{3,0},{4,7},{5,6},{6,5},{7,4},{8,11},{9,10},{10,... | collective-permute-start | bytes 393224 | tf_op jit(solution)/shard_map/ppermute | solution.py:424

commit v14 on v10

--- a/solution.py
+++ b/solution.py
@@ -287,9 +287,12 @@
     return [range(first, first + GROUP, CHUNK) for first in range(0, LANES, GROUP)]
 
 
-def gated_spectrum_kernel(gated_ref, wave_ref, twist_ref, out_ref, u, *scratch):
-    rows, waves = scratch[0:2], scratch[2:4]
+def gated_spectrum_kernel(gated_ref, wave_ref, twist_ref, *refs):
+    early = (len(refs) - 6) // 2
+    out_ref, u, rows, waves = refs[early], refs[-5], refs[-4:-2], refs[-2:]
     blocks = u.shape[0]
+    for code_ref, taps_ref in zip(refs[:early], refs[early + 1 :]):
+        taps_ref[...] = decode(code_ref[...], 1, math.log2(blocks * ROW))
     parts = ROW // gated_ref.shape[1]
     groups = row_groups()
 
@@ -316,16 +319,17 @@
 
 def conv_kernel(gated_ref, *refs):
     blocks = gated_ref.shape[0]
-    wave_ref, back_wave_ref, twist_ref, out_ref, codes, out, sems, *scratch = refs[blocks:]
+    wave_ref, back_wave_ref, twist_ref, out_ref, taps, out, sems, *scratch = refs[blocks:]
     rows, waves, back_rows, back_waves = (scratch[at : at + 2] for at in (0, 2, 4, 6))
     scale = math.log2(blocks * ROW)
     me = lax.axis_index("seq")
     groups = row_groups()
-    for turn, code_ref in enumerate(refs[:blocks]):
-        codes[me ^ turn] = code_ref[...]
+    for turn, taps_ref in enumerate(refs[:blocks]):
+        early = taps_ref.dtype == jnp.float32
+        taps[me ^ turn] = taps_ref[...] if early else decode(taps_ref[...], 1, scale)
 
     def forward(at, half):
-        taken = [decode(codes[n1, at : at + CHUNK, :], 1, scale) for n1 in range(blocks)]
+        taken = [taps[n1, at : at + CHUNK, :] for n1 in range(blocks)]
         mix_forward(taken, twist_ref, at % GROUP, rows[half])
 
     def product(at, half):
@@ -493,21 +497,23 @@
         scratch = [pltpu.VMEM((blocks * 2 * GROUP, 3 * ROW), jnp.bfloat16)] * 2
         scratch += [pltpu.VMEM((blocks * 2 * GROUP, ROW), jnp.float32)] * 2
         large = pltpu.CompilerParams(vmem_limit_bytes=VMEM_BYTES)
-        gated = pl.pallas_call(
+        early = groups // 2
+        gated, *known = pl.pallas_call(
             gated_spectrum_kernel,
-            out_shape=jax.ShapeDtypeStruct((blocks, 2, own, ROW), jnp.float32),
+            out_shape=[jax.ShapeDtypeStruct((blocks, 2, own, ROW), jnp.float32)]
+            + [jax.ShapeDtypeStruct((own, ROW), jnp.float32)] * early,
             scratch_shapes=[pltpu.VMEM((blocks, own, ROW), jnp.float32)] + scratch,
             compiler_params=large,
             cost_estimate=cost(2**32, 2**24),
             name="gated_spectrum",
-        )(gated, wave, twist)
+        )(gated, wave, twist, *taps[:early])
         convolved = pl.pallas_call(
             conv_kernel,
             out_shape=jax.ShapeDtypeStruct((blocks, own, ROW), jnp.bfloat16),
             in_specs=[pl.BlockSpec(memory_space=pltpu.VMEM)] * (groups + 4),
             out_specs=far,
             scratch_shapes=[
-                pltpu.VMEM((blocks, own, ROW), jnp.bfloat16),
+                pltpu.VMEM((blocks, own, ROW), jnp.float32),
                 pltpu.VMEM((blocks, own, ROW), jnp.bfloat16),
                 pltpu.SemaphoreType.DMA((own // GROUP,)),
             ]
@@ -515,7 +521,7 @@
             compiler_params=large,
             cost_estimate=cost(2**32, 2**24),
             name="convolve",
-        )(gated, *taps, wave, back_wave, twist)
+        )(gated, *known, *taps[early:], wave, back_wave, twist)
     else:
         gated = decode(gated, 1).reshape(blocks, ROW, own)
         taps = jnp.transpose(decode(taps, 2), (1, 0, 2)).reshape(own, blocks, ROW)

time: 60.4 us -> 59.8 us (0.990)
  transfers between devices with their start and end apart: 12 -> 12, of which waited for: 6 -> 5; matrix products, arithmetic and copies ran while one was open for 0% -> 0% of each run, Pallas kernels for 7% -> 8%
where the time goes in v14:
time: 59.8 us; the launch traced here: 59.5 us
  starting transfers between devices  27.7 us (46%)
  waiting for transfers between devices  18.6 us (31%)
  Pallas kernels  13.1 us (22%)
    ppermute x10, starting transfers between devices, scatter(): lax.ppermute(block, axis, [(i, i ^ turn) for i in range(count)])  16.2 us
    ppermute x10, waiting for transfers between devices, scatter(): lax.ppermute(block, axis, [(i, i ^ turn) for i in range(count)])  12.7 us
    all_to_all x1, starting transfers between devices, body(): gated = exchange(gated, ('seq', 'ch'))  7.32 us
    all_to_all x1, waiting for transfers between devices, body(): convolved = exchange(convolved, 'seq')  5.78 us
    pallas_call x1, Pallas kernels, body(): pl.pallas_call(conv_kernel, out_shape=jax.ShapeDtypeStruct((blocks, own,...  4.26 us
    all_to_all x1, starting transfers between devices, body(): convolved = exchange(convolved, 'seq')  4.16 us
    pallas_call x1, Pallas kernels, body(): pl.pallas_call(gated_spectrum_kernel, out_shape=[jax.ShapeDtypeStruct((bl...  2.93 us
    pallas_call x1, Pallas kernels, body(): pl.pallas_call(send_kernel, in_specs=[far], out_specs=far, out_shape=jax....  2.84 us
  transfers between devices with their start and end apart: 12, of which 5 were waited for; matrix products, arithmetic and copies ran while one was open for 0% of the time, Pallas kernels for 8%

profile of v14, /device:TPU:0, one launch (start us, length us, event | category | flops | bytes accessed | tf_op | source)
XLA Modules:
  0.0 59.5 jit_solution(9100975702830323555)
XLA Ops:
  0.0 2.8 %encode_gated.1 = bf16[8,4,64,128]{3,2,1,0:T(8,128)(2,1)} custom-call(bf16[3,64,4096]{2,1,0:T(8,128)(2,1)} %bitcast.4), custom_call_target="tpu_custom_call" | custom-call | flops 33554432 | bytes 8388608 | tf_op jit(solution)/shard_map/encode_gated/pallas_call | solution.py:444
  2.9 7.3 %all-to-all-start = ((bf16[32,64,128]{2,1,0:T(8,128)(2,1)}), bf16[32,64,128]{2,1,0:T(8,128)(2,1)S(1)}, u32[]{:S(2)}, u32[]{:S(2)}) async-start(bf16[32,64,128]{2,1,0:T(8,128)(2,1)} %bitcast.8), calls=%async_computation | async-start | bytes 1048576 | tf_op jit(solution)/shard_map/all_to_all | solution.py:488
  10.2 1.2 %encode_taps.1 = (bf16[128,256]{1,0:T(8,128)(2,1)S(1)}, bf16[128,256]{1,0:T(8,128)(2,1)S(1)}, bf16[128,256]{1,0:T(8,128)(2,1)S(1)}, bf16[128,256]{1,0:T(8,128)(2...) custom-call(f32[8,128,256]{2,1,0:T(8,128)S(1)} %bitcast.6, ...), custom_call_target="tpu_custom_call" | custom-call | flops 33554432 | bytes 8388608 | tf_op jit(solution)/shard_map/encode_taps/pallas_call | solution.py:470
  11.4 1.8 %collective-permute-start.3 = (bf16[128,256]{1,0:T(8,128)(2,1)S(1)}, bf16[128,256]{1,0:T(8,128)(2,1)S(1)}, u32[]{:S(2)}, u32[]{:S(2)}) collective-permute-start(bf16[128,256]{1,0:T(8,128)(2,1)S(1)} %get-tuple-element.27), channel_id=1, source_target_pairs={{0,4},{4,0},{8,12},{12,8},{16,20},{20,16},{24,28},{28,24},{1,5},{5... | collective-permute-start | bytes 196616 | tf_op jit(solution)/shard_map/ppermute | solution.py:425
  13.2 1.5 %collective-permute-start.4 = (bf16[128,256]{1,0:T(8,128)(2,1)S(1)}, bf16[128,256]{1,0:T(8,128)(2,1)S(1)}, u32[]{:S(2)}, u32[]{:S(2)}) collective-permute-start(bf16[128,256]{1,0:T(8,128)(2,1)S(1)} %get-tuple-element.28), channel_id=1, source_target_pairs={{0,8},{4,12},{8,0},{12,4},{16,24},{20,28},{24,16},{28,20},{1,9},{5... | collective-permute-start | bytes 196616 | tf_op jit(solution)/shard_map/ppermute | solution.py:425
  14.7 0.3 collective-permute-start.5
  15.0 2.7 %collective-permute-start.6 = (bf16[128,256]{1,0:T(8,128)(2,1)S(1)}, bf16[128,256]{1,0:T(8,128)(2,1)S(1)}, u32[]{:S(2)}, u32[]{:S(2)}) collective-permute-start(bf16[128,256]{1,0:T(8,128)(2,1)S(1)} %get-tuple-element.35), channel_id=1, source_target_pairs={{0,16},{4,20},{8,24},{12,28},{16,0},{20,4},{24,8},{28,12},{1,17},{... | collective-permute-start | bytes 196616 | tf_op jit(solution)/shard_map/ppermute | solution.py:425
  17.6 1.5 %collective-permute-start.7 = (bf16[128,256]{1,0:T(8,128)(2,1)S(1)}, bf16[128,256]{1,0:T(8,128)(2,1)S(1)}, u32[]{:S(2)}, u32[]{:S(2)}) collective-permute-start(bf16[128,256]{1,0:T(8,128)(2,1)S(1)} %get-tuple-element.36), channel_id=1, source_target_pairs={{0,20},{4,16},{8,28},{12,24},{16,4},{20,0},{24,12},{28,8},{1,21},{... | collective-permute-start | bytes 196616 | tf_op jit(solution)/shard_map/ppermute | solution.py:425
  19.1 3.3 %collective-permute-start.8 = (bf16[128,256]{1,0:T(8,128)(2,1)S(1)}, bf16[128,256]{1,0:T(8,128)(2,1)S(1)}, u32[]{:S(2)}, u32[]{:S(2)}) collective-permute-start(bf16[128,256]{1,0:T(8,128)(2,1)S(1)} %get-tuple-element.37), channel_id=1, source_target_pairs={{0,24},{4,28},{8,16},{12,20},{16,8},{20,12},{24,0},{28,4},{1,25},{... | collective-permute-start | bytes 196616 | tf_op jit(solution)/shard_map/ppermute | solution.py:425
  22.5 3.2 %collective-permute-start.9 = (bf16[128,256]{1,0:T(8,128)(2,1)S(1)}, bf16[128,256]{1,0:T(8,128)(2,1)S(1)}, u32[]{:S(2)}, u32[]{:S(2)}) collective-permute-start(bf16[128,256]{1,0:T(8,128)(2,1)S(1)} %get-tuple-element.38), channel_id=1, source_target_pairs={{0,28},{4,24},{8,20},{12,16},{16,12},{20,8},{24,4},{28,0},{1,29},{... | collective-permute-start | bytes 196616 | tf_op jit(solution)/shard_map/ppermute | solution.py:425
  25.7 2.9 %gated_spectrum.1 = (f32[8,2,128,256]{3,2,1,0:T(8,128)S(1)}, f32[128,256]{1,0:T(8,128)S(1)}, f32[128,256]{1,0:T(8,128)S(1)}, f32[128,256]{1,0:T(8,128)S(1)}, f32[128,256]{1,0:T(8,128)S(1)}) custom-call(bf16[32,64,128]{2,1,0:T(8,128)(2,1)S(1)} %all-to-all-done.gated_ref, bf16[768,256]{1,0:T(8,128)(2,1)S(1)} %copy-done.3, f32[8,2,256]{2,1,0:T(2,128)S(1)} %copy-done.5, ...), custom_call_target="tpu_custom_call" | custom-call | flops 4294967296 | bytes 16777216 | tf_op jit(solution)/shard_map/gated_spectrum/pallas_call | solution.py:501
  28.7 4.0 %collective-permute-done.6.refs_4_ = bf16[128,256]{1,0:T(8,128)(2,1)S(1)} collective-permute-done((bf16[128,256]{1,0:T(8,128)(2,1)S(1)}, bf16[128,256]{1,0:T(8,128)(2,1)S(1)}, u32[]{:S(2)}, u32[]{:S(2)}) %collective-permute-start.6) | collective-permute-done | bytes 65568 | tf_op jit(solution)/shard_map/ppermute | solution.py:425
  32.7 2.3 %collective-permute-done.7.refs_5_ = bf16[128,256]{1,0:T(8,128)(2,1)S(1)} collective-permute-done((bf16[128,256]{1,0:T(8,128)(2,1)S(1)}, bf16[128,256]{1,0:T(8,128)(2,1)S(1)}, u32[]{:S(2)}, u32[]{:S(2)}) %collective-permute-start.7) | collective-permute-done | bytes 65568 | tf_op jit(solution)/shard_map/ppermute | solution.py:425
  35.0 4.3 %convolve.1 = bf16[8,128,256]{2,1,0:T(8,128)(2,1)} custom-call(f32[8,2,128,256]{3,2,1,0:T(8,128)S(1)} %get-tuple-element.30.gated_ref, f32[128,256]{1,0:T(8,128)S(1)} %get-tuple-element.31.refs_0_, f32[128,256]{1,0:T(8,128)S(1)} %get-tuple-element.32.refs_1_, f32[128,256]{1,0:T(8,128)S(1)} %get-tuple-element.33.refs_2_, ...), custom_call_target="tpu_custom_call" | custom-call | flops 4294967296 | bytes 16777216 | tf_op jit(solution)/shard_map/convolve/pallas_call | solution.py:510
  39.3 4.2 %all-to-all-start.1 = ((bf16[8,128,256]{2,1,0:T(8,128)(2,1)}), bf16[8,128,256]{2,1,0:T(8,128)(2,1)S(1)}, u32[]{:S(2)}, u32[]{:S(2)}) async-start(bf16[8,128,256]{2,1,0:T(8,128)(2,1)} %convolve.1), calls=%async_computation.1 | async-start | bytes 1048576 | tf_op jit(solution)/shard_map/all_to_all | solution.py:531
  43.5 0.1 send_queries.1
  43.6 0.1 collective-permute-start
  43.7 1.5 %collective-permute-start.1 = (bf16[64,1024]{1,0:T(8,128)(2,1)S(1)}, bf16[64,1024]{1,0:T(8,128)(2,1)S(1)}, u32[]{:S(2)}, u32[]{:S(2)}) collective-permute-start(bf16[64,1024]{1,0:T(8,128)(2,1)S(1)} %get-tuple-element.24), channel_id=1, source_target_pairs={{0,2},{1,3},{2,0},{3,1},{4,6},{5,7},{6,4},{7,5},{8,10},{9,11},{10,... | collective-permute-start | bytes 393224 | tf_op jit(solution)/shard_map/ppermute | solution.py:425
  45.2 0.3 collective-permute-start.2
  45.6 4.5 %collective-permute-done.1.refs_2_ = bf16[64,1024]{1,0:T(8,128)(2,1)S(1)} collective-permute-done((bf16[64,1024]{1,0:T(8,128)(2,1)S(1)}, bf16[64,1024]{1,0:T(8,128)(2,1)S(1)}, u32[]{:S(2)}, u32[]{:S(2)}) %collective-permute-start.1) | collective-permute-done | bytes 131104 | tf_op jit(solution)/shard_map/ppermute | solution.py:425
  50.1 1.9 %collective-permute-done.2.refs_3_ = bf16[64,1024]{1,0:T(8,128)(2,1)S(1)} collective-permute-done((bf16[64,1024]{1,0:T(8,128)(2,1)S(1)}, bf16[64,1024]{1,0:T(8,128)(2,1)S(1)}, u32[]{:S(2)}, u32[]{:S(2)}) %collective-permute-start.2) | collective-permute-done | bytes 131104 | tf_op jit(solution)/shard_map/ppermute | solution.py:425
  52.0 0.3 turn_queries.1.query_ref
  52.2 5.8 %all-to-all-done.1.conv_ref = bf16[8,128,256]{2,1,0:T(8,128)(2,1)S(1)} async-done(((bf16[8,128,256]{2,1,0:T(8,128)(2,1)}), bf16[8,128,256]{2,1,0:T(8,128)(2,1)S(1)}, u32[]{:S(2)}, u32[]{:S(2)}) %all-to-all-start.1) | async-done | bytes 524320 | tf_op jit(solution)/shard_map/all_to_all | solution.py:531
  58.0 1.5 %mix_out.1 = bf16[1024,256]{1,0:T(8,128)(2,1)} custom-call(bf16[1024,256]{1,0:T(8,128)(2,1)S(1)} %turn_queries.1.query_ref, bf16[8,128,256]{2,1,0:T(8,128)(2,1)S(1)} %all-to-all-done.1.conv_ref), custom_call_target="tpu_custom_call" | custom-call | tf_op jit(solution)/shard_map/mix_out/pallas_call | solution.py:541
  (19 shorter events, 0.1 us)
Async XLA Ops:
  0.0 10.2 %copy-start.1 = (f32[1024,256]{1,0:T(8,128)S(1)}, f32[1024,256]{1,0:T(8,128)}, u32[]{:S(2)}) copy-start(f32[1024,256]{1,0:T(8,128)} %param.7) | copy-start | bytes 3145732
  0.0 10.2 %copy-start.2 = (f32[1024]{0:T(1024)S(1)}, f32[1024]{0:T(1024)}, u32[]{:S(2)}) copy-start(f32[1024]{0:T(1024)} %param.8) | copy-start | bytes 12292
  0.0 25.7 %copy-start.3 = (bf16[768,256]{1,0:T(8,128)(2,1)S(1)}, bf16[768,256]{1,0:T(8,128)(2,1)}, u32[]{:S(2)}) copy-start(bf16[768,256]{1,0:T(8,128)(2,1)} %constant.6.clone.wave_ref.refs_8_) | copy-start | bytes 1179652
  0.0 25.7 %copy-start.5 = (f32[8,2,256]{2,1,0:T(2,128)S(1)}, f32[8,2,256]{2,1,0:T(2,128)}, u32[]{:S(2)}) copy-start(f32[8,2,256]{2,1,0:T(2,128)} %constant.7.clone.twist_ref.refs_10_) | copy-start | bytes 49156
  2.9 22.9 %all-to-all-start = ((bf16[32,64,128]{2,1,0:T(8,128)(2,1)}), bf16[32,64,128]{2,1,0:T(8,128)(2,1)S(1)}, u32[]{:S(2)}, u32[]{:S(2)}) async-start(bf16[32,64,128]{2,1,0:T(8,128)(2,1)} %bitcast.8), calls=%async_computation | async-start | bytes 1048576 | tf_op jit(solution)/shard_map/all_to_all | solution.py:488
  11.4 7.7 %collective-permute-start.3 = (bf16[128,256]{1,0:T(8,128)(2,1)S(1)}, bf16[128,256]{1,0:T(8,128)(2,1)S(1)}, u32[]{:S(2)}, u32[]{:S(2)}) collective-permute-start(bf16[128,256]{1,0:T(8,128)(2,1)S(1)} %get-tuple-element.27), channel_id=1, source_target_pairs={{0,4},{4,0},{8,12},{12,8},{16,20},{20,16},{24,28},{28,24},{1,5},{5... | collective-permute-start | bytes 196616 | tf_op jit(solution)/shard_map/ppermute | solution.py:425
  13.2 9.2 %collective-permute-start.4 = (bf16[128,256]{1,0:T(8,128)(2,1)S(1)}, bf16[128,256]{1,0:T(8,128)(2,1)S(1)}, u32[]{:S(2)}, u32[]{:S(2)}) collective-permute-start(bf16[128,256]{1,0:T(8,128)(2,1)S(1)} %get-tuple-element.28), channel_id=1, source_target_pairs={{0,8},{4,12},{8,0},{12,4},{16,24},{20,28},{24,16},{28,20},{1,9},{5... | collective-permute-start | bytes 196616 | tf_op jit(solution)/shard_map/ppermute | solution.py:425
  14.7 11.0 %collective-permute-start.5 = (bf16[128,256]{1,0:T(8,128)(2,1)S(1)}, bf16[128,256]{1,0:T(8,128)(2,1)S(1)}, u32[]{:S(2)}, u32[]{:S(2)}) collective-permute-start(bf16[128,256]{1,0:T(8,128)(2,1)S(1)} %get-tuple-element.29), channel_id=1, source_target_pairs={{0,12},{4,8},{8,4},{12,0},{16,28},{20,24},{24,20},{28,16},{1,13},{... | collective-permute-start | bytes 196616 | tf_op jit(solution)/shard_map/ppermute | solution.py:425
  15.0 17.7 %collective-permute-start.6 = (bf16[128,256]{1,0:T(8,128)(2,1)S(1)}, bf16[128,256]{1,0:T(8,128)(2,1)S(1)}, u32[]{:S(2)}, u32[]{:S(2)}) collective-permute-start(bf16[128,256]{1,0:T(8,128)(2,1)S(1)} %get-tuple-element.35), channel_id=1, source_target_pairs={{0,16},{4,20},{8,24},{12,28},{16,0},{20,4},{24,8},{28,12},{1,17},{... | collective-permute-start | bytes 196616 | tf_op jit(solution)/shard_map/ppermute | solution.py:425
  17.6 17.4 %collective-permute-start.7 = (bf16[128,256]{1,0:T(8,128)(2,1)S(1)}, bf16[128,256]{1,0:T(8,128)(2,1)S(1)}, u32[]{:S(2)}, u32[]{:S(2)}) collective-permute-start(bf16[128,256]{1,0:T(8,128)(2,1)S(1)} %get-tuple-element.36), channel_id=1, source_target_pairs={{0,20},{4,16},{8,28},{12,24},{16,4},{20,0},{24,12},{28,8},{1,21},{... | collective-permute-start | bytes 196616 | tf_op jit(solution)/shard_map/ppermute | solution.py:425
  19.1 15.9 %collective-permute-start.8 = (bf16[128,256]{1,0:T(8,128)(2,1)S(1)}, bf16[128,256]{1,0:T(8,128)(2,1)S(1)}, u32[]{:S(2)}, u32[]{:S(2)}) collective-permute-start(bf16[128,256]{1,0:T(8,128)(2,1)S(1)} %get-tuple-element.37), channel_id=1, source_target_pairs={{0,24},{4,28},{8,16},{12,20},{16,8},{20,12},{24,0},{28,4},{1,25},{... | collective-permute-start | bytes 196616 | tf_op jit(solution)/shard_map/ppermute | solution.py:425
  22.5 12.5 %collective-permute-start.9 = (bf16[128,256]{1,0:T(8,128)(2,1)S(1)}, bf16[128,256]{1,0:T(8,128)(2,1)S(1)}, u32[]{:S(2)}, u32[]{:S(2)}) collective-permute-start(bf16[128,256]{1,0:T(8,128)(2,1)S(1)} %get-tuple-element.38), channel_id=1, source_target_pairs={{0,28},{4,24},{8,20},{12,16},{16,12},{20,8},{24,4},{28,0},{1,29},{... | collective-permute-start | bytes 196616 | tf_op jit(solution)/shard_map/ppermute | solution.py:425
  25.7 9.3 %copy-start.4 = (bf16[768,256]{1,0:T(8,128)(2,1)S(1)}, bf16[768,256]{1,0:T(8,128)(2,1)}, u32[]{:S(2)}) copy-start(bf16[768,256]{1,0:T(8,128)(2,1)} %constant.8.clone.refs_9_) | copy-start | bytes 1179652
  35.0 8.4 %copy-start = (bf16[64,3,4096]{2,0,1:T(8,128)(2,1)S(1)}, bf16[64,3,4096]{2,0,1:T(8,128)(2,1)}, u32[]{:S(2)}) copy-start(bf16[64,3,4096]{2,0,1:T(8,128)(2,1)} %param.6) | copy-start | bytes 4718596
  39.3 18.7 %all-to-all-start.1 = ((bf16[8,128,256]{2,1,0:T(8,128)(2,1)}), bf16[8,128,256]{2,1,0:T(8,128)(2,1)S(1)}, u32[]{:S(2)}, u32[]{:S(2)}) async-start(bf16[8,128,256]{2,1,0:T(8,128)(2,1)} %convolve.1), calls=%async_computation.1 | async-start | bytes 1048576 | tf_op jit(solution)/shard_map/all_to_all | solution.py:531
  43.6 1.9 %collective-permute-start = (bf16[64,1024]{1,0:T(8,128)(2,1)S(1)}, bf16[64,1024]{1,0:T(8,128)(2,1)S(1)}, u32[]{:S(2)}, u32[]{:S(2)}) collective-permute-start(bf16[64,1024]{1,0:T(8,128)(2,1)S(1)} %get-tuple-element.23), channel_id=1, source_target_pairs={{0,1},{1,0},{2,3},{3,2},{4,5},{5,4},{6,7},{7,6},{8,9},{9,8},{10,11... | collective-permute-start | bytes 393224 | tf_op jit(solution)/shard_map/ppermute | solution.py:425
  43.7 6.4 %collective-permute-start.1 = (bf16[64,1024]{1,0:T(8,128)(2,1)S(1)}, bf16[64,1024]{1,0:T(8,128)(2,1)S(1)}, u32[]{:S(2)}, u32[]{:S(2)}) collective-permute-start(bf16[64,1024]{1,0:T(8,128)(2,1)S(1)} %get-tuple-element.24), channel_id=1, source_target_pairs={{0,2},{1,3},{2,0},{3,1},{4,6},{5,7},{6,4},{7,5},{8,10},{9,11},{10,... | collective-permute-start | bytes 393224 | tf_op jit(solution)/shard_map/ppermute | solution.py:425
  45.2 6.7 %collective-permute-start.2 = (bf16[64,1024]{1,0:T(8,128)(2,1)S(1)}, bf16[64,1024]{1,0:T(8,128)(2,1)S(1)}, u32[]{:S(2)}, u32[]{:S(2)}) collective-permute-start(bf16[64,1024]{1,0:T(8,128)(2,1)S(1)} %get-tuple-element.25), channel_id=1, source_target_pairs={{0,3},{1,2},{2,1},{3,0},{4,7},{5,6},{6,5},{7,4},{8,11},{9,10},{10,... | collective-permute-start | bytes 393224 | tf_op jit(solution)/shard_map/ppermute | solution.py:425

commit v15 on v14

--- a/solution.py
+++ b/solution.py
@@ -324,7 +324,7 @@
     scale = math.log2(blocks * ROW)
     me = lax.axis_index("seq")
     groups = row_groups()
-    for turn, taps_ref in enumerate(refs[:blocks]):
+    for turn, taps_ref in zip(turn_order(blocks), refs[:blocks]):
         early = taps_ref.dtype == jnp.float32
         taps[me ^ turn] = taps_ref[...] if early else decode(taps_ref[...], 1, scale)
 
@@ -417,6 +417,11 @@
     re, im = re * cos_twist - im * sin_twist, im * cos_twist + re * sin_twist
     total = dot("kcm,kn->ncm", re, mix[0]) - dot("kcm,kn->ncm", im, mix[1])
     return total * (1.0 / (blocks * ROW))
+
+
+def turn_order(count):
+    far = range(4, count, 2)
+    return [0, 1, 2, 3, *far, *(turn + 1 for turn in far)]
 
 
 def scatter(blocks, axis):
@@ -521,7 +526,7 @@
             compiler_params=large,
             cost_estimate=cost(2**32, 2**24),
             name="convolve",
-        )(gated, *known, *taps[early:], wave, back_wave, twist)
+        )(gated, *known, *[taps[turn] for turn in turn_order(groups)[early:]], wave, back_wave, twist)
     else:
         gated = decode(gated, 1).reshape(blocks, ROW, own)
         taps = jnp.transpose(decode(taps, 2), (1, 0, 2)).reshape(own, blocks, ROW)

time: 59.8 us -> 60 us (level)
  waiting for transfers between devices: 18.6 us -> 19.5 us
  starting transfers between devices: 27.7 us -> 27 us
    ppermute x10, waiting for transfers between devices: 12.7 us -> 14.1 us  [scatter(): lax.ppermute(block, axis, [(i, i ^ turn) for i in range(count)])]
    all_to_all x1, starting transfers between devices: 4.16 us -> 3.51 us  [body(): convolved = exchange(convolved, 'seq')]
where the time goes in v15:
time: 60 us; the launch traced here: 59.7 us
  starting transfers between devices  27 us (45%)
  waiting for transfers between devices  19.5 us (32%)
  Pallas kernels  13.1 us (22%)
    ppermute x10, starting transfers between devices, scatter(): lax.ppermute(block, axis, [(i, i ^ turn) for i in range(count)])  16.2 us
    ppermute x10, waiting for transfers between devices, scatter(): lax.ppermute(block, axis, [(i, i ^ turn) for i in range(count)])  14.1 us
    all_to_all x1, starting transfers between devices, body(): gated = exchange(gated, ('seq', 'ch'))  7.32 us
    all_to_all x1, waiting for transfers between devices, body(): convolved = exchange(convolved, 'seq')  5.26 us
    pallas_call x1, Pallas kernels, body(): pl.pallas_call(conv_kernel, out_shape=jax.ShapeDtypeStruct((blocks, own,...  4.26 us
    all_to_all x1, starting transfers between devices, body(): convolved = exchange(convolved, 'seq')  3.51 us
    pallas_call x1, Pallas kernels, body(): pl.pallas_call(gated_spectrum_kernel, out_shape=[jax.ShapeDtypeStruct((bl...  2.93 us
    pallas_call x1, Pallas kernels, body(): pl.pallas_call(send_kernel, in_specs=[far], out_specs=far, out_shape=jax....  2.84 us
  transfers between devices with their start and end apart: 12, of which 5 were waited for; matrix products, arithmetic and copies ran while one was open for 0% of the time, Pallas kernels for 8%

profile of v15, /device:TPU:0, one launch (start us, length us, event | category | flops | bytes accessed | tf_op | source)
XLA Modules:
  0.0 59.7 jit_solution(7521278414850871401)
XLA Ops:
  0.0 2.8 %encode_gated.1 = bf16[8,4,64,128]{3,2,1,0:T(8,128)(2,1)} custom-call(bf16[3,64,4096]{2,1,0:T(8,128)(2,1)} %bitcast.4), custom_call_target="tpu_custom_call" | custom-call | flops 33554432 | bytes 8388608 | tf_op jit(solution)/shard_map/encode_gated/pallas_call | solution.py:449
  2.9 7.3 %all-to-all-start = ((bf16[32,64,128]{2,1,0:T(8,128)(2,1)}), bf16[32,64,128]{2,1,0:T(8,128)(2,1)S(1)}, u32[]{:S(2)}, u32[]{:S(2)}) async-start(bf16[32,64,128]{2,1,0:T(8,128)(2,1)} %bitcast.8), calls=%async_computation | async-start | bytes 1048576 | tf_op jit(solution)/shard_map/all_to_all | solution.py:493
  10.2 1.2 %encode_taps.1 = (bf16[128,256]{1,0:T(8,128)(2,1)S(1)}, bf16[128,256]{1,0:T(8,128)(2,1)S(1)}, bf16[128,256]{1,0:T(8,128)(2,1)S(1)}, bf16[128,256]{1,0:T(8,128)(2...) custom-call(f32[8,128,256]{2,1,0:T(8,128)S(1)} %bitcast.6, ...), custom_call_target="tpu_custom_call" | custom-call | flops 33554432 | bytes 8388608 | tf_op jit(solution)/shard_map/encode_taps/pallas_call | solution.py:475
  11.4 1.8 %collective-permute-start.3 = (bf16[128,256]{1,0:T(8,128)(2,1)S(1)}, bf16[128,256]{1,0:T(8,128)(2,1)S(1)}, u32[]{:S(2)}, u32[]{:S(2)}) collective-permute-start(bf16[128,256]{1,0:T(8,128)(2,1)S(1)} %get-tuple-element.27), channel_id=1, source_target_pairs={{0,4},{4,0},{8,12},{12,8},{16,20},{20,16},{24,28},{28,24},{1,5},{5... | collective-permute-start | bytes 196616 | tf_op jit(solution)/shard_map/ppermute | solution.py:430
  13.2 1.5 %collective-permute-start.4 = (bf16[128,256]{1,0:T(8,128)(2,1)S(1)}, bf16[128,256]{1,0:T(8,128)(2,1)S(1)}, u32[]{:S(2)}, u32[]{:S(2)}) collective-permute-start(bf16[128,256]{1,0:T(8,128)(2,1)S(1)} %get-tuple-element.28), channel_id=1, source_target_pairs={{0,8},{4,12},{8,0},{12,4},{16,24},{20,28},{24,16},{28,20},{1,9},{5... | collective-permute-start | bytes 196616 | tf_op jit(solution)/shard_map/ppermute | solution.py:430
  14.7 0.3 collective-permute-start.5
  15.0 2.7 %collective-permute-start.6 = (bf16[128,256]{1,0:T(8,128)(2,1)S(1)}, bf16[128,256]{1,0:T(8,128)(2,1)S(1)}, u32[]{:S(2)}, u32[]{:S(2)}) collective-permute-start(bf16[128,256]{1,0:T(8,128)(2,1)S(1)} %get-tuple-element.35), channel_id=1, source_target_pairs={{0,16},{4,20},{8,24},{12,28},{16,0},{20,4},{24,8},{28,12},{1,17},{... | collective-permute-start | bytes 196616 | tf_op jit(solution)/shard_map/ppermute | solution.py:430
  17.6 1.5 %collective-permute-start.7 = (bf16[128,256]{1,0:T(8,128)(2,1)S(1)}, bf16[128,256]{1,0:T(8,128)(2,1)S(1)}, u32[]{:S(2)}, u32[]{:S(2)}) collective-permute-start(bf16[128,256]{1,0:T(8,128)(2,1)S(1)} %get-tuple-element.36), channel_id=1, source_target_pairs={{0,24},{4,28},{8,16},{12,20},{16,8},{20,12},{24,0},{28,4},{1,25},{... | collective-permute-start | bytes 196616 | tf_op jit(solution)/shard_map/ppermute | solution.py:430
  19.1 2.4 %collective-permute-start.8 = (bf16[128,256]{1,0:T(8,128)(2,1)S(1)}, bf16[128,256]{1,0:T(8,128)(2,1)S(1)}, u32[]{:S(2)}, u32[]{:S(2)}) collective-permute-start(bf16[128,256]{1,0:T(8,128)(2,1)S(1)} %get-tuple-element.37), channel_id=1, source_target_pairs={{0,20},{4,16},{8,28},{12,24},{16,4},{20,0},{24,12},{28,8},{1,21},{... | collective-permute-start | bytes 196616 | tf_op jit(solution)/shard_map/ppermute | solution.py:430
  21.6 4.1 %collective-permute-start.9 = (bf16[128,256]{1,0:T(8,128)(2,1)S(1)}, bf16[128,256]{1,0:T(8,128)(2,1)S(1)}, u32[]{:S(2)}, u32[]{:S(2)}) collective-permute-start(bf16[128,256]{1,0:T(8,128)(2,1)S(1)} %get-tuple-element.38), channel_id=1, source_target_pairs={{0,28},{4,24},{8,20},{12,16},{16,12},{20,8},{24,4},{28,0},{1,29},{... | collective-permute-start | bytes 196616 | tf_op jit(solution)/shard_map/ppermute | solution.py:430
  25.7 2.9 %gated_spectrum.1 = (f32[8,2,128,256]{3,2,1,0:T(8,128)S(1)}, f32[128,256]{1,0:T(8,128)S(1)}, f32[128,256]{1,0:T(8,128)S(1)}, f32[128,256]{1,0:T(8,128)S(1)}, f32[128,256]{1,0:T(8,128)S(1)}) custom-call(bf16[32,64,128]{2,1,0:T(8,128)(2,1)S(1)} %all-to-all-done.gated_ref, bf16[768,256]{1,0:T(8,128)(2,1)S(1)} %copy-done.3, f32[8,2,256]{2,1,0:T(2,128)S(1)} %copy-done.5, ...), custom_call_target="tpu_custom_call" | custom-call | flops 4294967296 | bytes 16777216 | tf_op jit(solution)/shard_map/gated_spectrum/pallas_call | solution.py:506
  28.7 4.0 %collective-permute-done.6.refs_4_ = bf16[128,256]{1,0:T(8,128)(2,1)S(1)} collective-permute-done((bf16[128,256]{1,0:T(8,128)(2,1)S(1)}, bf16[128,256]{1,0:T(8,128)(2,1)S(1)}, u32[]{:S(2)}, u32[]{:S(2)}) %collective-permute-start.6) | collective-permute-done | bytes 65568 | tf_op jit(solution)/shard_map/ppermute | solution.py:430
  32.7 3.7 %collective-permute-done.8.refs_6_ = bf16[128,256]{1,0:T(8,128)(2,1)S(1)} collective-permute-done((bf16[128,256]{1,0:T(8,128)(2,1)S(1)}, bf16[128,256]{1,0:T(8,128)(2,1)S(1)}, u32[]{:S(2)}, u32[]{:S(2)}) %collective-permute-start.8) | collective-permute-done | bytes 65568 | tf_op jit(solution)/shard_map/ppermute | solution.py:430
  36.4 4.3 %convolve.1 = bf16[8,128,256]{2,1,0:T(8,128)(2,1)} custom-call(f32[8,2,128,256]{3,2,1,0:T(8,128)S(1)} %get-tuple-element.30.gated_ref, f32[128,256]{1,0:T(8,128)S(1)} %get-tuple-element.31.refs_0_, f32[128,256]{1,0:T(8,128)S(1)} %get-tuple-element.32.refs_1_, f32[128,256]{1,0:T(8,128)S(1)} %get-tuple-element.33.refs_2_, ...), custom_call_target="tpu_custom_call" | custom-call | flops 4294967296 | bytes 16777216 | tf_op jit(solution)/shard_map/convolve/pallas_call | solution.py:515
  40.7 3.5 %all-to-all-start.1 = ((bf16[8,128,256]{2,1,0:T(8,128)(2,1)}), bf16[8,128,256]{2,1,0:T(8,128)(2,1)S(1)}, u32[]{:S(2)}, u32[]{:S(2)}) async-start(bf16[8,128,256]{2,1,0:T(8,128)(2,1)} %convolve.1), calls=%async_computation.1 | async-start | bytes 1048576 | tf_op jit(solution)/shard_map/all_to_all | solution.py:536
  44.2 0.1 send_queries.1
  44.4 0.1 collective-permute-start
  44.4 1.5 %collective-permute-start.1 = (bf16[64,1024]{1,0:T(8,128)(2,1)S(1)}, bf16[64,1024]{1,0:T(8,128)(2,1)S(1)}, u32[]{:S(2)}, u32[]{:S(2)}) collective-permute-start(bf16[64,1024]{1,0:T(8,128)(2,1)S(1)} %get-tuple-element.24), channel_id=1, source_target_pairs={{0,2},{1,3},{2,0},{3,1},{4,6},{5,7},{6,4},{7,5},{8,10},{9,11},{10,... | collective-permute-start | bytes 393224 | tf_op jit(solution)/shard_map/ppermute | solution.py:430
  46.0 0.3 collective-permute-start.2
  46.3 4.5 %collective-permute-done.1.refs_2_ = bf16[64,1024]{1,0:T(8,128)(2,1)S(1)} collective-permute-done((bf16[64,1024]{1,0:T(8,128)(2,1)S(1)}, bf16[64,1024]{1,0:T(8,128)(2,1)S(1)}, u32[]{:S(2)}, u32[]{:S(2)}) %collective-permute-start.1) | collective-permute-done | bytes 131104 | tf_op jit(solution)/shard_map/ppermute | solution.py:430
  50.8 1.9 %collective-permute-done.2.refs_3_ = bf16[64,1024]{1,0:T(8,128)(2,1)S(1)} collective-permute-done((bf16[64,1024]{1,0:T(8,128)(2,1)S(1)}, bf16[64,1024]{1,0:T(8,128)(2,1)S(1)}, u32[]{:S(2)}, u32[]{:S(2)}) %collective-permute-start.2) | collective-permute-done | bytes 131104 | tf_op jit(solution)/shard_map/ppermute | solution.py:430
  52.7 0.3 turn_queries.1.query_ref
  53.0 5.3 %all-to-all-done.1.conv_ref = bf16[8,128,256]{2,1,0:T(8,128)(2,1)S(1)} async-done(((bf16[8,128,256]{2,1,0:T(8,128)(2,1)}), bf16[8,128,256]{2,1,0:T(8,128)(2,1)S(1)}, u32[]{:S(2)}, u32[]{:S(2)}) %all-to-all-start.1) | async-done | bytes 524320 | tf_op jit(solution)/shard_map/all_to_all | solution.py:536
  58.3 1.5 %mix_out.1 = bf16[1024,256]{1,0:T(8,128)(2,1)} custom-call(bf16[1024,256]{1,0:T(8,128)(2,1)S(1)} %turn_queries.1.query_ref, bf16[8,128,256]{2,1,0:T(8,128)(2,1)S(1)} %all-to-all-done.1.conv_ref), custom_call_target="tpu_custom_call" | custom-call | tf_op jit(solution)/shard_map/mix_out/pallas_call | solution.py:546
  (19 shorter events, 0.1 us)
Async XLA Ops:
  0.0 10.2 %copy-start.1 = (f32[1024,256]{1,0:T(8,128)S(1)}, f32[1024,256]{1,0:T(8,128)}, u32[]{:S(2)}) copy-start(f32[1024,256]{1,0:T(8,128)} %param.7) | copy-start | bytes 3145732
  0.0 10.2 %copy-start.2 = (f32[1024]{0:T(1024)S(1)}, f32[1024]{0:T(1024)}, u32[]{:S(2)}) copy-start(f32[1024]{0:T(1024)} %param.8) | copy-start | bytes 12292
  0.0 25.7 %copy-start.3 = (bf16[768,256]{1,0:T(8,128)(2,1)S(1)}, bf16[768,256]{1,0:T(8,128)(2,1)}, u32[]{:S(2)}) copy-start(bf16[768,256]{1,0:T(8,128)(2,1)} %constant.6.clone.wave_ref.refs_8_) | copy-start | bytes 1179652
  0.0 25.7 %copy-start.5 = (f32[8,2,256]{2,1,0:T(2,128)S(1)}, f32[8,2,256]{2,1,0:T(2,128)}, u32[]{:S(2)}) copy-start(f32[8,2,256]{2,1,0:T(2,128)} %constant.7.clone.twist_ref.refs_10_) | copy-start | bytes 49156
  2.9 22.9 %all-to-all-start = ((bf16[32,64,128]{2,1,0:T(8,128)(2,1)}), bf16[32,64,128]{2,1,0:T(8,128)(2,1)S(1)}, u32[]{:S(2)}, u32[]{:S(2)}) async-start(bf16[32,64,128]{2,1,0:T(8,128)(2,1)} %bitcast.8), calls=%async_computation | async-start | bytes 1048576 | tf_op jit(solution)/shard_map/all_to_all | solution.py:493
  11.4 7.7 %collective-permute-start.3 = (bf16[128,256]{1,0:T(8,128)(2,1)S(1)}, bf16[128,256]{1,0:T(8,128)(2,1)S(1)}, u32[]{:S(2)}, u32[]{:S(2)}) collective-permute-start(bf16[128,256]{1,0:T(8,128)(2,1)S(1)} %get-tuple-element.27), channel_id=1, source_target_pairs={{0,4},{4,0},{8,12},{12,8},{16,20},{20,16},{24,28},{28,24},{1,5},{5... | collective-permute-start | bytes 196616 | tf_op jit(solution)/shard_map/ppermute | solution.py:430
  13.2 8.3 %collective-permute-start.4 = (bf16[128,256]{1,0:T(8,128)(2,1)S(1)}, bf16[128,256]{1,0:T(8,128)(2,1)S(1)}, u32[]{:S(2)}, u32[]{:S(2)}) collective-permute-start(bf16[128,256]{1,0:T(8,128)(2,1)S(1)} %get-tuple-element.28), channel_id=1, source_target_pairs={{0,8},{4,12},{8,0},{12,4},{16,24},{20,28},{24,16},{28,20},{1,9},{5... | collective-permute-start | bytes 196616 | tf_op jit(solution)/shard_map/ppermute | solution.py:430
  14.7 11.0 %collective-permute-start.5 = (bf16[128,256]{1,0:T(8,128)(2,1)S(1)}, bf16[128,256]{1,0:T(8,128)(2,1)S(1)}, u32[]{:S(2)}, u32[]{:S(2)}) collective-permute-start(bf16[128,256]{1,0:T(8,128)(2,1)S(1)} %get-tuple-element.29), channel_id=1, source_target_pairs={{0,12},{4,8},{8,4},{12,0},{16,28},{20,24},{24,20},{28,16},{1,13},{... | collective-permute-start | bytes 196616 | tf_op jit(solution)/shard_map/ppermute | solution.py:430
  15.0 17.7 %collective-permute-start.6 = (bf16[128,256]{1,0:T(8,128)(2,1)S(1)}, bf16[128,256]{1,0:T(8,128)(2,1)S(1)}, u32[]{:S(2)}, u32[]{:S(2)}) collective-permute-start(bf16[128,256]{1,0:T(8,128)(2,1)S(1)} %get-tuple-element.35), channel_id=1, source_target_pairs={{0,16},{4,20},{8,24},{12,28},{16,0},{20,4},{24,8},{28,12},{1,17},{... | collective-permute-start | bytes 196616 | tf_op jit(solution)/shard_map/ppermute | solution.py:430
  17.6 15.0 %collective-permute-start.7 = (bf16[128,256]{1,0:T(8,128)(2,1)S(1)}, bf16[128,256]{1,0:T(8,128)(2,1)S(1)}, u32[]{:S(2)}, u32[]{:S(2)}) collective-permute-start(bf16[128,256]{1,0:T(8,128)(2,1)S(1)} %get-tuple-element.36), channel_id=1, source_target_pairs={{0,24},{4,28},{8,16},{12,20},{16,8},{20,12},{24,0},{28,4},{1,25},{... | collective-permute-start | bytes 196616 | tf_op jit(solution)/shard_map/ppermute | solution.py:430
  19.1 17.3 %collective-permute-start.8 = (bf16[128,256]{1,0:T(8,128)(2,1)S(1)}, bf16[128,256]{1,0:T(8,128)(2,1)S(1)}, u32[]{:S(2)}, u32[]{:S(2)}) collective-permute-start(bf16[128,256]{1,0:T(8,128)(2,1)S(1)} %get-tuple-element.37), channel_id=1, source_target_pairs={{0,20},{4,16},{8,28},{12,24},{16,4},{20,0},{24,12},{28,8},{1,21},{... | collective-permute-start | bytes 196616 | tf_op jit(solution)/shard_map/ppermute | solution.py:430
  21.6 14.8 %collective-permute-start.9 = (bf16[128,256]{1,0:T(8,128)(2,1)S(1)}, bf16[128,256]{1,0:T(8,128)(2,1)S(1)}, u32[]{:S(2)}, u32[]{:S(2)}) collective-permute-start(bf16[128,256]{1,0:T(8,128)(2,1)S(1)} %get-tuple-element.38), channel_id=1, source_target_pairs={{0,28},{4,24},{8,20},{12,16},{16,12},{20,8},{24,4},{28,0},{1,29},{... | collective-permute-start | bytes 196616 | tf_op jit(solution)/shard_map/ppermute | solution.py:430
  25.7 10.7 %copy-start.4 = (bf16[768,256]{1,0:T(8,128)(2,1)S(1)}, bf16[768,256]{1,0:T(8,128)(2,1)}, u32[]{:S(2)}) copy-start(bf16[768,256]{1,0:T(8,128)(2,1)} %constant.8.clone.refs_9_) | copy-start | bytes 1179652
  36.4 7.8 %copy-start = (bf16[64,3,4096]{2,0,1:T(8,128)(2,1)S(1)}, bf16[64,3,4096]{2,0,1:T(8,128)(2,1)}, u32[]{:S(2)}) copy-start(bf16[64,3,4096]{2,0,1:T(8,128)(2,1)} %param.6) | copy-start | bytes 4718596
  40.7 17.6 %all-to-all-start.1 = ((bf16[8,128,256]{2,1,0:T(8,128)(2,1)}), bf16[8,128,256]{2,1,0:T(8,128)(2,1)S(1)}, u32[]{:S(2)}, u32[]{:S(2)}) async-start(bf16[8,128,256]{2,1,0:T(8,128)(2,1)} %convolve.1), calls=%async_computation.1 | async-start | bytes 1048576 | tf_op jit(solution)/shard_map/all_to_all | solution.py:536
  44.4 1.9 %collective-permute-start = (bf16[64,1024]{1,0:T(8,128)(2,1)S(1)}, bf16[64,1024]{1,0:T(8,128)(2,1)S(1)}, u32[]{:S(2)}, u32[]{:S(2)}) collective-permute-start(bf16[64,1024]{1,0:T(8,128)(2,1)S(1)} %get-tuple-element.23), channel_id=1, source_target_pairs={{0,1},{1,0},{2,3},{3,2},{4,5},{5,4},{6,7},{7,6},{8,9},{9,8},{10,11... | collective-permute-start | bytes 393224 | tf_op jit(solution)/shard_map/ppermute | solution.py:430
  44.4 6.4 %collective-permute-start.1 = (bf16[64,1024]{1,0:T(8,128)(2,1)S(1)}, bf16[64,1024]{1,0:T(8,128)(2,1)S(1)}, u32[]{:S(2)}, u32[]{:S(2)}) collective-permute-start(bf16[64,1024]{1,0:T(8,128)(2,1)S(1)} %get-tuple-element.24), channel_id=1, source_target_pairs={{0,2},{1,3},{2,0},{3,1},{4,6},{5,7},{6,4},{7,5},{8,10},{9,11},{10,... | collective-permute-start | bytes 393224 | tf_op jit(solution)/shard_map/ppermute | solution.py:430
  46.0 6.7 %collective-permute-start.2 = (bf16[64,1024]{1,0:T(8,128)(2,1)S(1)}, bf16[64,1024]{1,0:T(8,128)(2,1)S(1)}, u32[]{:S(2)}, u32[]{:S(2)}) collective-permute-start(bf16[64,1024]{1,0:T(8,128)(2,1)S(1)} %get-tuple-element.25), channel_id=1, source_target_pairs={{0,3},{1,2},{2,1},{3,0},{4,7},{5,6},{6,5},{7,4},{8,11},{9,10},{10,... | collective-permute-start | bytes 393224 | tf_op jit(solution)/shard_map/ppermute | solution.py:430
